TPU v7x, 256 devices: a whole 4x4x8 slice. The times are simulated.
256 devices in a mesh: ord: 8 (over y, core), lat: 16 (over x, z_lo), lev: 2 (over z_hi).
Axes of the slice: x: 4, y: 4, z: 8 (z_hi: 2, z_lo: 4; z = z_hi * 4 + z_lo), core: 2. Of those that a mesh axis runs over, the one named last changes fastest.
Arguments:
- spectral_state: float32 [720, 720, 16, 7, 2], P('ord', 'lat', 'lev'), may hold values from -6 to 6
- legendre: bfloat16 [720, 720, 720], P('ord', 'lat'), may hold values from -0.21875 to 0.21875
- quad_weight: float32 [720], P('lat'), may hold values from 0.5 to 2
- weight_in: bfloat16 [112, 256], replicated, may hold values from -0.5 to 0.5
- bias_in: float32 [256], replicated, may hold values from -3 to 3
- weight_hidden: bfloat16 [4, 256, 256], replicated, may hold values from -0.375 to 0.375
- weight_out: bfloat16 [256, 112], replicated, may hold values from -0.375 to 0.375
Outputs:
- new_state: float32 [720, 720, 16, 7, 2], P('ord', 'lat', 'lev')
All inputs are finite; a program needn't handle non-finite values.
Results may differ from a plain program's by a relative error of at most 0.017.
Values may be sent and summed in bfloat16 or wider, within the bound.
No kernel may reach another device: no remote copies, remote signals or barrier semaphores. Data moves between devices by JAX's collectives and lax.ppermute only.
A program may use at most 128 MiB of HBM per device.

v0:
```python
import math

import jax
import jax.numpy as jnp
from jax import lax
from jax.sharding import PartitionSpec as P

L = 720
NLON = 1440


time_step = 1.0
hyper_rate = 2.0


def fourier_lookup(order_ids, lon_ids):
    phase_index = order_ids[:, None] * lon_ids[None, :] % NLON
    angles = 2.0 * math.pi / NLON * phase_index.astype(jnp.float32)
    return jnp.stack([jnp.cos(angles), -jnp.sin(angles)], axis=1).astype(jnp.bfloat16)


def column_network(features, weight_in, bias_in, weight_hidden, weight_out):
    hidden = jax.nn.silu(
        jnp.dot(features, weight_in, preferred_element_type=jnp.float32) + bias_in
    ).astype(jnp.bfloat16)
    for layer_index in range(weight_hidden.shape[0]):
        update = jax.nn.silu(
            jnp.dot(hidden, weight_hidden[layer_index], preferred_element_type=jnp.float32)
        )
        hidden = (hidden.astype(jnp.float32) + update).astype(jnp.bfloat16)
    return jnp.dot(hidden, weight_out, preferred_element_type=jnp.float32).astype(jnp.bfloat16)


def on_device(spectral_state, legendre, quad_weight, weight_in, bias_in, weight_hidden, weight_out):
    ord_size = lax.axis_size("ord")
    lev_size = lax.axis_size("lev")
    order_local, degree_local, lev_local, field_count, part_count = spectral_state.shape
    lat_local = quad_weight.shape[0]
    row_count = lev_local * field_count
    channel_count = row_count * part_count
    row_share = row_count // ord_size
    order_ids = lax.axis_index("ord") * order_local + lax.iota(jnp.int32, order_local)
    degree_ids = lax.axis_index("lat") * degree_local + lax.iota(jnp.int32, degree_local)
    keep_mask = (degree_ids[None, :] >= order_ids[:, None]).astype(jnp.float32)
    coefficients = (
        (spectral_state * keep_mask[:, :, None, None, None])
        .reshape(order_local, degree_local, channel_count)
        .astype(jnp.bfloat16)
    )
    lookup_rows = legendre
    fourier = lax.psum_scatter(
        jnp.einsum(
            "mlj,mlc->jmc", lookup_rows, coefficients, preferred_element_type=jnp.float32
        ).astype(jnp.bfloat16),
        "lat",
        scatter_dimension=0,
        tiled=True,
    ).astype(jnp.float32)
    fourier = fourier.astype(jnp.bfloat16).reshape(lat_local, order_local, row_count, part_count)
    transform_scale = math.sqrt(2.0 / NLON)
    lon_block = NLON // (ord_size * lev_size)
    full_lookup = fourier_lookup(lax.iota(jnp.int32, L), lax.iota(jnp.int32, NLON))
    raw_grid = jnp.einsum(
        "jmrp,mpx->xjr",
        lax.all_to_all(fourier, "ord", split_axis=2, concat_axis=1, tiled=True),
        full_lookup,
        preferred_element_type=jnp.float32,
    )
    grid_values = (transform_scale * raw_grid).astype(jnp.bfloat16)
    blocks = grid_values.reshape(ord_size, lev_size, lon_block, lat_local, 1, 1, row_share)
    columns = lax.all_to_all(
        lax.all_to_all(blocks, "ord", split_axis=0, concat_axis=5, tiled=True),
        "lev",
        split_axis=1,
        concat_axis=4,
        tiled=True,
    )
    columns = columns.reshape(lon_block * lat_local, row_count * lev_size)
    tendency = column_network(columns, weight_in, bias_in, weight_hidden, weight_out)
    tendency = tendency.reshape(lon_block, lat_local, row_count * lev_size)
    weight_rows = transform_scale * quad_weight[None, :, None, None]
    pieces = tendency.reshape(1, 1, lon_block, lat_local, lev_size, ord_size, row_share)
    returned = lax.all_to_all(
        lax.all_to_all(pieces, "ord", split_axis=5, concat_axis=0, tiled=True),
        "lev",
        split_axis=4,
        concat_axis=1,
        tiled=True,
    )
    returned = returned.reshape(NLON, lat_local, row_share)
    spectral_sums = jnp.einsum(
        "xjr,mpx->mjrp", returned, full_lookup, preferred_element_type=jnp.float32
    )
    weighted = (weight_rows * spectral_sums).astype(jnp.bfloat16)
    weighted = lax.all_to_all(weighted, "ord", split_axis=0, concat_axis=2, tiled=True)
    weighted = weighted.reshape(order_local, lat_local, channel_count)
    lookup_rows = legendre
    forcing = jnp.einsum(
        "mlj,mjc->mlc",
        lookup_rows,
        lax.all_gather(weighted, "lat", axis=1, tiled=True),
        preferred_element_type=jnp.float32,
    )
    degree_ratio = (degree_ids * (degree_ids + 1)).astype(jnp.float32) / ((L - 1) * L)
    damping = 1.0 / (1.0 + hyper_rate * degree_ratio * degree_ratio)
    updated = (
        keep_mask[:, :, None, None, None]
        * (spectral_state + time_step * forcing.reshape(spectral_state.shape))
        * damping[None, :, None, None, None]
    )
    return updated


def solution(mesh):
    return jax.shard_map(
        on_device,
        mesh=mesh,
        in_specs=(
            P("ord", "lat", "lev", None, None),
            P("ord", "lat", None),
            P("lat"),
            P(),
            P(),
            P(),
            P(),
        ),
        out_specs=P("ord", "lat", "lev", None, None),
        check_vma=False,
    )
```

profile of v0, /device:TPU:2, one launch (start us, length us, event | category | flops | bytes accessed | tf_op | source)
XLA Modules:
  0.0 1081.0 jit_solution(2956616006874107157)
XLA Ops:
  6.6 2.8 multiply_convert_fusion.1
  10.8 12.5 %convert_bitcast_fusion = bf16[720,90,112]{0,2,1:T(8,128)(2,1)} fusion(bf16[90,45,112]{2,1,0:T(8,128)(2,1)S(1)} %copy.68, bf16[90,45,720]{2,1,0:T(8,128)(2,1)} %param.8), kind=kOutput, calls=%fused_computation.2 | convolution fusion | flops 660441600 | bytes 21254400 | tf_op jit(solution)/shard_map/mlj,mlc->jmc/dot_general | solution.py:52
  23.3 23.7 %copy.69 = bf16[720,90,112]{2,1,0:T(8,128)(2,1)} copy(bf16[720,90,112]{0,2,1:T(8,128)(2,1)} %convert_bitcast_fusion) | data formatting | bytes 29030400 | tf_op jit(solution)/shard_map/convert_element_type | solution.py:54
  47.0 374.9 %reduce-scatter.2.cloned.1.call-done = bf16[45,90,112]{2,1,0:T(8,128)(2,1)} async-done(((bf16[720,90,112]{2,1,0:T(8,128)(2,1)}), bf16[45,90,112]{2,1,0:T(8,128)(2,1)}) %reduce-scatter.2.cloned.1.call-update) | async-done | bytes 907216 | tf_op jit(solution)/shard_map/reduce_scatter | solution.py:51
  426.1 4.5 all-to-all-start
  430.6 20.0 %negate_convert_fusion = (bf16[720,1,1440]{2,0,1:T(8,128)(2,1)}, bf16[720,1,1440]{2,0,1:T(8,128)(2,1)}) fusion(), kind=kLoop, calls=%fused_computation.13 | loop fusion | flops 12441600 | bytes 4147200 | tf_op jit(solution)/shard_map/convert.1
  452.1 4.1 fusion.17
  456.2 2.7 reshape.129
  459.8 23.3 %all_to_all.99 = bf16[8,2,90,45,1,1,7]{2,1,6,5,4,3,0:T(2,128)(2,1)S(1)} all-to-all(bf16[8,2,90,45,1,1,7]{2,1,6,5,4,3,0:T(2,128)(2,1)S(1)} %copy.75), channel_id=1, replica_groups=mesh['ord'=8,'lat'=16,'lev'=2] {'ord'}, dimensions={0} | all-to-all | bytes 1814400 | tf_op jit(solution)/shard_map/all_to_all | solution.py:72
  483.3 39.0 %all_to_all.100 = bf16[1,2,90,45,1,8,7]{2,5,6,4,3,0,1:T(8,128)(2,1)} all-to-all(bf16[1,2,90,45,1,8,7]{2,5,6,4,3,0,1:T(8,128)(2,1)S(1)} %copy.76), channel_id=1, replica_groups=mesh['ord'=8,'lat'=16,'lev'=2] {'lev'}, dimensions={1} | all-to-all | bytes 1814400 | tf_op jit(solution)/shard_map/all_to_all | solution.py:71
  522.3 4.2 copy.77
  526.5 5.0 reshape.130
  531.5 2.6 multiply_convert_fusion
  534.7 3.4 add_convert_fusion.2
  538.1 2.7 fusion.34
  540.8 8.2 convolution_convert_fusion
  549.1 8.5 reshape_reshape.3
  557.6 3.9 copy.78
  561.5 22.3 %all_to_all.101 = bf16[1,1,90,45,2,8,7]{2,4,6,3,1,0,5:T(2,128)(2,1)S(1)} all-to-all(bf16[1,1,90,45,2,8,7]{2,4,6,3,1,0,5:T(2,128)(2,1)} %copy.78), channel_id=1, replica_groups=mesh['ord'=8,'lat'=16,'lev'=2] {'ord'}, dimensions={5} | all-to-all | bytes 1814400 | tf_op jit(solution)/shard_map/all_to_all | solution.py:84
  585.0 3.6 all-to-all-start.4
  588.7 33.6 %all-to-all-done.4 = bf16[8,1,90,45,2,1,7]{2,0,6,5,3,1,4:T(8,128)(2,1)S(1)} async-done(((bf16[8,1,90,45,2,1,7]{2,0,6,5,3,1,4:T(8,128)(2,1)}), bf16[8,1,90,45,2,1,7]{2,0,6,5,3,1,4:T(8,128)(2,1)S(1)}, u32[]{:S(2)}, u32[]{:S(2)}) %all-to-all-start.4) | async-done | bytes 907232 | tf_op jit(solution)/shard_map/all_to_all | solution.py:83
  625.3 5.1 fusion.25
  630.4 7.5 copy.81
  637.8 3.5 reshape.139
  641.3 17.7 %all_to_all.102 = bf16[8,2,28350]{2,1,0:T(2,128)(2,1)} all-to-all(bf16[8,2,28350]{2,1,0:T(2,128)(2,1)S(1)} %reshape.139), channel_id=1, replica_groups=mesh['ord'=8,'lat'=16,'lev'=2] {'ord'}, dimensions={0} | all-to-all | bytes 1814400 | tf_op jit(solution)/shard_map/all_to_all | solution.py:95
  659.0 5.1 reshape.140
  664.2 4.9 copy.91
  669.0 2.3 copy.83
  673.4 367.5 %all-gather.2.cloned.1.call-done = bf16[90,720,112]{2,0,1:T(8,128)(2,1)} async-done(((bf16[90,45,112]{2,0,1:T(8,128)(2,1)}), bf16[90,720,112]{2,0,1:T(8,128)(2,1)}) %all-gather.2.cloned.1.call-update) | async-done | bytes 14515216 | tf_op jit(solution)/shard_map/all_gather | solution.py:101
  1040.9 24.0 %fusion.20 = f32[90,45,112]{2,1,0:T(8,128)} fusion(bf16[90,45,720]{2,1,0:T(8,128)(2,1)} %param.8, bf16[90,720,112]{2,0,1:T(8,128)(2,1)} %all-gather.2.cloned.1.call-done), kind=kOutput, calls=%fused_computation.30 | convolution fusion | flops 653184000 | bytes 22161600 | tf_op jit(solution)/shard_map/mlj,mjc->mlc/dot_general | solution.py:98
  1064.9 3.3 copy.86
  1068.2 5.7 multiply_multiply_fusion
  (40 shorter events, 15.1 us)
Async XLA Ops:
  6.5 524.9 %copy-start = (bf16[112,256]{1,0:T(8,128)(2,1)S(1)}, bf16[112,256]{1,0:T(8,128)(2,1)}, u32[]{:S(2)}) copy-start(bf16[112,256]{1,0:T(8,128)(2,1)} %param.10) | copy-start | bytes 172036
  6.5 415.4 %reduce-scatter.2.cloned.1.call-start = ((), (), s32[]{:S(2)}) async-start(), calls=%async_computation.7 | async-start | bytes 18800640 | tf_op jit(solution)/shard_map/reduce_scatter | solution.py:51
  6.6 2.8 copy-start.3
  426.1 24.5 %all-to-all-start = ((bf16[45,90,56,2]{1,3,0,2:T(2,128)(2,1)}), bf16[45,90,56,2]{1,3,0,2:T(2,128)(2,1)S(1)}, u32[]{:S(2)}, u32[]{:S(2)}) async-start(bf16[45,90,56,2]{1,3,0,2:T(2,128)(2,1)} %copy.71), calls=%async_computation.1 | async-start | bytes 2580480 | tf_op jit(solution)/shard_map/all_to_all | solution.py:65
  522.3 9.2 copy-start.7
  531.5 2.6 copy-start.5
  538.1 2.7 copy-start.6
  561.5 27.2 %copy-start.8 = (f32[45]{0:T(128)S(1)}, f32[45]{0:T(128)}, u32[]{:S(2)}) copy-start(f32[45]{0:T(128)} %param.9) | copy-start | bytes 544
  585.0 37.3 %all-to-all-start.4 = ((bf16[8,1,90,45,2,1,7]{2,0,6,5,3,1,4:T(8,128)(2,1)}), bf16[8,1,90,45,2,1,7]{2,0,6,5,3,1,4:T(8,128)(2,1)S(1)}, u32[]{:S(2)}, u32[]{:S(2)}) async-start(bf16[8,1,90,45,2,1,7]{2,0,6,5,3,1,4:T(8,128)(2,1)} %copy.79), calls=%async_computation.5 | async-start | bytes 2580480 | tf_op jit(solution)/shard_map/all_to_all | solution.py:83
  588.7 452.3 %all-gather.2.cloned.1.call-start = ((), (), s32[]{:S(2)}) async-start(), calls=%async_computation.8 | async-start | bytes 18800640 | tf_op jit(solution)/shard_map/all_gather | solution.py:101
  1064.9 3.4 copy-start.2
  1064.9 3.4 copy-start.4
  1064.9 9.1 copy-start.1
Sparse Core Ops, SparseCore 0:
  47.1 374.7 reduce-scatter.1
  673.5 367.3 all-gather.1
where the time goes:
time: 1090 us; the launch traced here: 1080 us
  waiting for transfers between devices  776 us (71%)
  blocking collectives  102 us (9%)
  local copies, waits for them, and re-layouts  88.9 us (8%)
  matrix products  63.1 us (6%)
  other arithmetic  28.6 us (3%)
  between operations  13.8 us (1%)
    reduce_scatter x1, waiting for transfers between devices, on_device(): lax.psum_scatter(jnp.einsum('mlj,mlc->jmc', lookup_rows, coefficients, pr...  375 us
    all_gather x1, waiting for transfers between devices, on_device(): lax.all_gather(weighted, 'lat', axis=1, tiled=True)  368 us
    all_to_all x1, blocking collectives, on_device(): lax.all_to_all(lax.all_to_all(blocks, 'ord', split_axis=0, concat_axis=5,...  39 us
    all_to_all x1, waiting for transfers between devices, on_device(): lax.all_to_all(lax.all_to_all(pieces, 'ord', split_axis=5, concat_axis=0,...  33.6 us
    dot_general x1, matrix products, on_device(): jnp.einsum('mlj,mjc->mlc', lookup_rows, lax.all_gather(weighted, 'lat', a...  24 us
    convert_element_type x1, local copies, waits for them, and re-layouts, on_device(): fourier = lax.psum_scatter(jnp.einsum('mlj,mlc->jmc', lookup_rows, coeffi...  23.7 us
    all_to_all x1, blocking collectives, on_device(): lax.all_to_all(blocks, 'ord', split_axis=0, concat_axis=5, tiled=True)  23.3 us
    all_to_all x1, blocking collectives, on_device(): lax.all_to_all(pieces, 'ord', split_axis=5, concat_axis=0, tiled=True)  22.3 us
  transfers between devices with their start and end apart: 4, of which 3 were waited for; matrix products, arithmetic and copies ran while one was open for 2% of the time, Pallas kernels for 0%

commit v1 on v0

v1 whole, which is shorter than its diff:
```python
import functools
import math

import jax
import jax.numpy as jnp
from jax import lax
from jax.experimental import pallas as pl
from jax.experimental.pallas import tpu as pltpu
from jax.sharding import PartitionSpec as P

L = 720
NLON = 1440
OWN = 3

time_step = 1.0
hyper_rate = 2.0
transform_scale = math.sqrt(2.0 / NLON)


def lookup_of(order_ids, valid):
    phase_index = order_ids[:, None] * lax.iota(jnp.int32, NLON)[None, :] % NLON
    angles = 2.0 * math.pi / NLON * phase_index.astype(jnp.float32)
    keep = valid[:, None]
    return jnp.stack(
        [jnp.where(keep, jnp.cos(angles), 0.0), jnp.where(keep, -jnp.sin(angles), 0.0)]
    ).astype(jnp.bfloat16)


def silu(v):
    return 0.5 * v * (1.0 + jnp.tanh(0.5 * v))


def column_kernel(
    weight_ref, fourier_ref, to_grid_ref, to_orders_ref, w_in_ref, bias_ref, w_hid_ref, w_out_ref,
    out_ref, tendency_ref, *, x_rows, m_rows,
):
    dot = functools.partial(jnp.dot, preferred_element_type=jnp.float32)

    def grid_rows(step, carry):
        rows = pl.ds(pl.multiple_of(step * x_rows, x_rows), x_rows)
        raw = dot(to_grid_ref[0, rows, :], fourier_ref[0, 0]) + dot(
            to_grid_ref[1, rows, :], fourier_ref[0, 1]
        )
        features = (transform_scale * raw).astype(jnp.bfloat16)
        hidden = silu(dot(features, w_in_ref[...]) + bias_ref[...]).astype(jnp.bfloat16)
        for layer in range(w_hid_ref.shape[0]):
            update = silu(dot(hidden, w_hid_ref[layer]))
            hidden = (hidden.astype(jnp.float32) + update).astype(jnp.bfloat16)
        tendency_ref[rows, :] = dot(hidden, w_out_ref[...]).astype(jnp.bfloat16)
        return carry

    lax.fori_loop(0, NLON // x_rows, grid_rows, 0)
    weight = weight_ref[pl.program_id(0)] * transform_scale

    def order_rows(step, carry):
        rows = pl.ds(pl.multiple_of(step * m_rows, m_rows), m_rows)
        for part in range(2):
            sums = dot(to_orders_ref[part, rows, :], tendency_ref[...])
            out_ref[0, part, rows, :] = (weight * sums).astype(jnp.bfloat16)
        return carry

    lax.fori_loop(0, out_ref.shape[2] // m_rows, order_rows, 0)


def columns(weights, fourier, to_grid, to_orders, w_in, bias, w_hid, w_out):
    lats, parts, orders, rows = fourier.shape
    whole = lambda a: pl.BlockSpec(a.shape, lambda i: (0,) * a.ndim)
    mine = pl.BlockSpec((1, parts, orders, rows), lambda i: (i, 0, 0, 0))
    return pl.pallas_call(
        functools.partial(column_kernel, x_rows=288, m_rows=256),
        grid=(lats,),
        in_specs=[pl.BlockSpec(memory_space=pltpu.SMEM), mine]
        + [whole(a) for a in (to_grid, to_orders, w_in, bias, w_hid, w_out)],
        out_specs=mine,
        out_shape=jax.ShapeDtypeStruct(fourier.shape, jnp.bfloat16),
        scratch_shapes=[pltpu.VMEM((NLON, rows), jnp.bfloat16)],
        compiler_params=pltpu.CompilerParams(vmem_limit_bytes=48 * 2**20),
        name="columns",
    )(weights, fourier, to_grid, to_orders, w_in, bias, w_hid, w_out)


def on_device(spectral_state, legendre, quad_weight, weight_in, bias_in, weight_hidden, weight_out):
    ord_size, lat_size, lev_size = (lax.axis_size(a) for a in ("ord", "lat", "lev"))
    ord_at, lat_at, lev_at = (lax.axis_index(a) for a in ("ord", "lat", "lev"))
    order_local, degree_local = spectral_state.shape[:2]
    lat_local = quad_weight.shape[0]
    row_local = spectral_state.shape[2] * spectral_state.shape[3]
    channels = 2 * row_local
    slots = lat_size * OWN
    shift = order_local - slots
    everyone = ("lat", "ord", "lev")

    order_ids = ord_at * order_local + lax.iota(jnp.int32, order_local)
    degree_ids = lat_at * degree_local + lax.iota(jnp.int32, degree_local)
    keep_mask = (degree_ids[None, :] >= order_ids[:, None]).astype(jnp.float32)

    coefficients = (spectral_state * keep_mask[:, :, None, None, None]).astype(jnp.bfloat16)
    coefficients = coefficients.reshape(order_local, degree_local, row_local, 2)
    coefficients = coefficients.swapaxes(2, 3).reshape(order_local, degree_local, channels)
    sent = jnp.concatenate([coefficients[:slots], coefficients[shift:]])
    sent = sent.reshape(lev_size * lat_size, OWN, degree_local, channels)
    coefficients = lax.all_to_all(sent, ("lev", "lat"), 0, 0, tiled=True)
    coefficients = coefficients.reshape(lev_size, lat_size, OWN, degree_local, 2, row_local)
    table = lax.dynamic_slice_in_dim(legendre, lev_at * shift, slots, 0)
    table = table.reshape(lat_size, OWN, degree_local, -1)
    table = lax.all_to_all(table, "lat", 0, 0, tiled=True)

    fourier = jnp.einsum(
        "smlj,vsmlpr->jmpvr", table, coefficients, preferred_element_type=jnp.float32
    ).astype(jnp.bfloat16)
    fourier = fourier.reshape(lat_size, lat_local, OWN, 2, lev_size * row_local)
    lat_slots = ord_size * lev_size * OWN
    fourier = jnp.pad(fourier, ((0, 0), (0, lat_slots - lat_local), (0, 0), (0, 0), (0, 0)))
    fourier = fourier.reshape(-1, OWN, OWN, 2, lev_size * row_local)
    fourier = lax.all_to_all(fourier, everyone, 0, 0, tiled=True)

    slot = lax.iota(jnp.int32, lat_size * ord_size * lev_size * OWN)
    slot_own = slot % OWN
    slot_lev = slot // OWN % lev_size
    slot_ord = slot // (OWN * lev_size) % ord_size
    slot_lat = slot // (OWN * lev_size * ord_size)
    within = slot_lev * shift + slot_lat * OWN + slot_own
    valid = (within >= order_local // 2) == (slot_lev == 1)
    to_orders = lookup_of(slot_ord * order_local + within, valid)
    to_grid = to_orders.swapaxes(1, 2)
    fourier = fourier.transpose(1, 3, 0, 2, 4).reshape(OWN, 2, -1, lev_size * row_local)
    first = (ord_at * lev_size + lev_at) * OWN
    weights = lax.dynamic_slice_in_dim(jnp.pad(quad_weight, (0, lat_slots - lat_local)), first, OWN)
    weighted = columns(
        weights, fourier, to_grid, to_orders, weight_in, bias_in[None, :], weight_hidden, weight_out
    )
    weighted = weighted.reshape(OWN, 2, -1, OWN, lev_size * row_local).transpose(2, 0, 3, 1, 4)

    weighted = lax.all_to_all(weighted, everyone, 0, 0, tiled=True)
    weighted = weighted.reshape(lat_size, lat_slots, OWN, 2, lev_size, row_local)[:, :lat_local]
    weighted = weighted.reshape(-1, OWN, 2, lev_size, row_local)
    forcing = jnp.einsum(
        "smlj,jmpvr->vsmlpr", table, weighted, preferred_element_type=jnp.float32
    ).astype(jnp.bfloat16)
    forcing = forcing.reshape(lev_size * lat_size, OWN, degree_local, channels)
    forcing = lax.all_to_all(forcing, ("lev", "lat"), 0, 0, tiled=True)
    forcing = forcing.reshape(lev_size, slots, degree_local, 2, row_local)
    half = order_local // 2
    forcing = jnp.concatenate([forcing[0, :half], forcing[1, half - shift :]])
    forcing = forcing.swapaxes(2, 3).astype(jnp.float32)

    degree_ratio = (degree_ids * (degree_ids + 1)).astype(jnp.float32) / ((L - 1) * L)
    damping = 1.0 / (1.0 + hyper_rate * degree_ratio * degree_ratio)
    return (
        keep_mask[:, :, None, None, None]
        * (spectral_state + time_step * forcing.reshape(spectral_state.shape))
        * damping[None, :, None, None, None]
    )


def solution(mesh):
    return jax.shard_map(
        on_device,
        mesh=mesh,
        in_specs=(
            P("ord", "lat", "lev", None, None),
            P("ord", "lat", None),
            P("lat"),
            P(),
            P(),
            P(),
            P(),
        ),
        out_specs=P("ord", "lat", "lev", None, None),
        check_vma=False,
    )
```

time: 1090 us -> 349 us (0.32)
  waiting for transfers between devices: 776 us -> 135 us
  matrix products: 63.1 us -> 6.95 us
  blocking collectives: 102 us -> 46.2 us
  Pallas kernels: 0 us -> 29.3 us
  local copies, waits for them, and re-layouts: 88.9 us -> 61.2 us
  starting transfers between devices: 8.14 us -> 30.4 us
  between operations: 13.8 us -> 0.23 us
    reduce_scatter x1 -> x0, waiting for transfers between devices: 375 us -> none  [on_device(): lax.psum_scatter(jnp.einsum('mlj,mlc->jmc', lookup_rows, coefficients, pr...]
    all_gather x1 -> x0, waiting for transfers between devices: 368 us -> none  [on_device(): lax.all_gather(weighted, 'lat', axis=1, tiled=True)]
    all_to_all x2 -> x4, waiting for transfers between devices: 33.6 us -> 135 us  [the longest x1 76.4 us: on_device(): table = lax.all_to_all(table, 'lat', 0, 0, tiled=True)]
    dot_general x9 -> x2, matrix products: 63.1 us -> 6.95 us  [the longest x1 4.95 us: on_device(): jnp.einsum('smlj,vsmlpr->jmpvr', table, coefficients, preferred_element_t...]
    all_to_all x4 -> x1, blocking collectives: 102 us -> 46.2 us  [on_device(): weighted = lax.all_to_all(weighted, everyone, 0, 0, tiled=True)]
    pallas_call x0 -> x1, Pallas kernels: none -> 29.3 us  [columns(): pl.pallas_call(functools.partial(column_kernel, x_rows=288, m_rows=256),...]
    convert_element_type x3 -> x1, local copies, waits for them, and re-layouts: 32.5 us -> 6.48 us  [on_device(): fourier = jnp.einsum('smlj,vsmlpr->jmpvr', table, coefficients, preferred...]
    all_to_all x2 -> x4, starting transfers between devices: 8.1 us -> 30.4 us  [the longest x1 11.6 us: on_device(): coefficients = lax.all_to_all(sent, ('lev', 'lat'), 0, 0, tiled=True)]
  transfers between devices with their start and end apart: 4 -> 4, of which waited for: 3 -> 4; matrix products, arithmetic and copies ran while one was open for 2% -> 12% of each run, Pallas kernels for 0% -> 0%
where the time goes in v1:
time: 349 us; the launch traced here: 348 us
  waiting for transfers between devices  135 us (39%)
  local copies, waits for them, and re-layouts  61.2 us (18%)
  blocking collectives  46.2 us (13%)
  other arithmetic  38.6 us (11%)
  starting transfers between devices  30.4 us (9%)
  Pallas kernels  29.3 us (8%)
  matrix products  6.95 us (2%)
    all_to_all x1, waiting for transfers between devices, on_device(): table = lax.all_to_all(table, 'lat', 0, 0, tiled=True)  76.4 us
    all_to_all x1, blocking collectives, on_device(): weighted = lax.all_to_all(weighted, everyone, 0, 0, tiled=True)  46.2 us
    all_to_all x1, waiting for transfers between devices, on_device(): forcing = lax.all_to_all(forcing, ('lev', 'lat'), 0, 0, tiled=True)  29.7 us
    pallas_call x1, Pallas kernels, columns(): pl.pallas_call(functools.partial(column_kernel, x_rows=288, m_rows=256),...  29.3 us
    all_to_all x1, waiting for transfers between devices, on_device(): coefficients = lax.all_to_all(sent, ('lev', 'lat'), 0, 0, tiled=True)  26.5 us
    another operation x1, other arithmetic  21.4 us
    all_to_all x1, starting transfers between devices, on_device(): coefficients = lax.all_to_all(sent, ('lev', 'lat'), 0, 0, tiled=True)  11.6 us
    all_to_all x1, starting transfers between devices, on_device(): fourier = lax.all_to_all(fourier, everyone, 0, 0, tiled=True)  8.5 us
  transfers between devices with their start and end apart: 4, of which 4 were waited for; matrix products, arithmetic and copies ran while one was open for 12% of the time, Pallas kernels for 0%

profile of v1, /device:TPU:2, one launch (start us, length us, event | category | flops | bytes accessed | tf_op | source)
XLA Modules:
  0.0 347.5 jit_solution(14116429179037366723)
XLA Ops:
  0.1 2.8 multiply_convert_fusion
  2.9 2.0 copy.41
  4.8 2.4 fusion.44
  7.2 2.5 slice.22
  10.4 1.5 copy.42
  11.9 11.6 %all-to-all-start = ((bf16[32,3,45,112]{3,2,1,0:T(8,128)(2,1)}), bf16[32,3,45,112]{3,2,1,0:T(8,128)(2,1)S(1)}, u32[]{:S(2)}, u32[]{:S(2)}) async-start(bf16[32,3,45,112]{3,2,1,0:T(8,128)(2,1)} %bitcast.2), calls=%async_computation | async-start | bytes 2359296 | tf_op jit(solution)/shard_map/all_to_all | solution.py:102
  23.5 4.0 %constant_dynamic-slice_fusion = bf16[48,45,720]{2,1,0:T(8,128)(2,1)} fusion(bf16[90,45,720]{2,1,0:T(8,128)(2,1)} %param.8, s32[]{:T(128)S(6)} %select_n.121), kind=kLoop, calls=%fused_computation.67 | loop fusion | bytes 6220804 | tf_op jit(solution)/shard_map/dynamic_slice | solution.py:104
  27.5 26.5 %all-to-all-done = bf16[32,3,45,112]{3,2,1,0:T(8,128)(2,1)S(1)} async-done(((bf16[32,3,45,112]{3,2,1,0:T(8,128)(2,1)}), bf16[32,3,45,112]{3,2,1,0:T(8,128)(2,1)S(1)}, u32[]{:S(2)}, u32[]{:S(2)}) %all-to-all-start) | async-done | bytes 967712 | tf_op jit(solution)/shard_map/all_to_all | solution.py:102
  55.0 5.3 %all-to-all-start.1 = ((bf16[16,3,45,720]{3,2,1,0:T(8,128)(2,1)}), bf16[16,3,45,720]{3,2,1,0:T(8,128)(2,1)S(1)}, u32[]{:S(2)}, u32[]{:S(2)}) async-start(bf16[16,3,45,720]{3,2,1,0:T(8,128)(2,1)} %bitcast.3), calls=%async_computation.1 | async-start | bytes 7077888 | tf_op jit(solution)/shard_map/all_to_all | solution.py:106
  60.3 5.1 %reshape.310 = bf16[2,16,3,45,2,56]{5,4,3,2,1,0:T(2,128)(2,1)} reshape(bf16[32,3,45,112]{3,2,1,0:T(8,128)(2,1)} %copy-done.6) | data formatting | bytes 1935360 | tf_op jit(solution)/shard_map/reshape | solution.py:103
  65.3 76.4 %all-to-all-done.1 = bf16[16,3,45,720]{3,2,1,0:T(8,128)(2,1)S(1)} async-done(((bf16[16,3,45,720]{3,2,1,0:T(8,128)(2,1)}), bf16[16,3,45,720]{3,2,1,0:T(8,128)(2,1)S(1)}, u32[]{:S(2)}, u32[]{:S(2)}) %all-to-all-start.1) | async-done | bytes 3110432 | tf_op jit(solution)/shard_map/all_to_all | solution.py:106
  141.7 5.0 %fusion.19 = bf16[720,3,2,2,56]{0,4,2,3,1:T(8,128)(2,1)} fusion(bf16[2,16,3,45,2,56]{5,4,3,2,1,0:T(2,128)(2,1)} %reshape.310, bf16[16,3,45,720]{3,2,1,0:T(8,128)(2,1)S(1)} %all-to-all-done.1), kind=kOutput, calls=%fused_computation.21 | convolution fusion | flops 697213440 | bytes 5045760 | tf_op jit(solution)/shard_map/smlj,vsmlpr->jmpvr/dot_general | solution.py:108
  146.7 6.5 %copy.46 = bf16[720,3,2,2,56]{4,3,2,1,0:T(2,128)(2,1)} copy(bf16[720,3,2,2,56]{0,4,2,3,1:T(8,128)(2,1)} %fusion.19) | data formatting | bytes 1935360 | tf_op jit(solution)/shard_map/convert_element_type | solution.py:110
  153.2 5.2 %reshape.293 = bf16[16,45,3,2,112]{4,3,2,1,0:T(2,128)(2,1)S(1)} reshape(bf16[720,3,2,2,56]{4,3,2,1,0:T(2,128)(2,1)} %copy.46) | data formatting | bytes 1935360 | tf_op jit(solution)/shard_map/reshape | solution.py:111
  158.4 2.2 pad.9
  160.6 8.5 %all-to-all-start.2 = ((bf16[256,3,3,2,112]{4,3,2,1,0:T(2,128)(2,1)}), bf16[256,3,3,2,112]{4,3,2,1,0:T(2,128)(2,1)S(1)}, u32[]{:S(2)}, u32[]{:S(2)}) async-start(bf16[256,3,3,2,112]{4,3,2,1,0:T(2,128)(2,1)} %bitcast.8), calls=%async_computation.2 | async-start | bytes 2359296 | tf_op jit(solution)/shard_map/all_to_all | solution.py:115
  169.2 21.4 %select_convert_fusion.1 = (bf16[1,768,1440]{2,1,0:T(8,128)(2,1)S(1)}, bf16[1,768,1440]{2,1,0:T(8,128)(2,1)S(1)}) fusion(s32[768]{0:T(1024)S(1)} %fusion.37, pred[768]{0:T(1024)(128)(4,1)S(1)} %compare_compare_fusion), kind=kLoop, calls=%fused_computation.5 | loop fusion | flops 15482880 | bytes 4427520 | tf_op jit(solution)/shard_map/convert.2
  190.6 4.3 %pad_maximum_fusion = (bf16[2,768,1440]{2,1,0:T(8,128)(2,1)}, bf16[2,1440,768]{1,2,0:T(8,128)(2,1)}) fusion(bf16[1,768,1440]{2,1,0:T(8,128)(2,1)S(1)} %get-tuple-element.12, bf16[1,768,1440]{2,1,0:T(8,128)(2,1)S(1)} %get-tuple-element.11), kind=kLoop, calls=%fused_computation.3 | loop fusion | flops 2211840 | bytes 13271040 | tf_op jit(solution)/shard_map/stack | solution.py:24
  194.9 6.7 %copy.49.to_grid_ref = bf16[2,1440,768]{2,1,0:T(8,128)(2,1)} copy(bf16[2,1440,768]{1,2,0:T(8,128)(2,1)} %get-tuple-element.6) | data formatting | bytes 8847360 | tf_op jit(solution)/shard_map/transpose | solution.py:125
  201.8 2.0 all-to-all-done.2
  204.8 29.3 %columns.1 = bf16[3,2,768,112]{3,2,1,0:T(8,128)(2,1)S(1)} custom-call(f32[3]{0:T(128)S(1)} %pad_dynamic-slice_fusion.weight_ref, bf16[3,2,768,112]{3,2,1,0:T(8,128)(2,1)S(1)} %copy.48.fourier_ref, bf16[2,1440,768]{2,1,0:T(8,128)(2,1)} %copy.49.to_grid_ref, bf16[2,768,1440]{2,1,0:T(8,128)(2,1)} %get-tuple-element.5.to_orders_ref, ...), custom_call_target="tpu_custom_call" | custom-call | tf_op jit(solution)/shard_map/columns/pallas_call | solution.py:69
  236.1 46.2 %all_to_all.25 = bf16[256,3,3,2,112]{4,3,2,1,0:T(2,128)(2,1)S(1)} all-to-all(bf16[256,3,3,2,112]{4,3,2,1,0:T(2,128)(2,1)S(1)} %copy.52), channel_id=1, replica_groups=mesh['ord'=8,'lat'=16,'lev'=2] {'lat','ord','lev'}, dimensions={0} | all-to-all | bytes 2064384 | tf_op jit(solution)/shard_map/all_to_all | solution.py:134
  283.4 1.5 slice.30
  285.4 2.0 convert_bitcast_fusion.1
  287.4 3.0 copy.71
  290.4 2.4 reshape.311
  292.8 5.1 %all-to-all-start.4 = ((bf16[32,3,45,112]{3,2,1,0:T(8,128)(2,1)}), bf16[32,3,45,112]{3,2,1,0:T(8,128)(2,1)S(1)}, u32[]{:S(2)}, u32[]{:S(2)}) async-start(bf16[32,3,45,112]{3,2,1,0:T(8,128)(2,1)} %reshape.311), calls=%async_computation.4 | async-start | bytes 2359296 | tf_op jit(solution)/shard_map/all_to_all | solution.py:141
  297.9 29.7 %all-to-all-done.4 = bf16[32,3,45,112]{3,2,1,0:T(8,128)(2,1)S(1)} async-done(((bf16[32,3,45,112]{3,2,1,0:T(8,128)(2,1)}), bf16[32,3,45,112]{3,2,1,0:T(8,128)(2,1)S(1)}, u32[]{:S(2)}, u32[]{:S(2)}) %all-to-all-start.4) | async-done | bytes 967712 | tf_op jit(solution)/shard_map/all_to_all | solution.py:141
  328.6 1.5 slice_bitcast_fusion.1
  330.1 4.6 %convert_bitcast_fusion = f32[90,45,56,2]{2,3,1,0:T(2,128)} fusion(bf16[45,45,2,56]{3,2,1,0:T(2,128)(2,1)S(1)} %get-tuple-element.8, bf16[45,45,2,56]{3,2,1,0:T(2,128)(2,1)S(1)} %get-tuple-element.7), kind=kLoop, calls=%fused_computation.10 | loop fusion | flops 907200 | bytes 2721600 | tf_op jit(solution)/shard_map/reshape | solution.py:151
  334.7 7.6 %copy.57 = f32[90,45,56,2]{0,3,2,1:T(2,128)} copy(f32[90,45,56,2]{2,3,1,0:T(2,128)} %convert_bitcast_fusion) | data formatting | bytes 3628800 | tf_op jit(solution)/shard_map/reshape | solution.py:151
  342.3 5.2 %multiply_multiply_fusion = f32[90,45,8,7,2]{0,4,3,2,1:T(2,128)} fusion(f32[90,45,8,7,2]{0,4,3,2,1:T(2,128)S(1)} %copy-done.5, f32[90,45,8,7,2]{0,4,3,2,1:T(2,128)} %bitcast.45, f32[45]{0:T(128)S(1)} %add_divide_fusion, f32[90,45]{0,1:T(8,128)S(1)} %copy-done.8), kind=kLoop, calls=%fused_computation.15 | loop fusion | flops 1360800 | bytes 5459580 | tf_op jit(solution)/shard_map/mul | solution.py:150
  (38 shorter events, 7.6 us)
Async XLA Ops:
  0.1 2.8 copy-start.7
  11.9 42.1 %all-to-all-start = ((bf16[32,3,45,112]{3,2,1,0:T(8,128)(2,1)}), bf16[32,3,45,112]{3,2,1,0:T(8,128)(2,1)S(1)}, u32[]{:S(2)}, u32[]{:S(2)}) async-start(bf16[32,3,45,112]{3,2,1,0:T(8,128)(2,1)} %bitcast.2), calls=%async_computation | async-start | bytes 2359296 | tf_op jit(solution)/shard_map/all_to_all | solution.py:102
  54.0 1.0 copy-start.6
  55.0 86.7 %all-to-all-start.1 = ((bf16[16,3,45,720]{3,2,1,0:T(8,128)(2,1)}), bf16[16,3,45,720]{3,2,1,0:T(8,128)(2,1)S(1)}, u32[]{:S(2)}, u32[]{:S(2)}) async-start(bf16[16,3,45,720]{3,2,1,0:T(8,128)(2,1)} %bitcast.3), calls=%async_computation.1 | async-start | bytes 7077888 | tf_op jit(solution)/shard_map/all_to_all | solution.py:106
  141.7 5.0 %copy-start.3 = (bf16[16,3,45,720]{3,2,1,0:T(8,128)(2,1)}, bf16[16,3,45,720]{3,2,1,0:T(8,128)(2,1)S(1)}, u32[]{:S(2)}) copy-start(bf16[16,3,45,720]{3,2,1,0:T(8,128)(2,1)S(1)} %all-to-all-done.1) | copy-start | bytes 9331204
  160.6 43.1 %all-to-all-start.2 = ((bf16[256,3,3,2,112]{4,3,2,1,0:T(2,128)(2,1)}), bf16[256,3,3,2,112]{4,3,2,1,0:T(2,128)(2,1)S(1)}, u32[]{:S(2)}, u32[]{:S(2)}) async-start(bf16[256,3,3,2,112]{4,3,2,1,0:T(2,128)(2,1)} %bitcast.8), calls=%async_computation.2 | async-start | bytes 2359296 | tf_op jit(solution)/shard_map/all_to_all | solution.py:115
  194.9 6.7 %copy-start.9 = (bf16[256,112]{0,1:T(8,128)(2,1)S(1)}, bf16[256,112]{0,1:T(8,128)(2,1)}, u32[]{:S(2)}) copy-start(bf16[256,112]{0,1:T(8,128)(2,1)} %param.13) | copy-start | bytes 172036
  194.9 6.8 %copy-start.10 = (f32[45]{0:T(128)S(1)}, f32[45]{0:T(128)}, u32[]{:S(2)}) copy-start(f32[45]{0:T(128)} %param.9) | copy-start | bytes 544
  203.8 1.0 copy-start
  203.8 1.0 copy-start.1
  203.8 1.0 copy-start.2
  283.4 2.0 copy-start.4
  292.8 34.8 %all-to-all-start.4 = ((bf16[32,3,45,112]{3,2,1,0:T(8,128)(2,1)}), bf16[32,3,45,112]{3,2,1,0:T(8,128)(2,1)S(1)}, u32[]{:S(2)}, u32[]{:S(2)}) async-start(bf16[32,3,45,112]{3,2,1,0:T(8,128)(2,1)} %reshape.311), calls=%async_computation.4 | async-start | bytes 2359296 | tf_op jit(solution)/shard_map/all_to_all | solution.py:141
  334.7 7.6 %copy-start.5 = (f32[90,45,8,7,2]{0,4,3,2,1:T(2,128)S(1)}, f32[90,45,8,7,2]{0,4,3,2,1:T(2,128)}, u32[]{:S(2)}) copy-start(f32[90,45,8,7,2]{0,4,3,2,1:T(2,128)} %param.7) | copy-start | bytes 5443204
  334.7 7.6 %copy-start.8 = (f32[90,45]{0,1:T(8,128)S(1)}, f32[90,45]{0,1:T(8,128)}, u32[]{:S(2)}) copy-start(f32[90,45]{0,1:T(8,128)} %copy-done.7) | copy-start | bytes 48604

commit v2 on v1

v2 whole, which is shorter than its diff:
```python
import functools
import math

import jax
import jax.numpy as jnp
import numpy as np
from jax import lax
from jax.experimental import pallas as pl
from jax.experimental.pallas import tpu as pltpu
from jax.sharding import PartitionSpec as P

L = 720
NLON = 1440
OWN = 3
LANES = 128
SPARE = 14

time_step = 1.0
hyper_rate = 2.0
transform_scale = math.sqrt(2.0 / NLON)

f32, bf16 = jnp.float32, jnp.bfloat16
dot = functools.partial(jnp.dot, preferred_element_type=jnp.float32)


def lookup_of(order_ids, valid):
    phase_index = order_ids[:, None] * lax.iota(jnp.int32, NLON)[None, :] % NLON
    angles = 2.0 * math.pi / NLON * phase_index.astype(f32)
    keep = valid[:, None]
    return jnp.stack(
        [jnp.where(keep, jnp.cos(angles), 0.0), jnp.where(keep, -jnp.sin(angles), 0.0)]
    ).astype(bf16)


def silu(v):
    return 0.5 * v * (1.0 + jnp.tanh(0.5 * v))


def lane_maps(levs, row_local):
    maps = np.zeros((levs, 2 * LANES, 2 * row_local), np.float32)
    for lev in range(levs):
        for row in range(row_local):
            for part in range(2):
                maps[lev, part * LANES + lev * row_local + row, 2 * row + part] = 1.0
    return jnp.asarray(maps, bf16)


def pack_rows(slab_of, out_ref, scr_ref, peers, width):
    lane = lax.broadcasted_iota(jnp.int32, (peers, LANES), 1)
    spare = (lane >= width) & (lane < width + SPARE)
    for part in range(2):
        last = slab_of(part, 2, 2)
        for k in range(8):
            moved = pltpu.roll(last, (width - SPARE * k) % LANES, 1)
            scr_ref[part, pl.ds(k, peers, 8), :] = jnp.where(
                spare, moved, slab_of(part, k // OWN, k % OWN)
            )
        out_ref[:, part * LANES : (part + 1) * LANES] = scr_ref[part].astype(bf16)


def unpack_rows(in_ref, scr_ref, put_slab, peers, width):
    lane = lax.broadcasted_iota(jnp.int32, (peers, LANES), 1)
    for part in range(2):
        scr_ref[part] = in_ref[:, part * LANES : (part + 1) * LANES].astype(f32)
        last = jnp.zeros((peers, LANES), f32)
        for k in range(8):
            slab = scr_ref[part, pl.ds(k, peers, 8), :]
            put_slab(part, k // OWN, k % OWN, slab)
            moved = pltpu.roll(slab, (SPARE * k - width) % LANES, 1)
            last = jnp.where((lane >= SPARE * k) & (lane < SPARE * (k + 1)), moved, last)
        put_slab(part, 2, 2, last)


def prep_kernel(at_ref, state_ref, out_ref, scr_ref, *, degrees):
    orders = state_ref.shape[2]
    slots = out_ref.shape[1]
    step = pl.program_id(0) * 8
    order = lax.broadcasted_iota(jnp.int32, state_ref.shape[1:], 1) + at_ref[0]
    for i in range(8):
        degree = step + i
        keep = (degree + at_ref[1] >= order) & (degree < degrees)
        scr_ref[pl.ds(i, orders, 8), :] = jnp.where(keep, state_ref[i], 0.0).T
    rows = scr_ref[...].astype(bf16).reshape(orders, 8, -1)
    out_ref[0] = rows[:slots]
    out_ref[1] = rows[orders - slots :]


def prep(at, state, slots):
    degrees, channels, orders = state.shape
    padded = -(-degrees // 8) * 8
    return pl.pallas_call(
        functools.partial(prep_kernel, degrees=degrees),
        grid=(padded // 8,),
        in_specs=[
            pl.BlockSpec(memory_space=pltpu.SMEM),
            pl.BlockSpec((8, channels, orders), lambda i: (i, 0, 0)),
        ],
        out_specs=pl.BlockSpec((2, slots, 8, channels), lambda i: (0, 0, i, 0)),
        out_shape=jax.ShapeDtypeStruct((2, slots, padded, channels), bf16),
        scratch_shapes=[pltpu.VMEM((orders * 8, channels), f32)],
        cost_estimate=pl.CostEstimate(flops=10**6, bytes_accessed=4 * 10**6, transcendentals=0),
        name="prep",
    )(at, state)


def table_kernel(at_ref, in_ref, out_ref):
    out_ref[...] = jnp.zeros_like(out_ref)
    out_ref[:, : in_ref.shape[1], : in_ref.shape[2]] = in_ref[...]


def table_part(block_at, legendre, slots):
    _, degrees, lats = legendre.shape
    padded, lanes = -(-degrees // 8) * 8, -(-lats // LANES) * LANES
    return pl.pallas_call(
        table_kernel,
        grid_spec=pltpu.PrefetchScalarGridSpec(
            num_scalar_prefetch=1,
            grid=(slots // OWN,),
            in_specs=[pl.BlockSpec((OWN, degrees, lats), lambda i, at: (at[0] + i, 0, 0))],
            out_specs=pl.BlockSpec((OWN, padded, lanes), lambda i, at: (i, 0, 0)),
        ),
        out_shape=jax.ShapeDtypeStruct((slots, padded, lanes), bf16),
        name="table",
    )(block_at, legendre)


def inverse_kernel(
    table_ref, coef_ref, maps_ref, out_ref, sums_ref, scr_ref, *, lats, lat_local, lat_slots, width
):
    m = pl.program_id(0)
    degrees = table_ref.shape[0] * table_ref.shape[1]
    table = table_ref[...].reshape(degrees, -1)
    swapped = sum(
        lax.dot_general(
            maps_ref[v],
            coef_ref[v].reshape(degrees, -1),
            (((1,), (1,)), ((), ())),
            preferred_element_type=f32,
        )
        for v in range(maps_ref.shape[0])
    ).astype(bf16)
    sums = dot(swapped, table).T
    for part in range(2):
        lanes = slice(part * LANES, (part + 1) * LANES)
        for lat in range(lats):
            sums_ref[m, part, lat * lat_slots : lat * lat_slots + lat_local, :] = sums[
                lat * lat_local : (lat + 1) * lat_local, lanes
            ]
            sums_ref[m, part, lat * lat_slots + lat_local : (lat + 1) * lat_slots, :] = jnp.zeros(
                (lat_slots - lat_local, LANES), f32
            )

    @pl.when(m == OWN - 1)
    def _():
        peers = out_ref.shape[0] // 8
        slab_of = lambda part, i, m: sums_ref[m, part, pl.ds(i, peers, OWN), :]
        pack_rows(slab_of, out_ref, scr_ref, peers, width)


def inverse(table, coef, maps, peers, lat_local, lat_slots, width):
    lats, _, padded, lanes = table.shape
    levs, channels = coef.shape[0], coef.shape[-1]
    return pl.pallas_call(
        functools.partial(
            inverse_kernel, lats=lats, lat_local=lat_local, lat_slots=lat_slots, width=width
        ),
        grid=(OWN,),
        in_specs=[
            pl.BlockSpec((lats, None, padded, lanes), lambda m: (0, m, 0, 0)),
            pl.BlockSpec((levs, lats, None, padded, channels), lambda m: (0, 0, m, 0, 0)),
            pl.BlockSpec(maps.shape, lambda m: (0, 0, 0)),
        ],
        out_specs=pl.BlockSpec((peers * 8, 2 * LANES), lambda m: (0, 0)),
        out_shape=jax.ShapeDtypeStruct((peers * 8, 2 * LANES), bf16),
        scratch_shapes=[
            pltpu.VMEM((OWN, 2, lats * lat_slots, LANES), f32),
            pltpu.VMEM((2, peers * 8, LANES), f32),
        ],
        compiler_params=pltpu.CompilerParams(vmem_limit_bytes=40 * 2**20),
        name="inverse",
    )(table, coef, maps)


def column_kernel(
    weight_ref, in_ref, to_grid_ref, to_orders_ref, w_in_ref, bias_ref, w_hid_ref, w_out_ref,
    out_ref, fourier_ref, tendency_ref, sums_ref, scr_ref, *, x_rows, width,
):
    peers = in_ref.shape[0] // 8

    def put(part, i, m, slab):
        fourier_ref[part, m * peers : (m + 1) * peers, i * LANES : (i + 1) * LANES] = slab.astype(
            bf16
        )

    unpack_rows(in_ref, scr_ref, put, peers, width)

    def grid_rows(step, carry):
        rows = pl.ds(pl.multiple_of(step * x_rows, x_rows), x_rows)
        raw = dot(to_grid_ref[0, rows, :], fourier_ref[0]) + dot(
            to_grid_ref[1, rows, :], fourier_ref[1]
        )
        features = (transform_scale * raw).astype(bf16)
        for i in range(OWN):
            lanes = slice(i * LANES, (i + 1) * LANES)
            hidden = silu(dot(features[:, lanes], w_in_ref[...]) + bias_ref[...]).astype(bf16)
            for layer in range(w_hid_ref.shape[0]):
                update = silu(dot(hidden, w_hid_ref[layer]))
                hidden = (hidden.astype(f32) + update).astype(bf16)
            tendency_ref[rows, lanes] = dot(hidden, w_out_ref[...]).astype(bf16)
        return carry

    lax.fori_loop(0, NLON // x_rows, grid_rows, 0)

    for part in range(2):

        def order_rows(m, carry):
            rows = pl.ds(pl.multiple_of(m * peers, peers), peers)
            sums = dot(to_orders_ref[part, rows, :], tendency_ref[...])
            for i in range(OWN):
                weight = weight_ref[i] * transform_scale
                sums_ref[part, i, m] = weight * sums[:, i * LANES : (i + 1) * LANES]
            return carry

        lax.fori_loop(0, OWN, order_rows, 0)

    slab_of = lambda part, i, m: sums_ref[part, i, m]
    pack_rows(slab_of, out_ref, scr_ref, peers, width)


def columns(weights, fourier, to_grid, to_orders, w_in, bias, w_hid, w_out, width):
    peers = fourier.shape[0] // 8
    vmem = pl.BlockSpec(memory_space=pltpu.VMEM)
    return pl.pallas_call(
        functools.partial(column_kernel, x_rows=240, width=width),
        in_specs=[pl.BlockSpec(memory_space=pltpu.SMEM)] + [vmem] * 7,
        out_specs=vmem,
        out_shape=jax.ShapeDtypeStruct(fourier.shape, bf16),
        scratch_shapes=[
            pltpu.VMEM((2, OWN * peers, OWN * LANES), bf16),
            pltpu.VMEM((NLON, OWN * LANES), bf16),
            pltpu.VMEM((2, OWN, OWN, peers, LANES), f32),
            pltpu.VMEM((2, peers * 8, LANES), f32),
        ],
        compiler_params=pltpu.CompilerParams(vmem_limit_bytes=48 * 2**20),
        name="columns",
    )(weights, fourier, to_grid, to_orders, w_in, bias, w_hid, w_out)


def forward_kernel(
    in_ref, table_ref, maps_ref, out_ref, sums_ref, scr_ref, *, lats, lat_local, lat_slots, width
):
    m = pl.program_id(0)
    peers = in_ref.shape[0] // 8

    @pl.when(m == 0)
    def _():
        def put(part, i, m, slab):
            sums_ref[m, part, pl.ds(i, peers, OWN), :] = slab

        unpack_rows(in_ref, scr_ref, put, peers, width)

    lanes = table_ref.shape[-1]
    weighted = jnp.concatenate(
        [
            jnp.concatenate(
                [
                    sums_ref[m, part, lat * lat_slots : lat * lat_slots + lat_local, :]
                    for lat in range(lats)
                ]
                + [jnp.zeros((lanes - lats * lat_local, LANES), f32)]
            )
            for part in range(2)
        ],
        axis=1,
    ).astype(bf16)
    degrees = table_ref.shape[0] * table_ref.shape[1]
    forcing = dot(table_ref[...].reshape(degrees, lanes), weighted).astype(bf16)
    for v in range(maps_ref.shape[0]):
        moved = dot(forcing, maps_ref[v]).astype(bf16)
        out_ref[v] = moved.reshape(out_ref.shape[1:])


def forward(weighted, table, maps, peers, lat_local, lat_slots, width):
    lats, _, padded, lanes = table.shape
    levs, _, channels = maps.shape
    return pl.pallas_call(
        functools.partial(
            forward_kernel, lats=lats, lat_local=lat_local, lat_slots=lat_slots, width=width
        ),
        grid=(OWN,),
        in_specs=[
            pl.BlockSpec(weighted.shape, lambda m: (0, 0)),
            pl.BlockSpec((lats, None, padded, lanes), lambda m: (0, m, 0, 0)),
            pl.BlockSpec(maps.shape, lambda m: (0, 0, 0)),
        ],
        out_specs=pl.BlockSpec((levs, lats, None, padded, channels), lambda m: (0, 0, m, 0, 0)),
        out_shape=jax.ShapeDtypeStruct((levs, lats, OWN, padded, channels), bf16),
        scratch_shapes=[
            pltpu.VMEM((OWN, 2, lats * lat_slots, LANES), f32),
            pltpu.VMEM((2, peers * 8, LANES), f32),
        ],
        compiler_params=pltpu.CompilerParams(vmem_limit_bytes=40 * 2**20),
        name="forward",
    )(weighted, table, maps)


def update_kernel(at_ref, state_ref, forcing_ref, out_ref, scr_ref):
    _, channels, orders = state_ref.shape
    half, slots = orders // 2, forcing_ref.shape[1]
    first = forcing_ref[0, :half].astype(f32)
    second = forcing_ref[1, slots - half :].astype(f32)
    scr_ref[: half * 8, :] = first.reshape(half * 8, channels)
    scr_ref[half * 8 :, :] = second.reshape(half * 8, channels)
    order = lax.broadcasted_iota(jnp.int32, (channels, orders), 1) + at_ref[0]
    for i in range(8):
        degree = jnp.full((channels, orders), pl.program_id(0) * 8 + i + at_ref[1], jnp.int32)
        ratio = (degree * (degree + 1)).astype(f32) / ((L - 1) * L)
        damping = 1.0 / (1.0 + hyper_rate * ratio * ratio)
        forcing = scr_ref[pl.ds(i, orders, 8), :].T
        new = (state_ref[i] + time_step * forcing) * damping
        out_ref[i] = jnp.where(degree >= order, new, 0.0)


def update(at, state, forcing):
    degrees, channels, orders = state.shape
    _, slots, padded, _ = forcing.shape
    block = pl.BlockSpec((8, channels, orders), lambda i: (i, 0, 0))
    return pl.pallas_call(
        update_kernel,
        grid=(padded // 8,),
        in_specs=[
            pl.BlockSpec(memory_space=pltpu.SMEM),
            block,
            pl.BlockSpec((2, slots, 8, channels), lambda i: (0, 0, i, 0)),
        ],
        out_specs=block,
        out_shape=jax.ShapeDtypeStruct(state.shape, f32),
        scratch_shapes=[pltpu.VMEM((orders * 8, channels), f32)],
        name="update",
    )(at, state, forcing)


def on_device(spectral_state, legendre, quad_weight, weight_in, bias_in, weight_hidden, weight_out):
    ord_size, lat_size, lev_size = (lax.axis_size(a) for a in ("ord", "lat", "lev"))
    ord_at, lat_at, lev_at = (lax.axis_index(a) for a in ("ord", "lat", "lev"))
    order_local, degree_local = spectral_state.shape[:2]
    lat_local = quad_weight.shape[0]
    row_local = spectral_state.shape[2] * spectral_state.shape[3]
    channels = 2 * row_local
    width = lev_size * row_local
    slots = lat_size * OWN
    shift = order_local - slots
    peers = ord_size * lat_size * lev_size
    lat_slots = ord_size * lev_size * OWN
    everyone = ("lat", "ord", "lev")
    at = jnp.stack([ord_at * order_local, lat_at * degree_local]).astype(jnp.int32)
    maps = lane_maps(lev_size, row_local)
    state = spectral_state.transpose(1, 2, 3, 4, 0).reshape(degree_local, channels, order_local)

    table = table_part((lev_at * (shift // OWN))[None], legendre, slots)
    table = table.reshape(lat_size, OWN, *table.shape[1:])
    table = lax.all_to_all(table, "lat", 0, 0, tiled=True)
    coefficients = prep(at, state, slots)
    coefficients = coefficients.reshape(lev_size * lat_size, OWN, -1, channels)
    coefficients, table = lax.optimization_barrier((coefficients, table))
    coefficients = lax.all_to_all(coefficients, ("lev", "lat"), 0, 0, tiled=True)
    coefficients = coefficients.reshape(lev_size, lat_size, OWN, -1, channels)

    slot = lax.iota(jnp.int32, OWN * peers)
    slot_lev = slot % lev_size
    slot_ord = slot // lev_size % ord_size
    slot_lat = slot // (lev_size * ord_size) % lat_size
    within = slot_lev * shift + slot_lat * OWN + slot // peers
    valid = (within >= order_local // 2) == (slot_lev == 1)
    to_orders = lookup_of(slot_ord * order_local + within, valid)
    to_grid = to_orders.swapaxes(1, 2)

    fourier = inverse(table, coefficients, maps, peers, lat_local, lat_slots, width)
    fourier = lax.all_to_all(fourier.reshape(peers, 8, -1), everyone, 0, 0, tiled=True)
    first = (ord_at * lev_size + lev_at) * OWN
    weights = lax.dynamic_slice_in_dim(jnp.pad(quad_weight, (0, lat_slots - lat_local)), first, OWN)
    weighted = columns(
        weights,
        fourier.reshape(peers * 8, -1),
        to_grid,
        to_orders,
        jnp.pad(weight_in, ((0, LANES - width), (0, 0))),
        bias_in[None, :],
        weight_hidden,
        jnp.pad(weight_out, ((0, 0), (0, LANES - width))),
        width,
    )

    weighted = lax.all_to_all(weighted.reshape(peers, 8, -1), everyone, 0, 0, tiled=True)
    forcing = forward(
        weighted.reshape(peers * 8, -1), table, maps, peers, lat_local, lat_slots, width
    )
    forcing = forcing.reshape(lev_size * lat_size, OWN, -1, channels)
    forcing = lax.all_to_all(forcing, ("lev", "lat"), 0, 0, tiled=True)
    forcing = forcing.reshape(lev_size, slots, -1, channels)
    updated = update(at, state, forcing)
    updated = updated.reshape(degree_local, *spectral_state.shape[2:], order_local)
    return updated.transpose(4, 0, 1, 2, 3)


def solution(mesh):
    return jax.shard_map(
        on_device,
        mesh=mesh,
        in_specs=(
            P("ord", "lat", "lev", None, None),
            P("ord", "lat", None),
            P("lat"),
            P(),
            P(),
            P(),
            P(),
        ),
        out_specs=P("ord", "lat", "lev", None, None),
        check_vma=False,
    )
```

time: 349 us -> 313 us (0.90)
  blocking collectives: 46.2 us -> 123 us
  waiting for transfers between devices: 135 us -> 76 us
  local copies, waits for them, and re-layouts: 61.2 us -> 15.9 us
  Pallas kernels: 29.3 us -> 52.7 us
  starting transfers between devices: 30.4 us -> 17.5 us
  other arithmetic: 38.6 us -> 26.4 us
  matrix products: 6.95 us -> 0 us
    all_to_all x1 -> x3, blocking collectives: 46.2 us -> 123 us  [the longest x1 45.3 us: on_device(): lax.all_to_all(weighted.reshape(peers, 8, -1), everyone, 0, 0, tiled=True)]
    all_to_all x3 -> x1, waiting for transfers between devices: 58.2 us -> 0.01 us  [on_device(): lax.all_to_all(fourier.reshape(peers, 8, -1), everyone, 0, 0, tiled=True)]
    reshape x9 -> x0, local copies, waits for them, and re-layouts: 27.4 us -> none  [the longest x1 7.61 us: on_device(): forcing.reshape(spectral_state.shape)]
    pallas_call x1 -> x6, Pallas kernels: 29.3 us -> 52.7 us  [the longest x1 23.8 us: columns(): pl.pallas_call(functools.partial(column_kernel, x_rows=240, width=width),...]
    all_to_all x3 -> x1, starting transfers between devices: 25.2 us -> 8.6 us  [on_device(): lax.all_to_all(fourier.reshape(peers, 8, -1), everyone, 0, 0, tiled=True)]
    dot_general x2 -> x0, matrix products: 6.95 us -> none  [the longest x1 4.95 us: on_device(): jnp.einsum('smlj,vsmlpr->jmpvr', table, coefficients, preferred_element_t...]
    slice x4 -> x0, local copies, waits for them, and re-layouts: 6.87 us -> none  [the longest x3 5.35 us: on_device(): sent = jnp.concatenate([coefficients[:slots], coefficients[shift:]])]
    convert_element_type x1 -> x0, local copies, waits for them, and re-layouts: 6.48 us -> none  [on_device(): fourier = jnp.einsum('smlj,vsmlpr->jmpvr', table, coefficients, preferred...]
  transfers between devices with their start and end apart: 4 -> 2, of which waited for: 4 -> 1; matrix products, arithmetic and copies ran while one was open for 12% -> 12% of each run, Pallas kernels for 0% -> 2%
where the time goes in v2:
time: 313 us; the launch traced here: 311 us
  blocking collectives  123 us (39%)
  waiting for transfers between devices  76 us (24%)
  Pallas kernels  52.7 us (17%)
  other arithmetic  26.4 us (8%)
  starting transfers between devices  17.5 us (6%)
  local copies, waits for them, and re-layouts  15.9 us (5%)
    all_to_all x1, waiting for transfers between devices, on_device(): table = lax.all_to_all(table, 'lat', 0, 0, tiled=True)  76 us
    all_to_all x1, blocking collectives, on_device(): lax.all_to_all(weighted.reshape(peers, 8, -1), everyone, 0, 0, tiled=True)  45.3 us
    all_to_all x1, blocking collectives, on_device(): lax.all_to_all(coefficients, ('lev', 'lat'), 0, 0, tiled=True)  41.1 us
    all_to_all x1, blocking collectives, on_device(): forcing = lax.all_to_all(forcing, ('lev', 'lat'), 0, 0, tiled=True)  36.2 us
    pallas_call x1, Pallas kernels, columns(): pl.pallas_call(functools.partial(column_kernel, x_rows=240, width=width),...  23.8 us
    another operation x1, other arithmetic  21.4 us
    pallas_call x1, Pallas kernels, table_part(): pl.pallas_call(table_kernel, grid_spec=pltpu.PrefetchScalarGridSpec(num_s...  9.99 us
    all_to_all x1, starting transfers between devices, on_device(): table = lax.all_to_all(table, 'lat', 0, 0, tiled=True)  8.91 us
  transfers between devices with their start and end apart: 2, of which 1 were waited for; matrix products, arithmetic and copies ran while one was open for 12% of the time, Pallas kernels for 2%

profile of v2, /device:TPU:2, one launch (start us, length us, event | category | flops | bytes accessed | tf_op | source)
XLA Modules:
  0.0 311.1 jit_solution(16504913269987355459)
XLA Ops:
  0.0 10.0 %table.1 = bf16[48,48,768]{2,1,0:T(8,128)(2,1)} custom-call(s32[1]{0:T(128)} %bitcast.6.at_ref, bf16[90,45,720]{2,1,0:T(8,128)(2,1)} %in_ref.1), custom_call_target="tpu_custom_call" | custom-call | tf_op jit(solution)/shard_map/table/pallas_call | solution.py:114
  10.0 8.9 %all-to-all-start = ((bf16[16,3,48,768]{3,2,1,0:T(8,128)(2,1)}), bf16[16,3,48,768]{3,2,1,0:T(8,128)(2,1)S(1)}, u32[]{:S(2)}, u32[]{:S(2)}) async-start(bf16[16,3,48,768]{3,2,1,0:T(8,128)(2,1)} %bitcast.27), calls=%async_computation | async-start | bytes 7077888 | tf_op jit(solution)/shard_map/all_to_all | solution.py:362
  18.9 0.7 pad_add_fusion.at_ref
  19.6 5.2 %prep.1 = bf16[2,48,48,112]{3,2,1,0:T(8,128)(2,1)} custom-call(s32[2]{0:T(128)} %pad_add_fusion.at_ref, f32[45,112,90]{2,1,0:T(8,128)} %bitcast.28), custom_call_target="tpu_custom_call" | custom-call | flops 1000000 | bytes 4000000 | tf_op jit(solution)/shard_map/prep/pallas_call | solution.py:91
  24.7 76.0 %all-to-all-done.table_ref = bf16[16,3,48,768]{3,2,1,0:T(8,128)(2,1)S(1)} async-done(((bf16[16,3,48,768]{3,2,1,0:T(8,128)(2,1)}), bf16[16,3,48,768]{3,2,1,0:T(8,128)(2,1)S(1)}, u32[]{:S(2)}, u32[]{:S(2)}) %all-to-all-start) | async-done | bytes 3538976 | tf_op jit(solution)/shard_map/all_to_all | solution.py:362
  100.7 41.1 %all_to_all.25 = bf16[32,3,48,112]{3,2,1,0:T(8,128)(2,1)S(1)} all-to-all(bf16[32,3,48,112]{3,2,1,0:T(8,128)(2,1)} %bitcast.31), channel_id=1, replica_groups=mesh['ord'=8,'lat'=16,'lev'=2] {'lev','lat'}, dimensions={0} | all-to-all | bytes 2064384 | tf_op jit(solution)/shard_map/all_to_all | solution.py:366
  141.8 0.9 copy-done.2
  142.7 4.0 %inverse.1 = bf16[2048,256]{1,0:T(8,128)(2,1)S(1)} custom-call(bf16[16,3,48,768]{3,2,1,0:T(8,128)(2,1)S(1)} %all-to-all-done.table_ref, bf16[2,16,3,48,112]{4,3,2,1,0:T(8,128)(2,1)S(1)} %bitcast.22, bf16[2,256,112]{2,1,0:T(8,128)(2,1)S(1)} %copy-done.2), custom_call_target="tpu_custom_call" | custom-call | tf_op jit(solution)/shard_map/inverse/pallas_call | solution.py:163
  146.7 0.0 copy-start
  146.7 1.0 copy-done
  147.7 8.6 %all-to-all-start.2 = ((bf16[256,8,256]{2,1,0:T(8,128)(2,1)}), bf16[256,8,256]{2,1,0:T(8,128)(2,1)}, u32[]{:S(2)}, u32[]{:S(2)}) async-start(bf16[256,8,256]{2,1,0:T(8,128)(2,1)} %bitcast.24), calls=%async_computation.2 | async-start | bytes 2097152 | tf_op jit(solution)/shard_map/all_to_all | solution.py:379
  156.3 21.4 %select_convert_fusion.1 = (bf16[1,768,1440]{2,1,0:T(8,128)(2,1)S(1)}, bf16[1,768,1440]{2,1,0:T(8,128)(2,1)S(1)}) fusion(s32[768]{0:T(1024)S(1)} %fusion.17, pred[768]{0:T(1024)(128)(4,1)S(1)} %fusion.25), kind=kLoop, calls=%fused_computation.5 | loop fusion | flops 15482880 | bytes 4427520 | tf_op jit(solution)/shard_map/convert
  177.7 4.3 %pad_maximum_fusion = (bf16[2,768,1440]{2,1,0:T(8,128)(2,1)}, bf16[2,1440,768]{1,2,0:T(8,128)(2,1)}) fusion(bf16[1,768,1440]{2,1,0:T(8,128)(2,1)S(1)} %get-tuple-element.12, bf16[1,768,1440]{2,1,0:T(8,128)(2,1)S(1)} %get-tuple-element.11), kind=kLoop, calls=%fused_computation.3 | loop fusion | flops 2211840 | bytes 13271040 | tf_op jit(solution)/shard_map/stack | solution.py:30
  182.0 0.0 copy-start.7
  182.0 0.0 copy-start.6
  182.0 6.7 %copy.10.to_grid_ref = bf16[2,1440,768]{2,1,0:T(8,128)(2,1)} copy(bf16[2,1440,768]{1,2,0:T(8,128)(2,1)} %get-tuple-element.10) | data formatting | bytes 8847360 | tf_op jit(solution)/shard_map/transpose | solution.py:376
  188.7 1.5 copy.9
  190.2 1.5 pad.14.w_out_ref
  191.7 1.4 pad.13.w_in_ref
  193.2 0.0 copy-done.7
  193.2 0.1 pad_dynamic-slice_fusion.weight_ref
  193.2 0.0 all-to-all-done.2
  193.3 0.0 copy-done.6
  193.3 1.0 copy-done.1
  194.3 0.8 copy-done.4
  195.1 0.8 copy-done.5
  196.0 23.8 %columns.1 = bf16[2048,256]{1,0:T(8,128)(2,1)S(1)} custom-call(f32[3]{0:T(128)S(1)} %pad_dynamic-slice_fusion.weight_ref, bf16[2048,256]{1,0:T(8,128)(2,1)} %bitcast.10.in_ref, bf16[2,1440,768]{2,1,0:T(8,128)(2,1)} %copy.10.to_grid_ref, bf16[2,768,1440]{2,1,0:T(8,128)(2,1)} %get-tuple-element.9.to_orders_ref, bf16[128,256]{1,0:T(8,128)(2,1)S(1)} %copy-done.5, ...), custom_call_target="tpu_custom_call" | custom-call | tf_op jit(solution)/shard_map/columns/pallas_call | solution.py:233
  219.8 45.3 %all_to_all.26 = bf16[256,8,256]{2,1,0:T(8,128)(2,1)S(1)} all-to-all(bf16[256,8,256]{2,1,0:T(8,128)(2,1)S(1)} %bitcast.23), channel_id=1, replica_groups=mesh['ord'=8,'lat'=16,'lev'=2] {'lat','ord','lev'}, dimensions={0} | all-to-all | bytes 2097152 | tf_op jit(solution)/shard_map/all_to_all | solution.py:394
  265.1 0.0 copy-done.3
  265.1 4.1 %forward.1 = bf16[2,16,3,48,112]{4,3,2,1,0:T(8,128)(2,1)S(1)} custom-call(bf16[2048,256]{1,0:T(8,128)(2,1)S(1)} %bitcast.25, bf16[16,3,48,768]{3,2,1,0:T(8,128)(2,1)S(1)} %all-to-all-done.table_ref, bf16[2,256,112]{2,1,0:T(8,128)(2,1)S(1)} %copy-done.3), custom_call_target="tpu_custom_call" | custom-call | tf_op jit(solution)/shard_map/forward/pallas_call | solution.py:286
  269.3 36.2 %all_to_all.27 = bf16[32,3,48,112]{3,2,1,0:T(8,128)(2,1)} all-to-all(bf16[32,3,48,112]{3,2,1,0:T(8,128)(2,1)S(1)} %bitcast.21), channel_id=1, replica_groups=mesh['ord'=8,'lat'=16,'lev'=2] {'lev','lat'}, dimensions={0} | all-to-all | bytes 2064384 | tf_op jit(solution)/shard_map/all_to_all | solution.py:399
  305.5 5.7 %update.1 = f32[45,112,90]{2,1,0:T(8,128)} custom-call(s32[2]{0:T(128)} %pad_add_fusion.at_ref, f32[45,112,90]{2,1,0:T(8,128)} %bitcast.29, bf16[2,48,48,112]{3,2,1,0:T(8,128)(2,1)} %bitcast.30), custom_call_target="tpu_custom_call" | custom-call | tf_op jit(solution)/shard_map/update/pallas_call | solution.py:328
  (7 shorter events, 0.0 us)
Async XLA Ops:
  10.0 90.7 %all-to-all-start = ((bf16[16,3,48,768]{3,2,1,0:T(8,128)(2,1)}), bf16[16,3,48,768]{3,2,1,0:T(8,128)(2,1)S(1)}, u32[]{:S(2)}, u32[]{:S(2)}) async-start(bf16[16,3,48,768]{3,2,1,0:T(8,128)(2,1)} %bitcast.27), calls=%async_computation | async-start | bytes 7077888 | tf_op jit(solution)/shard_map/all_to_all | solution.py:362
  141.8 0.9 copy-start.2
  146.7 1.0 copy-start
  147.7 45.6 %all-to-all-start.2 = ((bf16[256,8,256]{2,1,0:T(8,128)(2,1)}), bf16[256,8,256]{2,1,0:T(8,128)(2,1)}, u32[]{:S(2)}, u32[]{:S(2)}) async-start(bf16[256,8,256]{2,1,0:T(8,128)(2,1)} %bitcast.24), calls=%async_computation.2 | async-start | bytes 2097152 | tf_op jit(solution)/shard_map/all_to_all | solution.py:379
  182.0 11.2 %copy-start.7 = (f32[45]{0:T(128)S(1)}, f32[45]{0:T(128)}, u32[]{:S(2)}) copy-start(f32[45]{0:T(128)} %param.10) | copy-start | bytes 544
  182.0 11.3 %copy-start.6 = (f32[256]{0:T(256)S(1)}, f32[256]{0:T(256)}, u32[]{:S(2)}) copy-start(f32[256]{0:T(256)} %param.12) | copy-start | bytes 3076
  193.3 1.0 copy-start.1
  194.3 0.8 copy-start.4
  195.1 0.8 copy-start.5
  196.0 69.2 %copy-start.3 = (bf16[2,256,112]{2,1,0:T(8,128)(2,1)S(1)}, bf16[2,256,112]{2,1,0:T(8,128)(2,1)}, u32[]{:S(2)}) copy-start(bf16[2,256,112]{2,1,0:T(8,128)(2,1)} %constant.129.clone.maps_ref) | copy-start | bytes 344068

commit v3 on v2

v3 whole, which is shorter than its diff:
```python
import functools
import math

import jax
import jax.numpy as jnp
import numpy as np
from jax import lax
from jax.experimental import pallas as pl
from jax.experimental.pallas import tpu as pltpu
from jax.sharding import PartitionSpec as P

L = 720
NLON = 1440
OWN = 3
LANES = 128
LAT_X, Z_LOW, Z_RING = 4, 4, 8
HALF = 384
SPARE = 14

time_step = 1.0
hyper_rate = 2.0
transform_scale = math.sqrt(2.0 / NLON)

f32, bf16 = jnp.float32, jnp.bfloat16
dot = functools.partial(jnp.dot, preferred_element_type=jnp.float32)


def first_group(x):
    return (22 * x + 1) // 3


def lookup_of(order_ids, valid):
    phase_index = order_ids[None, :] * lax.iota(jnp.int32, NLON)[:, None] % NLON
    angles = 2.0 * math.pi / NLON * phase_index.astype(f32)
    keep = valid[None, :]
    return jnp.stack(
        [jnp.where(keep, jnp.cos(angles), 0.0), jnp.where(keep, -jnp.sin(angles), 0.0)]
    ).astype(bf16)


def silu(v):
    return 0.5 * v * (1.0 + jnp.tanh(0.5 * v))


def lane_maps(levs, row_local):
    maps = np.zeros((levs, 2 * LANES, 2 * row_local), np.float32)
    for lev in range(levs):
        for row in range(row_local):
            for part in range(2):
                maps[lev, part * LANES + lev * row_local + row, 2 * row + part] = 1.0
    return jnp.asarray(maps, bf16)


def pack_rows(slab_of, out_ref, scr_ref, peers, width):
    lane = lax.broadcasted_iota(jnp.int32, (peers, LANES), 1)
    spare = (lane >= width) & (lane < width + SPARE)
    for part in range(2):
        last = slab_of(part, 2, 2)
        for k in range(8):
            moved = pltpu.roll(last, (width - SPARE * k) % LANES, 1)
            scr_ref[part, pl.ds(k, peers, 8), :] = jnp.where(
                spare, moved, slab_of(part, k // OWN, k % OWN)
            )
        out_ref[:, part * LANES : (part + 1) * LANES] = scr_ref[part].astype(bf16)


def unpack_rows(in_ref, scr_ref, put_slab, peers, width):
    lane = lax.broadcasted_iota(jnp.int32, (peers, LANES), 1)
    for part in range(2):
        scr_ref[part] = in_ref[:, part * LANES : (part + 1) * LANES].astype(f32)
        last = jnp.zeros((peers, LANES), f32)
        for k in range(8):
            slab = scr_ref[part, pl.ds(k, peers, 8), :]
            put_slab(part, k // OWN, k % OWN, slab)
            moved = pltpu.roll(slab, (SPARE * k - width) % LANES, 1)
            last = jnp.where((lane >= SPARE * k) & (lane < SPARE * (k + 1)), moved, last)
        put_slab(part, 2, 2, last)


def prep_kernel(at_ref, state_ref, out_ref, scr_ref, *, degrees):
    orders = state_ref.shape[2]
    group = out_ref.shape[1]
    step = pl.program_id(0) * 8
    order = lax.broadcasted_iota(jnp.int32, state_ref.shape[1:], 1) + at_ref[0]
    for i in range(8):
        degree = step + i
        keep = (degree + at_ref[1] >= order) & (degree < degrees)
        scr_ref[pl.ds(i, orders, 8), :] = jnp.where(keep, state_ref[i], 0.0).T
    rows = scr_ref[...].astype(bf16).reshape(orders, 8, -1)
    for x in range(LAT_X):
        first = OWN * first_group(x)
        out_ref[x] = rows[first : first + group]


def prep(at, state):
    group = OWN * Z_RING
    degrees, channels, orders = state.shape
    padded = -(-degrees // 8) * 8
    return pl.pallas_call(
        functools.partial(prep_kernel, degrees=degrees),
        grid=(padded // 8,),
        in_specs=[
            pl.BlockSpec(memory_space=pltpu.SMEM),
            pl.BlockSpec((8, channels, orders), lambda i: (i, 0, 0)),
        ],
        out_specs=pl.BlockSpec((LAT_X, group, 8, channels), lambda i: (0, 0, i, 0)),
        out_shape=jax.ShapeDtypeStruct((LAT_X, group, padded, channels), bf16),
        scratch_shapes=[pltpu.VMEM((orders * 8, channels), f32)],
        cost_estimate=pl.CostEstimate(flops=10**6, bytes_accessed=4 * 10**6, transcendentals=0),
        name="prep",
    )(at, state)


def pack_kernel(own_ref, in_ref, a_ref, *b_refs):
    degrees, lats = in_ref.shape[1:]
    half, rows = a_ref.shape[-1], a_ref.shape[-2]
    split = rows // 2
    a_ref[...] = jnp.zeros_like(a_ref)
    for ref in b_refs:
        ref[...] = jnp.zeros_like(ref)
    for k in range(3):
        mine = in_ref[pl.ds(own_ref[k], OWN)]
        a_ref[0, k, :, :degrees, :] = mine[:, :, :half]
        b_refs[k][0, :, :degrees, : lats - half] = mine[:, :, half:]
    mine = in_ref[pl.ds(own_ref[3], OWN)]
    a_ref[0, 3, :, :split, :] = mine[:, :split, :half]
    b_refs[3][0, :, :, : lats - half] = mine[:, :split, half:]
    mine = in_ref[pl.ds(own_ref[4], OWN)]
    a_ref[0, 3, :, split:degrees, :] = mine[:, split:, :half]
    b_refs[4][0, :, : degrees - split, : lats - half] = mine[:, split:, half:]


def pack_table(own, legendre, half, rows):
    _, degrees, lats = legendre.shape
    group = OWN * Z_RING
    b_shape = lambda r: jax.ShapeDtypeStruct((LAT_X, OWN, r, half), bf16)
    b_spec = lambda r: pl.BlockSpec((1, OWN, r, half), lambda x: (x, 0, 0, 0))
    b_rows = (rows, rows, rows, rows // 2, rows // 2)
    return pl.pallas_call(
        pack_kernel,
        grid=(LAT_X,),
        in_specs=[
            pl.BlockSpec(memory_space=pltpu.SMEM),
            pl.BlockSpec(
                (pl.Element(group), pl.Element(degrees), pl.Element(lats)),
                lambda x: (OWN * first_group(x), 0, 0),
            ),
        ],
        out_specs=[pl.BlockSpec((1, 4, OWN, rows, half), lambda x: (x, 0, 0, 0, 0))]
        + [b_spec(r) for r in b_rows],
        out_shape=[jax.ShapeDtypeStruct((LAT_X, 4, OWN, rows, half), bf16)]
        + [b_shape(r) for r in b_rows],
        compiler_params=pltpu.CompilerParams(vmem_limit_bytes=24 * 2**20),
        name="pack_table",
    )(own, legendre)


def inverse_kernel(
    class_ref, a_own_ref, a_left_ref, a_right_ref, a_low_ref, a_high_ref, b_ref, coef_ref, maps_ref,
    out_ref, table_ref, sums_ref, scr_ref, *, lats, lat_local, lat_slots, width,
):
    m = pl.program_id(0)
    rows, half = b_ref.shape[-2:]
    place = LAT_X * rows
    far = jnp.concatenate([a_low_ref[...], a_high_ref[...]], axis=1)
    for k, piece in enumerate((a_own_ref[:, 0], a_left_ref[...], a_right_ref[...], far)):
        table_ref[0, k * place : (k + 1) * place, :half] = piece.reshape(place, half)
        table_ref[0, k * place : (k + 1) * place, half:] = b_ref[:, k].reshape(place, half)
    swapped = 0.0
    for v in range(maps_ref.shape[0]):
        coef = jnp.concatenate(
            [coef_ref[x * Z_LOW + class_ref[k], v] for k in range(4) for x in range(LAT_X)]
        )
        swapped += lax.dot_general(
            maps_ref[v], coef, (((1,), (1,)), ((), ())), preferred_element_type=f32
        )
    sums = dot(swapped.astype(bf16), table_ref[0]).T
    for part in range(2):
        lanes = slice(part * LANES, (part + 1) * LANES)
        for lat in range(lats):
            sums_ref[m, part, lat * lat_slots : lat * lat_slots + lat_local, :] = sums[
                lat * lat_local : (lat + 1) * lat_local, lanes
            ]
            sums_ref[m, part, lat * lat_slots + lat_local : (lat + 1) * lat_slots, :] = jnp.zeros(
                (lat_slots - lat_local, LANES), f32
            )

    @pl.when(m == OWN - 1)
    def _():
        peers = out_ref.shape[0] // 8
        slab_of = lambda part, i, m: sums_ref[m, part, pl.ds(i, peers, OWN), :]
        pack_rows(slab_of, out_ref, scr_ref, peers, width)


def inverse(classes, a_own, a_near, a_far, b_all, coef, maps, peers, lat_local, lat_slots, width):
    rows, half = b_all.shape[-2:]
    lats, levs, _, _, channels = coef.shape
    size = 4 * LAT_X * rows
    near = pl.BlockSpec((LAT_X, None, rows, half), lambda m: (0, m, 0, 0))
    far = pl.BlockSpec((LAT_X, None, rows // 2, half), lambda m: (0, m, 0, 0))
    return pl.pallas_call(
        functools.partial(
            inverse_kernel, lats=lats, lat_local=lat_local, lat_slots=lat_slots, width=width
        ),
        grid=(OWN,),
        in_specs=[
            pl.BlockSpec(memory_space=pltpu.SMEM),
            pl.BlockSpec((LAT_X, 1, None, rows, half), lambda m: (0, 0, m, 0, 0)),
            near,
            near,
            far,
            far,
            pl.BlockSpec((LAT_X, 4, None, rows, half), lambda m: (0, 0, m, 0, 0)),
            pl.BlockSpec((lats, levs, None, rows, channels), lambda m: (0, 0, m, 0, 0)),
            pl.BlockSpec(maps.shape, lambda m: (0, 0, 0)),
        ],
        out_specs=[
            pl.BlockSpec((peers * 8, 2 * LANES), lambda m: (0, 0)),
            pl.BlockSpec((1, size, 2 * half), lambda m: (m, 0, 0)),
        ],
        out_shape=[
            jax.ShapeDtypeStruct((peers * 8, 2 * LANES), bf16),
            jax.ShapeDtypeStruct((OWN, size, 2 * half), bf16),
        ],
        scratch_shapes=[
            pltpu.VMEM((OWN, 2, lats * lat_slots, LANES), f32),
            pltpu.VMEM((2, peers * 8, LANES), f32),
        ],
        compiler_params=pltpu.CompilerParams(vmem_limit_bytes=40 * 2**20),
        name="inverse",
    )(classes, a_own, *a_near, *a_far, b_all, coef, maps)


def column_kernel(
    weight_ref, in_ref, to_grid_ref, w_in_ref, bias_ref, w_hid_ref, w_out_ref,
    out_ref, fourier_ref, tendency_ref, sums_ref, scr_ref, *, x_rows, width,
):
    peers = in_ref.shape[0] // 8

    def put(part, i, m, slab):
        fourier_ref[part, m * peers : (m + 1) * peers, i * LANES : (i + 1) * LANES] = slab.astype(
            bf16
        )

    unpack_rows(in_ref, scr_ref, put, peers, width)

    def grid_rows(step, carry):
        rows = pl.ds(pl.multiple_of(step * x_rows, x_rows), x_rows)
        raw = dot(to_grid_ref[0, rows, :], fourier_ref[0]) + dot(
            to_grid_ref[1, rows, :], fourier_ref[1]
        )
        features = (transform_scale * raw).astype(bf16)
        for i in range(OWN):
            lanes = slice(i * LANES, (i + 1) * LANES)
            hidden = silu(dot(features[:, lanes], w_in_ref[...]) + bias_ref[...]).astype(bf16)
            for layer in range(w_hid_ref.shape[0]):
                update = silu(dot(hidden, w_hid_ref[layer]))
                hidden = (hidden.astype(f32) + update).astype(bf16)
            tendency_ref[rows, lanes] = dot(hidden, w_out_ref[...]).astype(bf16)
        return carry

    lax.fori_loop(0, NLON // x_rows, grid_rows, 0)

    for part in range(2):
        sums = lax.dot_general(
            tendency_ref[...],
            to_grid_ref[part],
            (((0,), (0,)), ((), ())),
            preferred_element_type=f32,
        )
        for i in range(OWN):
            weight = weight_ref[i] * transform_scale
            for m in range(OWN):
                block = sums[i * LANES : (i + 1) * LANES, m * peers : (m + 1) * peers]
                sums_ref[part, i, m] = weight * block.T

    slab_of = lambda part, i, m: sums_ref[part, i, m]
    pack_rows(slab_of, out_ref, scr_ref, peers, width)


def columns(weights, fourier, to_grid, w_in, bias, w_hid, w_out, width):
    peers = fourier.shape[0] // 8
    vmem = pl.BlockSpec(memory_space=pltpu.VMEM)
    return pl.pallas_call(
        functools.partial(column_kernel, x_rows=240, width=width),
        in_specs=[pl.BlockSpec(memory_space=pltpu.SMEM)] + [vmem] * 6,
        out_specs=vmem,
        out_shape=jax.ShapeDtypeStruct(fourier.shape, bf16),
        scratch_shapes=[
            pltpu.VMEM((2, OWN * peers, OWN * LANES), bf16),
            pltpu.VMEM((NLON, OWN * LANES), bf16),
            pltpu.VMEM((2, OWN, OWN, peers, LANES), f32),
            pltpu.VMEM((2, peers * 8, LANES), f32),
        ],
        compiler_params=pltpu.CompilerParams(vmem_limit_bytes=48 * 2**20),
        name="columns",
    )(weights, fourier, to_grid, w_in, bias, w_hid, w_out)


def forward_kernel(
    class_ref, in_ref, table_ref, maps_ref, out_ref, sums_ref, scr_ref,
    *, lats, lat_local, lat_slots, width,
):
    m = pl.program_id(0)
    peers = in_ref.shape[0] // 8

    @pl.when(m == 0)
    def _():
        def put(part, i, m, slab):
            sums_ref[m, part, pl.ds(i, peers, OWN), :] = slab

        unpack_rows(in_ref, scr_ref, put, peers, width)

    lanes = table_ref.shape[-1]
    weighted = jnp.concatenate(
        [
            jnp.concatenate(
                [
                    sums_ref[m, part, lat * lat_slots : lat * lat_slots + lat_local, :]
                    for lat in range(lats)
                ]
                + [jnp.zeros((lanes - lats * lat_local, LANES), f32)]
            )
            for part in range(2)
        ],
        axis=1,
    ).astype(bf16)
    forcing = dot(table_ref[0], weighted).astype(bf16)
    rows = out_ref.shape[2]
    for v in range(maps_ref.shape[0]):
        moved = dot(forcing, maps_ref[v]).astype(bf16)
        for k in range(4):
            for x in range(LAT_X):
                at = (k * LAT_X + x) * rows
                out_ref[x * Z_LOW + class_ref[k], v] = moved[at : at + rows]


def forward(classes, weighted, table, maps, peers, lats, rows, lat_local, lat_slots, width):
    levs, _, channels = maps.shape
    return pl.pallas_call(
        functools.partial(
            forward_kernel, lats=lats, lat_local=lat_local, lat_slots=lat_slots, width=width
        ),
        grid=(OWN,),
        in_specs=[
            pl.BlockSpec(memory_space=pltpu.SMEM),
            pl.BlockSpec(weighted.shape, lambda m: (0, 0)),
            pl.BlockSpec((1, *table.shape[1:]), lambda m: (m, 0, 0)),
            pl.BlockSpec(maps.shape, lambda m: (0, 0, 0)),
        ],
        out_specs=pl.BlockSpec((lats, levs, None, rows, channels), lambda m: (0, 0, m, 0, 0)),
        out_shape=jax.ShapeDtypeStruct((lats, levs, OWN, rows, channels), bf16),
        scratch_shapes=[
            pltpu.VMEM((OWN, 2, lats * lat_slots, LANES), f32),
            pltpu.VMEM((2, peers * 8, LANES), f32),
        ],
        compiler_params=pltpu.CompilerParams(vmem_limit_bytes=40 * 2**20),
        name="forward",
    )(classes, weighted, table, maps)


def update_kernel(at_ref, state_ref, forcing_ref, out_ref, scr_ref):
    _, channels, orders = state_ref.shape
    for x in range(LAT_X):
        skip = OWN * (first_group(x - 1) + Z_RING - first_group(x)) if x else 0
        first = (OWN * first_group(x) + skip) * 8
        mine = forcing_ref[x, skip:].astype(f32)
        scr_ref[first : first + mine.shape[0] * 8, :] = mine.reshape(-1, channels)
    order = lax.broadcasted_iota(jnp.int32, (channels, orders), 1) + at_ref[0]
    for i in range(8):
        degree = jnp.full((channels, orders), pl.program_id(0) * 8 + i + at_ref[1], jnp.int32)
        ratio = (degree * (degree + 1)).astype(f32) / ((L - 1) * L)
        damping = 1.0 / (1.0 + hyper_rate * ratio * ratio)
        forcing = scr_ref[pl.ds(i, orders, 8), :].T
        new = (state_ref[i] + time_step * forcing) * damping
        out_ref[i] = jnp.where(degree >= order, new, 0.0)


def update(at, state, forcing):
    degrees, channels, orders = state.shape
    _, group, padded, _ = forcing.shape
    block = pl.BlockSpec((8, channels, orders), lambda i: (i, 0, 0))
    return pl.pallas_call(
        update_kernel,
        grid=(padded // 8,),
        in_specs=[
            pl.BlockSpec(memory_space=pltpu.SMEM),
            block,
            pl.BlockSpec((LAT_X, group, 8, channels), lambda i: (0, 0, i, 0)),
        ],
        out_specs=block,
        out_shape=jax.ShapeDtypeStruct(state.shape, f32),
        scratch_shapes=[pltpu.VMEM((orders * 8, channels), f32)],
        name="update",
    )(at, state, forcing)


def along_z(value, step):
    pairs = []
    flat = lambda x, z: x * Z_RING + 2 * (z % Z_LOW) + z // Z_LOW
    for x in range(LAT_X):
        pairs += [(flat(x, z), flat(x, (z + step) % Z_RING)) for z in range(Z_RING)]
    return lax.ppermute(value, ("lat", "lev"), pairs)


def along_x(value):
    groups = [[x * Z_LOW + z for x in range(LAT_X)] for z in range(Z_LOW)]
    return lax.all_to_all(value, "lat", 0, 0, axis_index_groups=groups, tiled=True)


def on_device(spectral_state, legendre, quad_weight, weight_in, bias_in, weight_hidden, weight_out):
    ord_size, lat_size, lev_size = (lax.axis_size(a) for a in ("ord", "lat", "lev"))
    ord_at, lat_at, lev_at = (lax.axis_index(a) for a in ("ord", "lat", "lev"))
    order_local, degree_local = spectral_state.shape[:2]
    lat_local = quad_weight.shape[0]
    row_local = spectral_state.shape[2] * spectral_state.shape[3]
    channels = 2 * row_local
    width = lev_size * row_local
    rows = -(-degree_local // 16) * 16
    peers = ord_size * lat_size * lev_size
    lat_slots = ord_size * lev_size * OWN
    everyone = ("lat", "ord", "lev")
    at = jnp.stack([ord_at * order_local, lat_at * degree_local]).astype(jnp.int32)
    maps = lane_maps(lev_size, row_local)
    state = spectral_state.transpose(1, 2, 3, 4, 0).reshape(degree_local, channels, order_local)

    z_at = lev_at * Z_LOW + lat_at % Z_LOW
    ring = (z_at + jnp.array([0, 1, -1, 2, -2], jnp.int32)) % Z_RING
    own = OWN * (2 * (ring % Z_LOW) + ring // Z_LOW)
    a_all, b_own, *b_rest = pack_table(own, legendre, HALF, rows)
    b_left, b_right, b_low, b_high = (along_z(v, k) for v, k in zip(b_rest, (1, -1, 2, -2)))
    a_all = along_x(a_all)
    a_near = [along_z(a_all[:, 1], 1), along_z(a_all[:, 2], -1)]
    a_far = [along_z(a_all[:, 3, :, : rows // 2], 2), along_z(a_all[:, 3, :, rows // 2 :], -2)]
    b_far = jnp.concatenate([b_low, b_high], axis=2)
    b_all = along_x(jnp.stack([b_own, b_left, b_right, b_far], axis=1))

    slot = lax.iota(jnp.int32, OWN * peers)
    slot_lev = slot % lev_size
    slot_ord = slot // lev_size % ord_size
    slot_lat = slot // (lev_size * ord_size) % lat_size
    slot_x, slot_w = slot_lat // Z_LOW, 2 * (slot_lat % Z_LOW) + slot_lev
    valid = (slot_x % 2 == 0) | (slot_w > 0)
    order_ids = slot_ord * order_local + OWN * (first_group(slot_x) + slot_w) + slot // peers
    to_grid = lookup_of(order_ids, valid)
    coefficients = prep(at, state)
    coefficients, b_all, to_grid = lax.optimization_barrier((coefficients, b_all, to_grid))

    coefficients = coefficients.reshape(lat_size * lev_size, OWN, rows, channels)
    coefficients = lax.all_to_all(coefficients, ("lat", "lev"), 0, 0, tiled=True)
    coefficients = coefficients.reshape(lat_size, lev_size, OWN, rows, channels)
    classes = (z_at + jnp.array([0, -1, 1, 2], jnp.int32)) % Z_LOW
    fourier, table = inverse(
        classes, a_all, a_near, a_far, b_all, coefficients, maps, peers, lat_local, lat_slots, width
    )

    fourier = lax.all_to_all(fourier.reshape(peers, 8, -1), everyone, 0, 0, tiled=True)
    first = (ord_at * lev_size + lev_at) * OWN
    weights = lax.dynamic_slice_in_dim(jnp.pad(quad_weight, (0, lat_slots - lat_local)), first, OWN)
    weighted = columns(
        weights,
        fourier.reshape(peers * 8, -1),
        to_grid,
        jnp.pad(weight_in, ((0, LANES - width), (0, 0))),
        bias_in[None, :],
        weight_hidden,
        jnp.pad(weight_out, ((0, 0), (0, LANES - width))),
        width,
    )

    weighted = lax.all_to_all(weighted.reshape(peers, 8, -1), everyone, 0, 0, tiled=True)
    weighted = weighted.reshape(peers * 8, -1)
    forcing = forward(
        classes, weighted, table, maps, peers, lat_size, rows, lat_local, lat_slots, width
    )
    forcing = forcing.reshape(lat_size * lev_size, OWN, rows, channels)
    forcing = lax.all_to_all(forcing, ("lat", "lev"), 0, 0, tiled=True)
    forcing = forcing.reshape(LAT_X, OWN * Z_RING, rows, channels)
    updated = update(at, state, forcing)
    updated = updated.reshape(degree_local, *spectral_state.shape[2:], order_local)
    return updated.transpose(4, 0, 1, 2, 3)


def solution(mesh):
    return jax.shard_map(
        on_device,
        mesh=mesh,
        in_specs=(
            P("ord", "lat", "lev", None, None),
            P("ord", "lat", None),
            P("lat"),
            P(),
            P(),
            P(),
            P(),
        ),
        out_specs=P("ord", "lat", "lev", None, None),
        check_vma=False,
    )
```

time: 313 us -> 303 us (0.968)
  blocking collectives: 123 us -> 74.4 us
  starting transfers between devices: 17.5 us -> 46.9 us
  waiting for transfers between devices: 76 us -> 97.9 us
  Pallas kernels: 52.7 us -> 42 us
    all_to_all x1 -> x3, waiting for transfers between devices: 76 us -> 13.7 us  [the longest x2 13.7 us: along_x(): lax.all_to_all(value, 'lat', 0, 0, axis_index_groups=groups, tiled=True)]
    ppermute x0 -> x8, waiting for transfers between devices: none -> 53.4 us  [along_z(): return lax.ppermute(value, ('lat', 'lev'), pairs)]
    all_to_all x2 -> x1, blocking collectives: 77.3 us -> 36.3 us  [on_device(): forcing = lax.all_to_all(forcing, ('lat', 'lev'), 0, 0, tiled=True)]
    all_to_all x1, waiting for transfers between devices: 0.01 us -> 30.7 us  [on_device(): lax.all_to_all(fourier.reshape(peers, 8, -1), everyone, 0, 0, tiled=True)]
    ppermute x0 -> x8, starting transfers between devices: none -> 16.3 us  [along_z(): return lax.ppermute(value, ('lat', 'lev'), pairs)]
    all_to_all x1 -> x3, starting transfers between devices: 8.91 us -> 19.1 us  [the longest x2 9.83 us: along_x(): lax.all_to_all(value, 'lat', 0, 0, axis_index_groups=groups, tiled=True)]
    unnamed x17 -> x41, local copies, waits for them, and re-layouts: 6.14 us -> 15.5 us
    pallas_call x1, Pallas kernels: 9.99 us -> 1.13 us  [pack_table(): pl.pallas_call(pack_kernel, grid=(LAT_X,), in_specs=[pl.BlockSpec(memory_...]
  transfers between devices with their start and end apart: 2 -> 12, of which waited for: 1 -> 5; matrix products, arithmetic and copies ran while one was open for 12% -> 8% of each run, Pallas kernels for 2% -> 2%
where the time goes in v3:
time: 303 us; the launch traced here: 302 us
  waiting for transfers between devices  97.9 us (32%)
  blocking collectives  74.4 us (25%)
  starting transfers between devices  46.9 us (15%)
  Pallas kernels  42 us (14%)
  other arithmetic  24.6 us (8%)
  local copies, waits for them, and re-layouts  15.7 us (5%)
    ppermute x8, waiting for transfers between devices, along_z(): return lax.ppermute(value, ('lat', 'lev'), pairs)  53.4 us
    all_to_all x1, blocking collectives, on_device(): lax.all_to_all(weighted.reshape(peers, 8, -1), everyone, 0, 0, tiled=True)  38.1 us
    all_to_all x1, blocking collectives, on_device(): forcing = lax.all_to_all(forcing, ('lat', 'lev'), 0, 0, tiled=True)  36.3 us
    all_to_all x1, waiting for transfers between devices, on_device(): lax.all_to_all(fourier.reshape(peers, 8, -1), everyone, 0, 0, tiled=True)  30.7 us
    pallas_call x1, Pallas kernels, columns(): pl.pallas_call(functools.partial(column_kernel, x_rows=240, width=width),...  20.5 us
    another operation x1, other arithmetic  19.3 us
    ppermute x8, starting transfers between devices, along_z(): return lax.ppermute(value, ('lat', 'lev'), pairs)  16.3 us
    unnamed x41, local copies, waits for them, and re-layouts  15.5 us
  transfers between devices with their start and end apart: 12, of which 5 were waited for; matrix products, arithmetic and copies ran while one was open for 8% of the time, Pallas kernels for 2%

profile of v3, /device:TPU:2, one launch (start us, length us, event | category | flops | bytes accessed | tf_op | source)
XLA Modules:
  0.0 301.7 jit_solution(17556997758661177778)
XLA Ops:
  0.7 2.9 copy-done
  3.6 1.1 pack_table.1
  4.7 1.2 copy-done.3
  5.9 5.9 %collective-permute-start.5 = (bf16[4,3,48,384]{3,2,1,0:T(8,128)(2,1)S(1)}, bf16[4,3,48,384]{3,2,1,0:T(8,128)(2,1)S(1)}, u32[]{:S(2)}, u32[]{:S(2)}) collective-permute-start(bf16[4,3,48,384]{3,2,1,0:T(8,128)(2,1)S(1)} %get-tuple-element.19), channel_id=1, source_target_pairs={{0,7},{2,0},{4,2},{6,4},{1,6},{3,1},{5,3},{7,5},{8,15},{10,8},{12,... | collective-permute-start | bytes 1327112 | tf_op jit(solution)/shard_map/ppermute | solution.py:403
  11.8 2.5 collective-permute-start.7
  14.7 16.0 %collective-permute-done.7 = bf16[4,3,24,384]{3,2,1,0:T(8,128)(2,1)S(1)} collective-permute-done((bf16[4,3,24,384]{3,2,1,0:T(8,128)(2,1)S(1)}, bf16[4,3,24,384]{3,2,1,0:T(8,128)(2,1)S(1)}, u32[]{:S(2)}, u32[]{:S(2)}) %collective-permute-start.7) | collective-permute-done | bytes 221216 | tf_op jit(solution)/shard_map/ppermute | solution.py:403
  30.7 1.2 collective-permute-done.6
  31.9 1.5 pad_maximum_fusion.1
  33.4 4.8 %all-to-all-start.1 = ((bf16[4,4,3,48,384]{4,3,2,1,0:T(8,128)(2,1)}), bf16[4,4,3,48,384]{4,3,2,1,0:T(8,128)(2,1)S(1)}, u32[]{:S(2)}, u32[]{:S(2)}) async-start(bf16[4,4,3,48,384]{4,3,2,1,0:T(8,128)(2,1)} %pad_maximum_fusion.1), calls=%async_computation.1 | async-start | bytes 3538944 | tf_op jit(solution)/shard_map/all_to_all | solution.py:408
  38.8 5.2 %prep.1 = bf16[4,24,48,112]{3,2,1,0:T(8,128)(2,1)} custom-call(s32[2]{0:T(128)} %pad_add_fusion.at_ref, f32[45,112,90]{2,1,0:T(8,128)} %bitcast.45), custom_call_target="tpu_custom_call" | custom-call | flops 1000000 | bytes 4000000 | tf_op jit(solution)/shard_map/prep/pallas_call | solution.py:99
  44.0 13.7 %all-to-all-done.1.b_ref = bf16[4,4,3,48,384]{4,3,2,1,0:T(8,128)(2,1)S(1)} async-done(((bf16[4,4,3,48,384]{4,3,2,1,0:T(8,128)(2,1)}), bf16[4,4,3,48,384]{4,3,2,1,0:T(8,128)(2,1)S(1)}, u32[]{:S(2)}, u32[]{:S(2)}) %all-to-all-start.1) | async-done | bytes 1769504 | tf_op jit(solution)/shard_map/all_to_all | solution.py:408
  57.8 5.0 %all-to-all-start = ((bf16[4,4,3,48,384]{4,3,2,1,0:T(8,128)(2,1)}), bf16[4,4,3,48,384]{4,3,2,1,0:T(8,128)(2,1)S(1)}, u32[]{:S(2)}, u32[]{:S(2)}) async-start(bf16[4,4,3,48,384]{4,3,2,1,0:T(8,128)(2,1)} %copy-done.3), calls=%async_computation | async-start | bytes 3538944 | tf_op jit(solution)/shard_map/all_to_all | solution.py:408
  62.8 19.3 %select_convert_fusion.1 = (bf16[1,1440,768]{2,1,0:T(8,128)(2,1)S(1)}, bf16[1,1440,768]{2,1,0:T(8,128)(2,1)S(1)}) fusion(s32[768]{0:T(1024)S(1)} %fusion.19, pred[768]{0:T(1024)(128)(4,1)S(1)} %fusion.29), kind=kLoop, calls=%fused_computation.5 | loop fusion | flops 15482880 | bytes 4427520 | tf_op jit(solution)/shard_map/convert
  82.2 2.4 pad_maximum_fusion.to_grid_ref
  84.6 9.3 %all-to-all-start.2 = ((bf16[32,3,48,112]{3,2,1,0:T(8,128)(2,1)}), bf16[32,3,48,112]{3,2,1,0:T(8,128)(2,1)}, u32[]{:S(2)}, u32[]{:S(2)}) async-start(bf16[32,3,48,112]{3,2,1,0:T(8,128)(2,1)} %bitcast.48), calls=%async_computation.2 | async-start | bytes 2359296 | tf_op jit(solution)/shard_map/all_to_all | solution.py:450
  94.0 1.5 collective-permute-start
  95.5 1.8 collective-permute-start.1
  97.3 1.2 collective-permute-start.2
  98.6 3.0 collective-permute-start.3
  101.6 36.2 %collective-permute-done.2.a_low_ref = bf16[4,3,24,384]{3,2,1,0:T(8,128)(2,1)S(1)} collective-permute-done((bf16[4,3,24,384]{3,2,1,0:T(8,128)(2,1)S(1)}, bf16[4,3,24,384]{3,2,1,0:T(8,128)(2,1)S(1)}, u32[]{:S(2)}, u32[]{:S(2)}) %collective-permute-start.2) | collective-permute-done | bytes 221216 | tf_op jit(solution)/shard_map/ppermute | solution.py:403
  141.6 1.0 copy-done.9
  142.6 1.0 copy-done.11
  145.5 5.0 %inverse.1 = (bf16[2048,256]{1,0:T(8,128)(2,1)S(1)}, bf16[3,768,768]{2,1,0:T(8,128)(2,1)S(1)}) custom-call(s32[4]{0:T(128)S(1)} %and_select_fusion.3.class_ref, bf16[4,4,3,48,384]{4,3,2,1,0:T(8,128)(2,1)S(1)} %all-to-all-done.a_own_ref, bf16[4,3,48,384]{3,2,1,0:T(8,128)(2,1)S(1)} %copy-done.9, bf16[4,3,48,384]{3,2,1,0:T(8,128)(2,1)S(1)} %copy-done.11, ...), custom_call_target="tpu_custom_call" | custom-call | tf_op jit(solution)/shard_map/inverse/pallas_call | solution.py:201
  150.5 1.8 copy-done.1
  152.3 1.0 copy-done.4
  153.3 11.5 %all-to-all-start.3 = ((bf16[256,8,256]{2,1,0:T(8,128)(2,1)}), bf16[256,8,256]{2,1,0:T(8,128)(2,1)S(1)}, u32[]{:S(2)}, u32[]{:S(2)}) async-start(bf16[256,8,256]{2,1,0:T(8,128)(2,1)} %bitcast.42), calls=%async_computation.3 | async-start | bytes 2097152 | tf_op jit(solution)/shard_map/all_to_all | solution.py:457
  165.8 30.7 %all-to-all-done.3 = bf16[256,8,256]{2,1,0:T(8,128)(2,1)S(1)} async-done(((bf16[256,8,256]{2,1,0:T(8,128)(2,1)}), bf16[256,8,256]{2,1,0:T(8,128)(2,1)S(1)}, u32[]{:S(2)}, u32[]{:S(2)}) %all-to-all-start.3) | async-done | bytes 1048608 | tf_op jit(solution)/shard_map/all_to_all | solution.py:457
  196.6 20.5 %columns.1 = bf16[2048,256]{1,0:T(8,128)(2,1)S(1)} custom-call(f32[3]{0:T(128)S(1)} %pad_dynamic-slice_fusion.weight_ref, bf16[2048,256]{1,0:T(8,128)(2,1)S(1)} %bitcast.39, bf16[2,1440,768]{2,1,0:T(8,128)(2,1)} %pad_maximum_fusion.to_grid_ref, bf16[128,256]{1,0:T(8,128)(2,1)S(1)} %pad.13.w_in_ref, f32[1,256]{1,0:T(1,128)S(1)} %bitcast.44, ...), custom_call_target="tpu_custom_call" | custom-call | tf_op jit(solution)/shard_map/columns/pallas_call | solution.py:284
  217.1 38.1 %all_to_all.30 = bf16[256,8,256]{2,1,0:T(8,128)(2,1)S(1)} all-to-all(bf16[256,8,256]{2,1,0:T(8,128)(2,1)S(1)} %bitcast.40), channel_id=1, replica_groups=mesh['ord'=8,'lat'=16,'lev'=2] {'lat','ord','lev'}, dimensions={0} | all-to-all | bytes 2097152 | tf_op jit(solution)/shard_map/all_to_all | solution.py:471
  255.2 4.5 %forward.1 = bf16[16,2,3,48,112]{4,3,2,1,0:T(8,128)(2,1)S(1)} custom-call(s32[4]{0:T(128)S(1)} %and_select_fusion.3.class_ref, bf16[2048,256]{1,0:T(8,128)(2,1)S(1)} %bitcast.41, bf16[3,768,768]{2,1,0:T(8,128)(2,1)S(1)} %copy-done.2, bf16[2,256,112]{2,1,0:T(8,128)(2,1)S(1)} %copy-done.6), custom_call_target="tpu_custom_call" | custom-call | tf_op jit(solution)/shard_map/forward/pallas_call | solution.py:340
  259.7 36.3 %all_to_all.31 = bf16[32,3,48,112]{3,2,1,0:T(8,128)(2,1)} all-to-all(bf16[32,3,48,112]{3,2,1,0:T(8,128)(2,1)S(1)} %bitcast.38), channel_id=1, replica_groups=mesh['ord'=8,'lat'=16,'lev'=2] {'lat','lev'}, dimensions={0} | all-to-all | bytes 2064384 | tf_op jit(solution)/shard_map/all_to_all | solution.py:477
  296.0 5.7 %update.1 = f32[45,112,90]{2,1,0:T(8,128)} custom-call(s32[2]{0:T(128)} %pad_add_fusion.at_ref, f32[45,112,90]{2,1,0:T(8,128)} %bitcast.46, bf16[4,24,48,112]{3,2,1,0:T(8,128)(2,1)} %bitcast.47), custom_call_target="tpu_custom_call" | custom-call | tf_op jit(solution)/shard_map/update/pallas_call | solution.py:383
  (55 shorter events, 8.7 us)
Async XLA Ops:
  0.7 2.9 copy-start
  4.7 1.2 copy-start.3
  5.9 26.0 %collective-permute-start.5 = (bf16[4,3,48,384]{3,2,1,0:T(8,128)(2,1)S(1)}, bf16[4,3,48,384]{3,2,1,0:T(8,128)(2,1)S(1)}, u32[]{:S(2)}, u32[]{:S(2)}) collective-permute-start(bf16[4,3,48,384]{3,2,1,0:T(8,128)(2,1)S(1)} %get-tuple-element.19), channel_id=1, source_target_pairs={{0,7},{2,0},{4,2},{6,4},{1,6},{3,1},{5,3},{7,5},{8,15},{10,8},{12,... | collective-permute-start | bytes 1327112 | tf_op jit(solution)/shard_map/ppermute | solution.py:403
  11.8 20.2 %collective-permute-start.4 = (bf16[4,3,48,384]{3,2,1,0:T(8,128)(2,1)S(1)}, bf16[4,3,48,384]{3,2,1,0:T(8,128)(2,1)S(1)}, u32[]{:S(2)}, u32[]{:S(2)}) collective-permute-start(bf16[4,3,48,384]{3,2,1,0:T(8,128)(2,1)S(1)} %get-tuple-element.18), channel_id=1, source_target_pairs={{0,2},{2,4},{4,6},{6,1},{1,3},{3,5},{5,7},{7,0},{8,10},{10,12},{12... | collective-permute-start | bytes 1327112 | tf_op jit(solution)/shard_map/ppermute | solution.py:403
  11.8 18.9 %collective-permute-start.7 = (bf16[4,3,24,384]{3,2,1,0:T(8,128)(2,1)S(1)}, bf16[4,3,24,384]{3,2,1,0:T(8,128)(2,1)S(1)}, u32[]{:S(2)}, u32[]{:S(2)}) collective-permute-start(bf16[4,3,24,384]{3,2,1,0:T(8,128)(2,1)S(1)} %get-tuple-element.21), channel_id=1, source_target_pairs={{0,5},{2,7},{4,0},{6,2},{1,4},{3,6},{5,1},{7,3},{8,13},{10,15},{12... | collective-permute-start | bytes 663560 | tf_op jit(solution)/shard_map/ppermute | solution.py:403
  14.2 17.6 %collective-permute-start.6 = (bf16[4,3,24,384]{3,2,1,0:T(8,128)(2,1)S(1)}, bf16[4,3,24,384]{3,2,1,0:T(8,128)(2,1)S(1)}, u32[]{:S(2)}, u32[]{:S(2)}) collective-permute-start(bf16[4,3,24,384]{3,2,1,0:T(8,128)(2,1)S(1)} %get-tuple-element.20), channel_id=1, source_target_pairs={{0,4},{2,6},{4,1},{6,3},{1,5},{3,7},{5,0},{7,2},{8,12},{10,14},{12... | collective-permute-start | bytes 663560 | tf_op jit(solution)/shard_map/ppermute | solution.py:403
  33.4 24.4 %all-to-all-start.1 = ((bf16[4,4,3,48,384]{4,3,2,1,0:T(8,128)(2,1)}), bf16[4,4,3,48,384]{4,3,2,1,0:T(8,128)(2,1)S(1)}, u32[]{:S(2)}, u32[]{:S(2)}) async-start(bf16[4,4,3,48,384]{4,3,2,1,0:T(8,128)(2,1)} %pad_maximum_fusion.1), calls=%async_computation.1 | async-start | bytes 3538944 | tf_op jit(solution)/shard_map/all_to_all | solution.py:408
  57.8 26.8 %all-to-all-start = ((bf16[4,4,3,48,384]{4,3,2,1,0:T(8,128)(2,1)}), bf16[4,4,3,48,384]{4,3,2,1,0:T(8,128)(2,1)S(1)}, u32[]{:S(2)}, u32[]{:S(2)}) async-start(bf16[4,4,3,48,384]{4,3,2,1,0:T(8,128)(2,1)} %copy-done.3), calls=%async_computation | async-start | bytes 3538944 | tf_op jit(solution)/shard_map/all_to_all | solution.py:408
  84.6 16.9 %copy-start.19 = (s32[4]{0:T(128)S(1)}, s32[4]{0:T(128)}, u32[]{:S(2)}) copy-start(s32[4]{0:T(128)} %constant.196.clone) | copy-start | bytes 52
  84.6 56.1 %all-to-all-start.2 = ((bf16[32,3,48,112]{3,2,1,0:T(8,128)(2,1)}), bf16[32,3,48,112]{3,2,1,0:T(8,128)(2,1)}, u32[]{:S(2)}, u32[]{:S(2)}) async-start(bf16[32,3,48,112]{3,2,1,0:T(8,128)(2,1)} %bitcast.48), calls=%async_computation.2 | async-start | bytes 2359296 | tf_op jit(solution)/shard_map/all_to_all | solution.py:450
  94.0 45.2 %collective-permute-start = (bf16[4,3,48,384]{3,2,1,0:T(8,128)(2,1)S(1)}, bf16[4,3,48,384]{3,2,1,0:T(8,128)(2,1)S(1)}, u32[]{:S(2)}, u32[]{:S(2)}) collective-permute-start(bf16[4,3,48,384]{3,2,1,0:T(8,128)(2,1)S(1)} %get-tuple-element.30), channel_id=1, source_target_pairs={{0,2},{2,4},{4,6},{6,1},{1,3},{3,5},{5,7},{7,0},{8,10},{10,12},{12... | collective-permute-start | bytes 1327112 | tf_op jit(solution)/shard_map/ppermute | solution.py:403
  95.5 44.4 %collective-permute-start.1 = (bf16[4,3,48,384]{3,2,1,0:T(8,128)(2,1)S(1)}, bf16[4,3,48,384]{3,2,1,0:T(8,128)(2,1)S(1)}, u32[]{:S(2)}, u32[]{:S(2)}) collective-permute-start(bf16[4,3,48,384]{3,2,1,0:T(8,128)(2,1)S(1)} %get-tuple-element.29), channel_id=1, source_target_pairs={{0,7},{2,0},{4,2},{6,4},{1,6},{3,1},{5,3},{7,5},{8,15},{10,8},{12,... | collective-permute-start | bytes 1327112 | tf_op jit(solution)/shard_map/ppermute | solution.py:403
  97.3 40.4 %collective-permute-start.2 = (bf16[4,3,24,384]{3,2,1,0:T(8,128)(2,1)S(1)}, bf16[4,3,24,384]{3,2,1,0:T(8,128)(2,1)S(1)}, u32[]{:S(2)}, u32[]{:S(2)}) collective-permute-start(bf16[4,3,24,384]{3,2,1,0:T(8,128)(2,1)S(1)} %get-tuple-element.28), channel_id=1, source_target_pairs={{0,4},{2,6},{4,1},{6,3},{1,5},{3,7},{5,0},{7,2},{8,12},{10,14},{12... | collective-permute-start | bytes 663560 | tf_op jit(solution)/shard_map/ppermute | solution.py:403
  98.6 39.9 %collective-permute-start.3 = (bf16[4,3,24,384]{3,2,1,0:T(8,128)(2,1)S(1)}, bf16[4,3,24,384]{3,2,1,0:T(8,128)(2,1)S(1)}, u32[]{:S(2)}, u32[]{:S(2)}) collective-permute-start(bf16[4,3,24,384]{3,2,1,0:T(8,128)(2,1)S(1)} %get-tuple-element.27), channel_id=1, source_target_pairs={{0,5},{2,7},{4,0},{6,2},{1,4},{3,6},{5,1},{7,3},{8,13},{10,15},{12... | collective-permute-start | bytes 663560 | tf_op jit(solution)/shard_map/ppermute | solution.py:403
  137.8 0.7 copy-start.12
  138.4 0.7 copy-start.14
  139.1 0.8 copy-start.8
  139.9 0.8 copy-start.10
  140.7 0.9 copy-start.5
  141.6 1.0 copy-start.9
  142.6 1.0 copy-start.11
  143.6 0.9 copy-start.13
  144.5 0.9 copy-start.15
  150.5 1.8 copy-start.1
  152.3 1.0 copy-start.4
  153.2 12.4 %copy-start.17 = (bf16[112,256]{1,0:T(8,128)(2,1)S(1)}, bf16[112,256]{1,0:T(8,128)(2,1)}, u32[]{:S(2)}) copy-start(bf16[112,256]{1,0:T(8,128)(2,1)} %param.13) | copy-start | bytes 172036
  153.2 12.5 %copy-start.18 = (f32[45]{0:T(128)S(1)}, f32[45]{0:T(128)}, u32[]{:S(2)}) copy-start(f32[45]{0:T(128)} %param.12) | copy-start | bytes 544
  153.3 43.3 %copy-start.7 = (bf16[4,256,256]{2,1,0:T(8,128)(2,1)S(1)}, bf16[4,256,256]{2,1,0:T(8,128)(2,1)}, u32[]{:S(2)}) copy-start(bf16[4,256,256]{2,1,0:T(8,128)(2,1)} %w_hid_ref.1) | copy-start | bytes 1572868
  153.3 43.3 %copy-start.16 = (f32[256]{0:T(256)S(1)}, f32[256]{0:T(256)}, u32[]{:S(2)}) copy-start(f32[256]{0:T(256)} %param.14) | copy-start | bytes 3076
  153.3 43.3 %all-to-all-start.3 = ((bf16[256,8,256]{2,1,0:T(8,128)(2,1)}), bf16[256,8,256]{2,1,0:T(8,128)(2,1)S(1)}, u32[]{:S(2)}, u32[]{:S(2)}) async-start(bf16[256,8,256]{2,1,0:T(8,128)(2,1)} %bitcast.42), calls=%async_computation.3 | async-start | bytes 2097152 | tf_op jit(solution)/shard_map/all_to_all | solution.py:457
  196.6 58.7 %copy-start.2 = (bf16[3,768,768]{2,1,0:T(8,128)(2,1)S(1)}, bf16[3,768,768]{2,1,0:T(8,128)(2,1)}, u32[]{:S(2)}) copy-start(bf16[3,768,768]{2,1,0:T(8,128)(2,1)} %copy-done.1) | copy-start | bytes 10616836
  196.6 58.7 %copy-start.6 = (bf16[2,256,112]{2,1,0:T(8,128)(2,1)S(1)}, bf16[2,256,112]{2,1,0:T(8,128)(2,1)}, u32[]{:S(2)}) copy-start(bf16[2,256,112]{2,1,0:T(8,128)(2,1)} %constant.194.clone.maps_ref) | copy-start | bytes 344068

commit v4 on v3

--- a/solution.py
+++ b/solution.py
@@ -150,7 +150,7 @@
         + [b_spec(r) for r in b_rows],
         out_shape=[jax.ShapeDtypeStruct((LAT_X, 4, OWN, rows, half), bf16)]
         + [b_shape(r) for r in b_rows],
-        compiler_params=pltpu.CompilerParams(vmem_limit_bytes=24 * 2**20),
+        compiler_params=pltpu.CompilerParams(vmem_limit_bytes=16 * 2**20),
         name="pack_table",
     )(own, legendre)
 
@@ -226,7 +226,7 @@
             pltpu.VMEM((OWN, 2, lats * lat_slots, LANES), f32),
             pltpu.VMEM((2, peers * 8, LANES), f32),
         ],
-        compiler_params=pltpu.CompilerParams(vmem_limit_bytes=40 * 2**20),
+        compiler_params=pltpu.CompilerParams(vmem_limit_bytes=20 * 2**20),
         name="inverse",
     )(classes, a_own, *a_near, *a_far, b_all, coef, maps)
 
@@ -292,7 +292,7 @@
             pltpu.VMEM((2, OWN, OWN, peers, LANES), f32),
             pltpu.VMEM((2, peers * 8, LANES), f32),
         ],
-        compiler_params=pltpu.CompilerParams(vmem_limit_bytes=48 * 2**20),
+        compiler_params=pltpu.CompilerParams(vmem_limit_bytes=28 * 2**20),
         name="columns",
     )(weights, fourier, to_grid, w_in, bias, w_hid, w_out)
 
@@ -354,7 +354,7 @@
             pltpu.VMEM((OWN, 2, lats * lat_slots, LANES), f32),
             pltpu.VMEM((2, peers * 8, LANES), f32),
         ],
-        compiler_params=pltpu.CompilerParams(vmem_limit_bytes=40 * 2**20),
+        compiler_params=pltpu.CompilerParams(vmem_limit_bytes=16 * 2**20),
         name="forward",
     )(classes, weighted, table, maps)
 
@@ -430,10 +430,12 @@
     a_all, b_own, *b_rest = pack_table(own, legendre, HALF, rows)
     b_left, b_right, b_low, b_high = (along_z(v, k) for v, k in zip(b_rest, (1, -1, 2, -2)))
     a_all = along_x(a_all)
+    b_far = jnp.concatenate([b_low, b_high], axis=2)
+    b_all = jnp.stack([b_own, b_left, b_right, b_far], axis=1)
+    a_all, b_all = lax.optimization_barrier((a_all, b_all))
     a_near = [along_z(a_all[:, 1], 1), along_z(a_all[:, 2], -1)]
     a_far = [along_z(a_all[:, 3, :, : rows // 2], 2), along_z(a_all[:, 3, :, rows // 2 :], -2)]
-    b_far = jnp.concatenate([b_low, b_high], axis=2)
-    b_all = along_x(jnp.stack([b_own, b_left, b_right, b_far], axis=1))
+    b_all = along_x(b_all)
 
     slot = lax.iota(jnp.int32, OWN * peers)
     slot_lev = slot % lev_size
@@ -444,7 +446,9 @@
     order_ids = slot_ord * order_local + OWN * (first_group(slot_x) + slot_w) + slot // peers
     to_grid = lookup_of(order_ids, valid)
     coefficients = prep(at, state)
-    coefficients, b_all, to_grid = lax.optimization_barrier((coefficients, b_all, to_grid))
+    coefficients, a_near, a_far, b_all, to_grid = lax.optimization_barrier(
+        (coefficients, a_near, a_far, b_all, to_grid)
+    )
 
     coefficients = coefficients.reshape(lat_size * lev_size, OWN, rows, channels)
     coefficients = lax.all_to_all(coefficients, ("lat", "lev"), 0, 0, tiled=True)

time: 303 us -> 286 us (0.944)
  waiting for transfers between devices: 97.9 us -> 79.5 us
    ppermute x8, waiting for transfers between devices: 53.4 us -> 21.7 us  [along_z(): return lax.ppermute(value, ('lat', 'lev'), pairs)]
    all_to_all x1, waiting for transfers between devices: 0.01 us -> 27 us  [on_device(): lax.all_to_all(coefficients, ('lat', 'lev'), 0, 0, tiled=True)]
    all_to_all x2, waiting for transfers between devices: 13.7 us -> 0.01 us  [along_x(): lax.all_to_all(value, 'lat', 0, 0, axis_index_groups=groups, tiled=True)]
  transfers between devices with their start and end apart: 12 -> 12, of which waited for: 5 -> 8; matrix products, arithmetic and copies ran while one was open for 8% -> 10% of each run, Pallas kernels for 2% -> 2%
where the time goes in v4:
time: 286 us; the launch traced here: 284 us
  waiting for transfers between devices  79.5 us (28%)
  blocking collectives  74.4 us (26%)
  starting transfers between devices  45.1 us (16%)
  Pallas kernels  41.6 us (15%)
  other arithmetic  26.8 us (9%)
  local copies, waits for them, and re-layouts  16.8 us (6%)
    all_to_all x1, blocking collectives, on_device(): lax.all_to_all(weighted.reshape(peers, 8, -1), everyone, 0, 0, tiled=True)  38.1 us
    all_to_all x1, blocking collectives, on_device(): forcing = lax.all_to_all(forcing, ('lat', 'lev'), 0, 0, tiled=True)  36.3 us
    all_to_all x1, waiting for transfers between devices, on_device(): lax.all_to_all(fourier.reshape(peers, 8, -1), everyone, 0, 0, tiled=True)  30.7 us
    all_to_all x1, waiting for transfers between devices, on_device(): lax.all_to_all(coefficients, ('lat', 'lev'), 0, 0, tiled=True)  27 us
    ppermute x8, waiting for transfers between devices, along_z(): return lax.ppermute(value, ('lat', 'lev'), pairs)  21.7 us
    another operation x1, other arithmetic  19.3 us
    pallas_call x1, Pallas kernels, columns(): pl.pallas_call(functools.partial(column_kernel, x_rows=240, width=width),...  18.6 us
    unnamed x41, local copies, waits for them, and re-layouts  16.6 us
  transfers between devices with their start and end apart: 12, of which 8 were waited for; matrix products, arithmetic and copies ran while one was open for 10% of the time, Pallas kernels for 2%

profile of v4, /device:TPU:2, one launch (start us, length us, event | category | flops | bytes accessed | tf_op | source)
XLA Modules:
  0.0 284.4 jit_solution(12600368443365929355)
XLA Ops:
  0.7 2.9 %copy-done.1 = bf16[90,45,720]{2,1,0:T(8,128)(2,1)S(1)} copy-done((bf16[90,45,720]{2,1,0:T(8,128)(2,1)S(1)}, bf16[90,45,720]{2,1,0:T(8,128)(2,1)}, u32[]{:S(2)}) %copy-start.1) | copy-done | bytes 5832024
  3.6 2.5 pack_table.1
  6.0 5.8 %all-to-all-start = ((bf16[4,4,3,48,384]{4,3,2,1,0:T(8,128)(2,1)}), bf16[4,4,3,48,384]{4,3,2,1,0:T(8,128)(2,1)S(1)}, u32[]{:S(2)}, u32[]{:S(2)}) async-start(bf16[4,4,3,48,384]{4,3,2,1,0:T(8,128)(2,1)} %get-tuple-element.22), calls=%async_computation | async-start | bytes 3538944 | tf_op jit(solution)/shard_map/all_to_all | solution.py:408
  11.9 5.3 %collective-permute-start.3 = (bf16[4,3,24,384]{3,2,1,0:T(8,128)(2,1)S(1)}, bf16[4,3,24,384]{3,2,1,0:T(8,128)(2,1)}, u32[]{:S(2)}, u32[]{:S(2)}) collective-permute-start(bf16[4,3,24,384]{3,2,1,0:T(8,128)(2,1)S(1)} %get-tuple-element.27), channel_id=1, source_target_pairs={{0,5},{2,7},{4,0},{6,2},{1,4},{3,6},{5,1},{7,3},{8,13},{10,15},{12... | collective-permute-start | bytes 663560 | tf_op jit(solution)/shard_map/ppermute | solution.py:403
  17.2 3.7 %collective-permute-start.1 = (bf16[4,3,48,384]{3,2,1,0:T(8,128)(2,1)S(1)}, bf16[4,3,48,384]{3,2,1,0:T(8,128)(2,1)}, u32[]{:S(2)}, u32[]{:S(2)}) collective-permute-start(bf16[4,3,48,384]{3,2,1,0:T(8,128)(2,1)S(1)} %get-tuple-element.25), channel_id=1, source_target_pairs={{0,7},{2,0},{4,2},{6,4},{1,6},{3,1},{5,3},{7,5},{8,15},{10,8},{12,... | collective-permute-start | bytes 1327112 | tf_op jit(solution)/shard_map/ppermute | solution.py:403
  21.5 5.3 %prep.1 = bf16[4,24,48,112]{3,2,1,0:T(8,128)(2,1)} custom-call(s32[2]{0:T(128)} %pad_add_fusion.at_ref, f32[45,112,90]{2,1,0:T(8,128)} %bitcast.37), custom_call_target="tpu_custom_call" | custom-call | flops 1000000 | bytes 4000000 | tf_op jit(solution)/shard_map/prep/pallas_call | solution.py:99
  27.4 3.9 %collective-permute-done.2 = bf16[4,3,24,384]{3,2,1,0:T(8,128)(2,1)} collective-permute-done((bf16[4,3,24,384]{3,2,1,0:T(8,128)(2,1)S(1)}, bf16[4,3,24,384]{3,2,1,0:T(8,128)(2,1)}, u32[]{:S(2)}, u32[]{:S(2)}) %collective-permute-start.2) | collective-permute-done | bytes 221216 | tf_op jit(solution)/shard_map/ppermute | solution.py:403
  31.3 1.1 maximum_bitcast_fusion
  32.4 3.2 %collective-permute-done.1 = bf16[4,3,48,384]{3,2,1,0:T(8,128)(2,1)} collective-permute-done((bf16[4,3,48,384]{3,2,1,0:T(8,128)(2,1)S(1)}, bf16[4,3,48,384]{3,2,1,0:T(8,128)(2,1)}, u32[]{:S(2)}, u32[]{:S(2)}) %collective-permute-start.1) | collective-permute-done | bytes 442400 | tf_op jit(solution)/shard_map/ppermute | solution.py:403
  35.6 3.9 %collective-permute-done = bf16[4,3,48,384]{3,2,1,0:T(8,128)(2,1)} collective-permute-done((bf16[4,3,48,384]{3,2,1,0:T(8,128)(2,1)S(1)}, bf16[4,3,48,384]{3,2,1,0:T(8,128)(2,1)}, u32[]{:S(2)}, u32[]{:S(2)}) %collective-permute-start) | collective-permute-done | bytes 442400 | tf_op jit(solution)/shard_map/ppermute | solution.py:403
  39.5 2.7 pad_maximum_fusion.1
  42.2 4.8 %all-to-all-start.1 = ((bf16[4,4,3,48,384]{4,3,2,1,0:T(8,128)(2,1)}), bf16[4,4,3,48,384]{4,3,2,1,0:T(8,128)(2,1)S(1)}, u32[]{:S(2)}, u32[]{:S(2)}) async-start(bf16[4,4,3,48,384]{4,3,2,1,0:T(8,128)(2,1)} %pad_maximum_fusion.1), calls=%async_computation.1 | async-start | bytes 3538944 | tf_op jit(solution)/shard_map/all_to_all | solution.py:408
  47.0 19.3 %select_convert_fusion.1 = (bf16[1,1440,768]{2,1,0:T(8,128)(2,1)S(1)}, bf16[1,1440,768]{2,1,0:T(8,128)(2,1)S(1)}) fusion(s32[768]{0:T(1024)S(1)} %fusion.19, pred[768]{0:T(1024)(128)(4,1)S(1)} %fusion.29), kind=kLoop, calls=%fused_computation.5 | loop fusion | flops 15482880 | bytes 4427520 | tf_op jit(solution)/shard_map/convert
  66.5 3.2 %collective-permute-start.5 = (bf16[4,3,48,384]{3,2,1,0:T(8,128)(2,1)S(1)}, bf16[4,3,48,384]{3,2,1,0:T(8,128)(2,1)S(1)}, u32[]{:S(2)}, u32[]{:S(2)}) collective-permute-start(bf16[4,3,48,384]{3,2,1,0:T(8,128)(2,1)S(1)} %get-tuple-element.41), channel_id=1, source_target_pairs={{0,7},{2,0},{4,2},{6,4},{1,6},{3,1},{5,3},{7,5},{8,15},{10,8},{12,... | collective-permute-start | bytes 1327112 | tf_op jit(solution)/shard_map/ppermute | solution.py:403
  69.8 4.1 %collective-permute-start.7 = (bf16[4,3,24,384]{3,2,1,0:T(8,128)(2,1)S(1)}, bf16[4,3,24,384]{3,2,1,0:T(8,128)(2,1)S(1)}, u32[]{:S(2)}, u32[]{:S(2)}) collective-permute-start(bf16[4,3,24,384]{3,2,1,0:T(8,128)(2,1)S(1)} %get-tuple-element.39), channel_id=1, source_target_pairs={{0,5},{2,7},{4,0},{6,2},{1,4},{3,6},{5,1},{7,3},{8,13},{10,15},{12... | collective-permute-start | bytes 663560 | tf_op jit(solution)/shard_map/ppermute | solution.py:403
  73.9 2.4 pad_maximum_fusion.to_grid_ref
  76.4 6.8 %collective-permute-done.6.a_low_ref = bf16[4,3,24,384]{3,2,1,0:T(8,128)(2,1)S(1)} collective-permute-done((bf16[4,3,24,384]{3,2,1,0:T(8,128)(2,1)S(1)}, bf16[4,3,24,384]{3,2,1,0:T(8,128)(2,1)S(1)}, u32[]{:S(2)}, u32[]{:S(2)}) %collective-permute-start.6) | collective-permute-done | bytes 221216 | tf_op jit(solution)/shard_map/ppermute | solution.py:403
  83.9 3.3 %collective-permute-done.7.a_high_ref = bf16[4,3,24,384]{3,2,1,0:T(8,128)(2,1)S(1)} collective-permute-done((bf16[4,3,24,384]{3,2,1,0:T(8,128)(2,1)S(1)}, bf16[4,3,24,384]{3,2,1,0:T(8,128)(2,1)S(1)}, u32[]{:S(2)}, u32[]{:S(2)}) %collective-permute-start.7) | collective-permute-done | bytes 221216 | tf_op jit(solution)/shard_map/ppermute | solution.py:403
  89.5 9.0 %all-to-all-start.2 = ((bf16[32,3,48,112]{3,2,1,0:T(8,128)(2,1)}), bf16[32,3,48,112]{3,2,1,0:T(8,128)(2,1)}, u32[]{:S(2)}, u32[]{:S(2)}) async-start(bf16[32,3,48,112]{3,2,1,0:T(8,128)(2,1)} %bitcast.40), calls=%async_computation.2 | async-start | bytes 2359296 | tf_op jit(solution)/shard_map/all_to_all | solution.py:454
  98.5 27.0 %all-to-all-done.2 = bf16[32,3,48,112]{3,2,1,0:T(8,128)(2,1)} async-done(((bf16[32,3,48,112]{3,2,1,0:T(8,128)(2,1)}), bf16[32,3,48,112]{3,2,1,0:T(8,128)(2,1)}, u32[]{:S(2)}, u32[]{:S(2)}) %all-to-all-start.2) | async-done | bytes 1032224 | tf_op jit(solution)/shard_map/all_to_all | solution.py:454
  126.5 1.0 copy-done.9
  127.5 1.0 copy-done.11
  130.4 5.0 %inverse.1 = (bf16[2048,256]{1,0:T(8,128)(2,1)S(1)}, bf16[3,768,768]{2,1,0:T(8,128)(2,1)S(1)}) custom-call(s32[4]{0:T(128)S(1)} %and_select_fusion.3.class_ref, bf16[4,4,3,48,384]{4,3,2,1,0:T(8,128)(2,1)S(1)} %all-to-all-done.a_own_ref, bf16[4,3,48,384]{3,2,1,0:T(8,128)(2,1)S(1)} %copy-done.9, bf16[4,3,48,384]{3,2,1,0:T(8,128)(2,1)S(1)} %copy-done.11, ...), custom_call_target="tpu_custom_call" | custom-call | tf_op jit(solution)/shard_map/inverse/pallas_call | solution.py:201
  135.4 1.8 copy-done.2
  138.2 9.0 %all-to-all-start.3 = ((bf16[256,8,256]{2,1,0:T(8,128)(2,1)}), bf16[256,8,256]{2,1,0:T(8,128)(2,1)S(1)}, u32[]{:S(2)}, u32[]{:S(2)}) async-start(bf16[256,8,256]{2,1,0:T(8,128)(2,1)} %bitcast.34), calls=%async_computation.3 | async-start | bytes 2097152 | tf_op jit(solution)/shard_map/all_to_all | solution.py:461
  148.2 30.7 %all-to-all-done.3 = bf16[256,8,256]{2,1,0:T(8,128)(2,1)S(1)} async-done(((bf16[256,8,256]{2,1,0:T(8,128)(2,1)}), bf16[256,8,256]{2,1,0:T(8,128)(2,1)S(1)}, u32[]{:S(2)}, u32[]{:S(2)}) %all-to-all-start.3) | async-done | bytes 1048608 | tf_op jit(solution)/shard_map/all_to_all | solution.py:461
  179.0 2.3 copy-done
  181.2 18.6 %columns.1 = bf16[2048,256]{1,0:T(8,128)(2,1)S(1)} custom-call(f32[3]{0:T(128)S(1)} %pad_dynamic-slice_fusion.weight_ref, bf16[2048,256]{1,0:T(8,128)(2,1)S(1)} %bitcast.31, bf16[2,1440,768]{2,1,0:T(8,128)(2,1)S(1)} %copy-done, bf16[128,256]{1,0:T(8,128)(2,1)S(1)} %pad.13.w_in_ref, f32[1,256]{1,0:T(1,128)S(1)} %bitcast.36, ...), custom_call_target="tpu_custom_call" | custom-call | tf_op jit(solution)/shard_map/columns/pallas_call | solution.py:284
  199.9 38.1 %all_to_all.30 = bf16[256,8,256]{2,1,0:T(8,128)(2,1)S(1)} all-to-all(bf16[256,8,256]{2,1,0:T(8,128)(2,1)S(1)} %bitcast.32), channel_id=1, replica_groups=mesh['ord'=8,'lat'=16,'lev'=2] {'lat','ord','lev'}, dimensions={0} | all-to-all | bytes 2097152 | tf_op jit(solution)/shard_map/all_to_all | solution.py:475
  238.0 4.5 %forward.1 = bf16[16,2,3,48,112]{4,3,2,1,0:T(8,128)(2,1)S(1)} custom-call(s32[4]{0:T(128)S(1)} %and_select_fusion.3.class_ref, bf16[2048,256]{1,0:T(8,128)(2,1)S(1)} %bitcast.33, bf16[3,768,768]{2,1,0:T(8,128)(2,1)S(1)} %copy-done.3, bf16[2,256,112]{2,1,0:T(8,128)(2,1)S(1)} %copy-done.6), custom_call_target="tpu_custom_call" | custom-call | tf_op jit(solution)/shard_map/forward/pallas_call | solution.py:340
  242.5 36.3 %all_to_all.31 = bf16[32,3,48,112]{3,2,1,0:T(8,128)(2,1)} all-to-all(bf16[32,3,48,112]{3,2,1,0:T(8,128)(2,1)S(1)} %bitcast.30), channel_id=1, replica_groups=mesh['ord'=8,'lat'=16,'lev'=2] {'lat','lev'}, dimensions={0} | all-to-all | bytes 2064384 | tf_op jit(solution)/shard_map/all_to_all | solution.py:481
  278.8 5.7 %update.1 = f32[45,112,90]{2,1,0:T(8,128)} custom-call(s32[2]{0:T(128)} %pad_add_fusion.at_ref, f32[45,112,90]{2,1,0:T(8,128)} %bitcast.38, bf16[4,24,48,112]{3,2,1,0:T(8,128)(2,1)} %bitcast.39), custom_call_target="tpu_custom_call" | custom-call | tf_op jit(solution)/shard_map/update/pallas_call | solution.py:383
  (55 shorter events, 10.0 us)
Async XLA Ops:
  0.7 2.9 %copy-start.1 = (bf16[90,45,720]{2,1,0:T(8,128)(2,1)S(1)}, bf16[90,45,720]{2,1,0:T(8,128)(2,1)}, u32[]{:S(2)}) copy-start(bf16[90,45,720]{2,1,0:T(8,128)(2,1)} %in_ref.1) | copy-start | bytes 17496004
  6.0 36.1 %all-to-all-start = ((bf16[4,4,3,48,384]{4,3,2,1,0:T(8,128)(2,1)}), bf16[4,4,3,48,384]{4,3,2,1,0:T(8,128)(2,1)S(1)}, u32[]{:S(2)}, u32[]{:S(2)}) async-start(bf16[4,4,3,48,384]{4,3,2,1,0:T(8,128)(2,1)} %get-tuple-element.22), calls=%async_computation | async-start | bytes 3538944 | tf_op jit(solution)/shard_map/all_to_all | solution.py:408
  11.9 15.5 %collective-permute-start.3 = (bf16[4,3,24,384]{3,2,1,0:T(8,128)(2,1)S(1)}, bf16[4,3,24,384]{3,2,1,0:T(8,128)(2,1)}, u32[]{:S(2)}, u32[]{:S(2)}) collective-permute-start(bf16[4,3,24,384]{3,2,1,0:T(8,128)(2,1)S(1)} %get-tuple-element.27), channel_id=1, source_target_pairs={{0,5},{2,7},{4,0},{6,2},{1,4},{3,6},{5,1},{7,3},{8,13},{10,15},{12... | collective-permute-start | bytes 663560 | tf_op jit(solution)/shard_map/ppermute | solution.py:403
  17.2 14.2 %collective-permute-start.2 = (bf16[4,3,24,384]{3,2,1,0:T(8,128)(2,1)S(1)}, bf16[4,3,24,384]{3,2,1,0:T(8,128)(2,1)}, u32[]{:S(2)}, u32[]{:S(2)}) collective-permute-start(bf16[4,3,24,384]{3,2,1,0:T(8,128)(2,1)S(1)} %get-tuple-element.26), channel_id=1, source_target_pairs={{0,4},{2,6},{4,1},{6,3},{1,5},{3,7},{5,0},{7,2},{8,12},{10,14},{12... | collective-permute-start | bytes 663560 | tf_op jit(solution)/shard_map/ppermute | solution.py:403
  17.2 18.5 %collective-permute-start.1 = (bf16[4,3,48,384]{3,2,1,0:T(8,128)(2,1)S(1)}, bf16[4,3,48,384]{3,2,1,0:T(8,128)(2,1)}, u32[]{:S(2)}, u32[]{:S(2)}) collective-permute-start(bf16[4,3,48,384]{3,2,1,0:T(8,128)(2,1)S(1)} %get-tuple-element.25), channel_id=1, source_target_pairs={{0,7},{2,0},{4,2},{6,4},{1,6},{3,1},{5,3},{7,5},{8,15},{10,8},{12,... | collective-permute-start | bytes 1327112 | tf_op jit(solution)/shard_map/ppermute | solution.py:403
  20.9 18.6 %collective-permute-start = (bf16[4,3,48,384]{3,2,1,0:T(8,128)(2,1)S(1)}, bf16[4,3,48,384]{3,2,1,0:T(8,128)(2,1)}, u32[]{:S(2)}, u32[]{:S(2)}) collective-permute-start(bf16[4,3,48,384]{3,2,1,0:T(8,128)(2,1)S(1)} %get-tuple-element.24), channel_id=1, source_target_pairs={{0,2},{2,4},{4,6},{6,1},{1,3},{3,5},{5,7},{7,0},{8,10},{10,12},{12... | collective-permute-start | bytes 1327112 | tf_op jit(solution)/shard_map/ppermute | solution.py:403
  42.2 47.3 %all-to-all-start.1 = ((bf16[4,4,3,48,384]{4,3,2,1,0:T(8,128)(2,1)}), bf16[4,4,3,48,384]{4,3,2,1,0:T(8,128)(2,1)S(1)}, u32[]{:S(2)}, u32[]{:S(2)}) async-start(bf16[4,4,3,48,384]{4,3,2,1,0:T(8,128)(2,1)} %pad_maximum_fusion.1), calls=%async_computation.1 | async-start | bytes 3538944 | tf_op jit(solution)/shard_map/all_to_all | solution.py:408
  66.4 21.5 %collective-permute-start.4 = (bf16[4,3,48,384]{3,2,1,0:T(8,128)(2,1)S(1)}, bf16[4,3,48,384]{3,2,1,0:T(8,128)(2,1)S(1)}, u32[]{:S(2)}, u32[]{:S(2)}) collective-permute-start(bf16[4,3,48,384]{3,2,1,0:T(8,128)(2,1)S(1)} %get-tuple-element.42), channel_id=1, source_target_pairs={{0,2},{2,4},{4,6},{6,1},{1,3},{3,5},{5,7},{7,0},{8,10},{10,12},{12... | collective-permute-start | bytes 1327112 | tf_op jit(solution)/shard_map/ppermute | solution.py:403
  66.5 22.2 %collective-permute-start.5 = (bf16[4,3,48,384]{3,2,1,0:T(8,128)(2,1)S(1)}, bf16[4,3,48,384]{3,2,1,0:T(8,128)(2,1)S(1)}, u32[]{:S(2)}, u32[]{:S(2)}) collective-permute-start(bf16[4,3,48,384]{3,2,1,0:T(8,128)(2,1)S(1)} %get-tuple-element.41), channel_id=1, source_target_pairs={{0,7},{2,0},{4,2},{6,4},{1,6},{3,1},{5,3},{7,5},{8,15},{10,8},{12,... | collective-permute-start | bytes 1327112 | tf_op jit(solution)/shard_map/ppermute | solution.py:403
  69.7 13.4 %collective-permute-start.6 = (bf16[4,3,24,384]{3,2,1,0:T(8,128)(2,1)S(1)}, bf16[4,3,24,384]{3,2,1,0:T(8,128)(2,1)S(1)}, u32[]{:S(2)}, u32[]{:S(2)}) collective-permute-start(bf16[4,3,24,384]{3,2,1,0:T(8,128)(2,1)S(1)} %get-tuple-element.40), channel_id=1, source_target_pairs={{0,4},{2,6},{4,1},{6,3},{1,5},{3,7},{5,0},{7,2},{8,12},{10,14},{12... | collective-permute-start | bytes 663560 | tf_op jit(solution)/shard_map/ppermute | solution.py:403
  69.8 17.4 %collective-permute-start.7 = (bf16[4,3,24,384]{3,2,1,0:T(8,128)(2,1)S(1)}, bf16[4,3,24,384]{3,2,1,0:T(8,128)(2,1)S(1)}, u32[]{:S(2)}, u32[]{:S(2)}) collective-permute-start(bf16[4,3,24,384]{3,2,1,0:T(8,128)(2,1)S(1)} %get-tuple-element.39), channel_id=1, source_target_pairs={{0,5},{2,7},{4,0},{6,2},{1,4},{3,6},{5,1},{7,3},{8,13},{10,15},{12... | collective-permute-start | bytes 663560 | tf_op jit(solution)/shard_map/ppermute | solution.py:403
  76.4 22.1 %copy-start.19 = (s32[4]{0:T(128)S(1)}, s32[4]{0:T(128)}, u32[]{:S(2)}) copy-start(s32[4]{0:T(128)} %constant.196.clone) | copy-start | bytes 52
  83.2 0.7 copy-start.12
  87.2 0.7 copy-start.14
  87.9 0.8 copy-start.8
  88.6 0.8 copy-start.10
  89.5 36.1 %all-to-all-start.2 = ((bf16[32,3,48,112]{3,2,1,0:T(8,128)(2,1)}), bf16[32,3,48,112]{3,2,1,0:T(8,128)(2,1)}, u32[]{:S(2)}, u32[]{:S(2)}) async-start(bf16[32,3,48,112]{3,2,1,0:T(8,128)(2,1)} %bitcast.40), calls=%async_computation.2 | async-start | bytes 2359296 | tf_op jit(solution)/shard_map/all_to_all | solution.py:454
  125.6 0.9 copy-start.5
  126.5 1.0 copy-start.9
  127.5 1.0 copy-start.11
  128.5 0.9 copy-start.13
  129.4 0.9 copy-start.15
  135.4 1.8 copy-start.2
  137.2 1.0 copy-start.4
  138.2 9.9 %copy-start.17 = (bf16[112,256]{1,0:T(8,128)(2,1)S(1)}, bf16[112,256]{1,0:T(8,128)(2,1)}, u32[]{:S(2)}) copy-start(bf16[112,256]{1,0:T(8,128)(2,1)} %param.13) | copy-start | bytes 172036
  138.2 10.0 %copy-start.18 = (f32[45]{0:T(128)S(1)}, f32[45]{0:T(128)}, u32[]{:S(2)}) copy-start(f32[45]{0:T(128)} %param.12) | copy-start | bytes 544
  138.2 40.8 %copy-start.7 = (bf16[4,256,256]{2,1,0:T(8,128)(2,1)S(1)}, bf16[4,256,256]{2,1,0:T(8,128)(2,1)}, u32[]{:S(2)}) copy-start(bf16[4,256,256]{2,1,0:T(8,128)(2,1)} %w_hid_ref.1) | copy-start | bytes 1572868
  138.2 40.8 %copy-start.16 = (f32[256]{0:T(256)S(1)}, f32[256]{0:T(256)}, u32[]{:S(2)}) copy-start(f32[256]{0:T(256)} %param.14) | copy-start | bytes 3076
  138.2 40.8 %all-to-all-start.3 = ((bf16[256,8,256]{2,1,0:T(8,128)(2,1)}), bf16[256,8,256]{2,1,0:T(8,128)(2,1)S(1)}, u32[]{:S(2)}, u32[]{:S(2)}) async-start(bf16[256,8,256]{2,1,0:T(8,128)(2,1)} %bitcast.34), calls=%async_computation.3 | async-start | bytes 2097152 | tf_op jit(solution)/shard_map/all_to_all | solution.py:461
  179.0 2.3 copy-start
  181.2 56.8 %copy-start.3 = (bf16[3,768,768]{2,1,0:T(8,128)(2,1)S(1)}, bf16[3,768,768]{2,1,0:T(8,128)(2,1)}, u32[]{:S(2)}) copy-start(bf16[3,768,768]{2,1,0:T(8,128)(2,1)} %copy-done.2) | copy-start | bytes 10616836
  181.2 56.8 %copy-start.6 = (bf16[2,256,112]{2,1,0:T(8,128)(2,1)S(1)}, bf16[2,256,112]{2,1,0:T(8,128)(2,1)}, u32[]{:S(2)}) copy-start(bf16[2,256,112]{2,1,0:T(8,128)(2,1)} %constant.194.clone.maps_ref) | copy-start | bytes 344068

commit v5 on v4

--- a/solution.py
+++ b/solution.py
@@ -43,7 +43,7 @@
 
 
 def lane_maps(levs, row_local):
-    maps = np.zeros((levs, 2 * LANES, 2 * row_local), np.float32)
+    maps = np.zeros((levs, 2 * LANES, LANES), np.float32)
     for lev in range(levs):
         for row in range(row_local):
             for part in range(2):
@@ -77,38 +77,61 @@
         put_slab(part, 2, 2, last)
 
 
-def prep_kernel(at_ref, state_ref, out_ref, scr_ref, *, degrees):
-    orders = state_ref.shape[2]
-    group = out_ref.shape[1]
-    step = pl.program_id(0) * 8
-    order = lax.broadcasted_iota(jnp.int32, state_ref.shape[1:], 1) + at_ref[0]
-    for i in range(8):
-        degree = step + i
-        keep = (degree + at_ref[1] >= order) & (degree < degrees)
-        scr_ref[pl.ds(i, orders, 8), :] = jnp.where(keep, state_ref[i], 0.0).T
-    rows = scr_ref[...].astype(bf16).reshape(orders, 8, -1)
+def spare_lanes(shape, width):
+    lane = lax.broadcasted_iota(jnp.int32, shape, len(shape) - 1)
+    return (lane >= width) & (lane < width + SPARE)
+
+
+def scatter_last(row, t, width):
+    return pltpu.roll(row, (width - SPARE * t) % LANES, 1)
+
+
+def gather_last(last, slab, t, width):
+    lane = lax.broadcasted_iota(jnp.int32, slab.shape, 1)
+    moved = pltpu.roll(slab, (SPARE * t - width) % LANES, 1)
+    return jnp.where((lane >= SPARE * t) & (lane < SPARE * (t + 1)), moved, last)
+
+
+def wide(value):
+    return jnp.pad(value, ((0, 0), (0, LANES - value.shape[1])))
+
+
+def prep_kernel(at_ref, state_ref, last_ref, out_ref, scr_ref):
+    _, channels, orders = state_ref.shape
+    group, rows = out_ref.shape[1], 8 * pl.num_programs(0)
+    b = pl.program_id(0)
+    order = lax.broadcasted_iota(jnp.int32, (channels, orders), 1) + at_ref[0]
+    masked = lambda value, degree: wide(jnp.where(degree + at_ref[1] >= order, value, 0.0).T)
+    last = masked(last_ref[b], rows + b)
+    spare = spare_lanes(last.shape, channels)
+    for t in range(8):
+        scr_ref[pl.ds(t, orders, 8), :] = jnp.where(
+            spare, scatter_last(last, t, channels), masked(state_ref[t], 8 * b + t)
+        )
+    packed = scr_ref[...].astype(bf16).reshape(orders, 8, LANES)
     for x in range(LAT_X):
         first = OWN * first_group(x)
-        out_ref[x] = rows[first : first + group]
-
-
-def prep(at, state):
+        out_ref[x] = packed[first : first + group]
+
+
+def prep(at, state, rows):
     group = OWN * Z_RING
-    degrees, channels, orders = state.shape
-    padded = -(-degrees // 8) * 8
-    return pl.pallas_call(
-        functools.partial(prep_kernel, degrees=degrees),
-        grid=(padded // 8,),
+    _, channels, orders = state.shape
+    steps = rows // 8
+    return pl.pallas_call(
+        prep_kernel,
+        grid=(steps,),
         in_specs=[
             pl.BlockSpec(memory_space=pltpu.SMEM),
             pl.BlockSpec((8, channels, orders), lambda i: (i, 0, 0)),
-        ],
-        out_specs=pl.BlockSpec((LAT_X, group, 8, channels), lambda i: (0, 0, i, 0)),
-        out_shape=jax.ShapeDtypeStruct((LAT_X, group, padded, channels), bf16),
-        scratch_shapes=[pltpu.VMEM((orders * 8, channels), f32)],
+            pl.BlockSpec((8, channels, orders), lambda i: (steps, 0, 0)),
+        ],
+        out_specs=pl.BlockSpec((LAT_X, group, 8, LANES), lambda i: (0, 0, i, 0)),
+        out_shape=jax.ShapeDtypeStruct((LAT_X, group, rows, LANES), bf16),
+        scratch_shapes=[pltpu.VMEM((orders * 8, LANES), f32)],
         cost_estimate=pl.CostEstimate(flops=10**6, bytes_accessed=4 * 10**6, transcendentals=0),
         name="prep",
-    )(at, state)
+    )(at, state, state)
 
 
 def pack_kernel(own_ref, in_ref, a_ref, *b_refs):
@@ -155,24 +178,64 @@
     )(own, legendre)
 
 
-def inverse_kernel(
-    class_ref, a_own_ref, a_left_ref, a_right_ref, a_low_ref, a_high_ref, b_ref, coef_ref, maps_ref,
-    out_ref, table_ref, sums_ref, scr_ref, *, lats, lat_local, lat_slots, width,
-):
-    m = pl.program_id(0)
+def assemble_kernel(a_own_ref, a_left_ref, a_right_ref, a_low_ref, a_high_ref, b_ref, out_ref):
     rows, half = b_ref.shape[-2:]
     place = LAT_X * rows
     far = jnp.concatenate([a_low_ref[...], a_high_ref[...]], axis=1)
     for k, piece in enumerate((a_own_ref[:, 0], a_left_ref[...], a_right_ref[...], far)):
-        table_ref[0, k * place : (k + 1) * place, :half] = piece.reshape(place, half)
-        table_ref[0, k * place : (k + 1) * place, half:] = b_ref[:, k].reshape(place, half)
+        out_ref[0, k * place : (k + 1) * place, :half] = piece.reshape(place, half)
+        out_ref[0, k * place : (k + 1) * place, half:] = b_ref[:, k].reshape(place, half)
+
+
+def assemble(a_own, a_near, a_far, b_all):
+    rows, half = b_all.shape[-2:]
+    size = 4 * LAT_X * rows
+    near = pl.BlockSpec((LAT_X, None, rows, half), lambda m: (0, m, 0, 0))
+    far = pl.BlockSpec((LAT_X, None, rows // 2, half), lambda m: (0, m, 0, 0))
+    return pl.pallas_call(
+        assemble_kernel,
+        grid=(OWN,),
+        in_specs=[
+            pl.BlockSpec((LAT_X, 1, None, rows, half), lambda m: (0, 0, m, 0, 0)),
+            near,
+            near,
+            far,
+            far,
+            pl.BlockSpec((LAT_X, 4, None, rows, half), lambda m: (0, 0, m, 0, 0)),
+        ],
+        out_specs=pl.BlockSpec((1, size, 2 * half), lambda m: (m, 0, 0)),
+        out_shape=jax.ShapeDtypeStruct((OWN, size, 2 * half), bf16),
+        cost_estimate=pl.CostEstimate(flops=10**6, bytes_accessed=8 * 10**6, transcendentals=0),
+        name="assemble",
+    )(a_own, *a_near, *a_far, b_all)
+
+
+def inverse_kernel(
+    class_ref, table_ref, coef_ref, maps_ref, out_ref, sums_ref, scr_ref, sent_ref, full_ref,
+    *, lats, lat_local, lat_slots, width,
+):
+    m = pl.program_id(0)
+    sent = coef_ref.shape[2]
+    rows = full_ref.shape[0] // lats
     swapped = 0.0
     for v in range(maps_ref.shape[0]):
-        coef = jnp.concatenate(
-            [coef_ref[x * Z_LOW + class_ref[k], v] for k in range(4) for x in range(LAT_X)]
-        )
+        for q in range(lats):
+            k, x = divmod(q, LAT_X)
+            piece = coef_ref[x * Z_LOW + class_ref[k], v].astype(f32)
+            sent_ref[q * sent : (q + 1) * sent, :] = piece
+            full_ref[q * rows : q * rows + sent, :] = piece
+            full_ref[q * rows + sent : (q + 1) * rows, :] = jnp.zeros((rows - sent, LANES), f32)
+        for b in range(sent // 8):
+            last = jnp.zeros((lats, LANES), f32)
+            for t in range(8):
+                slab = sent_ref[pl.ds(8 * b + t, lats, sent), :]
+                last = gather_last(last, slab, t, width)
+            full_ref[pl.ds(sent + b, lats, rows), :] = last
         swapped += lax.dot_general(
-            maps_ref[v], coef, (((1,), (1,)), ((), ())), preferred_element_type=f32
+            maps_ref[v],
+            full_ref[...].astype(bf16),
+            (((1,), (1,)), ((), ())),
+            preferred_element_type=f32,
         )
     sums = dot(swapped.astype(bf16), table_ref[0]).T
     for part in range(2):
@@ -192,12 +255,9 @@
         pack_rows(slab_of, out_ref, scr_ref, peers, width)
 
 
-def inverse(classes, a_own, a_near, a_far, b_all, coef, maps, peers, lat_local, lat_slots, width):
-    rows, half = b_all.shape[-2:]
-    lats, levs, _, _, channels = coef.shape
-    size = 4 * LAT_X * rows
-    near = pl.BlockSpec((LAT_X, None, rows, half), lambda m: (0, m, 0, 0))
-    far = pl.BlockSpec((LAT_X, None, rows // 2, half), lambda m: (0, m, 0, 0))
+def inverse(classes, table, coef, maps, peers, lat_local, lat_slots, width):
+    lats, levs, _, sent, lanes = coef.shape
+    size = table.shape[1]
     return pl.pallas_call(
         functools.partial(
             inverse_kernel, lats=lats, lat_local=lat_local, lat_slots=lat_slots, width=width
@@ -205,30 +265,21 @@
         grid=(OWN,),
         in_specs=[
             pl.BlockSpec(memory_space=pltpu.SMEM),
-            pl.BlockSpec((LAT_X, 1, None, rows, half), lambda m: (0, 0, m, 0, 0)),
-            near,
-            near,
-            far,
-            far,
-            pl.BlockSpec((LAT_X, 4, None, rows, half), lambda m: (0, 0, m, 0, 0)),
-            pl.BlockSpec((lats, levs, None, rows, channels), lambda m: (0, 0, m, 0, 0)),
+            pl.BlockSpec((1, *table.shape[1:]), lambda m: (m, 0, 0)),
+            pl.BlockSpec((lats, levs, None, sent, lanes), lambda m: (0, 0, m, 0, 0)),
             pl.BlockSpec(maps.shape, lambda m: (0, 0, 0)),
         ],
-        out_specs=[
-            pl.BlockSpec((peers * 8, 2 * LANES), lambda m: (0, 0)),
-            pl.BlockSpec((1, size, 2 * half), lambda m: (m, 0, 0)),
-        ],
-        out_shape=[
-            jax.ShapeDtypeStruct((peers * 8, 2 * LANES), bf16),
-            jax.ShapeDtypeStruct((OWN, size, 2 * half), bf16),
-        ],
+        out_specs=pl.BlockSpec((peers * 8, 2 * LANES), lambda m: (0, 0)),
+        out_shape=jax.ShapeDtypeStruct((peers * 8, 2 * LANES), bf16),
         scratch_shapes=[
             pltpu.VMEM((OWN, 2, lats * lat_slots, LANES), f32),
             pltpu.VMEM((2, peers * 8, LANES), f32),
+            pltpu.VMEM((lats * sent, LANES), f32),
+            pltpu.VMEM((size, LANES), f32),
         ],
         compiler_params=pltpu.CompilerParams(vmem_limit_bytes=20 * 2**20),
         name="inverse",
-    )(classes, a_own, *a_near, *a_far, b_all, coef, maps)
+    )(classes, table, coef, maps)
 
 
 def column_kernel(
@@ -298,7 +349,7 @@
 
 
 def forward_kernel(
-    class_ref, in_ref, table_ref, maps_ref, out_ref, sums_ref, scr_ref,
+    class_ref, in_ref, table_ref, maps_ref, out_ref, sums_ref, scr_ref, sent_ref, full_ref,
     *, lats, lat_local, lat_slots, width,
 ):
     m = pl.program_id(0)
@@ -326,17 +377,27 @@
         axis=1,
     ).astype(bf16)
     forcing = dot(table_ref[0], weighted).astype(bf16)
-    rows = out_ref.shape[2]
+    sent = out_ref.shape[2]
+    rows = full_ref.shape[0] // lats
+    spare = spare_lanes((lats, LANES), width)
     for v in range(maps_ref.shape[0]):
-        moved = dot(forcing, maps_ref[v]).astype(bf16)
-        for k in range(4):
-            for x in range(LAT_X):
-                at = (k * LAT_X + x) * rows
-                out_ref[x * Z_LOW + class_ref[k], v] = moved[at : at + rows]
-
-
-def forward(classes, weighted, table, maps, peers, lats, rows, lat_local, lat_slots, width):
-    levs, _, channels = maps.shape
+        full_ref[...] = dot(forcing, maps_ref[v])
+        for b in range(sent // 8):
+            last = full_ref[pl.ds(sent + b, lats, rows), :]
+            for t in range(8):
+                main = full_ref[pl.ds(8 * b + t, lats, rows), :]
+                sent_ref[pl.ds(8 * b + t, lats, sent), :] = jnp.where(
+                    spare, scatter_last(last, t, width), main
+                )
+        for q in range(lats):
+            k, x = divmod(q, LAT_X)
+            out_ref[x * Z_LOW + class_ref[k], v] = sent_ref[q * sent : (q + 1) * sent, :].astype(
+                bf16
+            )
+
+
+def forward(classes, weighted, table, maps, peers, lats, sent, lat_local, lat_slots, width):
+    levs = maps.shape[0]
     return pl.pallas_call(
         functools.partial(
             forward_kernel, lats=lats, lat_local=lat_local, lat_slots=lat_slots, width=width
@@ -348,49 +409,71 @@
             pl.BlockSpec((1, *table.shape[1:]), lambda m: (m, 0, 0)),
             pl.BlockSpec(maps.shape, lambda m: (0, 0, 0)),
         ],
-        out_specs=pl.BlockSpec((lats, levs, None, rows, channels), lambda m: (0, 0, m, 0, 0)),
-        out_shape=jax.ShapeDtypeStruct((lats, levs, OWN, rows, channels), bf16),
+        out_specs=pl.BlockSpec((lats, levs, None, sent, LANES), lambda m: (0, 0, m, 0, 0)),
+        out_shape=jax.ShapeDtypeStruct((lats, levs, OWN, sent, LANES), bf16),
         scratch_shapes=[
             pltpu.VMEM((OWN, 2, lats * lat_slots, LANES), f32),
             pltpu.VMEM((2, peers * 8, LANES), f32),
-        ],
-        compiler_params=pltpu.CompilerParams(vmem_limit_bytes=16 * 2**20),
+            pltpu.VMEM((lats * sent, LANES), f32),
+            pltpu.VMEM((table.shape[1], LANES), f32),
+        ],
+        compiler_params=pltpu.CompilerParams(vmem_limit_bytes=20 * 2**20),
         name="forward",
     )(classes, weighted, table, maps)
 
 
-def update_kernel(at_ref, state_ref, forcing_ref, out_ref, scr_ref):
+def update_kernel(at_ref, state_ref, forcing_ref, out_ref, scr_ref, last_ref):
     _, channels, orders = state_ref.shape
-    for x in range(LAT_X):
-        skip = OWN * (first_group(x - 1) + Z_RING - first_group(x)) if x else 0
-        first = (OWN * first_group(x) + skip) * 8
-        mine = forcing_ref[x, skip:].astype(f32)
-        scr_ref[first : first + mine.shape[0] * 8, :] = mine.reshape(-1, channels)
+    b = pl.program_id(0)
+    main = pl.num_programs(0) - 1
     order = lax.broadcasted_iota(jnp.int32, (channels, orders), 1) + at_ref[0]
-    for i in range(8):
-        degree = jnp.full((channels, orders), pl.program_id(0) * 8 + i + at_ref[1], jnp.int32)
+
+    def put(i, forcing):
+        degree = jnp.full((channels, orders), b * 8 + i + at_ref[1], jnp.int32)
         ratio = (degree * (degree + 1)).astype(f32) / ((L - 1) * L)
         damping = 1.0 / (1.0 + hyper_rate * ratio * ratio)
-        forcing = scr_ref[pl.ds(i, orders, 8), :].T
-        new = (state_ref[i] + time_step * forcing) * damping
+        new = (state_ref[i] + time_step * forcing[:, :channels].T) * damping
         out_ref[i] = jnp.where(degree >= order, new, 0.0)
+
+    @pl.when(b < main)
+    def _():
+        for x in range(LAT_X):
+            skip = OWN * (first_group(x - 1) + Z_RING - first_group(x)) if x else 0
+            first = (OWN * first_group(x) + skip) * 8
+            mine = forcing_ref[x, skip:].astype(f32)
+            scr_ref[first : first + mine.shape[0] * 8, :] = mine.reshape(-1, LANES)
+        last = jnp.zeros((orders, LANES), f32)
+        for t in range(8):
+            slab = scr_ref[pl.ds(t, orders, 8), :]
+            put(t, slab)
+            last = gather_last(last, slab, t, channels)
+        last_ref[b] = last
+
+    @pl.when(b == main)
+    def _():
+        for i in range(last_ref.shape[0]):
+            put(i, last_ref[i])
 
 
 def update(at, state, forcing):
     degrees, channels, orders = state.shape
-    _, group, padded, _ = forcing.shape
+    _, group, sent, _ = forcing.shape
+    main = sent // 8
     block = pl.BlockSpec((8, channels, orders), lambda i: (i, 0, 0))
     return pl.pallas_call(
         update_kernel,
-        grid=(padded // 8,),
+        grid=(main + 1,),
         in_specs=[
             pl.BlockSpec(memory_space=pltpu.SMEM),
             block,
-            pl.BlockSpec((LAT_X, group, 8, channels), lambda i: (0, 0, i, 0)),
+            pl.BlockSpec((LAT_X, group, 8, LANES), lambda i: (0, 0, jnp.minimum(i, main - 1), 0)),
         ],
         out_specs=block,
         out_shape=jax.ShapeDtypeStruct(state.shape, f32),
-        scratch_shapes=[pltpu.VMEM((orders * 8, channels), f32)],
+        scratch_shapes=[
+            pltpu.VMEM((orders * 8, LANES), f32),
+            pltpu.VMEM((degrees - sent, orders, LANES), f32),
+        ],
         name="update",
     )(at, state, forcing)
 
@@ -417,6 +500,7 @@
     channels = 2 * row_local
     width = lev_size * row_local
     rows = -(-degree_local // 16) * 16
+    sent = degree_local // 8 * 8
     peers = ord_size * lat_size * lev_size
     lat_slots = ord_size * lev_size * OWN
     everyone = ("lat", "ord", "lev")
@@ -444,19 +528,19 @@
     slot_x, slot_w = slot_lat // Z_LOW, 2 * (slot_lat % Z_LOW) + slot_lev
     valid = (slot_x % 2 == 0) | (slot_w > 0)
     order_ids = slot_ord * order_local + OWN * (first_group(slot_x) + slot_w) + slot // peers
+    coefficients = prep(at, state, sent)
+    coefficients, a_near, a_far, b_all = lax.optimization_barrier(
+        (coefficients, a_near, a_far, b_all)
+    )
+
+    coefficients = coefficients.reshape(lat_size * lev_size, OWN, sent, LANES)
+    coefficients = lax.all_to_all(coefficients, ("lat", "lev"), 0, 0, tiled=True)
+    coefficients = coefficients.reshape(lat_size, lev_size, OWN, sent, LANES)
+    classes = (z_at + jnp.array([0, -1, 1, 2], jnp.int32)) % Z_LOW
+    table = assemble(a_all, a_near, a_far, b_all)
+    fourier = inverse(classes, table, coefficients, maps, peers, lat_local, lat_slots, width)
+    fourier, order_ids, valid = lax.optimization_barrier((fourier, order_ids, valid))
     to_grid = lookup_of(order_ids, valid)
-    coefficients = prep(at, state)
-    coefficients, a_near, a_far, b_all, to_grid = lax.optimization_barrier(
-        (coefficients, a_near, a_far, b_all, to_grid)
-    )
-
-    coefficients = coefficients.reshape(lat_size * lev_size, OWN, rows, channels)
-    coefficients = lax.all_to_all(coefficients, ("lat", "lev"), 0, 0, tiled=True)
-    coefficients = coefficients.reshape(lat_size, lev_size, OWN, rows, channels)
-    classes = (z_at + jnp.array([0, -1, 1, 2], jnp.int32)) % Z_LOW
-    fourier, table = inverse(
-        classes, a_all, a_near, a_far, b_all, coefficients, maps, peers, lat_local, lat_slots, width
-    )
 
     fourier = lax.all_to_all(fourier.reshape(peers, 8, -1), everyone, 0, 0, tiled=True)
     first = (ord_at * lev_size + lev_at) * OWN
@@ -475,11 +559,11 @@
     weighted = lax.all_to_all(weighted.reshape(peers, 8, -1), everyone, 0, 0, tiled=True)
     weighted = weighted.reshape(peers * 8, -1)
     forcing = forward(
-        classes, weighted, table, maps, peers, lat_size, rows, lat_local, lat_slots, width
+        classes, weighted, table, maps, peers, lat_size, sent, lat_local, lat_slots, width
     )
-    forcing = forcing.reshape(lat_size * lev_size, OWN, rows, channels)
+    forcing = forcing.reshape(lat_size * lev_size, OWN, sent, LANES)
     forcing = lax.all_to_all(forcing, ("lat", "lev"), 0, 0, tiled=True)
-    forcing = forcing.reshape(LAT_X, OWN * Z_RING, rows, channels)
+    forcing = forcing.reshape(LAT_X, OWN * Z_RING, sent, LANES)
     updated = update(at, state, forcing)
     updated = updated.reshape(degree_local, *spectral_state.shape[2:], order_local)
     return updated.transpose(4, 0, 1, 2, 3)

time: 286 us -> 244 us (0.85)
  waiting for transfers between devices: 79.5 us -> 50.5 us
  local copies, waits for them, and re-layouts: 16.8 us -> 9.24 us
  Pallas kernels: 41.6 us -> 47.8 us
  blocking collectives: 74.4 us -> 68.9 us
  starting transfers between devices: 45.1 us -> 41.9 us
    all_to_all x1, waiting for transfers between devices: 30.7 us -> 9.79 us  [on_device(): lax.all_to_all(fourier.reshape(peers, 8, -1), everyone, 0, 0, tiled=True)]
    all_to_all x1, waiting for transfers between devices: 27 us -> 16.3 us  [on_device(): lax.all_to_all(coefficients, ('lat', 'lev'), 0, 0, tiled=True)]
    unnamed x41 -> x31, local copies, waits for them, and re-layouts: 16.6 us -> 7.3 us
    all_to_all x1, blocking collectives: 36.3 us -> 30.8 us  [on_device(): forcing = lax.all_to_all(forcing, ('lat', 'lev'), 0, 0, tiled=True)]
    pallas_call x2 -> x3, Pallas kernels: 10.9 us -> 15.8 us  [the longest x1 5.71 us: update(): pl.pallas_call(update_kernel, grid=(main + 1,), in_specs=[pl.BlockSpec(me...]
  transfers between devices with their start and end apart: 12 -> 12, of which waited for: 8 -> 6; matrix products, arithmetic and copies ran while one was open for 10% -> 11% of each run, Pallas kernels for 2% -> 4%
where the time goes in v5:
time: 244 us; the launch traced here: 243 us
  blocking collectives  68.9 us (28%)
  waiting for transfers between devices  50.5 us (21%)
  Pallas kernels  47.8 us (20%)
  starting transfers between devices  41.9 us (17%)
  other arithmetic  24.6 us (10%)
  local copies, waits for them, and re-layouts  9.24 us (4%)
    all_to_all x1, blocking collectives, on_device(): lax.all_to_all(weighted.reshape(peers, 8, -1), everyone, 0, 0, tiled=True)  38.1 us
    all_to_all x1, blocking collectives, on_device(): forcing = lax.all_to_all(forcing, ('lat', 'lev'), 0, 0, tiled=True)  30.8 us
    ppermute x8, waiting for transfers between devices, along_z(): return lax.ppermute(value, ('lat', 'lev'), pairs)  24.4 us
    another operation x1, other arithmetic  19.3 us
    pallas_call x1, Pallas kernels, columns(): pl.pallas_call(functools.partial(column_kernel, x_rows=240, width=width),...  18.6 us
    all_to_all x1, waiting for transfers between devices, on_device(): lax.all_to_all(coefficients, ('lat', 'lev'), 0, 0, tiled=True)  16.3 us
    ppermute x8, starting transfers between devices, along_z(): return lax.ppermute(value, ('lat', 'lev'), pairs)  15.4 us
    all_to_all x2, starting transfers between devices, along_x(): lax.all_to_all(value, 'lat', 0, 0, axis_index_groups=groups, tiled=True)  10.6 us
  transfers between devices with their start and end apart: 12, of which 6 were waited for; matrix products, arithmetic and copies ran while one was open for 11% of the time, Pallas kernels for 4%

profile of v5, /device:TPU:2, one launch (start us, length us, event | category | flops | bytes accessed | tf_op | source)
XLA Modules:
  0.0 243.3 jit_solution(3993627391047503979)
XLA Ops:
  0.7 2.9 %copy-done.3 = bf16[90,45,720]{2,1,0:T(8,128)(2,1)S(1)} copy-done((bf16[90,45,720]{2,1,0:T(8,128)(2,1)S(1)}, bf16[90,45,720]{2,1,0:T(8,128)(2,1)}, u32[]{:S(2)}) %copy-start.3) | copy-done | bytes 5832024
  3.6 2.5 %pack_table.1 = (bf16[4,4,3,48,384]{4,3,2,1,0:T(8,128)(2,1)}, bf16[4,3,48,384]{3,2,1,0:T(8,128)(2,1)S(1)}, bf16[4,3,48,384]{3,2,1,0:T(8,128)(2,1)S(1)}, bf16[4,3...) custom-call(s32[5]{0:T(128)S(1)} %fusion.35.own_ref, ...), custom_call_target="tpu_custom_call" | custom-call | tf_op jit(solution)/shard_map/pack_table/pallas_call | solution.py:162
  6.0 5.8 %all-to-all-start = ((bf16[4,4,3,48,384]{4,3,2,1,0:T(8,128)(2,1)}), bf16[4,4,3,48,384]{4,3,2,1,0:T(8,128)(2,1)S(1)}, u32[]{:S(2)}, u32[]{:S(2)}) async-start(bf16[4,4,3,48,384]{4,3,2,1,0:T(8,128)(2,1)} %get-tuple-element.22), calls=%async_computation | async-start | bytes 3538944 | tf_op jit(solution)/shard_map/all_to_all | solution.py:491
  11.9 4.9 %collective-permute-start.1 = (bf16[4,3,48,384]{3,2,1,0:T(8,128)(2,1)S(1)}, bf16[4,3,48,384]{3,2,1,0:T(8,128)(2,1)S(1)}, u32[]{:S(2)}, u32[]{:S(2)}) collective-permute-start(bf16[4,3,48,384]{3,2,1,0:T(8,128)(2,1)S(1)} %get-tuple-element.25), channel_id=1, source_target_pairs={{0,7},{2,0},{4,2},{6,4},{1,6},{3,1},{5,3},{7,5},{8,15},{10,8},{12,... | collective-permute-start | bytes 1327112 | tf_op jit(solution)/shard_map/ppermute | solution.py:486
  16.7 2.5 %collective-permute-start.3 = (bf16[4,3,24,384]{3,2,1,0:T(8,128)(2,1)S(1)}, bf16[4,3,24,384]{3,2,1,0:T(8,128)(2,1)S(1)}, u32[]{:S(2)}, u32[]{:S(2)}) collective-permute-start(bf16[4,3,24,384]{3,2,1,0:T(8,128)(2,1)S(1)} %get-tuple-element.27), channel_id=1, source_target_pairs={{0,5},{2,7},{4,0},{6,2},{1,4},{3,6},{5,1},{7,3},{8,13},{10,15},{12... | collective-permute-start | bytes 663560 | tf_op jit(solution)/shard_map/ppermute | solution.py:486
  19.7 15.4 %collective-permute-done.3 = bf16[4,3,24,384]{3,2,1,0:T(8,128)(2,1)S(1)} collective-permute-done((bf16[4,3,24,384]{3,2,1,0:T(8,128)(2,1)S(1)}, bf16[4,3,24,384]{3,2,1,0:T(8,128)(2,1)S(1)}, u32[]{:S(2)}, u32[]{:S(2)}) %collective-permute-start.3) | collective-permute-done | bytes 221216 | tf_op jit(solution)/shard_map/ppermute | solution.py:486
  35.1 1.4 collective-permute-done.2
  36.6 1.5 pad_maximum_fusion.1
  38.1 4.8 %all-to-all-start.1 = ((bf16[4,4,3,48,384]{4,3,2,1,0:T(8,128)(2,1)}), bf16[4,4,3,48,384]{4,3,2,1,0:T(8,128)(2,1)S(1)}, u32[]{:S(2)}, u32[]{:S(2)}) async-start(bf16[4,4,3,48,384]{4,3,2,1,0:T(8,128)(2,1)} %pad_maximum_fusion.1), calls=%async_computation.1 | async-start | bytes 3538944 | tf_op jit(solution)/shard_map/all_to_all | solution.py:491
  42.9 1.0 slice_bitcast_fusion
  43.9 3.4 %collective-permute-start.4 = (bf16[4,3,48,384]{3,2,1,0:T(8,128)(2,1)}, bf16[4,3,48,384]{3,2,1,0:T(8,128)(2,1)}, u32[]{:S(2)}, u32[]{:S(2)}) collective-permute-start(bf16[4,3,48,384]{3,2,1,0:T(8,128)(2,1)} %get-tuple-element.42), channel_id=1, source_target_pairs={{0,2},{2,4},{4,6},{6,1},{1,3},{3,5},{5,7},{7,0},{8,10},{10,12},{12... | collective-permute-start | bytes 1327112 | tf_op jit(solution)/shard_map/ppermute | solution.py:486
  47.3 0.8 slice_bitcast_fusion.2
  48.2 1.5 collective-permute-start.6
  49.6 2.7 %collective-permute-start.7 = (bf16[4,3,24,384]{3,2,1,0:T(8,128)(2,1)}, bf16[4,3,24,384]{3,2,1,0:T(8,128)(2,1)S(1)}, u32[]{:S(2)}, u32[]{:S(2)}) collective-permute-start(bf16[4,3,24,384]{3,2,1,0:T(8,128)(2,1)} %get-tuple-element.39), channel_id=1, source_target_pairs={{0,5},{2,7},{4,0},{6,2},{1,4},{3,6},{5,1},{7,3},{8,13},{10,15},{12... | collective-permute-start | bytes 663560 | tf_op jit(solution)/shard_map/ppermute | solution.py:486
  52.9 5.3 %prep.1 = bf16[4,24,40,128]{3,2,1,0:T(8,128)(2,1)} custom-call(s32[2]{0:T(128)} %pad_add_fusion.at_ref, f32[45,112,90]{2,1,0:T(8,128)} %bitcast.37, f32[45,112,90]{2,1,0:T(8,128)} %bitcast.38), custom_call_target="tpu_custom_call" | custom-call | flops 1000000 | bytes 4000000 | tf_op jit(solution)/shard_map/prep/pallas_call | solution.py:121
  58.1 5.7 %collective-permute-done.6.a_low_ref = bf16[4,3,24,384]{3,2,1,0:T(8,128)(2,1)S(1)} collective-permute-done((bf16[4,3,24,384]{3,2,1,0:T(8,128)(2,1)}, bf16[4,3,24,384]{3,2,1,0:T(8,128)(2,1)S(1)}, u32[]{:S(2)}, u32[]{:S(2)}) %collective-permute-start.6) | collective-permute-done | bytes 221216 | tf_op jit(solution)/shard_map/ppermute | solution.py:486
  63.8 1.9 collective-permute-done.7.a_high_ref
  65.8 7.4 %all-to-all-start.2 = ((bf16[32,3,40,128]{3,2,1,0:T(8,128)(2,1)}), bf16[32,3,40,128]{3,2,1,0:T(8,128)(2,1)S(1)}, u32[]{:S(2)}, u32[]{:S(2)}) async-start(bf16[32,3,40,128]{3,2,1,0:T(8,128)(2,1)} %bitcast.40), calls=%async_computation.2 | async-start | bytes 1966080 | tf_op jit(solution)/shard_map/all_to_all | solution.py:537
  73.3 4.8 %assemble.1.table_ref = bf16[3,768,768]{2,1,0:T(8,128)(2,1)} custom-call(bf16[4,4,3,48,384]{4,3,2,1,0:T(8,128)(2,1)} %copy-done.7, bf16[4,3,48,384]{3,2,1,0:T(8,128)(2,1)} %collective-permute-done.4.a_left_ref, bf16[4,3,48,384]{3,2,1,0:T(8,128)(2,1)} %collective-permute-done.5.a_right_ref, bf16[4,3,24,384]{3,2,1,0:T(8,128)(2,1)} %copy-done.9, ...), custom_call_target="tpu_custom_call" | custom-call | flops 1000000 | bytes 8000000 | tf_op jit(solution)/shard_map/assemble/pallas_call | solution.py:195
  78.1 16.3 %all-to-all-done.2 = bf16[32,3,40,128]{3,2,1,0:T(8,128)(2,1)S(1)} async-done(((bf16[32,3,40,128]{3,2,1,0:T(8,128)(2,1)}), bf16[32,3,40,128]{3,2,1,0:T(8,128)(2,1)S(1)}, u32[]{:S(2)}, u32[]{:S(2)}) %all-to-all-start.2) | async-done | bytes 983072 | tf_op jit(solution)/shard_map/all_to_all | solution.py:537
  94.4 2.0 copy-done
  96.4 5.9 %inverse.1 = bf16[2048,256]{1,0:T(8,128)(2,1)} custom-call(s32[4]{0:T(128)S(1)} %and_select_fusion.3.class_ref, bf16[3,768,768]{2,1,0:T(8,128)(2,1)S(1)} %copy-done, bf16[16,2,3,40,128]{4,3,2,1,0:T(8,128)(2,1)S(1)} %bitcast.33, bf16[2,256,128]{2,1,0:T(8,128)(2,1)S(1)} %copy-done.4), custom_call_target="tpu_custom_call" | custom-call | tf_op jit(solution)/shard_map/inverse/pallas_call | solution.py:261
  102.3 8.6 %all-to-all-start.3 = ((bf16[256,8,256]{2,1,0:T(8,128)(2,1)}), bf16[256,8,256]{2,1,0:T(8,128)(2,1)S(1)}, u32[]{:S(2)}, u32[]{:S(2)}) async-start(bf16[256,8,256]{2,1,0:T(8,128)(2,1)} %bitcast.15), calls=%async_computation.3 | async-start | bytes 2097152 | tf_op jit(solution)/shard_map/all_to_all | solution.py:545
  111.2 19.3 %select_convert_fusion.1 = (bf16[1,1440,768]{2,1,0:T(8,128)(2,1)S(1)}, bf16[1,1440,768]{2,1,0:T(8,128)(2,1)S(1)}) fusion(s32[768]{0:T(1024)S(1)} %fusion.14, pred[768]{0:T(1024)(128)(4,1)S(1)} %fusion.29), kind=kLoop, calls=%fused_computation.5 | loop fusion | flops 15482880 | bytes 4427520 | tf_op jit(solution)/shard_map/convert
  130.5 2.4 pad_maximum_fusion.to_grid_ref
  132.9 9.8 %all-to-all-done.3 = bf16[256,8,256]{2,1,0:T(8,128)(2,1)S(1)} async-done(((bf16[256,8,256]{2,1,0:T(8,128)(2,1)}), bf16[256,8,256]{2,1,0:T(8,128)(2,1)S(1)}, u32[]{:S(2)}, u32[]{:S(2)}) %all-to-all-start.3) | async-done | bytes 1048608 | tf_op jit(solution)/shard_map/all_to_all | solution.py:545
  142.7 2.3 copy-done.2
  145.0 18.6 %columns.1 = bf16[2048,256]{1,0:T(8,128)(2,1)S(1)} custom-call(f32[3]{0:T(128)S(1)} %pad_dynamic-slice_fusion.weight_ref, bf16[2048,256]{1,0:T(8,128)(2,1)S(1)} %bitcast.30, bf16[2,1440,768]{2,1,0:T(8,128)(2,1)S(1)} %copy-done.2, bf16[128,256]{1,0:T(8,128)(2,1)S(1)} %pad.13.w_in_ref, f32[1,256]{1,0:T(1,128)S(1)} %bitcast.36, ...), custom_call_target="tpu_custom_call" | custom-call | tf_op jit(solution)/shard_map/columns/pallas_call | solution.py:335
  163.6 38.1 %all_to_all.30 = bf16[256,8,256]{2,1,0:T(8,128)(2,1)S(1)} all-to-all(bf16[256,8,256]{2,1,0:T(8,128)(2,1)S(1)} %bitcast.31), channel_id=1, replica_groups=mesh['ord'=8,'lat'=16,'lev'=2] {'lat','ord','lev'}, dimensions={0} | all-to-all | bytes 2097152 | tf_op jit(solution)/shard_map/all_to_all | solution.py:559
  201.8 5.0 %forward.1 = bf16[16,2,3,40,128]{4,3,2,1,0:T(8,128)(2,1)S(1)} custom-call(s32[4]{0:T(128)S(1)} %and_select_fusion.3.class_ref, bf16[2048,256]{1,0:T(8,128)(2,1)S(1)} %bitcast.32, bf16[3,768,768]{2,1,0:T(8,128)(2,1)S(1)} %copy-done.1, bf16[2,256,128]{2,1,0:T(8,128)(2,1)S(1)} %copy-done.4), custom_call_target="tpu_custom_call" | custom-call | tf_op jit(solution)/shard_map/forward/pallas_call | solution.py:401
  206.8 30.8 %all_to_all.31 = bf16[32,3,40,128]{3,2,1,0:T(8,128)(2,1)} all-to-all(bf16[32,3,40,128]{3,2,1,0:T(8,128)(2,1)S(1)} %bitcast.34), channel_id=1, replica_groups=mesh['ord'=8,'lat'=16,'lev'=2] {'lat','lev'}, dimensions={0} | all-to-all | bytes 1966080 | tf_op jit(solution)/shard_map/all_to_all | solution.py:565
  237.6 5.7 %update.1 = f32[45,112,90]{2,1,0:T(8,128)} custom-call(s32[2]{0:T(128)} %pad_add_fusion.at_ref, f32[45,112,90]{2,1,0:T(8,128)} %bitcast.39, bf16[4,24,40,128]{3,2,1,0:T(8,128)(2,1)} %bitcast.41), custom_call_target="tpu_custom_call" | custom-call | tf_op jit(solution)/shard_map/update/pallas_call | solution.py:463
  (46 shorter events, 2.1 us)
Async XLA Ops:
  0.7 2.9 %copy-start.3 = (bf16[90,45,720]{2,1,0:T(8,128)(2,1)S(1)}, bf16[90,45,720]{2,1,0:T(8,128)(2,1)}, u32[]{:S(2)}) copy-start(bf16[90,45,720]{2,1,0:T(8,128)(2,1)} %in_ref.1) | copy-start | bytes 17496004
  6.0 32.0 %all-to-all-start = ((bf16[4,4,3,48,384]{4,3,2,1,0:T(8,128)(2,1)}), bf16[4,4,3,48,384]{4,3,2,1,0:T(8,128)(2,1)S(1)}, u32[]{:S(2)}, u32[]{:S(2)}) async-start(bf16[4,4,3,48,384]{4,3,2,1,0:T(8,128)(2,1)} %get-tuple-element.22), calls=%async_computation | async-start | bytes 3538944 | tf_op jit(solution)/shard_map/all_to_all | solution.py:491
  11.9 24.7 %collective-permute-start.1 = (bf16[4,3,48,384]{3,2,1,0:T(8,128)(2,1)S(1)}, bf16[4,3,48,384]{3,2,1,0:T(8,128)(2,1)S(1)}, u32[]{:S(2)}, u32[]{:S(2)}) collective-permute-start(bf16[4,3,48,384]{3,2,1,0:T(8,128)(2,1)S(1)} %get-tuple-element.25), channel_id=1, source_target_pairs={{0,7},{2,0},{4,2},{6,4},{1,6},{3,1},{5,3},{7,5},{8,15},{10,8},{12,... | collective-permute-start | bytes 1327112 | tf_op jit(solution)/shard_map/ppermute | solution.py:486
  16.7 19.8 %collective-permute-start = (bf16[4,3,48,384]{3,2,1,0:T(8,128)(2,1)S(1)}, bf16[4,3,48,384]{3,2,1,0:T(8,128)(2,1)S(1)}, u32[]{:S(2)}, u32[]{:S(2)}) collective-permute-start(bf16[4,3,48,384]{3,2,1,0:T(8,128)(2,1)S(1)} %get-tuple-element.24), channel_id=1, source_target_pairs={{0,2},{2,4},{4,6},{6,1},{1,3},{3,5},{5,7},{7,0},{8,10},{10,12},{12... | collective-permute-start | bytes 1327112 | tf_op jit(solution)/shard_map/ppermute | solution.py:486
  16.7 18.3 %collective-permute-start.3 = (bf16[4,3,24,384]{3,2,1,0:T(8,128)(2,1)S(1)}, bf16[4,3,24,384]{3,2,1,0:T(8,128)(2,1)S(1)}, u32[]{:S(2)}, u32[]{:S(2)}) collective-permute-start(bf16[4,3,24,384]{3,2,1,0:T(8,128)(2,1)S(1)} %get-tuple-element.27), channel_id=1, source_target_pairs={{0,5},{2,7},{4,0},{6,2},{1,4},{3,6},{5,1},{7,3},{8,13},{10,15},{12... | collective-permute-start | bytes 663560 | tf_op jit(solution)/shard_map/ppermute | solution.py:486
  19.2 17.3 %collective-permute-start.2 = (bf16[4,3,24,384]{3,2,1,0:T(8,128)(2,1)S(1)}, bf16[4,3,24,384]{3,2,1,0:T(8,128)(2,1)S(1)}, u32[]{:S(2)}, u32[]{:S(2)}) collective-permute-start(bf16[4,3,24,384]{3,2,1,0:T(8,128)(2,1)S(1)} %get-tuple-element.26), channel_id=1, source_target_pairs={{0,4},{2,6},{4,1},{6,3},{1,5},{3,7},{5,0},{7,2},{8,12},{10,14},{12... | collective-permute-start | bytes 663560 | tf_op jit(solution)/shard_map/ppermute | solution.py:486
  38.1 9.3 %copy-start.7 = (bf16[4,4,3,48,384]{4,3,2,1,0:T(8,128)(2,1)}, bf16[4,4,3,48,384]{4,3,2,1,0:T(8,128)(2,1)S(1)}, u32[]{:S(2)}) copy-start(bf16[4,4,3,48,384]{4,3,2,1,0:T(8,128)(2,1)S(1)} %all-to-all-done.a_own_ref) | copy-start | bytes 5308420
  38.1 27.7 %all-to-all-start.1 = ((bf16[4,4,3,48,384]{4,3,2,1,0:T(8,128)(2,1)}), bf16[4,4,3,48,384]{4,3,2,1,0:T(8,128)(2,1)S(1)}, u32[]{:S(2)}, u32[]{:S(2)}) async-start(bf16[4,4,3,48,384]{4,3,2,1,0:T(8,128)(2,1)} %pad_maximum_fusion.1), calls=%async_computation.1 | async-start | bytes 3538944 | tf_op jit(solution)/shard_map/all_to_all | solution.py:491
  43.9 21.9 %collective-permute-start.4 = (bf16[4,3,48,384]{3,2,1,0:T(8,128)(2,1)}, bf16[4,3,48,384]{3,2,1,0:T(8,128)(2,1)}, u32[]{:S(2)}, u32[]{:S(2)}) collective-permute-start(bf16[4,3,48,384]{3,2,1,0:T(8,128)(2,1)} %get-tuple-element.42), channel_id=1, source_target_pairs={{0,2},{2,4},{4,6},{6,1},{1,3},{3,5},{5,7},{7,0},{8,10},{10,12},{12... | collective-permute-start | bytes 1327112 | tf_op jit(solution)/shard_map/ppermute | solution.py:486
  47.3 18.4 %collective-permute-start.5 = (bf16[4,3,48,384]{3,2,1,0:T(8,128)(2,1)}, bf16[4,3,48,384]{3,2,1,0:T(8,128)(2,1)}, u32[]{:S(2)}, u32[]{:S(2)}) collective-permute-start(bf16[4,3,48,384]{3,2,1,0:T(8,128)(2,1)} %get-tuple-element.41), channel_id=1, source_target_pairs={{0,7},{2,0},{4,2},{6,4},{1,6},{3,1},{5,3},{7,5},{8,15},{10,8},{12,... | collective-permute-start | bytes 1327112 | tf_op jit(solution)/shard_map/ppermute | solution.py:486
  48.2 15.6 %collective-permute-start.6 = (bf16[4,3,24,384]{3,2,1,0:T(8,128)(2,1)}, bf16[4,3,24,384]{3,2,1,0:T(8,128)(2,1)S(1)}, u32[]{:S(2)}, u32[]{:S(2)}) collective-permute-start(bf16[4,3,24,384]{3,2,1,0:T(8,128)(2,1)} %get-tuple-element.40), channel_id=1, source_target_pairs={{0,4},{2,6},{4,1},{6,3},{1,5},{3,7},{5,0},{7,2},{8,12},{10,14},{12... | collective-permute-start | bytes 663560 | tf_op jit(solution)/shard_map/ppermute | solution.py:486
  49.6 16.1 %collective-permute-start.7 = (bf16[4,3,24,384]{3,2,1,0:T(8,128)(2,1)}, bf16[4,3,24,384]{3,2,1,0:T(8,128)(2,1)S(1)}, u32[]{:S(2)}, u32[]{:S(2)}) collective-permute-start(bf16[4,3,24,384]{3,2,1,0:T(8,128)(2,1)} %get-tuple-element.39), channel_id=1, source_target_pairs={{0,5},{2,7},{4,0},{6,2},{1,4},{3,6},{5,1},{7,3},{8,13},{10,15},{12... | collective-permute-start | bytes 663560 | tf_op jit(solution)/shard_map/ppermute | solution.py:486
  52.9 20.3 %copy-start.14 = (s32[4]{0:T(128)S(1)}, s32[4]{0:T(128)}, u32[]{:S(2)}) copy-start(s32[4]{0:T(128)} %constant.194.clone) | copy-start | bytes 52
  63.8 9.4 %copy-start.9 = (bf16[4,3,24,384]{3,2,1,0:T(8,128)(2,1)}, bf16[4,3,24,384]{3,2,1,0:T(8,128)(2,1)S(1)}, u32[]{:S(2)}) copy-start(bf16[4,3,24,384]{3,2,1,0:T(8,128)(2,1)S(1)} %collective-permute-done.6.a_low_ref) | copy-start | bytes 663556
  65.7 7.5 %copy-start.10 = (bf16[4,3,24,384]{3,2,1,0:T(8,128)(2,1)}, bf16[4,3,24,384]{3,2,1,0:T(8,128)(2,1)S(1)}, u32[]{:S(2)}) copy-start(bf16[4,3,24,384]{3,2,1,0:T(8,128)(2,1)S(1)} %collective-permute-done.7.a_high_ref) | copy-start | bytes 663556
  65.8 7.5 %copy-start.8 = (bf16[4,4,3,48,384]{4,3,2,1,0:T(8,128)(2,1)}, bf16[4,4,3,48,384]{4,3,2,1,0:T(8,128)(2,1)S(1)}, u32[]{:S(2)}) copy-start(bf16[4,4,3,48,384]{4,3,2,1,0:T(8,128)(2,1)S(1)} %all-to-all-done.1.b_ref) | copy-start | bytes 5308420
  65.8 28.6 %all-to-all-start.2 = ((bf16[32,3,40,128]{3,2,1,0:T(8,128)(2,1)}), bf16[32,3,40,128]{3,2,1,0:T(8,128)(2,1)S(1)}, u32[]{:S(2)}, u32[]{:S(2)}) async-start(bf16[32,3,40,128]{3,2,1,0:T(8,128)(2,1)} %bitcast.40), calls=%async_computation.2 | async-start | bytes 1966080 | tf_op jit(solution)/shard_map/all_to_all | solution.py:537
  73.2 21.1 %copy-start.4 = (bf16[2,256,128]{2,1,0:T(8,128)(2,1)S(1)}, bf16[2,256,128]{2,1,0:T(8,128)(2,1)}, u32[]{:S(2)}) copy-start(bf16[2,256,128]{2,1,0:T(8,128)(2,1)} %constant.192.clone.maps_ref) | copy-start | bytes 393220
  94.4 2.0 copy-start
  96.4 14.5 %copy-start.11 = (bf16[256,112]{0,1:T(8,128)(2,1)S(1)}, bf16[256,112]{0,1:T(8,128)(2,1)}, u32[]{:S(2)}) copy-start(bf16[256,112]{0,1:T(8,128)(2,1)} %param.16) | copy-start | bytes 172036
  102.3 8.7 %copy-start.12 = (bf16[112,256]{1,0:T(8,128)(2,1)S(1)}, bf16[112,256]{1,0:T(8,128)(2,1)}, u32[]{:S(2)}) copy-start(bf16[112,256]{1,0:T(8,128)(2,1)} %param.13) | copy-start | bytes 172036
  102.3 8.8 %copy-start.13 = (f32[45]{0:T(128)S(1)}, f32[45]{0:T(128)}, u32[]{:S(2)}) copy-start(f32[45]{0:T(128)} %param.12) | copy-start | bytes 544
  102.3 40.4 %all-to-all-start.3 = ((bf16[256,8,256]{2,1,0:T(8,128)(2,1)}), bf16[256,8,256]{2,1,0:T(8,128)(2,1)S(1)}, u32[]{:S(2)}, u32[]{:S(2)}) async-start(bf16[256,8,256]{2,1,0:T(8,128)(2,1)} %bitcast.15), calls=%async_computation.3 | async-start | bytes 2097152 | tf_op jit(solution)/shard_map/all_to_all | solution.py:545
  130.5 12.2 %copy-start.5 = (bf16[4,256,256]{2,1,0:T(8,128)(2,1)S(1)}, bf16[4,256,256]{2,1,0:T(8,128)(2,1)}, u32[]{:S(2)}) copy-start(bf16[4,256,256]{2,1,0:T(8,128)(2,1)} %w_hid_ref.1) | copy-start | bytes 1572868
  130.5 12.2 %copy-start.6 = (f32[256]{0:T(256)S(1)}, f32[256]{0:T(256)}, u32[]{:S(2)}) copy-start(f32[256]{0:T(256)} %param.14) | copy-start | bytes 3076
  142.7 2.3 copy-start.2
  145.0 56.8 %copy-start.1 = (bf16[3,768,768]{2,1,0:T(8,128)(2,1)S(1)}, bf16[3,768,768]{2,1,0:T(8,128)(2,1)}, u32[]{:S(2)}) copy-start(bf16[3,768,768]{2,1,0:T(8,128)(2,1)} %assemble.1.table_ref) | copy-start | bytes 10616836

commit v6 on v5

--- a/solution.py
+++ b/solution.py
@@ -15,6 +15,7 @@
 LANES = 128
 LAT_X, Z_LOW, Z_RING = 4, 4, 8
 HALF = 384
+X_ROWS = 1440
 SPARE = 14
 
 time_step = 1.0
@@ -30,16 +31,25 @@
 
 
 def lookup_of(order_ids, valid):
-    phase_index = order_ids[None, :] * lax.iota(jnp.int32, NLON)[:, None] % NLON
-    angles = 2.0 * math.pi / NLON * phase_index.astype(f32)
-    keep = valid[None, :]
-    return jnp.stack(
-        [jnp.where(keep, jnp.cos(angles), 0.0), jnp.where(keep, -jnp.sin(angles), 0.0)]
-    ).astype(bf16)
-
-
-def silu(v):
-    return 0.5 * v * (1.0 + jnp.tanh(0.5 * v))
+    low = 32
+
+    def waves(x):
+        phase_index = order_ids[None, :] * x[:, None] % NLON
+        angles = 2.0 * math.pi / NLON * phase_index.astype(f32)
+        return jnp.cos(angles), jnp.sin(angles)
+
+    high_cos, high_sin = waves(low * lax.iota(jnp.int32, NLON // low))
+    high_cos = jnp.where(valid[None, :], high_cos, 0.0)[:, None]
+    high_sin = jnp.where(valid[None, :], high_sin, 0.0)[:, None]
+    low_cos, low_sin = (w[None] for w in waves(lax.iota(jnp.int32, low)))
+    cosines = high_cos * low_cos - high_sin * low_sin
+    sines = -(high_sin * low_cos + high_cos * low_sin)
+    shape = (NLON, order_ids.shape[0])
+    return cosines.astype(bf16).reshape(shape), sines.astype(bf16).reshape(shape)
+
+
+def half_silu(u):
+    return u + u * jnp.tanh(u)
 
 
 def lane_maps(levs, row_local):
@@ -173,7 +183,7 @@
         + [b_spec(r) for r in b_rows],
         out_shape=[jax.ShapeDtypeStruct((LAT_X, 4, OWN, rows, half), bf16)]
         + [b_shape(r) for r in b_rows],
-        compiler_params=pltpu.CompilerParams(vmem_limit_bytes=16 * 2**20),
+        compiler_params=pltpu.CompilerParams(vmem_limit_bytes=60 * 2**20),
         name="pack_table",
     )(own, legendre)
 
@@ -214,76 +224,69 @@
     class_ref, table_ref, coef_ref, maps_ref, out_ref, sums_ref, scr_ref, sent_ref, full_ref,
     *, lats, lat_local, lat_slots, width,
 ):
-    m = pl.program_id(0)
-    sent = coef_ref.shape[2]
+    sent = coef_ref.shape[3]
     rows = full_ref.shape[0] // lats
-    swapped = 0.0
-    for v in range(maps_ref.shape[0]):
-        for q in range(lats):
-            k, x = divmod(q, LAT_X)
-            piece = coef_ref[x * Z_LOW + class_ref[k], v].astype(f32)
-            sent_ref[q * sent : (q + 1) * sent, :] = piece
-            full_ref[q * rows : q * rows + sent, :] = piece
-            full_ref[q * rows + sent : (q + 1) * rows, :] = jnp.zeros((rows - sent, LANES), f32)
-        for b in range(sent // 8):
-            last = jnp.zeros((lats, LANES), f32)
-            for t in range(8):
-                slab = sent_ref[pl.ds(8 * b + t, lats, sent), :]
-                last = gather_last(last, slab, t, width)
-            full_ref[pl.ds(sent + b, lats, rows), :] = last
-        swapped += lax.dot_general(
-            maps_ref[v],
-            full_ref[...].astype(bf16),
-            (((1,), (1,)), ((), ())),
-            preferred_element_type=f32,
-        )
-    sums = dot(swapped.astype(bf16), table_ref[0]).T
-    for part in range(2):
-        lanes = slice(part * LANES, (part + 1) * LANES)
-        for lat in range(lats):
-            sums_ref[m, part, lat * lat_slots : lat * lat_slots + lat_local, :] = sums[
-                lat * lat_local : (lat + 1) * lat_local, lanes
-            ]
-            sums_ref[m, part, lat * lat_slots + lat_local : (lat + 1) * lat_slots, :] = jnp.zeros(
-                (lat_slots - lat_local, LANES), f32
+    for m in range(OWN):
+        swapped = 0.0
+        for v in range(maps_ref.shape[0]):
+            for q in range(lats):
+                k, x = divmod(q, LAT_X)
+                piece = coef_ref[x * Z_LOW + class_ref[k], v, m].astype(f32)
+                sent_ref[q * sent : (q + 1) * sent, :] = piece
+                full_ref[q * rows : q * rows + sent, :] = piece
+                full_ref[q * rows + sent : (q + 1) * rows, :] = jnp.zeros((rows - sent, LANES), f32)
+            for b in range(sent // 8):
+                last = jnp.zeros((lats, LANES), f32)
+                for t in range(8):
+                    slab = sent_ref[pl.ds(8 * b + t, lats, sent), :]
+                    last = gather_last(last, slab, t, width)
+                full_ref[pl.ds(sent + b, lats, rows), :] = last
+            swapped += lax.dot_general(
+                maps_ref[v],
+                full_ref[...].astype(bf16),
+                (((1,), (1,)), ((), ())),
+                preferred_element_type=f32,
             )
-
-    @pl.when(m == OWN - 1)
-    def _():
-        peers = out_ref.shape[0] // 8
-        slab_of = lambda part, i, m: sums_ref[m, part, pl.ds(i, peers, OWN), :]
-        pack_rows(slab_of, out_ref, scr_ref, peers, width)
+        sums = dot(swapped.astype(bf16), table_ref[m]).T
+        for part in range(2):
+            lanes = slice(part * LANES, (part + 1) * LANES)
+            for lat in range(lats):
+                first = lat * lat_slots
+                sums_ref[m, part, first : first + lat_local, :] = sums[
+                    lat * lat_local : (lat + 1) * lat_local, lanes
+                ]
+                sums_ref[m, part, first + lat_local : first + lat_slots, :] = jnp.zeros(
+                    (lat_slots - lat_local, LANES), f32
+                )
+
+    peers = out_ref.shape[0] // 8
+    slab_of = lambda part, i, m: sums_ref[m, part, pl.ds(i, peers, OWN), :]
+    pack_rows(slab_of, out_ref, scr_ref, peers, width)
 
 
 def inverse(classes, table, coef, maps, peers, lat_local, lat_slots, width):
-    lats, levs, _, sent, lanes = coef.shape
-    size = table.shape[1]
+    lats, _, _, sent, _ = coef.shape
+    vmem = pl.BlockSpec(memory_space=pltpu.VMEM)
     return pl.pallas_call(
         functools.partial(
             inverse_kernel, lats=lats, lat_local=lat_local, lat_slots=lat_slots, width=width
         ),
-        grid=(OWN,),
-        in_specs=[
-            pl.BlockSpec(memory_space=pltpu.SMEM),
-            pl.BlockSpec((1, *table.shape[1:]), lambda m: (m, 0, 0)),
-            pl.BlockSpec((lats, levs, None, sent, lanes), lambda m: (0, 0, m, 0, 0)),
-            pl.BlockSpec(maps.shape, lambda m: (0, 0, 0)),
-        ],
-        out_specs=pl.BlockSpec((peers * 8, 2 * LANES), lambda m: (0, 0)),
+        in_specs=[pl.BlockSpec(memory_space=pltpu.SMEM), vmem, vmem, vmem],
+        out_specs=vmem,
         out_shape=jax.ShapeDtypeStruct((peers * 8, 2 * LANES), bf16),
         scratch_shapes=[
             pltpu.VMEM((OWN, 2, lats * lat_slots, LANES), f32),
             pltpu.VMEM((2, peers * 8, LANES), f32),
             pltpu.VMEM((lats * sent, LANES), f32),
-            pltpu.VMEM((size, LANES), f32),
+            pltpu.VMEM((table.shape[1], LANES), f32),
         ],
-        compiler_params=pltpu.CompilerParams(vmem_limit_bytes=20 * 2**20),
+        compiler_params=pltpu.CompilerParams(vmem_limit_bytes=24 * 2**20),
         name="inverse",
     )(classes, table, coef, maps)
 
 
 def column_kernel(
-    weight_ref, in_ref, to_grid_ref, w_in_ref, bias_ref, w_hid_ref, w_out_ref,
+    weight_ref, in_ref, cos_ref, sin_ref, w_in_ref, bias_ref, w_hid_ref, w_out_ref,
     out_ref, fourier_ref, tendency_ref, sums_ref, scr_ref, *, x_rows, width,
 ):
     peers = in_ref.shape[0] // 8
@@ -297,25 +300,24 @@
 
     def grid_rows(step, carry):
         rows = pl.ds(pl.multiple_of(step * x_rows, x_rows), x_rows)
-        raw = dot(to_grid_ref[0, rows, :], fourier_ref[0]) + dot(
-            to_grid_ref[1, rows, :], fourier_ref[1]
-        )
+        raw = dot(cos_ref[rows, :], fourier_ref[0]) + dot(sin_ref[rows, :], fourier_ref[1])
         features = (transform_scale * raw).astype(bf16)
-        for i in range(OWN):
-            lanes = slice(i * LANES, (i + 1) * LANES)
-            hidden = silu(dot(features[:, lanes], w_in_ref[...]) + bias_ref[...]).astype(bf16)
-            for layer in range(w_hid_ref.shape[0]):
-                update = silu(dot(hidden, w_hid_ref[layer]))
-                hidden = (hidden.astype(f32) + update).astype(bf16)
-            tendency_ref[rows, lanes] = dot(hidden, w_out_ref[...]).astype(bf16)
+        lanes = [slice(i * LANES, (i + 1) * LANES) for i in range(OWN)]
+        hidden = [half_silu(dot(features[:, at], w_in_ref[...]) + bias_ref[...]) for at in lanes]
+        hidden = [h.astype(bf16) for h in hidden]
+        for layer in range(w_hid_ref.shape[0]):
+            update = [half_silu(dot(h, w_hid_ref[layer])) for h in hidden]
+            hidden = [(h.astype(f32) + u).astype(bf16) for h, u in zip(hidden, update)]
+        for at, h in zip(lanes, hidden):
+            tendency_ref[rows, at] = dot(h, w_out_ref[...]).astype(bf16)
         return carry
 
     lax.fori_loop(0, NLON // x_rows, grid_rows, 0)
 
-    for part in range(2):
+    for part, table_ref in enumerate((cos_ref, sin_ref)):
         sums = lax.dot_general(
             tendency_ref[...],
-            to_grid_ref[part],
+            table_ref[...],
             (((0,), (0,)), ((), ())),
             preferred_element_type=f32,
         )
@@ -329,12 +331,12 @@
     pack_rows(slab_of, out_ref, scr_ref, peers, width)
 
 
-def columns(weights, fourier, to_grid, w_in, bias, w_hid, w_out, width):
+def columns(weights, fourier, cosines, sines, w_in, bias, w_hid, w_out, width):
     peers = fourier.shape[0] // 8
     vmem = pl.BlockSpec(memory_space=pltpu.VMEM)
     return pl.pallas_call(
-        functools.partial(column_kernel, x_rows=240, width=width),
-        in_specs=[pl.BlockSpec(memory_space=pltpu.SMEM)] + [vmem] * 6,
+        functools.partial(column_kernel, x_rows=X_ROWS, width=width),
+        in_specs=[pl.BlockSpec(memory_space=pltpu.SMEM)] + [vmem] * 7,
         out_specs=vmem,
         out_shape=jax.ShapeDtypeStruct(fourier.shape, bf16),
         scratch_shapes=[
@@ -343,73 +345,64 @@
             pltpu.VMEM((2, OWN, OWN, peers, LANES), f32),
             pltpu.VMEM((2, peers * 8, LANES), f32),
         ],
-        compiler_params=pltpu.CompilerParams(vmem_limit_bytes=28 * 2**20),
+        compiler_params=pltpu.CompilerParams(vmem_limit_bytes=40 * 2**20),
         name="columns",
-    )(weights, fourier, to_grid, w_in, bias, w_hid, w_out)
+    )(weights, fourier, cosines, sines, w_in, bias, w_hid, w_out)
 
 
 def forward_kernel(
     class_ref, in_ref, table_ref, maps_ref, out_ref, sums_ref, scr_ref, sent_ref, full_ref,
     *, lats, lat_local, lat_slots, width,
 ):
-    m = pl.program_id(0)
     peers = in_ref.shape[0] // 8
 
-    @pl.when(m == 0)
-    def _():
-        def put(part, i, m, slab):
-            sums_ref[m, part, pl.ds(i, peers, OWN), :] = slab
-
-        unpack_rows(in_ref, scr_ref, put, peers, width)
-
+    def put(part, i, m, slab):
+        sums_ref[m, part, pl.ds(i, peers, OWN), :] = slab
+
+    unpack_rows(in_ref, scr_ref, put, peers, width)
     lanes = table_ref.shape[-1]
-    weighted = jnp.concatenate(
-        [
-            jnp.concatenate(
-                [
-                    sums_ref[m, part, lat * lat_slots : lat * lat_slots + lat_local, :]
-                    for lat in range(lats)
-                ]
-                + [jnp.zeros((lanes - lats * lat_local, LANES), f32)]
-            )
-            for part in range(2)
-        ],
-        axis=1,
-    ).astype(bf16)
-    forcing = dot(table_ref[0], weighted).astype(bf16)
-    sent = out_ref.shape[2]
+    sent = out_ref.shape[3]
     rows = full_ref.shape[0] // lats
     spare = spare_lanes((lats, LANES), width)
-    for v in range(maps_ref.shape[0]):
-        full_ref[...] = dot(forcing, maps_ref[v])
-        for b in range(sent // 8):
-            last = full_ref[pl.ds(sent + b, lats, rows), :]
-            for t in range(8):
-                main = full_ref[pl.ds(8 * b + t, lats, rows), :]
-                sent_ref[pl.ds(8 * b + t, lats, sent), :] = jnp.where(
-                    spare, scatter_last(last, t, width), main
+    for m in range(OWN):
+        weighted = jnp.concatenate(
+            [
+                jnp.concatenate(
+                    [
+                        sums_ref[m, part, lat * lat_slots : lat * lat_slots + lat_local, :]
+                        for lat in range(lats)
+                    ]
+                    + [jnp.zeros((lanes - lats * lat_local, LANES), f32)]
                 )
-        for q in range(lats):
-            k, x = divmod(q, LAT_X)
-            out_ref[x * Z_LOW + class_ref[k], v] = sent_ref[q * sent : (q + 1) * sent, :].astype(
-                bf16
-            )
+                for part in range(2)
+            ],
+            axis=1,
+        ).astype(bf16)
+        forcing = dot(table_ref[m], weighted).astype(bf16)
+        for v in range(maps_ref.shape[0]):
+            full_ref[...] = dot(forcing, maps_ref[v])
+            for b in range(sent // 8):
+                last = full_ref[pl.ds(sent + b, lats, rows), :]
+                for t in range(8):
+                    main = full_ref[pl.ds(8 * b + t, lats, rows), :]
+                    sent_ref[pl.ds(8 * b + t, lats, sent), :] = jnp.where(
+                        spare, scatter_last(last, t, width), main
+                    )
+            for q in range(lats):
+                k, x = divmod(q, LAT_X)
+                piece = sent_ref[q * sent : (q + 1) * sent, :].astype(bf16)
+                out_ref[x * Z_LOW + class_ref[k], v, m] = piece
 
 
 def forward(classes, weighted, table, maps, peers, lats, sent, lat_local, lat_slots, width):
     levs = maps.shape[0]
+    vmem = pl.BlockSpec(memory_space=pltpu.VMEM)
     return pl.pallas_call(
         functools.partial(
             forward_kernel, lats=lats, lat_local=lat_local, lat_slots=lat_slots, width=width
         ),
-        grid=(OWN,),
-        in_specs=[
-            pl.BlockSpec(memory_space=pltpu.SMEM),
-            pl.BlockSpec(weighted.shape, lambda m: (0, 0)),
-            pl.BlockSpec((1, *table.shape[1:]), lambda m: (m, 0, 0)),
-            pl.BlockSpec(maps.shape, lambda m: (0, 0, 0)),
-        ],
-        out_specs=pl.BlockSpec((lats, levs, None, sent, LANES), lambda m: (0, 0, m, 0, 0)),
+        in_specs=[pl.BlockSpec(memory_space=pltpu.SMEM), vmem, vmem, vmem],
+        out_specs=vmem,
         out_shape=jax.ShapeDtypeStruct((lats, levs, OWN, sent, LANES), bf16),
         scratch_shapes=[
             pltpu.VMEM((OWN, 2, lats * lat_slots, LANES), f32),
@@ -417,65 +410,61 @@
             pltpu.VMEM((lats * sent, LANES), f32),
             pltpu.VMEM((table.shape[1], LANES), f32),
         ],
-        compiler_params=pltpu.CompilerParams(vmem_limit_bytes=20 * 2**20),
+        compiler_params=pltpu.CompilerParams(vmem_limit_bytes=24 * 2**20),
         name="forward",
     )(classes, weighted, table, maps)
 
 
-def update_kernel(at_ref, state_ref, forcing_ref, out_ref, scr_ref, last_ref):
-    _, channels, orders = state_ref.shape
-    b = pl.program_id(0)
-    main = pl.num_programs(0) - 1
+def turn_maps(channels):
+    maps = np.zeros((8, 2 * channels, LANES), np.float32)
+    for t in range(8):
+        maps[t, np.arange(channels), np.arange(channels)] = 1.0
+        piece = np.arange(SPARE)
+        maps[t, channels + SPARE * t + piece, channels + piece] = 1.0
+    return jnp.asarray(maps, bf16)
+
+
+def update_kernel(at_ref, damping_ref, state_ref, forcing_ref, maps_ref, out_ref, scr_ref):
+    degrees, channels, orders = state_ref.shape
     order = lax.broadcasted_iota(jnp.int32, (channels, orders), 1) + at_ref[0]
 
-    def put(i, forcing):
-        degree = jnp.full((channels, orders), b * 8 + i + at_ref[1], jnp.int32)
-        ratio = (degree * (degree + 1)).astype(f32) / ((L - 1) * L)
-        damping = 1.0 / (1.0 + hyper_rate * ratio * ratio)
-        new = (state_ref[i] + time_step * forcing[:, :channels].T) * damping
-        out_ref[i] = jnp.where(degree >= order, new, 0.0)
-
-    @pl.when(b < main)
-    def _():
+    def put(degree, forcing):
+        new = (state_ref[degree] + time_step * forcing) * damping_ref[degree]
+        out_ref[degree] = jnp.where(degree + at_ref[1] >= order, new, 0.0)
+
+    sent = forcing_ref.shape[2]
+    for b in range(sent // 8):
         for x in range(LAT_X):
             skip = OWN * (first_group(x - 1) + Z_RING - first_group(x)) if x else 0
             first = (OWN * first_group(x) + skip) * 8
-            mine = forcing_ref[x, skip:].astype(f32)
-            scr_ref[first : first + mine.shape[0] * 8, :] = mine.reshape(-1, LANES)
-        last = jnp.zeros((orders, LANES), f32)
+            mine = forcing_ref[x, skip:, 8 * b : 8 * b + 8, :].astype(f32)
+            scr_ref[b, first : first + mine.shape[0] * 8, :] = mine.reshape(-1, LANES)
+        last = 0.0
         for t in range(8):
-            slab = scr_ref[pl.ds(t, orders, 8), :]
-            put(t, slab)
-            last = gather_last(last, slab, t, channels)
-        last_ref[b] = last
-
-    @pl.when(b == main)
-    def _():
-        for i in range(last_ref.shape[0]):
-            put(i, last_ref[i])
-
-
-def update(at, state, forcing):
+            turned = lax.dot_general(
+                maps_ref[t],
+                scr_ref[b, pl.ds(t, orders, 8), :].astype(bf16),
+                (((1,), (1,)), ((), ())),
+                preferred_element_type=f32,
+            )
+            put(8 * b + t, turned[:channels])
+            last += turned[channels:]
+        put(sent + b, last)
+
+
+def update(at, damping, state, forcing):
     degrees, channels, orders = state.shape
-    _, group, sent, _ = forcing.shape
-    main = sent // 8
-    block = pl.BlockSpec((8, channels, orders), lambda i: (i, 0, 0))
+    _, _, sent, _ = forcing.shape
+    smem, vmem = (pl.BlockSpec(memory_space=m) for m in (pltpu.SMEM, pltpu.VMEM))
     return pl.pallas_call(
         update_kernel,
-        grid=(main + 1,),
-        in_specs=[
-            pl.BlockSpec(memory_space=pltpu.SMEM),
-            block,
-            pl.BlockSpec((LAT_X, group, 8, LANES), lambda i: (0, 0, jnp.minimum(i, main - 1), 0)),
-        ],
-        out_specs=block,
+        in_specs=[smem, smem, vmem, vmem, vmem],
+        out_specs=vmem,
         out_shape=jax.ShapeDtypeStruct(state.shape, f32),
-        scratch_shapes=[
-            pltpu.VMEM((orders * 8, LANES), f32),
-            pltpu.VMEM((degrees - sent, orders, LANES), f32),
-        ],
+        scratch_shapes=[pltpu.VMEM((sent // 8, orders * 8, LANES), f32)],
+        compiler_params=pltpu.CompilerParams(vmem_limit_bytes=24 * 2**20),
         name="update",
-    )(at, state, forcing)
+    )(at, damping, state, forcing, turn_maps(channels))
 
 
 def along_z(value, step):
@@ -540,7 +529,7 @@
     table = assemble(a_all, a_near, a_far, b_all)
     fourier = inverse(classes, table, coefficients, maps, peers, lat_local, lat_slots, width)
     fourier, order_ids, valid = lax.optimization_barrier((fourier, order_ids, valid))
-    to_grid = lookup_of(order_ids, valid)
+    cosines, sines = lookup_of(order_ids, valid)
 
     fourier = lax.all_to_all(fourier.reshape(peers, 8, -1), everyone, 0, 0, tiled=True)
     first = (ord_at * lev_size + lev_at) * OWN
@@ -548,10 +537,11 @@
     weighted = columns(
         weights,
         fourier.reshape(peers * 8, -1),
-        to_grid,
-        jnp.pad(weight_in, ((0, LANES - width), (0, 0))),
-        bias_in[None, :],
-        weight_hidden,
+        cosines,
+        sines,
+        jnp.pad(0.5 * weight_in, ((0, LANES - width), (0, 0))),
+        0.5 * bias_in[None, :],
+        0.5 * weight_hidden,
         jnp.pad(weight_out, ((0, 0), (0, LANES - width))),
         width,
     )
@@ -564,7 +554,10 @@
     forcing = forcing.reshape(lat_size * lev_size, OWN, sent, LANES)
     forcing = lax.all_to_all(forcing, ("lat", "lev"), 0, 0, tiled=True)
     forcing = forcing.reshape(LAT_X, OWN * Z_RING, sent, LANES)
-    updated = update(at, state, forcing)
+    degree_ids = lat_at * degree_local + lax.iota(jnp.int32, degree_local)
+    degree_ratio = (degree_ids * (degree_ids + 1)).astype(f32) / ((L - 1) * L)
+    damping = 1.0 / (1.0 + hyper_rate * degree_ratio * degree_ratio)
+    updated = update(at, damping, state, forcing)
     updated = updated.reshape(degree_local, *spectral_state.shape[2:], order_local)
     return updated.transpose(4, 0, 1, 2, 3)
 

time: 244 us -> 236 us (0.967)
  waiting for transfers between devices: 50.5 us -> 91.5 us
  blocking collectives: 68.9 us -> 38.1 us
  other arithmetic: 24.6 us -> 8.5 us
  Pallas kernels: 47.8 us -> 37.8 us
  starting transfers between devices: 41.9 us -> 51 us
    all_to_all x1 -> x0, blocking collectives: 30.8 us -> none  [on_device(): forcing = lax.all_to_all(forcing, ('lat', 'lev'), 0, 0, tiled=True)]
    all_to_all x0 -> x1, waiting for transfers between devices: none -> 26 us  [on_device(): forcing = lax.all_to_all(forcing, ('lat', 'lev'), 0, 0, tiled=True)]
    another operation x2 -> x0, other arithmetic: 21.7 us -> none
    all_to_all x1, waiting for transfers between devices: 9.79 us -> 26.2 us  [on_device(): lax.all_to_all(fourier.reshape(peers, 8, -1), everyone, 0, 0, tiled=True)]
    pallas_call x2, Pallas kernels: 24.4 us -> 13.9 us  [the longest x1 10.3 us: columns(): pl.pallas_call(functools.partial(column_kernel, x_rows=X_ROWS, width=widt...]
    all_to_all x0 -> x1, starting transfers between devices: none -> 5.85 us  [on_device(): forcing = lax.all_to_all(forcing, ('lat', 'lev'), 0, 0, tiled=True)]
    convert_element_type x0 -> x1, other arithmetic: none -> 3.09 us  [lookup_of(): sines.astype(bf16).reshape(shape)]
    pallas_call x1, Pallas kernels: 2.48 us -> 5.19 us  [pack_table(): pl.pallas_call(pack_kernel, grid=(LAT_X,), in_specs=[pl.BlockSpec(memory_...]
  transfers between devices with their start and end apart: 12 -> 13, of which waited for: 6 -> 7; matrix products, arithmetic and copies ran while one was open for 11% -> 4% of each run, Pallas kernels for 4% -> 4%
where the time goes in v6:
time: 236 us; the launch traced here: 235 us
  waiting for transfers between devices  91.5 us (39%)
  starting transfers between devices  51 us (22%)
  blocking collectives  38.1 us (16%)
  Pallas kernels  37.8 us (16%)
  other arithmetic  8.5 us (4%)
  local copies, waits for them, and re-layouts  7.75 us (3%)
    all_to_all x1, blocking collectives, on_device(): lax.all_to_all(weighted.reshape(peers, 8, -1), everyone, 0, 0, tiled=True)  38.1 us
    all_to_all x1, waiting for transfers between devices, on_device(): lax.all_to_all(fourier.reshape(peers, 8, -1), everyone, 0, 0, tiled=True)  26.2 us
    all_to_all x1, waiting for transfers between devices, on_device(): forcing = lax.all_to_all(forcing, ('lat', 'lev'), 0, 0, tiled=True)  26 us
    ppermute x8, waiting for transfers between devices, along_z(): return lax.ppermute(value, ('lat', 'lev'), pairs)  23.1 us
    ppermute x8, starting transfers between devices, along_z(): return lax.ppermute(value, ('lat', 'lev'), pairs)  16.3 us
    all_to_all x1, waiting for transfers between devices, on_device(): lax.all_to_all(coefficients, ('lat', 'lev'), 0, 0, tiled=True)  16.2 us
    all_to_all x2, starting transfers between devices, along_x(): lax.all_to_all(value, 'lat', 0, 0, axis_index_groups=groups, tiled=True)  10.8 us
    pallas_call x1, Pallas kernels, columns(): pl.pallas_call(functools.partial(column_kernel, x_rows=X_ROWS, width=widt...  10.3 us
  transfers between devices with their start and end apart: 13, of which 7 were waited for; matrix products, arithmetic and copies ran while one was open for 4% of the time, Pallas kernels for 4%

profile of v6, /device:TPU:2, one launch (start us, length us, event | category | flops | bytes accessed | tf_op | source)
XLA Modules:
  0.0 235.0 jit_solution(6829272836360009798)
XLA Ops:
  0.0 1.2 fusion.43.own_ref
  1.2 5.2 %pack_table.1 = (bf16[4,4,3,48,384]{4,3,2,1,0:T(8,128)(2,1)}, bf16[4,3,48,384]{3,2,1,0:T(8,128)(2,1)}, bf16[4,3,48,384]{3,2,1,0:T(8,128)(2,1)}, bf16[4,3,48,384]...) custom-call(s32[5]{0:T(128)} %fusion.43.own_ref, bf16[90,45,720]{2,1,0:T(8,128)(2,1)} %in_ref.1), custom_call_target="tpu_custom_call" | custom-call | tf_op jit(solution)/shard_map/pack_table/pallas_call | solution.py:172
  6.4 6.0 %all-to-all-start = ((bf16[4,4,3,48,384]{4,3,2,1,0:T(8,128)(2,1)}), bf16[4,4,3,48,384]{4,3,2,1,0:T(8,128)(2,1)S(1)}, u32[]{:S(2)}, u32[]{:S(2)}) async-start(bf16[4,4,3,48,384]{4,3,2,1,0:T(8,128)(2,1)} %get-tuple-element.22), calls=%async_computation | async-start | bytes 3538944 | tf_op jit(solution)/shard_map/all_to_all | solution.py:480
  13.3 4.0 %collective-permute-start.1 = (bf16[4,3,48,384]{3,2,1,0:T(8,128)(2,1)S(1)}, bf16[4,3,48,384]{3,2,1,0:T(8,128)(2,1)S(1)}, u32[]{:S(2)}, u32[]{:S(2)}) collective-permute-start(bf16[4,3,48,384]{3,2,1,0:T(8,128)(2,1)S(1)} %copy-done.18), channel_id=1, source_target_pairs={{0,7},{2,0},{4,2},{6,4},{1,6},{3,1},{5,3},{7,5},{8,15},{10,8},{12,... | collective-permute-start | bytes 1327112 | tf_op jit(solution)/shard_map/ppermute | solution.py:475
  17.4 4.1 %collective-permute-start.3 = (bf16[4,3,24,384]{3,2,1,0:T(8,128)(2,1)S(1)}, bf16[4,3,24,384]{3,2,1,0:T(8,128)(2,1)S(1)}, u32[]{:S(2)}, u32[]{:S(2)}) collective-permute-start(bf16[4,3,24,384]{3,2,1,0:T(8,128)(2,1)S(1)} %copy-done.20), channel_id=1, source_target_pairs={{0,5},{2,7},{4,0},{6,2},{1,4},{3,6},{5,1},{7,3},{8,13},{10,15},{12... | collective-permute-start | bytes 663560 | tf_op jit(solution)/shard_map/ppermute | solution.py:475
  21.5 12.8 %collective-permute-done.2 = bf16[4,3,24,384]{3,2,1,0:T(8,128)(2,1)S(1)} collective-permute-done((bf16[4,3,24,384]{3,2,1,0:T(8,128)(2,1)S(1)}, bf16[4,3,24,384]{3,2,1,0:T(8,128)(2,1)S(1)}, u32[]{:S(2)}, u32[]{:S(2)}) %collective-permute-start.2) | collective-permute-done | bytes 221216 | tf_op jit(solution)/shard_map/ppermute | solution.py:475
  34.3 1.4 collective-permute-done.3
  35.8 1.5 pad_maximum_fusion
  37.3 4.8 %all-to-all-start.1 = ((bf16[4,4,3,48,384]{4,3,2,1,0:T(8,128)(2,1)}), bf16[4,4,3,48,384]{4,3,2,1,0:T(8,128)(2,1)S(1)}, u32[]{:S(2)}, u32[]{:S(2)}) async-start(bf16[4,4,3,48,384]{4,3,2,1,0:T(8,128)(2,1)} %pad_maximum_fusion), calls=%async_computation.1 | async-start | bytes 3538944 | tf_op jit(solution)/shard_map/all_to_all | solution.py:480
  42.1 1.0 slice_bitcast_fusion
  43.1 2.8 %collective-permute-start.5 = (bf16[4,3,48,384]{3,2,1,0:T(8,128)(2,1)}, bf16[4,3,48,384]{3,2,1,0:T(8,128)(2,1)}, u32[]{:S(2)}, u32[]{:S(2)}) collective-permute-start(bf16[4,3,48,384]{3,2,1,0:T(8,128)(2,1)} %get-tuple-element.41), channel_id=1, source_target_pairs={{0,7},{2,0},{4,2},{6,4},{1,6},{3,1},{5,3},{7,5},{8,15},{10,8},{12,... | collective-permute-start | bytes 1327112 | tf_op jit(solution)/shard_map/ppermute | solution.py:475
  46.8 3.8 %collective-permute-start.7 = (bf16[4,3,24,384]{3,2,1,0:T(8,128)(2,1)}, bf16[4,3,24,384]{3,2,1,0:T(8,128)(2,1)S(1)}, u32[]{:S(2)}, u32[]{:S(2)}) collective-permute-start(bf16[4,3,24,384]{3,2,1,0:T(8,128)(2,1)} %get-tuple-element.39), channel_id=1, source_target_pairs={{0,5},{2,7},{4,0},{6,2},{1,4},{3,6},{5,1},{7,3},{8,13},{10,15},{12... | collective-permute-start | bytes 663560 | tf_op jit(solution)/shard_map/ppermute | solution.py:475
  51.8 5.3 %prep.1 = bf16[4,24,40,128]{3,2,1,0:T(8,128)(2,1)} custom-call(s32[2]{0:T(128)} %pad_add_fusion.at_ref, f32[45,112,90]{2,1,0:T(8,128)} %bitcast.32, f32[45,112,90]{2,1,0:T(8,128)} %bitcast.33), custom_call_target="tpu_custom_call" | custom-call | flops 1000000 | bytes 4000000 | tf_op jit(solution)/shard_map/prep/pallas_call | solution.py:131
  57.1 6.4 %collective-permute-done.7.a_high_ref = bf16[4,3,24,384]{3,2,1,0:T(8,128)(2,1)S(1)} collective-permute-done((bf16[4,3,24,384]{3,2,1,0:T(8,128)(2,1)}, bf16[4,3,24,384]{3,2,1,0:T(8,128)(2,1)S(1)}, u32[]{:S(2)}, u32[]{:S(2)}) %collective-permute-start.7) | collective-permute-done | bytes 221216 | tf_op jit(solution)/shard_map/ppermute | solution.py:475
  63.5 2.5 %collective-permute-done.6.a_low_ref = bf16[4,3,24,384]{3,2,1,0:T(8,128)(2,1)S(1)} collective-permute-done((bf16[4,3,24,384]{3,2,1,0:T(8,128)(2,1)}, bf16[4,3,24,384]{3,2,1,0:T(8,128)(2,1)S(1)}, u32[]{:S(2)}, u32[]{:S(2)}) %collective-permute-start.6) | collective-permute-done | bytes 221216 | tf_op jit(solution)/shard_map/ppermute | solution.py:475
  66.0 9.3 %all-to-all-start.2 = ((bf16[32,3,40,128]{3,2,1,0:T(8,128)(2,1)}), bf16[32,3,40,128]{3,2,1,0:T(8,128)(2,1)S(1)}, u32[]{:S(2)}, u32[]{:S(2)}) async-start(bf16[32,3,40,128]{3,2,1,0:T(8,128)(2,1)} %bitcast.43), calls=%async_computation.2 | async-start | bytes 1966080 | tf_op jit(solution)/shard_map/all_to_all | solution.py:526
  75.5 4.8 %assemble.1.table_ref = bf16[3,768,768]{2,1,0:T(8,128)(2,1)} custom-call(bf16[4,4,3,48,384]{4,3,2,1,0:T(8,128)(2,1)} %copy-done.9, bf16[4,3,48,384]{3,2,1,0:T(8,128)(2,1)} %collective-permute-done.4.a_left_ref, bf16[4,3,48,384]{3,2,1,0:T(8,128)(2,1)} %collective-permute-done.5.a_right_ref, bf16[4,3,24,384]{3,2,1,0:T(8,128)(2,1)} %copy-done.14, ...), custom_call_target="tpu_custom_call" | custom-call | flops 1000000 | bytes 8000000 | tf_op jit(solution)/shard_map/assemble/pallas_call | solution.py:205
  80.3 16.2 %all-to-all-done.2 = bf16[32,3,40,128]{3,2,1,0:T(8,128)(2,1)S(1)} async-done(((bf16[32,3,40,128]{3,2,1,0:T(8,128)(2,1)}), bf16[32,3,40,128]{3,2,1,0:T(8,128)(2,1)S(1)}, u32[]{:S(2)}, u32[]{:S(2)}) %all-to-all-start.2) | async-done | bytes 983072 | tf_op jit(solution)/shard_map/all_to_all | solution.py:526
  96.4 2.0 copy-done
  98.5 4.7 %inverse.1 = bf16[2048,256]{1,0:T(8,128)(2,1)} custom-call(s32[4]{0:T(128)S(1)} %and_select_fusion.3.class_ref, bf16[3,768,768]{2,1,0:T(8,128)(2,1)S(1)} %copy-done, bf16[16,2,3,40,128]{4,3,2,1,0:T(8,128)(2,1)S(1)} %bitcast.40, bf16[2,256,128]{2,1,0:T(8,128)(2,1)S(1)} %copy-done.6), custom_call_target="tpu_custom_call" | custom-call | tf_op jit(solution)/shard_map/inverse/pallas_call | solution.py:270
  103.1 8.8 %all-to-all-start.3 = ((bf16[256,8,256]{2,1,0:T(8,128)(2,1)}), bf16[256,8,256]{2,1,0:T(8,128)(2,1)S(1)}, u32[]{:S(2)}, u32[]{:S(2)}) async-start(bf16[256,8,256]{2,1,0:T(8,128)(2,1)} %bitcast.15), calls=%async_computation.3 | async-start | bytes 2097152 | tf_op jit(solution)/shard_map/all_to_all | solution.py:534
  114.2 3.1 %negate_convert_fusion = (bf16[45,32,768]{2,1,0:T(8,128)(2,1)S(1)}, bf16[45,32,768]{2,1,0:T(8,128)(2,1)}) fusion(f32[32,768]{1,0:T(8,128)S(1)} %get-tuple-element.48, f32[45,768]{1,0:T(8,128)S(1)} %get-tuple-element.46, f32[32,768]{1,0:T(8,128)S(1)} %get-tuple-element.47, f32[45,768]{1,0:T(8,128)S(1)} %get-tuple-element.45), kind=kLoop, calls=%fused_computation | loop fusion | flops 9953280 | bytes 4896768 | tf_op jit(solution)/shard_map/convert_element_type | solution.py:48
  117.3 26.2 %all-to-all-done.3 = bf16[256,8,256]{2,1,0:T(8,128)(2,1)S(1)} async-done(((bf16[256,8,256]{2,1,0:T(8,128)(2,1)}), bf16[256,8,256]{2,1,0:T(8,128)(2,1)S(1)}, u32[]{:S(2)}, u32[]{:S(2)}) %all-to-all-start.3) | async-done | bytes 1048608 | tf_op jit(solution)/shard_map/all_to_all | solution.py:534
  143.6 1.6 copy-done.3
  145.2 1.0 copy-done.5
  146.2 10.3 %columns.1 = bf16[2048,256]{1,0:T(8,128)(2,1)S(1)} custom-call(f32[3]{0:T(128)S(1)} %pad_dynamic-slice_fusion.weight_ref, bf16[2048,256]{1,0:T(8,128)(2,1)S(1)} %bitcast.37, bf16[1440,768]{1,0:T(8,128)(2,1)S(1)} %bitcast.36, bf16[1440,768]{1,0:T(8,128)(2,1)S(1)} %bitcast.35, bf16[128,256]{1,0:T(8,128)(2,1)S(1)} %pad.13.w_in_ref, f32[1,256]{1,0:T(1,128)S(1)} %bitcast.42, ...), custom_call_target="tpu_custom_call" | custom-call | tf_op jit(solution)/shard_map/columns/pallas_call | solution.py:337
  156.6 38.1 %all_to_all.30 = bf16[256,8,256]{2,1,0:T(8,128)(2,1)S(1)} all-to-all(bf16[256,8,256]{2,1,0:T(8,128)(2,1)S(1)} %bitcast.38), channel_id=1, replica_groups=mesh['ord'=8,'lat'=16,'lev'=2] {'lat','ord','lev'}, dimensions={0} | all-to-all | bytes 2097152 | tf_op jit(solution)/shard_map/all_to_all | solution.py:549
  194.7 3.8 %forward.1 = bf16[16,2,3,40,128]{4,3,2,1,0:T(8,128)(2,1)S(1)} custom-call(s32[4]{0:T(128)S(1)} %and_select_fusion.3.class_ref, bf16[2048,256]{1,0:T(8,128)(2,1)S(1)} %bitcast.39, bf16[3,768,768]{2,1,0:T(8,128)(2,1)S(1)} %copy-done.1, bf16[2,256,128]{2,1,0:T(8,128)(2,1)S(1)} %copy-done.6), custom_call_target="tpu_custom_call" | custom-call | tf_op jit(solution)/shard_map/forward/pallas_call | solution.py:400
  198.5 0.9 copy-done.4
  199.5 5.9 %all-to-all-start.5 = ((bf16[32,3,40,128]{3,2,1,0:T(8,128)(2,1)}), bf16[32,3,40,128]{3,2,1,0:T(8,128)(2,1)}, u32[]{:S(2)}, u32[]{:S(2)}) async-start(bf16[32,3,40,128]{3,2,1,0:T(8,128)(2,1)} %bitcast.41), calls=%async_computation.5 | async-start | bytes 1966080 | tf_op jit(solution)/shard_map/all_to_all | solution.py:555
  205.4 26.0 %all-to-all-done.5 = bf16[32,3,40,128]{3,2,1,0:T(8,128)(2,1)} async-done(((bf16[32,3,40,128]{3,2,1,0:T(8,128)(2,1)}), bf16[32,3,40,128]{3,2,1,0:T(8,128)(2,1)}, u32[]{:S(2)}, u32[]{:S(2)}) %all-to-all-start.5) | async-done | bytes 983072 | tf_op jit(solution)/shard_map/all_to_all | solution.py:555
  231.4 3.6 %update.1 = f32[45,112,90]{2,1,0:T(8,128)} custom-call(s32[2]{0:T(128)S(1)} %copy-done.8, f32[45]{0:T(128)S(1)} %add_divide_fusion.damping_ref, f32[45,112,90]{2,1,0:T(8,128)S(1)} %bitcast.34, bf16[4,24,40,128]{3,2,1,0:T(8,128)(2,1)} %bitcast.23.forcing_ref, bf16[8,224,128]{2,1,0:T(8,128)(2,1)S(1)} %copy-done.7), custom_call_target="tpu_custom_call" | custom-call | tf_op jit(solution)/shard_map/update/pallas_call | solution.py:459
  (71 shorter events, 5.4 us)
Async XLA Ops:
  6.4 6.9 %copy-start.18 = (bf16[4,3,48,384]{3,2,1,0:T(8,128)(2,1)S(1)}, bf16[4,3,48,384]{3,2,1,0:T(8,128)(2,1)}, u32[]{:S(2)}) copy-start(bf16[4,3,48,384]{3,2,1,0:T(8,128)(2,1)} %get-tuple-element.25) | copy-start | bytes 1327108
  6.4 10.9 %copy-start.21 = (bf16[4,3,24,384]{3,2,1,0:T(8,128)(2,1)S(1)}, bf16[4,3,24,384]{3,2,1,0:T(8,128)(2,1)}, u32[]{:S(2)}) copy-start(bf16[4,3,24,384]{3,2,1,0:T(8,128)(2,1)} %get-tuple-element.26) | copy-start | bytes 663556
  6.4 10.9 %copy-start.20 = (bf16[4,3,24,384]{3,2,1,0:T(8,128)(2,1)S(1)}, bf16[4,3,24,384]{3,2,1,0:T(8,128)(2,1)}, u32[]{:S(2)}) copy-start(bf16[4,3,24,384]{3,2,1,0:T(8,128)(2,1)} %get-tuple-element.27) | copy-start | bytes 663556
  6.4 29.3 %copy-start.12 = (bf16[4,3,48,384]{3,2,1,0:T(8,128)(2,1)S(1)}, bf16[4,3,48,384]{3,2,1,0:T(8,128)(2,1)}, u32[]{:S(2)}) copy-start(bf16[4,3,48,384]{3,2,1,0:T(8,128)(2,1)} %get-tuple-element.23) | copy-start | bytes 1327108
  6.4 30.8 %all-to-all-start = ((bf16[4,4,3,48,384]{4,3,2,1,0:T(8,128)(2,1)}), bf16[4,4,3,48,384]{4,3,2,1,0:T(8,128)(2,1)S(1)}, u32[]{:S(2)}, u32[]{:S(2)}) async-start(bf16[4,4,3,48,384]{4,3,2,1,0:T(8,128)(2,1)} %get-tuple-element.22), calls=%async_computation | async-start | bytes 3538944 | tf_op jit(solution)/shard_map/all_to_all | solution.py:480
  12.4 23.3 %collective-permute-start = (bf16[4,3,48,384]{3,2,1,0:T(8,128)(2,1)S(1)}, bf16[4,3,48,384]{3,2,1,0:T(8,128)(2,1)S(1)}, u32[]{:S(2)}, u32[]{:S(2)}) collective-permute-start(bf16[4,3,48,384]{3,2,1,0:T(8,128)(2,1)S(1)} %copy-done.19), channel_id=1, source_target_pairs={{0,2},{2,4},{4,6},{6,1},{1,3},{3,5},{5,7},{7,0},{8,10},{10,12},{12... | collective-permute-start | bytes 1327112 | tf_op jit(solution)/shard_map/ppermute | solution.py:475
  13.3 22.4 %collective-permute-start.1 = (bf16[4,3,48,384]{3,2,1,0:T(8,128)(2,1)S(1)}, bf16[4,3,48,384]{3,2,1,0:T(8,128)(2,1)S(1)}, u32[]{:S(2)}, u32[]{:S(2)}) collective-permute-start(bf16[4,3,48,384]{3,2,1,0:T(8,128)(2,1)S(1)} %copy-done.18), channel_id=1, source_target_pairs={{0,7},{2,0},{4,2},{6,4},{1,6},{3,1},{5,3},{7,5},{8,15},{10,8},{12,... | collective-permute-start | bytes 1327112 | tf_op jit(solution)/shard_map/ppermute | solution.py:475
  17.3 16.9 %collective-permute-start.2 = (bf16[4,3,24,384]{3,2,1,0:T(8,128)(2,1)S(1)}, bf16[4,3,24,384]{3,2,1,0:T(8,128)(2,1)S(1)}, u32[]{:S(2)}, u32[]{:S(2)}) collective-permute-start(bf16[4,3,24,384]{3,2,1,0:T(8,128)(2,1)S(1)} %copy-done.21), channel_id=1, source_target_pairs={{0,4},{2,6},{4,1},{6,3},{1,5},{3,7},{5,0},{7,2},{8,12},{10,14},{12... | collective-permute-start | bytes 663560 | tf_op jit(solution)/shard_map/ppermute | solution.py:475
  17.4 18.3 %collective-permute-start.3 = (bf16[4,3,24,384]{3,2,1,0:T(8,128)(2,1)S(1)}, bf16[4,3,24,384]{3,2,1,0:T(8,128)(2,1)S(1)}, u32[]{:S(2)}, u32[]{:S(2)}) collective-permute-start(bf16[4,3,24,384]{3,2,1,0:T(8,128)(2,1)S(1)} %copy-done.20), channel_id=1, source_target_pairs={{0,5},{2,7},{4,0},{6,2},{1,4},{3,6},{5,1},{7,3},{8,13},{10,15},{12... | collective-permute-start | bytes 663560 | tf_op jit(solution)/shard_map/ppermute | solution.py:475
  37.3 8.7 %copy-start.9 = (bf16[4,4,3,48,384]{4,3,2,1,0:T(8,128)(2,1)}, bf16[4,4,3,48,384]{4,3,2,1,0:T(8,128)(2,1)S(1)}, u32[]{:S(2)}) copy-start(bf16[4,4,3,48,384]{4,3,2,1,0:T(8,128)(2,1)S(1)} %all-to-all-done.a_own_ref) | copy-start | bytes 5308420
  37.3 28.7 %all-to-all-start.1 = ((bf16[4,4,3,48,384]{4,3,2,1,0:T(8,128)(2,1)}), bf16[4,4,3,48,384]{4,3,2,1,0:T(8,128)(2,1)S(1)}, u32[]{:S(2)}, u32[]{:S(2)}) async-start(bf16[4,4,3,48,384]{4,3,2,1,0:T(8,128)(2,1)} %pad_maximum_fusion), calls=%async_computation.1 | async-start | bytes 3538944 | tf_op jit(solution)/shard_map/all_to_all | solution.py:480
  43.1 22.9 %collective-permute-start.5 = (bf16[4,3,48,384]{3,2,1,0:T(8,128)(2,1)}, bf16[4,3,48,384]{3,2,1,0:T(8,128)(2,1)}, u32[]{:S(2)}, u32[]{:S(2)}) collective-permute-start(bf16[4,3,48,384]{3,2,1,0:T(8,128)(2,1)} %get-tuple-element.41), channel_id=1, source_target_pairs={{0,7},{2,0},{4,2},{6,4},{1,6},{3,1},{5,3},{7,5},{8,15},{10,8},{12,... | collective-permute-start | bytes 1327112 | tf_op jit(solution)/shard_map/ppermute | solution.py:475
  45.9 20.1 %collective-permute-start.4 = (bf16[4,3,48,384]{3,2,1,0:T(8,128)(2,1)}, bf16[4,3,48,384]{3,2,1,0:T(8,128)(2,1)}, u32[]{:S(2)}, u32[]{:S(2)}) collective-permute-start(bf16[4,3,48,384]{3,2,1,0:T(8,128)(2,1)} %get-tuple-element.42), channel_id=1, source_target_pairs={{0,2},{2,4},{4,6},{6,1},{1,3},{3,5},{5,7},{7,0},{8,10},{10,12},{12... | collective-permute-start | bytes 1327112 | tf_op jit(solution)/shard_map/ppermute | solution.py:475
  46.8 16.7 %collective-permute-start.7 = (bf16[4,3,24,384]{3,2,1,0:T(8,128)(2,1)}, bf16[4,3,24,384]{3,2,1,0:T(8,128)(2,1)S(1)}, u32[]{:S(2)}, u32[]{:S(2)}) collective-permute-start(bf16[4,3,24,384]{3,2,1,0:T(8,128)(2,1)} %get-tuple-element.39), channel_id=1, source_target_pairs={{0,5},{2,7},{4,0},{6,2},{1,4},{3,6},{5,1},{7,3},{8,13},{10,15},{12... | collective-permute-start | bytes 663560 | tf_op jit(solution)/shard_map/ppermute | solution.py:475
  50.5 15.4 %collective-permute-start.6 = (bf16[4,3,24,384]{3,2,1,0:T(8,128)(2,1)}, bf16[4,3,24,384]{3,2,1,0:T(8,128)(2,1)S(1)}, u32[]{:S(2)}, u32[]{:S(2)}) collective-permute-start(bf16[4,3,24,384]{3,2,1,0:T(8,128)(2,1)} %get-tuple-element.40), channel_id=1, source_target_pairs={{0,4},{2,6},{4,1},{6,3},{1,5},{3,7},{5,0},{7,2},{8,12},{10,14},{12... | collective-permute-start | bytes 663560 | tf_op jit(solution)/shard_map/ppermute | solution.py:475
  51.8 23.6 %copy-start.23 = (s32[4]{0:T(128)S(1)}, s32[4]{0:T(128)}, u32[]{:S(2)}) copy-start(s32[4]{0:T(128)} %constant.219.clone) | copy-start | bytes 52
  63.5 12.0 %copy-start.13 = (bf16[4,3,24,384]{3,2,1,0:T(8,128)(2,1)}, bf16[4,3,24,384]{3,2,1,0:T(8,128)(2,1)S(1)}, u32[]{:S(2)}) copy-start(bf16[4,3,24,384]{3,2,1,0:T(8,128)(2,1)S(1)} %collective-permute-done.7.a_high_ref) | copy-start | bytes 663556
  66.0 9.4 %copy-start.14 = (bf16[4,3,24,384]{3,2,1,0:T(8,128)(2,1)}, bf16[4,3,24,384]{3,2,1,0:T(8,128)(2,1)S(1)}, u32[]{:S(2)}) copy-start(bf16[4,3,24,384]{3,2,1,0:T(8,128)(2,1)S(1)} %collective-permute-done.6.a_low_ref) | copy-start | bytes 663556
  66.0 9.4 %copy-start.10 = (bf16[4,4,3,48,384]{4,3,2,1,0:T(8,128)(2,1)}, bf16[4,4,3,48,384]{4,3,2,1,0:T(8,128)(2,1)S(1)}, u32[]{:S(2)}) copy-start(bf16[4,4,3,48,384]{4,3,2,1,0:T(8,128)(2,1)S(1)} %all-to-all-done.1.b_ref) | copy-start | bytes 5308420
  66.0 30.4 %all-to-all-start.2 = ((bf16[32,3,40,128]{3,2,1,0:T(8,128)(2,1)}), bf16[32,3,40,128]{3,2,1,0:T(8,128)(2,1)S(1)}, u32[]{:S(2)}, u32[]{:S(2)}) async-start(bf16[32,3,40,128]{3,2,1,0:T(8,128)(2,1)} %bitcast.43), calls=%async_computation.2 | async-start | bytes 1966080 | tf_op jit(solution)/shard_map/all_to_all | solution.py:526
  75.5 21.0 %copy-start.6 = (bf16[2,256,128]{2,1,0:T(8,128)(2,1)S(1)}, bf16[2,256,128]{2,1,0:T(8,128)(2,1)}, u32[]{:S(2)}) copy-start(bf16[2,256,128]{2,1,0:T(8,128)(2,1)} %constant.217.clone.maps_ref) | copy-start | bytes 393220
  98.4 13.5 %copy-start.16 = (bf16[256,112]{0,1:T(8,128)(2,1)S(1)}, bf16[256,112]{0,1:T(8,128)(2,1)}, u32[]{:S(2)}) copy-start(bf16[256,112]{0,1:T(8,128)(2,1)} %param.17) | copy-start | bytes 172036
  103.1 8.9 %copy-start.15 = (bf16[112,256]{1,0:T(8,128)(2,1)S(1)}, bf16[112,256]{1,0:T(8,128)(2,1)}, u32[]{:S(2)}) copy-start(bf16[112,256]{1,0:T(8,128)(2,1)} %param.14) | copy-start | bytes 172036
  103.1 9.0 %copy-start.22 = (f32[45]{0:T(128)S(1)}, f32[45]{0:T(128)}, u32[]{:S(2)}) copy-start(f32[45]{0:T(128)} %param.13) | copy-start | bytes 544
  103.1 9.1 %copy-start.17 = (f32[256]{0:T(256)S(1)}, f32[256]{0:T(256)}, u32[]{:S(2)}) copy-start(f32[256]{0:T(256)} %param.15) | copy-start | bytes 3076
  103.1 9.1 %copy-start.11 = (bf16[4,256,256]{2,1,0:T(8,128)(2,1)S(1)}, bf16[4,256,256]{2,1,0:T(8,128)(2,1)}, u32[]{:S(2)}) copy-start(bf16[4,256,256]{2,1,0:T(8,128)(2,1)} %param.16) | copy-start | bytes 1572868
  103.1 40.4 %all-to-all-start.3 = ((bf16[256,8,256]{2,1,0:T(8,128)(2,1)}), bf16[256,8,256]{2,1,0:T(8,128)(2,1)S(1)}, u32[]{:S(2)}, u32[]{:S(2)}) async-start(bf16[256,8,256]{2,1,0:T(8,128)(2,1)} %bitcast.15), calls=%async_computation.3 | async-start | bytes 2097152 | tf_op jit(solution)/shard_map/all_to_all | solution.py:534
  146.2 48.5 %copy-start.1 = (bf16[3,768,768]{2,1,0:T(8,128)(2,1)S(1)}, bf16[3,768,768]{2,1,0:T(8,128)(2,1)}, u32[]{:S(2)}) copy-start(bf16[3,768,768]{2,1,0:T(8,128)(2,1)} %assemble.1.table_ref) | copy-start | bytes 10616836
  194.7 36.7 %copy-start.2 = (f32[90,45,8,7,2]{0,4,3,2,1:T(2,128)S(1)}, f32[90,45,8,7,2]{0,4,3,2,1:T(2,128)}, u32[]{:S(2)}) copy-start(f32[90,45,8,7,2]{0,4,3,2,1:T(2,128)} %param.11) | copy-start | bytes 5443204
  194.7 36.7 %copy-start.8 = (s32[2]{0:T(128)S(1)}, s32[2]{0:T(128)}, u32[]{:S(2)}) copy-start(s32[2]{0:T(128)} %pad_add_fusion.at_ref) | copy-start | bytes 28
  199.5 31.9 %copy-start.7 = (bf16[8,224,128]{2,1,0:T(8,128)(2,1)S(1)}, bf16[8,224,128]{2,1,0:T(8,128)(2,1)}, u32[]{:S(2)}) copy-start(bf16[8,224,128]{2,1,0:T(8,128)(2,1)} %constant.220.clone.maps_ref) | copy-start | bytes 1376260
  199.5 31.9 %all-to-all-start.5 = ((bf16[32,3,40,128]{3,2,1,0:T(8,128)(2,1)}), bf16[32,3,40,128]{3,2,1,0:T(8,128)(2,1)}, u32[]{:S(2)}, u32[]{:S(2)}) async-start(bf16[32,3,40,128]{3,2,1,0:T(8,128)(2,1)} %bitcast.41), calls=%async_computation.5 | async-start | bytes 1966080 | tf_op jit(solution)/shard_map/all_to_all | solution.py:555
  (5 other events, 11.6 us)

commit v7 on v6

--- a/solution.py
+++ b/solution.py
@@ -144,7 +144,7 @@
     )(at, state, state)
 
 
-def pack_kernel(own_ref, in_ref, a_ref, *b_refs):
+def pack_kernel(meta_ref, in_ref, a_ref, *b_refs):
     degrees, lats = in_ref.shape[1:]
     half, rows = a_ref.shape[-1], a_ref.shape[-2]
     split = rows // 2
@@ -152,53 +152,62 @@
     for ref in b_refs:
         ref[...] = jnp.zeros_like(ref)
     for k in range(3):
-        mine = in_ref[pl.ds(own_ref[k], OWN)]
+        mine = in_ref[pl.ds(meta_ref[1 + k], OWN)]
         a_ref[0, k, :, :degrees, :] = mine[:, :, :half]
         b_refs[k][0, :, :degrees, : lats - half] = mine[:, :, half:]
-    mine = in_ref[pl.ds(own_ref[3], OWN)]
+    mine = in_ref[pl.ds(meta_ref[4], OWN)]
     a_ref[0, 3, :, :split, :] = mine[:, :split, :half]
     b_refs[3][0, :, :, : lats - half] = mine[:, :split, half:]
-    mine = in_ref[pl.ds(own_ref[4], OWN)]
+    mine = in_ref[pl.ds(meta_ref[5], OWN)]
     a_ref[0, 3, :, split:degrees, :] = mine[:, split:, :half]
     b_refs[4][0, :, : degrees - split, : lats - half] = mine[:, split:, half:]
 
 
-def pack_table(own, legendre, half, rows):
+def pack_table(meta, legendre, half, rows):
     _, degrees, lats = legendre.shape
     group = OWN * Z_RING
-    b_shape = lambda r: jax.ShapeDtypeStruct((LAT_X, OWN, r, half), bf16)
-    b_spec = lambda r: pl.BlockSpec((1, OWN, r, half), lambda x: (x, 0, 0, 0))
+    x_of = lambda d, meta: lax.rem(meta[0] + d, LAT_X)
     b_rows = (rows, rows, rows, rows // 2, rows // 2)
+    b_specs = [pl.BlockSpec((1, OWN, r, half), lambda d, meta: (d, 0, 0, 0)) for r in b_rows]
     return pl.pallas_call(
         pack_kernel,
-        grid=(LAT_X,),
-        in_specs=[
-            pl.BlockSpec(memory_space=pltpu.SMEM),
-            pl.BlockSpec(
-                (pl.Element(group), pl.Element(degrees), pl.Element(lats)),
-                lambda x: (OWN * first_group(x), 0, 0),
-            ),
-        ],
-        out_specs=[pl.BlockSpec((1, 4, OWN, rows, half), lambda x: (x, 0, 0, 0, 0))]
-        + [b_spec(r) for r in b_rows],
+        grid_spec=pltpu.PrefetchScalarGridSpec(
+            num_scalar_prefetch=1,
+            grid=(LAT_X,),
+            in_specs=[
+                pl.BlockSpec(
+                    (pl.Element(group), pl.Element(degrees), pl.Element(lats)),
+                    lambda d, meta: (OWN * first_group(x_of(d, meta)), 0, 0),
+                ),
+            ],
+            out_specs=[
+                pl.BlockSpec((1, 4, OWN, rows, half), lambda d, meta: (x_of(d, meta), 0, 0, 0, 0))
+            ]
+            + b_specs,
+        ),
         out_shape=[jax.ShapeDtypeStruct((LAT_X, 4, OWN, rows, half), bf16)]
-        + [b_shape(r) for r in b_rows],
-        compiler_params=pltpu.CompilerParams(vmem_limit_bytes=60 * 2**20),
+        + [jax.ShapeDtypeStruct((LAT_X, OWN, r, half), bf16) for r in b_rows],
+        compiler_params=pltpu.CompilerParams(vmem_limit_bytes=16 * 2**20),
         name="pack_table",
-    )(own, legendre)
-
-
-def assemble_kernel(a_own_ref, a_left_ref, a_right_ref, a_low_ref, a_high_ref, b_ref, out_ref):
-    rows, half = b_ref.shape[-2:]
+    )(meta, legendre)
+
+
+def assemble_kernel(
+    from_ref, a_own_ref, a_left_ref, a_right_ref, a_low_ref, a_high_ref, *refs
+):
+    out_ref, b_refs = refs[-1], refs[:-1]
+    rows, half = a_own_ref.shape[-2:]
     place = LAT_X * rows
     far = jnp.concatenate([a_low_ref[...], a_high_ref[...]], axis=1)
     for k, piece in enumerate((a_own_ref[:, 0], a_left_ref[...], a_right_ref[...], far)):
         out_ref[0, k * place : (k + 1) * place, :half] = piece.reshape(place, half)
-        out_ref[0, k * place : (k + 1) * place, half:] = b_ref[:, k].reshape(place, half)
-
-
-def assemble(a_own, a_near, a_far, b_all):
-    rows, half = b_all.shape[-2:]
+        for d, b_ref in enumerate(b_refs):
+            first = pl.multiple_of(k * place + from_ref[d] * rows, 16)
+            out_ref[0, pl.ds(first, rows), half:] = b_ref[k]
+
+
+def assemble(sources, a_own, a_near, a_far, b_all):
+    rows, half = a_own.shape[-2:]
     size = 4 * LAT_X * rows
     near = pl.BlockSpec((LAT_X, None, rows, half), lambda m: (0, m, 0, 0))
     far = pl.BlockSpec((LAT_X, None, rows // 2, half), lambda m: (0, m, 0, 0))
@@ -206,18 +215,19 @@
         assemble_kernel,
         grid=(OWN,),
         in_specs=[
+            pl.BlockSpec(memory_space=pltpu.SMEM),
             pl.BlockSpec((LAT_X, 1, None, rows, half), lambda m: (0, 0, m, 0, 0)),
             near,
             near,
             far,
             far,
-            pl.BlockSpec((LAT_X, 4, None, rows, half), lambda m: (0, 0, m, 0, 0)),
-        ],
+        ]
+        + [pl.BlockSpec((4, None, rows, half), lambda m: (0, m, 0, 0))] * LAT_X,
         out_specs=pl.BlockSpec((1, size, 2 * half), lambda m: (m, 0, 0)),
         out_shape=jax.ShapeDtypeStruct((OWN, size, 2 * half), bf16),
         cost_estimate=pl.CostEstimate(flops=10**6, bytes_accessed=8 * 10**6, transcendentals=0),
         name="assemble",
-    )(a_own, *a_near, *a_far, b_all)
+    )(sources, a_own, *a_near, *a_far, *b_all)
 
 
 def inverse_kernel(
@@ -467,12 +477,17 @@
     )(at, damping, state, forcing, turn_maps(channels))
 
 
-def along_z(value, step):
+def shifted(value, x_step, z_step):
     pairs = []
     flat = lambda x, z: x * Z_RING + 2 * (z % Z_LOW) + z // Z_LOW
     for x in range(LAT_X):
-        pairs += [(flat(x, z), flat(x, (z + step) % Z_RING)) for z in range(Z_RING)]
+        to_x = (x + x_step) % LAT_X
+        pairs += [(flat(x, z), flat(to_x, (z + z_step) % Z_RING)) for z in range(Z_RING)]
     return lax.ppermute(value, ("lat", "lev"), pairs)
+
+
+def along_z(value, step):
+    return shifted(value, 0, step)
 
 
 def along_x(value):
@@ -498,17 +513,21 @@
     state = spectral_state.transpose(1, 2, 3, 4, 0).reshape(degree_local, channels, order_local)
 
     z_at = lev_at * Z_LOW + lat_at % Z_LOW
+    x_at = lat_at // Z_LOW
     ring = (z_at + jnp.array([0, 1, -1, 2, -2], jnp.int32)) % Z_RING
     own = OWN * (2 * (ring % Z_LOW) + ring // Z_LOW)
-    a_all, b_own, *b_rest = pack_table(own, legendre, HALF, rows)
+    meta = jnp.concatenate([x_at[None], own]).astype(jnp.int32)
+    a_all, b_own, *b_rest = pack_table(meta, legendre, HALF, rows)
     b_left, b_right, b_low, b_high = (along_z(v, k) for v, k in zip(b_rest, (1, -1, 2, -2)))
     a_all = along_x(a_all)
     b_far = jnp.concatenate([b_low, b_high], axis=2)
-    b_all = jnp.stack([b_own, b_left, b_right, b_far], axis=1)
-    a_all, b_all = lax.optimization_barrier((a_all, b_all))
+    b_all = [jnp.stack([v[d] for v in (b_own, b_left, b_right, b_far)]) for d in range(LAT_X)]
+    coefficients = prep(at, state, sent)
+    a_all, b_all, coefficients = lax.optimization_barrier((a_all, b_all, coefficients))
     a_near = [along_z(a_all[:, 1], 1), along_z(a_all[:, 2], -1)]
     a_far = [along_z(a_all[:, 3, :, : rows // 2], 2), along_z(a_all[:, 3, :, rows // 2 :], -2)]
-    b_all = along_x(b_all)
+    b_all = [b_all[0]] + [shifted(b_all[d], step, 0) for d, step in ((1, 1), (2, 2), (3, -1))]
+    sources = (x_at - jnp.arange(LAT_X, dtype=jnp.int32)) % LAT_X
 
     slot = lax.iota(jnp.int32, OWN * peers)
     slot_lev = slot % lev_size
@@ -517,16 +536,11 @@
     slot_x, slot_w = slot_lat // Z_LOW, 2 * (slot_lat % Z_LOW) + slot_lev
     valid = (slot_x % 2 == 0) | (slot_w > 0)
     order_ids = slot_ord * order_local + OWN * (first_group(slot_x) + slot_w) + slot // peers
-    coefficients = prep(at, state, sent)
-    coefficients, a_near, a_far, b_all = lax.optimization_barrier(
-        (coefficients, a_near, a_far, b_all)
-    )
-
     coefficients = coefficients.reshape(lat_size * lev_size, OWN, sent, LANES)
     coefficients = lax.all_to_all(coefficients, ("lat", "lev"), 0, 0, tiled=True)
     coefficients = coefficients.reshape(lat_size, lev_size, OWN, sent, LANES)
     classes = (z_at + jnp.array([0, -1, 1, 2], jnp.int32)) % Z_LOW
-    table = assemble(a_all, a_near, a_far, b_all)
+    table = assemble(sources, a_all, a_near, a_far, b_all)
     fourier = inverse(classes, table, coefficients, maps, peers, lat_local, lat_slots, width)
     fourier, order_ids, valid = lax.optimization_barrier((fourier, order_ids, valid))
     cosines, sines = lookup_of(order_ids, valid)

time: 236 us -> 242 us (1.025)
  local copies, waits for them, and re-layouts: 7.75 us -> 14.6 us
  Pallas kernels: 37.8 us -> 35 us
    all_to_all x1, waiting for transfers between devices: 16.2 us -> 0.01 us  [on_device(): lax.all_to_all(coefficients, ('lat', 'lev'), 0, 0, tiled=True)]
    ppermute x8 -> x11, waiting for transfers between devices: 23.1 us -> 39.2 us  [shifted(): return lax.ppermute(value, ('lat', 'lev'), pairs)]
    all_to_all x2 -> x1, starting transfers between devices: 10.8 us -> 5.82 us  [along_x(): lax.all_to_all(value, 'lat', 0, 0, axis_index_groups=groups, tiled=True)]
    unnamed x49 -> x56, local copies, waits for them, and re-layouts: 5.8 us -> 10.4 us
    all_to_all x1, starting transfers between devices: 8.77 us -> 12.6 us  [on_device(): lax.all_to_all(fourier.reshape(peers, 8, -1), everyone, 0, 0, tiled=True)]
    slice x0 -> x4, local copies, waits for them, and re-layouts: none -> 3.03 us  [on_device(): v[d]]
    pallas_call x2, Pallas kernels: 10 us -> 7.29 us  [the longest x1 4.79 us: assemble(): pl.pallas_call(assemble_kernel, grid=(OWN,), in_specs=[pl.BlockSpec(memor...]
    ppermute x8 -> x11, starting transfers between devices: 16.3 us -> 19 us  [shifted(): return lax.ppermute(value, ('lat', 'lev'), pairs)]
  transfers between devices with their start and end apart: 13 -> 15, of which waited for: 7 -> 8; matrix products, arithmetic and copies ran while one was open for 4% -> 6% of each run, Pallas kernels for 4% -> 4%
where the time goes in v7:
time: 242 us; the launch traced here: 241 us
  waiting for transfers between devices  91.6 us (38%)
  starting transfers between devices  52.4 us (22%)
  blocking collectives  38.1 us (16%)
  Pallas kernels  35 us (14%)
  local copies, waits for them, and re-layouts  14.6 us (6%)
  other arithmetic  9.2 us (4%)
    ppermute x11, waiting for transfers between devices, shifted(): return lax.ppermute(value, ('lat', 'lev'), pairs)  39.2 us
    all_to_all x1, blocking collectives, on_device(): lax.all_to_all(weighted.reshape(peers, 8, -1), everyone, 0, 0, tiled=True)  38.1 us
    all_to_all x1, waiting for transfers between devices, on_device(): lax.all_to_all(fourier.reshape(peers, 8, -1), everyone, 0, 0, tiled=True)  26.4 us
    all_to_all x1, waiting for transfers between devices, on_device(): forcing = lax.all_to_all(forcing, ('lat', 'lev'), 0, 0, tiled=True)  26 us
    ppermute x11, starting transfers between devices, shifted(): return lax.ppermute(value, ('lat', 'lev'), pairs)  19 us
    all_to_all x1, starting transfers between devices, on_device(): lax.all_to_all(fourier.reshape(peers, 8, -1), everyone, 0, 0, tiled=True)  12.6 us
    unnamed x56, local copies, waits for them, and re-layouts  10.4 us
    pallas_call x1, Pallas kernels, columns(): pl.pallas_call(functools.partial(column_kernel, x_rows=X_ROWS, width=widt...  10.4 us
  transfers between devices with their start and end apart: 15, of which 8 were waited for; matrix products, arithmetic and copies ran while one was open for 6% of the time, Pallas kernels for 4%

profile of v7, /device:TPU:2, one launch (start us, length us, event | category | flops | bytes accessed | tf_op | source)
XLA Modules:
  0.0 241.3 jit_solution(6504299794312795382)
XLA Ops:
  0.8 2.9 %copy-done.4 = bf16[90,45,720]{2,1,0:T(8,128)(2,1)S(1)} copy-done((bf16[90,45,720]{2,1,0:T(8,128)(2,1)S(1)}, bf16[90,45,720]{2,1,0:T(8,128)(2,1)}, u32[]{:S(2)}) %copy-start.4) | copy-done | bytes 5832024
  3.6 2.5 %pack_table.1 = (bf16[4,4,3,48,384]{4,3,2,1,0:T(8,128)(2,1)}, bf16[4,3,48,384]{3,2,1,0:T(8,128)(2,1)S(1)}, bf16[4,3,48,384]{3,2,1,0:T(8,128)(2,1)S(1)}, bf16[4,3...) custom-call(s32[6]{0:T(128)S(1)} %pad_add_fusion.1.meta_ref, ...), custom_call_target="tpu_custom_call" | custom-call | tf_op jit(solution)/shard_map/pack_table/pallas_call | solution.py:172
  6.1 5.8 %all-to-all-start = ((bf16[4,4,3,48,384]{4,3,2,1,0:T(8,128)(2,1)}), bf16[4,4,3,48,384]{4,3,2,1,0:T(8,128)(2,1)S(1)}, u32[]{:S(2)}, u32[]{:S(2)}) async-start(bf16[4,4,3,48,384]{4,3,2,1,0:T(8,128)(2,1)} %get-tuple-element.20), calls=%async_computation | async-start | bytes 3538944 | tf_op jit(solution)/shard_map/all_to_all | solution.py:495
  12.0 2.3 collective-permute-start.2
  14.2 3.0 %collective-permute-start.3 = (bf16[4,3,24,384]{3,2,1,0:T(8,128)(2,1)S(1)}, bf16[4,3,24,384]{3,2,1,0:T(8,128)(2,1)}, u32[]{:S(2)}, u32[]{:S(2)}) collective-permute-start(bf16[4,3,24,384]{3,2,1,0:T(8,128)(2,1)S(1)} %get-tuple-element.25), channel_id=1, source_target_pairs={{0,5},{2,7},{4,0},{6,2},{1,4},{3,6},{5,1},{7,3},{8,13},{10,15},{12... | collective-permute-start | bytes 663560 | tf_op jit(solution)/shard_map/ppermute | solution.py:486
  18.3 2.2 collective-permute-start.1
  21.9 5.3 %prep.1 = bf16[4,24,40,128]{3,2,1,0:T(8,128)(2,1)} custom-call(s32[2]{0:T(128)} %pad_add_fusion.at_ref, f32[45,112,90]{2,1,0:T(8,128)} %bitcast.28, f32[45,112,90]{2,1,0:T(8,128)} %bitcast.29), custom_call_target="tpu_custom_call" | custom-call | flops 1000000 | bytes 4000000 | tf_op jit(solution)/shard_map/prep/pallas_call | solution.py:131
  27.2 1.2 collective-permute-done.2
  30.4 5.6 %collective-permute-done = bf16[4,3,48,384]{3,2,1,0:T(8,128)(2,1)} collective-permute-done((bf16[4,3,48,384]{3,2,1,0:T(8,128)(2,1)S(1)}, bf16[4,3,48,384]{3,2,1,0:T(8,128)(2,1)}, u32[]{:S(2)}, u32[]{:S(2)}) %collective-permute-start) | collective-permute-done | bytes 442400 | tf_op jit(solution)/shard_map/ppermute | solution.py:486
  36.0 1.1 fusion.46
  39.2 1.1 pad_maximum_fusion
  40.4 9.2 %all-to-all-start.1 = ((bf16[32,3,40,128]{3,2,1,0:T(8,128)(2,1)}), bf16[32,3,40,128]{3,2,1,0:T(8,128)(2,1)S(1)}, u32[]{:S(2)}, u32[]{:S(2)}) async-start(bf16[32,3,40,128]{3,2,1,0:T(8,128)(2,1)} %bitcast.39), calls=%async_computation.1 | async-start | bytes 1966080 | tf_op jit(solution)/shard_map/all_to_all | solution.py:540
  49.7 3.7 %collective-permute-start.7 = (bf16[4,3,24,384]{3,2,1,0:T(8,128)(2,1)S(1)}, bf16[4,3,24,384]{3,2,1,0:T(8,128)(2,1)S(1)}, u32[]{:S(2)}, u32[]{:S(2)}) collective-permute-start(bf16[4,3,24,384]{3,2,1,0:T(8,128)(2,1)S(1)} %get-tuple-element.35), channel_id=1, source_target_pairs={{0,5},{2,7},{4,0},{6,2},{1,4},{3,6},{5,1},{7,3},{8,13},{10,15},{12... | collective-permute-start | bytes 663560 | tf_op jit(solution)/shard_map/ppermute | solution.py:486
  53.3 1.5 collective-permute-start.8
  54.8 1.1 collective-permute-start.9
  55.9 2.1 collective-permute-start.10
  58.2 23.7 %collective-permute-done.7.a_high_ref = bf16[4,3,24,384]{3,2,1,0:T(8,128)(2,1)S(1)} collective-permute-done((bf16[4,3,24,384]{3,2,1,0:T(8,128)(2,1)S(1)}, bf16[4,3,24,384]{3,2,1,0:T(8,128)(2,1)S(1)}, u32[]{:S(2)}, u32[]{:S(2)}) %collective-permute-start.7) | collective-permute-done | bytes 221216 | tf_op jit(solution)/shard_map/ppermute | solution.py:486
  81.9 2.0 collective-permute-start.4
  84.6 7.8 %collective-permute-done.5.a_right_ref = bf16[4,3,48,384]{3,2,1,0:T(8,128)(2,1)S(1)} collective-permute-done((bf16[4,3,48,384]{3,2,1,0:T(8,128)(2,1)S(1)}, bf16[4,3,48,384]{3,2,1,0:T(8,128)(2,1)S(1)}, u32[]{:S(2)}, u32[]{:S(2)}) %collective-permute-start.5) | collective-permute-done | bytes 442400 | tf_op jit(solution)/shard_map/ppermute | solution.py:486
  94.1 4.8 %assemble.1.table_ref = bf16[3,768,768]{2,1,0:T(8,128)(2,1)} custom-call(s32[4]{0:T(128)} %and_select_fusion.3.from_ref, bf16[4,4,3,48,384]{4,3,2,1,0:T(8,128)(2,1)} %copy-done.10, bf16[4,3,48,384]{3,2,1,0:T(8,128)(2,1)} %collective-permute-done.4.a_left_ref, bf16[4,3,48,384]{3,2,1,0:T(8,128)(2,1)} %copy-done.19, bf16[4,3,24,384]{3,2,1,0:T(8,128)(2,1)} %copy-done.21, ...), custom_call_target="tpu_custom_call" | custom-call | flops 1000000 | bytes 8000000 | tf_op jit(solution)/shard_map/assemble/pallas_call | solution.py:214
  98.9 2.0 copy-done
  100.9 4.7 %inverse.1 = bf16[2048,256]{1,0:T(8,128)(2,1)} custom-call(s32[4]{0:T(128)S(1)} %and_select_fusion.4.class_ref, bf16[3,768,768]{2,1,0:T(8,128)(2,1)S(1)} %copy-done, bf16[16,2,3,40,128]{4,3,2,1,0:T(8,128)(2,1)S(1)} %bitcast.36, bf16[2,256,128]{2,1,0:T(8,128)(2,1)S(1)} %copy-done.7), custom_call_target="tpu_custom_call" | custom-call | tf_op jit(solution)/shard_map/inverse/pallas_call | solution.py:280
  105.6 12.6 %all-to-all-start.2 = ((bf16[256,8,256]{2,1,0:T(8,128)(2,1)}), bf16[256,8,256]{2,1,0:T(8,128)(2,1)S(1)}, u32[]{:S(2)}, u32[]{:S(2)}) async-start(bf16[256,8,256]{2,1,0:T(8,128)(2,1)} %bitcast.12), calls=%async_computation.2 | async-start | bytes 2097152 | tf_op jit(solution)/shard_map/all_to_all | solution.py:548
  120.5 3.1 %negate_convert_fusion = (bf16[45,32,768]{2,1,0:T(8,128)(2,1)S(1)}, bf16[45,32,768]{2,1,0:T(8,128)(2,1)}) fusion(f32[32,768]{1,0:T(8,128)S(1)} %get-tuple-element.60, f32[45,768]{1,0:T(8,128)S(1)} %get-tuple-element.58, f32[32,768]{1,0:T(8,128)S(1)} %get-tuple-element.59, f32[45,768]{1,0:T(8,128)S(1)} %get-tuple-element.57), kind=kLoop, calls=%fused_computation | loop fusion | flops 9953280 | bytes 4896768 | tf_op jit(solution)/shard_map/convert_element_type | solution.py:48
  123.6 26.4 %all-to-all-done.2 = bf16[256,8,256]{2,1,0:T(8,128)(2,1)S(1)} async-done(((bf16[256,8,256]{2,1,0:T(8,128)(2,1)}), bf16[256,8,256]{2,1,0:T(8,128)(2,1)S(1)}, u32[]{:S(2)}, u32[]{:S(2)}) %all-to-all-start.2) | async-done | bytes 1048608 | tf_op jit(solution)/shard_map/all_to_all | solution.py:548
  150.0 1.6 copy-done.3
  152.7 10.4 %columns.1 = bf16[2048,256]{1,0:T(8,128)(2,1)S(1)} custom-call(f32[3]{0:T(128)S(1)} %pad_dynamic-slice_fusion.weight_ref, bf16[2048,256]{1,0:T(8,128)(2,1)S(1)} %bitcast.33, bf16[1440,768]{1,0:T(8,128)(2,1)S(1)} %bitcast.32, bf16[1440,768]{1,0:T(8,128)(2,1)S(1)} %bitcast.31, bf16[128,256]{1,0:T(8,128)(2,1)S(1)} %pad.13.w_in_ref, f32[1,256]{1,0:T(1,128)S(1)} %bitcast.38, ...), custom_call_target="tpu_custom_call" | custom-call | tf_op jit(solution)/shard_map/columns/pallas_call | solution.py:347
  163.1 38.1 %all_to_all.25 = bf16[256,8,256]{2,1,0:T(8,128)(2,1)S(1)} all-to-all(bf16[256,8,256]{2,1,0:T(8,128)(2,1)S(1)} %bitcast.34), channel_id=1, replica_groups=mesh['ord'=8,'lat'=16,'lev'=2] {'lat','ord','lev'}, dimensions={0} | all-to-all | bytes 2097152 | tf_op jit(solution)/shard_map/all_to_all | solution.py:563
  201.2 3.8 %forward.1 = bf16[16,2,3,40,128]{4,3,2,1,0:T(8,128)(2,1)S(1)} custom-call(s32[4]{0:T(128)S(1)} %and_select_fusion.4.class_ref, bf16[2048,256]{1,0:T(8,128)(2,1)S(1)} %bitcast.35, bf16[3,768,768]{2,1,0:T(8,128)(2,1)S(1)} %copy-done.1, bf16[2,256,128]{2,1,0:T(8,128)(2,1)S(1)} %copy-done.7), custom_call_target="tpu_custom_call" | custom-call | tf_op jit(solution)/shard_map/forward/pallas_call | solution.py:410
  206.0 5.7 %all-to-all-start.4 = ((bf16[32,3,40,128]{3,2,1,0:T(8,128)(2,1)}), bf16[32,3,40,128]{3,2,1,0:T(8,128)(2,1)}, u32[]{:S(2)}, u32[]{:S(2)}) async-start(bf16[32,3,40,128]{3,2,1,0:T(8,128)(2,1)} %bitcast.37), calls=%async_computation.4 | async-start | bytes 1966080 | tf_op jit(solution)/shard_map/all_to_all | solution.py:569
  211.7 26.0 %all-to-all-done.4 = bf16[32,3,40,128]{3,2,1,0:T(8,128)(2,1)} async-done(((bf16[32,3,40,128]{3,2,1,0:T(8,128)(2,1)}), bf16[32,3,40,128]{3,2,1,0:T(8,128)(2,1)}, u32[]{:S(2)}, u32[]{:S(2)}) %all-to-all-start.4) | async-done | bytes 983072 | tf_op jit(solution)/shard_map/all_to_all | solution.py:569
  237.7 3.6 %update.1 = f32[45,112,90]{2,1,0:T(8,128)} custom-call(s32[2]{0:T(128)S(1)} %copy-done.9, f32[45]{0:T(128)S(1)} %add_divide_fusion.damping_ref, f32[45,112,90]{2,1,0:T(8,128)S(1)} %bitcast.30, bf16[4,24,40,128]{3,2,1,0:T(8,128)(2,1)} %bitcast.20.forcing_ref, bf16[8,224,128]{2,1,0:T(8,128)(2,1)S(1)} %copy-done.8), custom_call_target="tpu_custom_call" | custom-call | tf_op jit(solution)/shard_map/update/pallas_call | solution.py:469
  (89 shorter events, 14.0 us)
Async XLA Ops:
  6.1 34.2 %all-to-all-start = ((bf16[4,4,3,48,384]{4,3,2,1,0:T(8,128)(2,1)}), bf16[4,4,3,48,384]{4,3,2,1,0:T(8,128)(2,1)S(1)}, u32[]{:S(2)}, u32[]{:S(2)}) async-start(bf16[4,4,3,48,384]{4,3,2,1,0:T(8,128)(2,1)} %get-tuple-element.20), calls=%async_computation | async-start | bytes 3538944 | tf_op jit(solution)/shard_map/all_to_all | solution.py:495
  12.0 16.5 %collective-permute-start.2 = (bf16[4,3,24,384]{3,2,1,0:T(8,128)(2,1)S(1)}, bf16[4,3,24,384]{3,2,1,0:T(8,128)(2,1)}, u32[]{:S(2)}, u32[]{:S(2)}) collective-permute-start(bf16[4,3,24,384]{3,2,1,0:T(8,128)(2,1)S(1)} %get-tuple-element.24), channel_id=1, source_target_pairs={{0,4},{2,6},{4,1},{6,3},{1,5},{3,7},{5,0},{7,2},{8,12},{10,14},{12... | collective-permute-start | bytes 663560 | tf_op jit(solution)/shard_map/ppermute | solution.py:486
  14.2 15.2 %collective-permute-start.3 = (bf16[4,3,24,384]{3,2,1,0:T(8,128)(2,1)S(1)}, bf16[4,3,24,384]{3,2,1,0:T(8,128)(2,1)}, u32[]{:S(2)}, u32[]{:S(2)}) collective-permute-start(bf16[4,3,24,384]{3,2,1,0:T(8,128)(2,1)S(1)} %get-tuple-element.25), channel_id=1, source_target_pairs={{0,5},{2,7},{4,0},{6,2},{1,4},{3,6},{5,1},{7,3},{8,13},{10,15},{12... | collective-permute-start | bytes 663560 | tf_op jit(solution)/shard_map/ppermute | solution.py:486
  17.3 18.7 %collective-permute-start = (bf16[4,3,48,384]{3,2,1,0:T(8,128)(2,1)S(1)}, bf16[4,3,48,384]{3,2,1,0:T(8,128)(2,1)}, u32[]{:S(2)}, u32[]{:S(2)}) collective-permute-start(bf16[4,3,48,384]{3,2,1,0:T(8,128)(2,1)S(1)} %get-tuple-element.22), channel_id=1, source_target_pairs={{0,2},{2,4},{4,6},{6,1},{1,3},{3,5},{5,7},{7,0},{8,10},{10,12},{12... | collective-permute-start | bytes 1327112 | tf_op jit(solution)/shard_map/ppermute | solution.py:486
  18.3 18.9 %collective-permute-start.1 = (bf16[4,3,48,384]{3,2,1,0:T(8,128)(2,1)S(1)}, bf16[4,3,48,384]{3,2,1,0:T(8,128)(2,1)}, u32[]{:S(2)}, u32[]{:S(2)}) collective-permute-start(bf16[4,3,48,384]{3,2,1,0:T(8,128)(2,1)S(1)} %get-tuple-element.23), channel_id=1, source_target_pairs={{0,7},{2,0},{4,2},{6,4},{1,6},{3,1},{5,3},{7,5},{8,15},{10,8},{12,... | collective-permute-start | bytes 1327112 | tf_op jit(solution)/shard_map/ppermute | solution.py:486
  27.2 11.1 %copy-start.14 = (bf16[1,3,48,384]{3,2,1,0:T(8,128)(2,1)S(1)}, bf16[1,3,48,384]{3,2,1,0:T(8,128)(2,1)}, u32[]{:S(2)}) copy-start(bf16[1,3,48,384]{3,2,1,0:T(8,128)(2,1)} %get-tuple-element.41) | copy-start | bytes 331780
  27.2 11.1 %copy-start.15 = (bf16[1,3,48,384]{3,2,1,0:T(8,128)(2,1)S(1)}, bf16[1,3,48,384]{3,2,1,0:T(8,128)(2,1)}, u32[]{:S(2)}) copy-start(bf16[1,3,48,384]{3,2,1,0:T(8,128)(2,1)} %get-tuple-element.42) | copy-start | bytes 331780
  27.2 12.0 %copy-start.12 = (bf16[1,3,48,384]{3,2,1,0:T(8,128)(2,1)S(1)}, bf16[1,3,48,384]{3,2,1,0:T(8,128)(2,1)}, u32[]{:S(2)}) copy-start(bf16[1,3,48,384]{3,2,1,0:T(8,128)(2,1)} %get-tuple-element.43) | copy-start | bytes 331780
  27.2 12.0 %copy-start.13 = (bf16[1,3,48,384]{3,2,1,0:T(8,128)(2,1)S(1)}, bf16[1,3,48,384]{3,2,1,0:T(8,128)(2,1)}, u32[]{:S(2)}) copy-start(bf16[1,3,48,384]{3,2,1,0:T(8,128)(2,1)} %get-tuple-element.44) | copy-start | bytes 331780
  40.4 44.2 %copy-start.26 = (s32[4]{0:T(128)S(1)}, s32[4]{0:T(128)}, u32[]{:S(2)}) copy-start(s32[4]{0:T(128)} %constant.233.clone) | copy-start | bytes 52
  40.4 44.2 %copy-start.10 = (bf16[4,4,3,48,384]{4,3,2,1,0:T(8,128)(2,1)}, bf16[4,4,3,48,384]{4,3,2,1,0:T(8,128)(2,1)S(1)}, u32[]{:S(2)}) copy-start(bf16[4,4,3,48,384]{4,3,2,1,0:T(8,128)(2,1)S(1)} %all-to-all-done.a_own_ref) | copy-start | bytes 5308420
  40.4 58.5 %all-to-all-start.1 = ((bf16[32,3,40,128]{3,2,1,0:T(8,128)(2,1)}), bf16[32,3,40,128]{3,2,1,0:T(8,128)(2,1)S(1)}, u32[]{:S(2)}, u32[]{:S(2)}) async-start(bf16[32,3,40,128]{3,2,1,0:T(8,128)(2,1)} %bitcast.39), calls=%async_computation.1 | async-start | bytes 1966080 | tf_op jit(solution)/shard_map/all_to_all | solution.py:540
  49.7 32.2 %collective-permute-start.7 = (bf16[4,3,24,384]{3,2,1,0:T(8,128)(2,1)S(1)}, bf16[4,3,24,384]{3,2,1,0:T(8,128)(2,1)S(1)}, u32[]{:S(2)}, u32[]{:S(2)}) collective-permute-start(bf16[4,3,24,384]{3,2,1,0:T(8,128)(2,1)S(1)} %get-tuple-element.35), channel_id=1, source_target_pairs={{0,5},{2,7},{4,0},{6,2},{1,4},{3,6},{5,1},{7,3},{8,13},{10,15},{12... | collective-permute-start | bytes 663560 | tf_op jit(solution)/shard_map/ppermute | solution.py:486
  53.3 28.6 %collective-permute-start.6 = (bf16[4,3,24,384]{3,2,1,0:T(8,128)(2,1)S(1)}, bf16[4,3,24,384]{3,2,1,0:T(8,128)(2,1)S(1)}, u32[]{:S(2)}, u32[]{:S(2)}) collective-permute-start(bf16[4,3,24,384]{3,2,1,0:T(8,128)(2,1)S(1)} %get-tuple-element.36), channel_id=1, source_target_pairs={{0,4},{2,6},{4,1},{6,3},{1,5},{3,7},{5,0},{7,2},{8,12},{10,14},{12... | collective-permute-start | bytes 663560 | tf_op jit(solution)/shard_map/ppermute | solution.py:486
  53.3 31.3 %collective-permute-start.8 = (bf16[4,3,48,384]{3,2,1,0:T(8,128)(2,1)}, bf16[4,3,48,384]{3,2,1,0:T(8,128)(2,1)S(1)}, u32[]{:S(2)}, u32[]{:S(2)}) collective-permute-start(bf16[4,3,48,384]{3,2,1,0:T(8,128)(2,1)} %get-tuple-element.28), channel_id=1, source_target_pairs={{0,8},{2,10},{4,12},{6,14},{1,9},{3,11},{5,13},{7,15},{8,16},{10,1... | collective-permute-start | bytes 1327112 | tf_op jit(solution)/shard_map/ppermute | solution.py:486
  54.8 29.8 %collective-permute-start.9 = (bf16[4,3,48,384]{3,2,1,0:T(8,128)(2,1)}, bf16[4,3,48,384]{3,2,1,0:T(8,128)(2,1)S(1)}, u32[]{:S(2)}, u32[]{:S(2)}) collective-permute-start(bf16[4,3,48,384]{3,2,1,0:T(8,128)(2,1)} %get-tuple-element.29), channel_id=1, source_target_pairs={{0,16},{2,18},{4,20},{6,22},{1,17},{3,19},{5,21},{7,23},{8,24},{10... | collective-permute-start | bytes 1327112 | tf_op jit(solution)/shard_map/ppermute | solution.py:486
  55.9 28.7 %collective-permute-start.10 = (bf16[4,3,48,384]{3,2,1,0:T(8,128)(2,1)S(1)}, bf16[4,3,48,384]{3,2,1,0:T(8,128)(2,1)S(1)}, u32[]{:S(2)}, u32[]{:S(2)}) collective-permute-start(bf16[4,3,48,384]{3,2,1,0:T(8,128)(2,1)S(1)} %get-tuple-element.30), channel_id=1, source_target_pairs={{0,24},{2,26},{4,28},{6,30},{1,25},{3,27},{5,29},{7,31},{8,0},{10,... | collective-permute-start | bytes 1327112 | tf_op jit(solution)/shard_map/ppermute | solution.py:486
  81.9 12.2 %copy-start.20 = (bf16[4,3,24,384]{3,2,1,0:T(8,128)(2,1)}, bf16[4,3,24,384]{3,2,1,0:T(8,128)(2,1)S(1)}, u32[]{:S(2)}) copy-start(bf16[4,3,24,384]{3,2,1,0:T(8,128)(2,1)S(1)} %collective-permute-done.7.a_high_ref) | copy-start | bytes 663556
  81.9 10.6 %collective-permute-start.5 = (bf16[4,3,48,384]{3,2,1,0:T(8,128)(2,1)S(1)}, bf16[4,3,48,384]{3,2,1,0:T(8,128)(2,1)S(1)}, u32[]{:S(2)}, u32[]{:S(2)}) collective-permute-start(bf16[4,3,48,384]{3,2,1,0:T(8,128)(2,1)S(1)} %get-tuple-element.37), channel_id=1, source_target_pairs={{0,7},{2,0},{4,2},{6,4},{1,6},{3,1},{5,3},{7,5},{8,15},{10,8},{12,... | collective-permute-start | bytes 1327112 | tf_op jit(solution)/shard_map/ppermute | solution.py:486
  81.9 12.1 %collective-permute-start.4 = (bf16[4,3,48,384]{3,2,1,0:T(8,128)(2,1)S(1)}, bf16[4,3,48,384]{3,2,1,0:T(8,128)(2,1)}, u32[]{:S(2)}, u32[]{:S(2)}) collective-permute-start(bf16[4,3,48,384]{3,2,1,0:T(8,128)(2,1)S(1)} %get-tuple-element.38), channel_id=1, source_target_pairs={{0,2},{2,4},{4,6},{6,1},{1,3},{3,5},{5,7},{7,0},{8,10},{10,12},{12... | collective-permute-start | bytes 1327112 | tf_op jit(solution)/shard_map/ppermute | solution.py:486
  84.6 14.3 %copy-start.7 = (bf16[2,256,128]{2,1,0:T(8,128)(2,1)S(1)}, bf16[2,256,128]{2,1,0:T(8,128)(2,1)}, u32[]{:S(2)}) copy-start(bf16[2,256,128]{2,1,0:T(8,128)(2,1)} %constant.231.clone.maps_ref) | copy-start | bytes 393220
  100.9 17.4 %copy-start.23 = (bf16[256,112]{0,1:T(8,128)(2,1)S(1)}, bf16[256,112]{0,1:T(8,128)(2,1)}, u32[]{:S(2)}) copy-start(bf16[256,112]{0,1:T(8,128)(2,1)} %param.17) | copy-start | bytes 172036
  100.9 17.5 %copy-start.22 = (bf16[112,256]{1,0:T(8,128)(2,1)S(1)}, bf16[112,256]{1,0:T(8,128)(2,1)}, u32[]{:S(2)}) copy-start(bf16[112,256]{1,0:T(8,128)(2,1)} %param.14) | copy-start | bytes 172036
  105.6 12.9 %copy-start.25 = (f32[45]{0:T(128)S(1)}, f32[45]{0:T(128)}, u32[]{:S(2)}) copy-start(f32[45]{0:T(128)} %param.13) | copy-start | bytes 544
  105.6 13.0 %copy-start.24 = (f32[256]{0:T(256)S(1)}, f32[256]{0:T(256)}, u32[]{:S(2)}) copy-start(f32[256]{0:T(256)} %param.15) | copy-start | bytes 3076
  105.6 13.0 %copy-start.11 = (bf16[4,256,256]{2,1,0:T(8,128)(2,1)S(1)}, bf16[4,256,256]{2,1,0:T(8,128)(2,1)}, u32[]{:S(2)}) copy-start(bf16[4,256,256]{2,1,0:T(8,128)(2,1)} %param.16) | copy-start | bytes 1572868
  105.6 44.5 %all-to-all-start.2 = ((bf16[256,8,256]{2,1,0:T(8,128)(2,1)}), bf16[256,8,256]{2,1,0:T(8,128)(2,1)S(1)}, u32[]{:S(2)}, u32[]{:S(2)}) async-start(bf16[256,8,256]{2,1,0:T(8,128)(2,1)} %bitcast.12), calls=%async_computation.2 | async-start | bytes 2097152 | tf_op jit(solution)/shard_map/all_to_all | solution.py:548
  152.7 48.5 %copy-start.1 = (bf16[3,768,768]{2,1,0:T(8,128)(2,1)S(1)}, bf16[3,768,768]{2,1,0:T(8,128)(2,1)}, u32[]{:S(2)}) copy-start(bf16[3,768,768]{2,1,0:T(8,128)(2,1)} %assemble.1.table_ref) | copy-start | bytes 10616836
  201.2 36.5 %copy-start.2 = (f32[90,45,8,7,2]{0,4,3,2,1:T(2,128)S(1)}, f32[90,45,8,7,2]{0,4,3,2,1:T(2,128)}, u32[]{:S(2)}) copy-start(f32[90,45,8,7,2]{0,4,3,2,1:T(2,128)} %param.11) | copy-start | bytes 5443204
  201.2 36.5 %copy-start.8 = (bf16[8,224,128]{2,1,0:T(8,128)(2,1)S(1)}, bf16[8,224,128]{2,1,0:T(8,128)(2,1)}, u32[]{:S(2)}) copy-start(bf16[8,224,128]{2,1,0:T(8,128)(2,1)} %constant.234.clone.maps_ref) | copy-start | bytes 1376260
  201.2 36.5 %copy-start.9 = (s32[2]{0:T(128)S(1)}, s32[2]{0:T(128)}, u32[]{:S(2)}) copy-start(s32[2]{0:T(128)} %pad_add_fusion.at_ref) | copy-start | bytes 28
  206.0 31.8 %all-to-all-start.4 = ((bf16[32,3,40,128]{3,2,1,0:T(8,128)(2,1)}), bf16[32,3,40,128]{3,2,1,0:T(8,128)(2,1)}, u32[]{:S(2)}, u32[]{:S(2)}) async-start(bf16[32,3,40,128]{3,2,1,0:T(8,128)(2,1)} %bitcast.37), calls=%async_computation.4 | async-start | bytes 1966080 | tf_op jit(solution)/shard_map/all_to_all | solution.py:569
  (10 other events, 43.4 us)

commit v8 on v6

--- a/solution.py
+++ b/solution.py
@@ -298,15 +298,18 @@
 
     unpack_rows(in_ref, scr_ref, put, peers, width)
 
+    half_in, half_bias = 0.5 * w_in_ref[...], 0.5 * bias_ref[...]
+    half_hid = [0.5 * w_hid_ref[layer] for layer in range(w_hid_ref.shape[0])]
+
     def grid_rows(step, carry):
         rows = pl.ds(pl.multiple_of(step * x_rows, x_rows), x_rows)
         raw = dot(cos_ref[rows, :], fourier_ref[0]) + dot(sin_ref[rows, :], fourier_ref[1])
         features = (transform_scale * raw).astype(bf16)
         lanes = [slice(i * LANES, (i + 1) * LANES) for i in range(OWN)]
-        hidden = [half_silu(dot(features[:, at], w_in_ref[...]) + bias_ref[...]) for at in lanes]
+        hidden = [half_silu(dot(features[:, at], half_in) + half_bias) for at in lanes]
         hidden = [h.astype(bf16) for h in hidden]
-        for layer in range(w_hid_ref.shape[0]):
-            update = [half_silu(dot(h, w_hid_ref[layer])) for h in hidden]
+        for weights in half_hid:
+            update = [half_silu(dot(h, weights)) for h in hidden]
             hidden = [(h.astype(f32) + u).astype(bf16) for h, u in zip(hidden, update)]
         for at, h in zip(lanes, hidden):
             tendency_ref[rows, at] = dot(h, w_out_ref[...]).astype(bf16)
@@ -345,7 +348,7 @@
             pltpu.VMEM((2, OWN, OWN, peers, LANES), f32),
             pltpu.VMEM((2, peers * 8, LANES), f32),
         ],
-        compiler_params=pltpu.CompilerParams(vmem_limit_bytes=40 * 2**20),
+        compiler_params=pltpu.CompilerParams(vmem_limit_bytes=26 * 2**20),
         name="columns",
     )(weights, fourier, cosines, sines, w_in, bias, w_hid, w_out)
 
@@ -506,8 +509,10 @@
     b_far = jnp.concatenate([b_low, b_high], axis=2)
     b_all = jnp.stack([b_own, b_left, b_right, b_far], axis=1)
     a_all, b_all = lax.optimization_barrier((a_all, b_all))
-    a_near = [along_z(a_all[:, 1], 1), along_z(a_all[:, 2], -1)]
-    a_far = [along_z(a_all[:, 3, :, : rows // 2], 2), along_z(a_all[:, 3, :, rows // 2 :], -2)]
+    a_cut = [a_all[:, 1], a_all[:, 2], a_all[:, 3, :, : rows // 2], a_all[:, 3, :, rows // 2 :]]
+    a_cut, b_all = lax.optimization_barrier((a_cut, b_all))
+    a_near = [along_z(a_cut[0], 1), along_z(a_cut[1], -1)]
+    a_far = [along_z(a_cut[2], 2), along_z(a_cut[3], -2)]
     b_all = along_x(b_all)
 
     slot = lax.iota(jnp.int32, OWN * peers)
@@ -518,8 +523,8 @@
     valid = (slot_x % 2 == 0) | (slot_w > 0)
     order_ids = slot_ord * order_local + OWN * (first_group(slot_x) + slot_w) + slot // peers
     coefficients = prep(at, state, sent)
-    coefficients, a_near, a_far, b_all = lax.optimization_barrier(
-        (coefficients, a_near, a_far, b_all)
+    coefficients, a_near, a_far, b_all, order_ids, valid = lax.optimization_barrier(
+        (coefficients, a_near, a_far, b_all, order_ids, valid)
     )
 
     coefficients = coefficients.reshape(lat_size * lev_size, OWN, sent, LANES)
@@ -527,22 +532,30 @@
     coefficients = coefficients.reshape(lat_size, lev_size, OWN, sent, LANES)
     classes = (z_at + jnp.array([0, -1, 1, 2], jnp.int32)) % Z_LOW
     table = assemble(a_all, a_near, a_far, b_all)
-    fourier = inverse(classes, table, coefficients, maps, peers, lat_local, lat_slots, width)
-    fourier, order_ids, valid = lax.optimization_barrier((fourier, order_ids, valid))
-    cosines, sines = lookup_of(order_ids, valid)
-
-    fourier = lax.all_to_all(fourier.reshape(peers, 8, -1), everyone, 0, 0, tiled=True)
+
     first = (ord_at * lev_size + lev_at) * OWN
     weights = lax.dynamic_slice_in_dim(jnp.pad(quad_weight, (0, lat_slots - lat_local)), first, OWN)
+    w_in = jnp.pad(weight_in, ((0, LANES - width), (0, 0)))
+    w_out = jnp.pad(weight_out, ((0, 0), (0, LANES - width)))
+    degree_ids = lat_at * degree_local + lax.iota(jnp.int32, degree_local)
+    degree_ratio = (degree_ids * (degree_ids + 1)).astype(f32) / ((L - 1) * L)
+    damping = 1.0 / (1.0 + hyper_rate * degree_ratio * degree_ratio)
+    cosines, sines = lookup_of(order_ids, valid)
+    table, coefficients, cosines, sines, weights, w_in, w_out, damping = lax.optimization_barrier(
+        (table, coefficients, cosines, sines, weights, w_in, w_out, damping)
+    )
+    fourier = inverse(classes, table, coefficients, maps, peers, lat_local, lat_slots, width)
+
+    fourier = lax.all_to_all(fourier.reshape(peers, 8, -1), everyone, 0, 0, tiled=True)
     weighted = columns(
         weights,
         fourier.reshape(peers * 8, -1),
         cosines,
         sines,
-        jnp.pad(0.5 * weight_in, ((0, LANES - width), (0, 0))),
-        0.5 * bias_in[None, :],
-        0.5 * weight_hidden,
-        jnp.pad(weight_out, ((0, 0), (0, LANES - width))),
+        w_in,
+        bias_in[None, :],
+        weight_hidden,
+        w_out,
         width,
     )
 
@@ -554,9 +567,6 @@
     forcing = forcing.reshape(lat_size * lev_size, OWN, sent, LANES)
     forcing = lax.all_to_all(forcing, ("lat", "lev"), 0, 0, tiled=True)
     forcing = forcing.reshape(LAT_X, OWN * Z_RING, sent, LANES)
-    degree_ids = lat_at * degree_local + lax.iota(jnp.int32, degree_local)
-    degree_ratio = (degree_ids * (degree_ids + 1)).astype(f32) / ((L - 1) * L)
-    damping = 1.0 / (1.0 + hyper_rate * degree_ratio * degree_ratio)
     updated = update(at, damping, state, forcing)
     updated = updated.reshape(degree_local, *spectral_state.shape[2:], order_local)
     return updated.transpose(4, 0, 1, 2, 3)

time: 236 us -> 232 us (0.983)
  blocking collectives: 38.1 us -> 109 us
  waiting for transfers between devices: 91.5 us -> 35.5 us
  starting transfers between devices: 51 us -> 33.7 us
    all_to_all x0 -> x2, blocking collectives: none -> 71.3 us  [the longest x1 40.4 us: on_device(): lax.all_to_all(fourier.reshape(peers, 8, -1), everyone, 0, 0, tiled=True)]
    all_to_all x2 -> x0, waiting for transfers between devices: 52.3 us -> none  [the longest x1 26.2 us: on_device(): lax.all_to_all(fourier.reshape(peers, 8, -1), everyone, 0, 0, tiled=True)]
    all_to_all x2 -> x0, starting transfers between devices: 14.6 us -> none  [the longest x1 8.77 us: on_device(): lax.all_to_all(fourier.reshape(peers, 8, -1), everyone, 0, 0, tiled=True)]
    all_to_all x1, waiting for transfers between devices: 16.2 us -> 10.9 us  [on_device(): lax.all_to_all(coefficients, ('lat', 'lev'), 0, 0, tiled=True)]
    unnamed x49 -> x55, local copies, waits for them, and re-layouts: 5.8 us -> 1.95 us
    all_to_all x1, starting transfers between devices: 9.32 us -> 6.48 us  [on_device(): lax.all_to_all(coefficients, ('lat', 'lev'), 0, 0, tiled=True)]
  transfers between devices with their start and end apart: 13 -> 11, of which waited for: 7 -> 5; matrix products, arithmetic and copies ran while one was open for 4% -> 5% of each run, Pallas kernels for 4% -> 4%
where the time goes in v8:
time: 232 us; the launch traced here: 231 us
  blocking collectives  109 us (47%)
  Pallas kernels  36.9 us (16%)
  waiting for transfers between devices  35.5 us (15%)
  starting transfers between devices  33.7 us (15%)
  other arithmetic  9.55 us (4%)
  local copies, waits for them, and re-layouts  6.05 us (3%)
    all_to_all x1, blocking collectives, on_device(): lax.all_to_all(fourier.reshape(peers, 8, -1), everyone, 0, 0, tiled=True)  40.4 us
    all_to_all x1, blocking collectives, on_device(): lax.all_to_all(weighted.reshape(peers, 8, -1), everyone, 0, 0, tiled=True)  38.1 us
    all_to_all x1, blocking collectives, on_device(): forcing = lax.all_to_all(forcing, ('lat', 'lev'), 0, 0, tiled=True)  30.9 us
    ppermute x8, waiting for transfers between devices, along_z(): return lax.ppermute(value, ('lat', 'lev'), pairs)  24.6 us
    ppermute x8, starting transfers between devices, along_z(): return lax.ppermute(value, ('lat', 'lev'), pairs)  16.4 us
    all_to_all x1, waiting for transfers between devices, on_device(): lax.all_to_all(coefficients, ('lat', 'lev'), 0, 0, tiled=True)  10.9 us
    all_to_all x2, starting transfers between devices, along_x(): lax.all_to_all(value, 'lat', 0, 0, axis_index_groups=groups, tiled=True)  10.8 us
    pallas_call x1, Pallas kernels, columns(): pl.pallas_call(functools.partial(column_kernel, x_rows=X_ROWS, width=widt...  10.4 us
  transfers between devices with their start and end apart: 11, of which 5 were waited for; matrix products, arithmetic and copies ran while one was open for 5% of the time, Pallas kernels for 4%

profile of v8, /device:TPU:2, one launch (start us, length us, event | category | flops | bytes accessed | tf_op | source)
XLA Modules:
  0.0 231.4 jit_solution(5739530253279652816)
XLA Ops:
  0.0 1.2 fusion.43.own_ref
  1.2 5.2 %pack_table.1 = (bf16[4,4,3,48,384]{4,3,2,1,0:T(8,128)(2,1)}, bf16[4,3,48,384]{3,2,1,0:T(8,128)(2,1)}, bf16[4,3,48,384]{3,2,1,0:T(8,128)(2,1)}, bf16[4,3,48,384]...) custom-call(s32[5]{0:T(128)} %fusion.43.own_ref, bf16[90,45,720]{2,1,0:T(8,128)(2,1)} %in_ref.1), custom_call_target="tpu_custom_call" | custom-call | tf_op jit(solution)/shard_map/pack_table/pallas_call | solution.py:172
  6.5 6.0 %all-to-all-start = ((bf16[4,4,3,48,384]{4,3,2,1,0:T(8,128)(2,1)}), bf16[4,4,3,48,384]{4,3,2,1,0:T(8,128)(2,1)S(1)}, u32[]{:S(2)}, u32[]{:S(2)}) async-start(bf16[4,4,3,48,384]{4,3,2,1,0:T(8,128)(2,1)} %get-tuple-element.34), calls=%async_computation | async-start | bytes 3538944 | tf_op jit(solution)/shard_map/all_to_all | solution.py:483
  12.4 0.9 collective-permute-start
  13.3 4.0 %collective-permute-start.1 = (bf16[4,3,48,384]{3,2,1,0:T(8,128)(2,1)S(1)}, bf16[4,3,48,384]{3,2,1,0:T(8,128)(2,1)S(1)}, u32[]{:S(2)}, u32[]{:S(2)}) collective-permute-start(bf16[4,3,48,384]{3,2,1,0:T(8,128)(2,1)S(1)} %copy-done.22), channel_id=1, source_target_pairs={{0,7},{2,0},{4,2},{6,4},{1,6},{3,1},{5,3},{7,5},{8,15},{10,8},{12,... | collective-permute-start | bytes 1327112 | tf_op jit(solution)/shard_map/ppermute | solution.py:478
  17.4 4.1 %collective-permute-start.3 = (bf16[4,3,24,384]{3,2,1,0:T(8,128)(2,1)S(1)}, bf16[4,3,24,384]{3,2,1,0:T(8,128)(2,1)S(1)}, u32[]{:S(2)}, u32[]{:S(2)}) collective-permute-start(bf16[4,3,24,384]{3,2,1,0:T(8,128)(2,1)S(1)} %copy-done.24), channel_id=1, source_target_pairs={{0,5},{2,7},{4,0},{6,2},{1,4},{3,6},{5,1},{7,3},{8,13},{10,15},{12... | collective-permute-start | bytes 663560 | tf_op jit(solution)/shard_map/ppermute | solution.py:478
  21.5 12.8 %collective-permute-done.2 = bf16[4,3,24,384]{3,2,1,0:T(8,128)(2,1)S(1)} collective-permute-done((bf16[4,3,24,384]{3,2,1,0:T(8,128)(2,1)S(1)}, bf16[4,3,24,384]{3,2,1,0:T(8,128)(2,1)S(1)}, u32[]{:S(2)}, u32[]{:S(2)}) %collective-permute-start.2) | collective-permute-done | bytes 221216 | tf_op jit(solution)/shard_map/ppermute | solution.py:478
  34.3 1.4 collective-permute-done.3
  35.8 1.5 pad_maximum_fusion
  37.3 0.9 slice_bitcast_fusion.2
  38.2 1.0 slice_bitcast_fusion
  39.2 4.8 %all-to-all-start.1 = ((bf16[4,4,3,48,384]{4,3,2,1,0:T(8,128)(2,1)}), bf16[4,4,3,48,384]{4,3,2,1,0:T(8,128)(2,1)S(1)}, u32[]{:S(2)}, u32[]{:S(2)}) async-start(bf16[4,4,3,48,384]{4,3,2,1,0:T(8,128)(2,1)} %pad_maximum_fusion), calls=%async_computation.1 | async-start | bytes 3538944 | tf_op jit(solution)/shard_map/all_to_all | solution.py:483
  44.0 2.1 collective-permute-start.4
  46.2 1.1 collective-permute-start.5
  47.9 5.3 %prep.1 = bf16[4,24,40,128]{3,2,1,0:T(8,128)(2,1)} custom-call(s32[2]{0:T(128)} %pad_add_fusion.at_ref, f32[45,112,90]{2,1,0:T(8,128)} %bitcast.32, f32[45,112,90]{2,1,0:T(8,128)} %bitcast.33), custom_call_target="tpu_custom_call" | custom-call | flops 1000000 | bytes 4000000 | tf_op jit(solution)/shard_map/prep/pallas_call | solution.py:131
  53.2 4.0 %collective-permute-start.6 = (bf16[4,3,24,384]{3,2,1,0:T(8,128)(2,1)S(1)}, bf16[4,3,24,384]{3,2,1,0:T(8,128)(2,1)S(1)}, u32[]{:S(2)}, u32[]{:S(2)}) collective-permute-start(bf16[4,3,24,384]{3,2,1,0:T(8,128)(2,1)S(1)} %copy-done.18), channel_id=1, source_target_pairs={{0,4},{2,6},{4,1},{6,3},{1,5},{3,7},{5,0},{7,2},{8,12},{10,14},{12... | collective-permute-start | bytes 663560 | tf_op jit(solution)/shard_map/ppermute | solution.py:478
  57.9 6.4 %collective-permute-done.6.a_low_ref = bf16[4,3,24,384]{3,2,1,0:T(8,128)(2,1)S(1)} collective-permute-done((bf16[4,3,24,384]{3,2,1,0:T(8,128)(2,1)S(1)}, bf16[4,3,24,384]{3,2,1,0:T(8,128)(2,1)S(1)}, u32[]{:S(2)}, u32[]{:S(2)}) %collective-permute-start.6) | collective-permute-done | bytes 221216 | tf_op jit(solution)/shard_map/ppermute | solution.py:478
  64.3 4.0 %collective-permute-done.7.a_high_ref = bf16[4,3,24,384]{3,2,1,0:T(8,128)(2,1)S(1)} collective-permute-done((bf16[4,3,24,384]{3,2,1,0:T(8,128)(2,1)S(1)}, bf16[4,3,24,384]{3,2,1,0:T(8,128)(2,1)S(1)}, u32[]{:S(2)}, u32[]{:S(2)}) %collective-permute-start.7) | collective-permute-done | bytes 221216 | tf_op jit(solution)/shard_map/ppermute | solution.py:478
  68.3 6.5 %all-to-all-start.2 = ((bf16[32,3,40,128]{3,2,1,0:T(8,128)(2,1)}), bf16[32,3,40,128]{3,2,1,0:T(8,128)(2,1)}, u32[]{:S(2)}, u32[]{:S(2)}) async-start(bf16[32,3,40,128]{3,2,1,0:T(8,128)(2,1)} %bitcast.44), calls=%async_computation.2 | async-start | bytes 1966080 | tf_op jit(solution)/shard_map/all_to_all | solution.py:531
  74.8 0.9 copy.19
  75.7 1.4 pad.13.w_in_ref
  78.6 4.8 %assemble.1.table_ref = bf16[3,768,768]{2,1,0:T(8,128)(2,1)} custom-call(bf16[4,4,3,48,384]{4,3,2,1,0:T(8,128)(2,1)} %copy-done.12, bf16[4,3,48,384]{3,2,1,0:T(8,128)(2,1)} %copy-done.15, bf16[4,3,48,384]{3,2,1,0:T(8,128)(2,1)} %copy-done.16, bf16[4,3,24,384]{3,2,1,0:T(8,128)(2,1)} %copy-done.19, bf16[4,3,24,384]{3,2,1,0:T(8,128)(2,1)} %copy-done.20, ...), custom_call_target="tpu_custom_call" | custom-call | flops 1000000 | bytes 8000000 | tf_op jit(solution)/shard_map/assemble/pallas_call | solution.py:205
  84.6 3.8 %negate_convert_fusion = (bf16[45,32,768]{2,1,0:T(8,128)(2,1)}, bf16[45,32,768]{2,1,0:T(8,128)(2,1)}) fusion(f32[32,768]{1,0:T(8,128)S(1)} %get-tuple-element.72, f32[45,768]{1,0:T(8,128)S(1)} %get-tuple-element.70, f32[32,768]{1,0:T(8,128)S(1)} %get-tuple-element.71, f32[45,768]{1,0:T(8,128)S(1)} %get-tuple-element.69), kind=kLoop, calls=%fused_computation | loop fusion | flops 9953280 | bytes 4896768 | tf_op jit(solution)/shard_map/convert_element_type | solution.py:48
  88.4 10.9 %all-to-all-done.2 = bf16[32,3,40,128]{3,2,1,0:T(8,128)(2,1)} async-done(((bf16[32,3,40,128]{3,2,1,0:T(8,128)(2,1)}), bf16[32,3,40,128]{3,2,1,0:T(8,128)(2,1)}, u32[]{:S(2)}, u32[]{:S(2)}) %all-to-all-start.2) | async-done | bytes 983072 | tf_op jit(solution)/shard_map/all_to_all | solution.py:531
  99.3 0.9 copy-done.4
  100.2 4.5 %inverse.1 = bf16[2048,256]{1,0:T(8,128)(2,1)S(1)} custom-call(s32[4]{0:T(128)S(1)} %and_select_fusion.class_ref, bf16[3,768,768]{2,1,0:T(8,128)(2,1)S(1)} %copy-done, bf16[16,2,3,40,128]{4,3,2,1,0:T(8,128)(2,1)} %bitcast.13.coef_ref, bf16[2,256,128]{2,1,0:T(8,128)(2,1)S(1)} %copy-done.4), custom_call_target="tpu_custom_call" | custom-call | tf_op jit(solution)/shard_map/inverse/pallas_call | solution.py:270
  104.8 40.4 %all_to_all.30 = bf16[256,8,256]{2,1,0:T(8,128)(2,1)S(1)} all-to-all(bf16[256,8,256]{2,1,0:T(8,128)(2,1)S(1)} %bitcast.40), channel_id=1, replica_groups=mesh['ord'=8,'lat'=16,'lev'=2] {'lat','ord','lev'}, dimensions={0} | all-to-all | bytes 2097152 | tf_op jit(solution)/shard_map/all_to_all | solution.py:549
  145.3 10.4 %columns.1 = bf16[2048,256]{1,0:T(8,128)(2,1)S(1)} custom-call(f32[3]{0:T(128)S(1)} %pad_dynamic-slice_fusion.weight_ref, bf16[2048,256]{1,0:T(8,128)(2,1)S(1)} %bitcast.37, bf16[1440,768]{1,0:T(8,128)(2,1)S(1)} %bitcast.36, bf16[1440,768]{1,0:T(8,128)(2,1)S(1)} %bitcast.35, bf16[128,256]{1,0:T(8,128)(2,1)S(1)} %copy-done.9, f32[1,256]{1,0:T(1,128)S(1)} %bitcast.43, ...), custom_call_target="tpu_custom_call" | custom-call | tf_op jit(solution)/shard_map/columns/pallas_call | solution.py:340
  155.6 38.1 %all_to_all.31 = bf16[256,8,256]{2,1,0:T(8,128)(2,1)S(1)} all-to-all(bf16[256,8,256]{2,1,0:T(8,128)(2,1)S(1)} %bitcast.38), channel_id=1, replica_groups=mesh['ord'=8,'lat'=16,'lev'=2] {'lat','ord','lev'}, dimensions={0} | all-to-all | bytes 2097152 | tf_op jit(solution)/shard_map/all_to_all | solution.py:562
  193.8 3.8 %forward.1 = bf16[16,2,3,40,128]{4,3,2,1,0:T(8,128)(2,1)S(1)} custom-call(s32[4]{0:T(128)S(1)} %and_select_fusion.class_ref, bf16[2048,256]{1,0:T(8,128)(2,1)S(1)} %bitcast.39, bf16[3,768,768]{2,1,0:T(8,128)(2,1)S(1)} %copy-done, bf16[2,256,128]{2,1,0:T(8,128)(2,1)S(1)} %copy-done.5), custom_call_target="tpu_custom_call" | custom-call | tf_op jit(solution)/shard_map/forward/pallas_call | solution.py:403
  197.6 30.9 %all_to_all.32 = bf16[32,3,40,128]{3,2,1,0:T(8,128)(2,1)S(1)} all-to-all(bf16[32,3,40,128]{3,2,1,0:T(8,128)(2,1)S(1)} %bitcast.41), channel_id=1, replica_groups=mesh['ord'=8,'lat'=16,'lev'=2] {'lat','lev'}, dimensions={0} | all-to-all | bytes 1966080 | tf_op jit(solution)/shard_map/all_to_all | solution.py:568
  228.5 2.9 %update.1 = f32[45,112,90]{2,1,0:T(8,128)} custom-call(s32[2]{0:T(128)S(1)} %copy-done.10, f32[45]{0:T(128)S(1)} %add_divide_fusion.damping_ref, f32[45,112,90]{2,1,0:T(8,128)S(1)} %bitcast.34, bf16[4,24,40,128]{3,2,1,0:T(8,128)(2,1)S(1)} %bitcast.42, bf16[8,224,128]{2,1,0:T(8,128)(2,1)S(1)} %copy-done.7), custom_call_target="tpu_custom_call" | custom-call | tf_op jit(solution)/shard_map/update/pallas_call | solution.py:462
  (72 shorter events, 4.0 us)
Async XLA Ops:
  6.4 10.9 %copy-start.25 = (bf16[4,3,24,384]{3,2,1,0:T(8,128)(2,1)S(1)}, bf16[4,3,24,384]{3,2,1,0:T(8,128)(2,1)}, u32[]{:S(2)}) copy-start(bf16[4,3,24,384]{3,2,1,0:T(8,128)(2,1)} %get-tuple-element.38) | copy-start | bytes 663556
  6.4 10.9 %copy-start.24 = (bf16[4,3,24,384]{3,2,1,0:T(8,128)(2,1)S(1)}, bf16[4,3,24,384]{3,2,1,0:T(8,128)(2,1)}, u32[]{:S(2)}) copy-start(bf16[4,3,24,384]{3,2,1,0:T(8,128)(2,1)} %get-tuple-element.39) | copy-start | bytes 663556
  6.4 29.3 %copy-start.14 = (bf16[4,3,48,384]{3,2,1,0:T(8,128)(2,1)S(1)}, bf16[4,3,48,384]{3,2,1,0:T(8,128)(2,1)}, u32[]{:S(2)}) copy-start(bf16[4,3,48,384]{3,2,1,0:T(8,128)(2,1)} %get-tuple-element.35) | copy-start | bytes 1327108
  6.5 30.8 %all-to-all-start = ((bf16[4,4,3,48,384]{4,3,2,1,0:T(8,128)(2,1)}), bf16[4,4,3,48,384]{4,3,2,1,0:T(8,128)(2,1)S(1)}, u32[]{:S(2)}, u32[]{:S(2)}) async-start(bf16[4,4,3,48,384]{4,3,2,1,0:T(8,128)(2,1)} %get-tuple-element.34), calls=%async_computation | async-start | bytes 3538944 | tf_op jit(solution)/shard_map/all_to_all | solution.py:483
  12.4 23.3 %collective-permute-start = (bf16[4,3,48,384]{3,2,1,0:T(8,128)(2,1)S(1)}, bf16[4,3,48,384]{3,2,1,0:T(8,128)(2,1)S(1)}, u32[]{:S(2)}, u32[]{:S(2)}) collective-permute-start(bf16[4,3,48,384]{3,2,1,0:T(8,128)(2,1)S(1)} %copy-done.23), channel_id=1, source_target_pairs={{0,2},{2,4},{4,6},{6,1},{1,3},{3,5},{5,7},{7,0},{8,10},{10,12},{12... | collective-permute-start | bytes 1327112 | tf_op jit(solution)/shard_map/ppermute | solution.py:478
  13.3 22.4 %collective-permute-start.1 = (bf16[4,3,48,384]{3,2,1,0:T(8,128)(2,1)S(1)}, bf16[4,3,48,384]{3,2,1,0:T(8,128)(2,1)S(1)}, u32[]{:S(2)}, u32[]{:S(2)}) collective-permute-start(bf16[4,3,48,384]{3,2,1,0:T(8,128)(2,1)S(1)} %copy-done.22), channel_id=1, source_target_pairs={{0,7},{2,0},{4,2},{6,4},{1,6},{3,1},{5,3},{7,5},{8,15},{10,8},{12,... | collective-permute-start | bytes 1327112 | tf_op jit(solution)/shard_map/ppermute | solution.py:478
  17.4 16.9 %collective-permute-start.2 = (bf16[4,3,24,384]{3,2,1,0:T(8,128)(2,1)S(1)}, bf16[4,3,24,384]{3,2,1,0:T(8,128)(2,1)S(1)}, u32[]{:S(2)}, u32[]{:S(2)}) collective-permute-start(bf16[4,3,24,384]{3,2,1,0:T(8,128)(2,1)S(1)} %copy-done.25), channel_id=1, source_target_pairs={{0,4},{2,6},{4,1},{6,3},{1,5},{3,7},{5,0},{7,2},{8,12},{10,14},{12... | collective-permute-start | bytes 663560 | tf_op jit(solution)/shard_map/ppermute | solution.py:478
  17.4 18.3 %collective-permute-start.3 = (bf16[4,3,24,384]{3,2,1,0:T(8,128)(2,1)S(1)}, bf16[4,3,24,384]{3,2,1,0:T(8,128)(2,1)S(1)}, u32[]{:S(2)}, u32[]{:S(2)}) collective-permute-start(bf16[4,3,24,384]{3,2,1,0:T(8,128)(2,1)S(1)} %copy-done.24), channel_id=1, source_target_pairs={{0,5},{2,7},{4,0},{6,2},{1,4},{3,6},{5,1},{7,3},{8,13},{10,15},{12... | collective-permute-start | bytes 663560 | tf_op jit(solution)/shard_map/ppermute | solution.py:478
  39.2 29.0 %all-to-all-start.1 = ((bf16[4,4,3,48,384]{4,3,2,1,0:T(8,128)(2,1)}), bf16[4,4,3,48,384]{4,3,2,1,0:T(8,128)(2,1)S(1)}, u32[]{:S(2)}, u32[]{:S(2)}) async-start(bf16[4,4,3,48,384]{4,3,2,1,0:T(8,128)(2,1)} %pad_maximum_fusion), calls=%async_computation.1 | async-start | bytes 3538944 | tf_op jit(solution)/shard_map/all_to_all | solution.py:483
  44.0 24.2 %collective-permute-start.4 = (bf16[4,3,48,384]{3,2,1,0:T(8,128)(2,1)}, bf16[4,3,48,384]{3,2,1,0:T(8,128)(2,1)S(1)}, u32[]{:S(2)}, u32[]{:S(2)}) collective-permute-start(bf16[4,3,48,384]{3,2,1,0:T(8,128)(2,1)} %get-tuple-element.42), channel_id=1, source_target_pairs={{0,2},{2,4},{4,6},{6,1},{1,3},{3,5},{5,7},{7,0},{8,10},{10,12},{12... | collective-permute-start | bytes 1327112 | tf_op jit(solution)/shard_map/ppermute | solution.py:478
  46.2 22.1 %collective-permute-start.5 = (bf16[4,3,48,384]{3,2,1,0:T(8,128)(2,1)}, bf16[4,3,48,384]{3,2,1,0:T(8,128)(2,1)S(1)}, u32[]{:S(2)}, u32[]{:S(2)}) collective-permute-start(bf16[4,3,48,384]{3,2,1,0:T(8,128)(2,1)} %get-tuple-element.43), channel_id=1, source_target_pairs={{0,7},{2,0},{4,2},{6,4},{1,6},{3,1},{5,3},{7,5},{8,15},{10,8},{12,... | collective-permute-start | bytes 1327112 | tf_op jit(solution)/shard_map/ppermute | solution.py:478
  47.9 9.3 %copy-start.17 = (bf16[4,3,24,384]{3,2,1,0:T(8,128)(2,1)S(1)}, bf16[4,3,24,384]{3,2,1,0:T(8,128)(2,1)}, u32[]{:S(2)}) copy-start(bf16[4,3,24,384]{3,2,1,0:T(8,128)(2,1)} %get-tuple-element.45) | copy-start | bytes 663556
  53.2 24.7 %copy-start.26 = (f32[45]{0:T(128)S(1)}, f32[45]{0:T(128)}, u32[]{:S(2)}) copy-start(f32[45]{0:T(128)} %param.13) | copy-start | bytes 544
  53.2 11.1 %collective-permute-start.6 = (bf16[4,3,24,384]{3,2,1,0:T(8,128)(2,1)S(1)}, bf16[4,3,24,384]{3,2,1,0:T(8,128)(2,1)S(1)}, u32[]{:S(2)}, u32[]{:S(2)}) collective-permute-start(bf16[4,3,24,384]{3,2,1,0:T(8,128)(2,1)S(1)} %copy-done.18), channel_id=1, source_target_pairs={{0,4},{2,6},{4,1},{6,3},{1,5},{3,7},{5,0},{7,2},{8,12},{10,14},{12... | collective-permute-start | bytes 663560 | tf_op jit(solution)/shard_map/ppermute | solution.py:478
  57.2 11.1 %collective-permute-start.7 = (bf16[4,3,24,384]{3,2,1,0:T(8,128)(2,1)S(1)}, bf16[4,3,24,384]{3,2,1,0:T(8,128)(2,1)S(1)}, u32[]{:S(2)}, u32[]{:S(2)}) collective-permute-start(bf16[4,3,24,384]{3,2,1,0:T(8,128)(2,1)S(1)} %copy-done.17), channel_id=1, source_target_pairs={{0,5},{2,7},{4,0},{6,2},{1,4},{3,6},{5,1},{7,3},{8,13},{10,15},{12... | collective-permute-start | bytes 663560 | tf_op jit(solution)/shard_map/ppermute | solution.py:478
  64.3 14.3 %copy-start.19 = (bf16[4,3,24,384]{3,2,1,0:T(8,128)(2,1)}, bf16[4,3,24,384]{3,2,1,0:T(8,128)(2,1)S(1)}, u32[]{:S(2)}) copy-start(bf16[4,3,24,384]{3,2,1,0:T(8,128)(2,1)S(1)} %collective-permute-done.6.a_low_ref) | copy-start | bytes 663556
  68.3 10.3 %copy-start.20 = (bf16[4,3,24,384]{3,2,1,0:T(8,128)(2,1)}, bf16[4,3,24,384]{3,2,1,0:T(8,128)(2,1)S(1)}, u32[]{:S(2)}) copy-start(bf16[4,3,24,384]{3,2,1,0:T(8,128)(2,1)S(1)} %collective-permute-done.7.a_high_ref) | copy-start | bytes 663556
  68.3 10.3 %copy-start.15 = (bf16[4,3,48,384]{3,2,1,0:T(8,128)(2,1)}, bf16[4,3,48,384]{3,2,1,0:T(8,128)(2,1)S(1)}, u32[]{:S(2)}) copy-start(bf16[4,3,48,384]{3,2,1,0:T(8,128)(2,1)S(1)} %collective-permute-done.4.a_left_ref) | copy-start | bytes 1327108
  68.3 10.3 %copy-start.16 = (bf16[4,3,48,384]{3,2,1,0:T(8,128)(2,1)}, bf16[4,3,48,384]{3,2,1,0:T(8,128)(2,1)S(1)}, u32[]{:S(2)}) copy-start(bf16[4,3,48,384]{3,2,1,0:T(8,128)(2,1)S(1)} %collective-permute-done.5.a_right_ref) | copy-start | bytes 1327108
  68.3 10.3 %copy-start.13 = (bf16[4,4,3,48,384]{4,3,2,1,0:T(8,128)(2,1)}, bf16[4,4,3,48,384]{4,3,2,1,0:T(8,128)(2,1)S(1)}, u32[]{:S(2)}) copy-start(bf16[4,4,3,48,384]{4,3,2,1,0:T(8,128)(2,1)S(1)} %all-to-all-done.1.b_ref) | copy-start | bytes 5308420
  68.3 31.0 %all-to-all-start.2 = ((bf16[32,3,40,128]{3,2,1,0:T(8,128)(2,1)}), bf16[32,3,40,128]{3,2,1,0:T(8,128)(2,1)}, u32[]{:S(2)}, u32[]{:S(2)}) async-start(bf16[32,3,40,128]{3,2,1,0:T(8,128)(2,1)} %bitcast.44), calls=%async_computation.2 | async-start | bytes 1966080 | tf_op jit(solution)/shard_map/all_to_all | solution.py:531
  84.6 14.7 %copy-start = (bf16[3,768,768]{2,1,0:T(8,128)(2,1)S(1)}, bf16[3,768,768]{2,1,0:T(8,128)(2,1)}, u32[]{:S(2)}) copy-start(bf16[3,768,768]{2,1,0:T(8,128)(2,1)} %assemble.1.table_ref) | copy-start | bytes 10616836
  100.2 45.0 %copy-start.2 = (bf16[45,32,768]{2,1,0:T(8,128)(2,1)S(1)}, bf16[45,32,768]{2,1,0:T(8,128)(2,1)}, u32[]{:S(2)}) copy-start(bf16[45,32,768]{2,1,0:T(8,128)(2,1)} %get-tuple-element.67) | copy-start | bytes 6635524
  100.2 45.0 %copy-start.3 = (bf16[45,32,768]{2,1,0:T(8,128)(2,1)S(1)}, bf16[45,32,768]{2,1,0:T(8,128)(2,1)}, u32[]{:S(2)}) copy-start(bf16[45,32,768]{2,1,0:T(8,128)(2,1)} %get-tuple-element.68) | copy-start | bytes 6635524
  100.2 45.0 %copy-start.8 = (bf16[256,128]{1,0:T(8,128)(2,1)S(1)}, bf16[256,128]{1,0:T(8,128)(2,1)}, u32[]{:S(2)}) copy-start(bf16[256,128]{1,0:T(8,128)(2,1)} %pad.14.w_out_ref) | copy-start | bytes 196612
  100.2 45.0 %copy-start.9 = (bf16[128,256]{1,0:T(8,128)(2,1)S(1)}, bf16[128,256]{1,0:T(8,128)(2,1)}, u32[]{:S(2)}) copy-start(bf16[128,256]{1,0:T(8,128)(2,1)} %pad.13.w_in_ref) | copy-start | bytes 196612
  100.2 45.0 %copy-start.11 = (f32[256]{0:T(256)S(1)}, f32[256]{0:T(256)}, u32[]{:S(2)}) copy-start(f32[256]{0:T(256)} %param.15) | copy-start | bytes 3076
  104.8 40.5 %copy-start.6 = (bf16[4,256,256]{2,1,0:T(8,128)(2,1)S(1)}, bf16[4,256,256]{2,1,0:T(8,128)(2,1)}, u32[]{:S(2)}) copy-start(bf16[4,256,256]{2,1,0:T(8,128)(2,1)} %w_hid_ref.1) | copy-start | bytes 1572868
  145.2 48.5 %copy-start.5 = (bf16[2,256,128]{2,1,0:T(8,128)(2,1)S(1)}, bf16[2,256,128]{2,1,0:T(8,128)(2,1)}, u32[]{:S(2)}) copy-start(bf16[2,256,128]{2,1,0:T(8,128)(2,1)} %constant.212.clone.maps_ref) | copy-start | bytes 393220
  193.8 34.7 %copy-start.1 = (f32[90,45,8,7,2]{0,4,3,2,1:T(2,128)S(1)}, f32[90,45,8,7,2]{0,4,3,2,1:T(2,128)}, u32[]{:S(2)}) copy-start(f32[90,45,8,7,2]{0,4,3,2,1:T(2,128)} %param.11) | copy-start | bytes 5443204
  193.8 34.7 %copy-start.10 = (s32[2]{0:T(128)S(1)}, s32[2]{0:T(128)}, u32[]{:S(2)}) copy-start(s32[2]{0:T(128)} %pad_add_fusion.at_ref) | copy-start | bytes 28
  197.6 30.9 %copy-start.7 = (bf16[8,224,128]{2,1,0:T(8,128)(2,1)S(1)}, bf16[8,224,128]{2,1,0:T(8,128)(2,1)}, u32[]{:S(2)}) copy-start(bf16[8,224,128]{2,1,0:T(8,128)(2,1)} %constant.215.clone.maps_ref) | copy-start | bytes 1376260
  (6 other events, 26.3 us)

commit v9 on v8

--- a/solution.py
+++ b/solution.py
@@ -52,13 +52,13 @@
     return u + u * jnp.tanh(u)
 
 
-def lane_maps(levs, row_local):
-    maps = np.zeros((levs, 2 * LANES, LANES), np.float32)
-    for lev in range(levs):
-        for row in range(row_local):
-            for part in range(2):
-                maps[lev, part * LANES + lev * row_local + row, 2 * row + part] = 1.0
-    return jnp.asarray(maps, bf16)
+def lane_map(lev, row_local):
+    wide_lane = lax.broadcasted_iota(jnp.int32, (2 * LANES, LANES), 0)
+    lane = lax.broadcasted_iota(jnp.int32, (2 * LANES, LANES), 1)
+    part = (wide_lane >= LANES).astype(jnp.int32)
+    row = wide_lane - LANES * part - lev * row_local
+    hit = (row >= 0) & (row < row_local) & (lane == 2 * row + part)
+    return jnp.where(hit, 1.0, 0.0).astype(bf16)
 
 
 def pack_rows(slab_of, out_ref, scr_ref, peers, width):
@@ -221,14 +221,15 @@
 
 
 def inverse_kernel(
-    class_ref, table_ref, coef_ref, maps_ref, out_ref, sums_ref, scr_ref, sent_ref, full_ref,
+    class_ref, table_ref, coef_ref, out_ref, sums_ref, scr_ref, sent_ref, full_ref,
     *, lats, lat_local, lat_slots, width,
 ):
-    sent = coef_ref.shape[3]
+    levs, _, sent, _ = coef_ref.shape[1:]
     rows = full_ref.shape[0] // lats
+    maps = [lane_map(v, width // levs) for v in range(levs)]
     for m in range(OWN):
         swapped = 0.0
-        for v in range(maps_ref.shape[0]):
+        for v in range(levs):
             for q in range(lats):
                 k, x = divmod(q, LAT_X)
                 piece = coef_ref[x * Z_LOW + class_ref[k], v, m].astype(f32)
@@ -242,7 +243,7 @@
                     last = gather_last(last, slab, t, width)
                 full_ref[pl.ds(sent + b, lats, rows), :] = last
             swapped += lax.dot_general(
-                maps_ref[v],
+                maps[v],
                 full_ref[...].astype(bf16),
                 (((1,), (1,)), ((), ())),
                 preferred_element_type=f32,
@@ -264,14 +265,14 @@
     pack_rows(slab_of, out_ref, scr_ref, peers, width)
 
 
-def inverse(classes, table, coef, maps, peers, lat_local, lat_slots, width):
+def inverse(classes, table, coef, peers, lat_local, lat_slots, width):
     lats, _, _, sent, _ = coef.shape
     vmem = pl.BlockSpec(memory_space=pltpu.VMEM)
     return pl.pallas_call(
         functools.partial(
             inverse_kernel, lats=lats, lat_local=lat_local, lat_slots=lat_slots, width=width
         ),
-        in_specs=[pl.BlockSpec(memory_space=pltpu.SMEM), vmem, vmem, vmem],
+        in_specs=[pl.BlockSpec(memory_space=pltpu.SMEM), vmem, vmem],
         out_specs=vmem,
         out_shape=jax.ShapeDtypeStruct((peers * 8, 2 * LANES), bf16),
         scratch_shapes=[
@@ -282,7 +283,7 @@
         ],
         compiler_params=pltpu.CompilerParams(vmem_limit_bytes=24 * 2**20),
         name="inverse",
-    )(classes, table, coef, maps)
+    )(classes, table, coef)
 
 
 def column_kernel(
@@ -354,7 +355,7 @@
 
 
 def forward_kernel(
-    class_ref, in_ref, table_ref, maps_ref, out_ref, sums_ref, scr_ref, sent_ref, full_ref,
+    class_ref, in_ref, table_ref, out_ref, sums_ref, scr_ref, sent_ref, full_ref,
     *, lats, lat_local, lat_slots, width,
 ):
     peers = in_ref.shape[0] // 8
@@ -364,8 +365,9 @@
 
     unpack_rows(in_ref, scr_ref, put, peers, width)
     lanes = table_ref.shape[-1]
-    sent = out_ref.shape[3]
+    levs, _, sent, _ = out_ref.shape[1:]
     rows = full_ref.shape[0] // lats
+    maps = [lane_map(v, width // levs) for v in range(levs)]
     spare = spare_lanes((lats, LANES), width)
     for m in range(OWN):
         weighted = jnp.concatenate(
@@ -382,8 +384,8 @@
             axis=1,
         ).astype(bf16)
         forcing = dot(table_ref[m], weighted).astype(bf16)
-        for v in range(maps_ref.shape[0]):
-            full_ref[...] = dot(forcing, maps_ref[v])
+        for v in range(levs):
+            full_ref[...] = dot(forcing, maps[v])
             for b in range(sent // 8):
                 last = full_ref[pl.ds(sent + b, lats, rows), :]
                 for t in range(8):
@@ -397,14 +399,13 @@
                 out_ref[x * Z_LOW + class_ref[k], v, m] = piece
 
 
-def forward(classes, weighted, table, maps, peers, lats, sent, lat_local, lat_slots, width):
-    levs = maps.shape[0]
+def forward(classes, weighted, table, peers, lats, levs, sent, lat_local, lat_slots, width):
     vmem = pl.BlockSpec(memory_space=pltpu.VMEM)
     return pl.pallas_call(
         functools.partial(
             forward_kernel, lats=lats, lat_local=lat_local, lat_slots=lat_slots, width=width
         ),
-        in_specs=[pl.BlockSpec(memory_space=pltpu.SMEM), vmem, vmem, vmem],
+        in_specs=[pl.BlockSpec(memory_space=pltpu.SMEM), vmem, vmem],
         out_specs=vmem,
         out_shape=jax.ShapeDtypeStruct((lats, levs, OWN, sent, LANES), bf16),
         scratch_shapes=[
@@ -415,7 +416,7 @@
         ],
         compiler_params=pltpu.CompilerParams(vmem_limit_bytes=24 * 2**20),
         name="forward",
-    )(classes, weighted, table, maps)
+    )(classes, weighted, table)
 
 
 def turn_maps(channels):
@@ -497,7 +498,6 @@
     lat_slots = ord_size * lev_size * OWN
     everyone = ("lat", "ord", "lev")
     at = jnp.stack([ord_at * order_local, lat_at * degree_local]).astype(jnp.int32)
-    maps = lane_maps(lev_size, row_local)
     state = spectral_state.transpose(1, 2, 3, 4, 0).reshape(degree_local, channels, order_local)
 
     z_at = lev_at * Z_LOW + lat_at % Z_LOW
@@ -508,9 +508,9 @@
     a_all = along_x(a_all)
     b_far = jnp.concatenate([b_low, b_high], axis=2)
     b_all = jnp.stack([b_own, b_left, b_right, b_far], axis=1)
-    a_all, b_all = lax.optimization_barrier((a_all, b_all))
     a_cut = [a_all[:, 1], a_all[:, 2], a_all[:, 3, :, : rows // 2], a_all[:, 3, :, rows // 2 :]]
-    a_cut, b_all = lax.optimization_barrier((a_cut, b_all))
+    coefficients = prep(at, state, sent)
+    a_cut, b_all, coefficients = lax.optimization_barrier((a_cut, b_all, coefficients))
     a_near = [along_z(a_cut[0], 1), along_z(a_cut[1], -1)]
     a_far = [along_z(a_cut[2], 2), along_z(a_cut[3], -2)]
     b_all = along_x(b_all)
@@ -522,7 +522,6 @@
     slot_x, slot_w = slot_lat // Z_LOW, 2 * (slot_lat % Z_LOW) + slot_lev
     valid = (slot_x % 2 == 0) | (slot_w > 0)
     order_ids = slot_ord * order_local + OWN * (first_group(slot_x) + slot_w) + slot // peers
-    coefficients = prep(at, state, sent)
     coefficients, a_near, a_far, b_all, order_ids, valid = lax.optimization_barrier(
         (coefficients, a_near, a_far, b_all, order_ids, valid)
     )
@@ -544,7 +543,7 @@
     table, coefficients, cosines, sines, weights, w_in, w_out, damping = lax.optimization_barrier(
         (table, coefficients, cosines, sines, weights, w_in, w_out, damping)
     )
-    fourier = inverse(classes, table, coefficients, maps, peers, lat_local, lat_slots, width)
+    fourier = inverse(classes, table, coefficients, peers, lat_local, lat_slots, width)
 
     fourier = lax.all_to_all(fourier.reshape(peers, 8, -1), everyone, 0, 0, tiled=True)
     weighted = columns(
@@ -562,7 +561,7 @@
     weighted = lax.all_to_all(weighted.reshape(peers, 8, -1), everyone, 0, 0, tiled=True)
     weighted = weighted.reshape(peers * 8, -1)
     forcing = forward(
-        classes, weighted, table, maps, peers, lat_size, sent, lat_local, lat_slots, width
+        classes, weighted, table, peers, lat_size, lev_size, sent, lat_local, lat_slots, width
     )
     forcing = forcing.reshape(lat_size * lev_size, OWN, sent, LANES)
     forcing = lax.all_to_all(forcing, ("lat", "lev"), 0, 0, tiled=True)

time: 232 us -> 228 us (0.983)
    all_to_all x1, waiting for transfers between devices: 10.9 us -> 8.54 us  [on_device(): lax.all_to_all(coefficients, ('lat', 'lev'), 0, 0, tiled=True)]
where the time goes in v9:
time: 228 us; the launch traced here: 227 us
  blocking collectives  109 us (48%)
  Pallas kernels  36.6 us (16%)
  waiting for transfers between devices  33.9 us (15%)
  starting transfers between devices  33.6 us (15%)
  other arithmetic  8.47 us (4%)
  local copies, waits for them, and re-layouts  5.07 us (2%)
    all_to_all x1, blocking collectives, on_device(): lax.all_to_all(fourier.reshape(peers, 8, -1), everyone, 0, 0, tiled=True)  40.2 us
    all_to_all x1, blocking collectives, on_device(): lax.all_to_all(weighted.reshape(peers, 8, -1), everyone, 0, 0, tiled=True)  38.1 us
    all_to_all x1, blocking collectives, on_device(): forcing = lax.all_to_all(forcing, ('lat', 'lev'), 0, 0, tiled=True)  30.9 us
    ppermute x8, waiting for transfers between devices, along_z(): return lax.ppermute(value, ('lat', 'lev'), pairs)  25.4 us
    ppermute x8, starting transfers between devices, along_z(): return lax.ppermute(value, ('lat', 'lev'), pairs)  16.4 us
    all_to_all x2, starting transfers between devices, along_x(): lax.all_to_all(value, 'lat', 0, 0, axis_index_groups=groups, tiled=True)  10.8 us
    pallas_call x1, Pallas kernels, columns(): pl.pallas_call(functools.partial(column_kernel, x_rows=X_ROWS, width=widt...  10.1 us
    all_to_all x1, waiting for transfers between devices, on_device(): lax.all_to_all(coefficients, ('lat', 'lev'), 0, 0, tiled=True)  8.54 us
  transfers between devices with their start and end apart: 11, of which 5 were waited for; matrix products, arithmetic and copies ran while one was open for 5% of the time, Pallas kernels for 4%

profile of v9, /device:TPU:2, one launch (start us, length us, event | category | flops | bytes accessed | tf_op | source)
XLA Modules:
  0.0 227.0 jit_solution(15194284164897681482)
XLA Ops:
  0.0 1.3 fusion.43.own_ref
  1.3 5.2 %pack_table.1 = (bf16[4,4,3,48,384]{4,3,2,1,0:T(8,128)(2,1)}, bf16[4,3,48,384]{3,2,1,0:T(8,128)(2,1)}, bf16[4,3,48,384]{3,2,1,0:T(8,128)(2,1)}, bf16[4,3,48,384]...) custom-call(s32[5]{0:T(128)} %fusion.43.own_ref, bf16[90,45,720]{2,1,0:T(8,128)(2,1)} %in_ref.1), custom_call_target="tpu_custom_call" | custom-call | tf_op jit(solution)/shard_map/pack_table/pallas_call | solution.py:172
  6.4 5.8 %all-to-all-start = ((bf16[4,4,3,48,384]{4,3,2,1,0:T(8,128)(2,1)}), bf16[4,4,3,48,384]{4,3,2,1,0:T(8,128)(2,1)S(1)}, u32[]{:S(2)}, u32[]{:S(2)}) async-start(bf16[4,4,3,48,384]{4,3,2,1,0:T(8,128)(2,1)} %get-tuple-element.33), calls=%async_computation | async-start | bytes 3538944 | tf_op jit(solution)/shard_map/all_to_all | solution.py:484
  12.3 0.9 collective-permute-start
  13.2 3.9 %collective-permute-start.1 = (bf16[4,3,48,384]{3,2,1,0:T(8,128)(2,1)}, bf16[4,3,48,384]{3,2,1,0:T(8,128)(2,1)S(1)}, u32[]{:S(2)}, u32[]{:S(2)}) collective-permute-start(bf16[4,3,48,384]{3,2,1,0:T(8,128)(2,1)} %get-tuple-element.36), channel_id=1, source_target_pairs={{0,7},{2,0},{4,2},{6,4},{1,6},{3,1},{5,3},{7,5},{8,15},{10,8},{12,... | collective-permute-start | bytes 1327112 | tf_op jit(solution)/shard_map/ppermute | solution.py:479
  17.1 4.1 %collective-permute-start.3 = (bf16[4,3,24,384]{3,2,1,0:T(8,128)(2,1)}, bf16[4,3,24,384]{3,2,1,0:T(8,128)(2,1)S(1)}, u32[]{:S(2)}, u32[]{:S(2)}) collective-permute-start(bf16[4,3,24,384]{3,2,1,0:T(8,128)(2,1)} %get-tuple-element.38), channel_id=1, source_target_pairs={{0,5},{2,7},{4,0},{6,2},{1,4},{3,6},{5,1},{7,3},{8,13},{10,15},{12... | collective-permute-start | bytes 663560 | tf_op jit(solution)/shard_map/ppermute | solution.py:479
  21.9 5.3 %prep.1 = bf16[4,24,40,128]{3,2,1,0:T(8,128)(2,1)} custom-call(s32[2]{0:T(128)} %pad_add_fusion.at_ref, f32[45,112,90]{2,1,0:T(8,128)} %bitcast.40, f32[45,112,90]{2,1,0:T(8,128)} %bitcast.41), custom_call_target="tpu_custom_call" | custom-call | flops 1000000 | bytes 4000000 | tf_op jit(solution)/shard_map/prep/pallas_call | solution.py:131
  27.2 7.1 %collective-permute-done.2 = bf16[4,3,24,384]{3,2,1,0:T(8,128)(2,1)S(1)} collective-permute-done((bf16[4,3,24,384]{3,2,1,0:T(8,128)(2,1)}, bf16[4,3,24,384]{3,2,1,0:T(8,128)(2,1)S(1)}, u32[]{:S(2)}, u32[]{:S(2)}) %collective-permute-start.2) | collective-permute-done | bytes 221216 | tf_op jit(solution)/shard_map/ppermute | solution.py:479
  34.4 1.4 collective-permute-done.3
  35.9 1.5 pad_maximum_fusion
  37.4 0.9 slice_bitcast_fusion.2
  38.3 1.0 slice_bitcast_fusion
  39.3 4.9 %all-to-all-start.1 = ((bf16[4,4,3,48,384]{4,3,2,1,0:T(8,128)(2,1)}), bf16[4,4,3,48,384]{4,3,2,1,0:T(8,128)(2,1)S(1)}, u32[]{:S(2)}, u32[]{:S(2)}) async-start(bf16[4,4,3,48,384]{4,3,2,1,0:T(8,128)(2,1)} %pad_maximum_fusion), calls=%async_computation.1 | async-start | bytes 3538944 | tf_op jit(solution)/shard_map/all_to_all | solution.py:484
  44.2 2.1 collective-permute-start.4
  46.3 1.1 collective-permute-start.5
  47.4 4.0 %collective-permute-start.6 = (bf16[4,3,24,384]{3,2,1,0:T(8,128)(2,1)}, bf16[4,3,24,384]{3,2,1,0:T(8,128)(2,1)S(1)}, u32[]{:S(2)}, u32[]{:S(2)}) collective-permute-start(bf16[4,3,24,384]{3,2,1,0:T(8,128)(2,1)} %get-tuple-element.42), channel_id=1, source_target_pairs={{0,4},{2,6},{4,1},{6,3},{1,5},{3,7},{5,0},{7,2},{8,12},{10,14},{12... | collective-permute-start | bytes 663560 | tf_op jit(solution)/shard_map/ppermute | solution.py:479
  51.6 12.7 %collective-permute-done.6.a_low_ref = bf16[4,3,24,384]{3,2,1,0:T(8,128)(2,1)S(1)} collective-permute-done((bf16[4,3,24,384]{3,2,1,0:T(8,128)(2,1)}, bf16[4,3,24,384]{3,2,1,0:T(8,128)(2,1)S(1)}, u32[]{:S(2)}, u32[]{:S(2)}) %collective-permute-start.6) | collective-permute-done | bytes 221216 | tf_op jit(solution)/shard_map/ppermute | solution.py:479
  64.3 4.1 %collective-permute-done.7.a_high_ref = bf16[4,3,24,384]{3,2,1,0:T(8,128)(2,1)S(1)} collective-permute-done((bf16[4,3,24,384]{3,2,1,0:T(8,128)(2,1)}, bf16[4,3,24,384]{3,2,1,0:T(8,128)(2,1)S(1)}, u32[]{:S(2)}, u32[]{:S(2)}) %collective-permute-start.7) | collective-permute-done | bytes 221216 | tf_op jit(solution)/shard_map/ppermute | solution.py:479
  68.4 6.4 %all-to-all-start.2 = ((bf16[32,3,40,128]{3,2,1,0:T(8,128)(2,1)}), bf16[32,3,40,128]{3,2,1,0:T(8,128)(2,1)}, u32[]{:S(2)}, u32[]{:S(2)}) async-start(bf16[32,3,40,128]{3,2,1,0:T(8,128)(2,1)} %bitcast.52), calls=%async_computation.2 | async-start | bytes 1966080 | tf_op jit(solution)/shard_map/all_to_all | solution.py:530
  74.9 0.9 copy.18
  75.8 1.5 pad.13.w_in_ref
  78.1 4.8 %assemble.1.table_ref = bf16[3,768,768]{2,1,0:T(8,128)(2,1)} custom-call(bf16[4,4,3,48,384]{4,3,2,1,0:T(8,128)(2,1)} %copy-done.10, bf16[4,3,48,384]{3,2,1,0:T(8,128)(2,1)} %copy-done.13, bf16[4,3,48,384]{3,2,1,0:T(8,128)(2,1)} %copy-done.14, bf16[4,3,24,384]{3,2,1,0:T(8,128)(2,1)} %copy-done.15, bf16[4,3,24,384]{3,2,1,0:T(8,128)(2,1)} %copy-done.16, ...), custom_call_target="tpu_custom_call" | custom-call | flops 1000000 | bytes 8000000 | tf_op jit(solution)/shard_map/assemble/pallas_call | solution.py:205
  83.3 0.7 cosine_select_fusion
  84.0 3.8 %negate_convert_fusion = (bf16[45,32,768]{2,1,0:T(8,128)(2,1)}, bf16[45,32,768]{2,1,0:T(8,128)(2,1)}) fusion(f32[32,768]{1,0:T(8,128)S(1)} %get-tuple-element.70, f32[45,768]{1,0:T(8,128)S(1)} %get-tuple-element.68, f32[32,768]{1,0:T(8,128)S(1)} %get-tuple-element.69, f32[45,768]{1,0:T(8,128)S(1)} %get-tuple-element.67), kind=kLoop, calls=%fused_computation | loop fusion | flops 9953280 | bytes 4896768 | tf_op jit(solution)/shard_map/convert_element_type | solution.py:48
  87.9 8.5 %all-to-all-done.2 = bf16[32,3,40,128]{3,2,1,0:T(8,128)(2,1)} async-done(((bf16[32,3,40,128]{3,2,1,0:T(8,128)(2,1)}), bf16[32,3,40,128]{3,2,1,0:T(8,128)(2,1)}, u32[]{:S(2)}, u32[]{:S(2)}) %all-to-all-start.2) | async-done | bytes 983072 | tf_op jit(solution)/shard_map/all_to_all | solution.py:530
  96.4 4.6 %inverse.1 = bf16[2048,256]{1,0:T(8,128)(2,1)S(1)} custom-call(s32[4]{0:T(128)S(1)} %and_select_fusion.class_ref, bf16[3,768,768]{2,1,0:T(8,128)(2,1)S(1)} %copy-done, bf16[16,2,3,40,128]{4,3,2,1,0:T(8,128)(2,1)} %bitcast.13.coef_ref), custom_call_target="tpu_custom_call" | custom-call | tf_op jit(solution)/shard_map/inverse/pallas_call | solution.py:271
  101.0 40.2 %all_to_all.30 = bf16[256,8,256]{2,1,0:T(8,128)(2,1)S(1)} all-to-all(bf16[256,8,256]{2,1,0:T(8,128)(2,1)S(1)} %bitcast.48), channel_id=1, replica_groups=mesh['ord'=8,'lat'=16,'lev'=2] {'lat','ord','lev'}, dimensions={0} | all-to-all | bytes 2097152 | tf_op jit(solution)/shard_map/all_to_all | solution.py:548
  141.3 10.1 %columns.1 = bf16[2048,256]{1,0:T(8,128)(2,1)S(1)} custom-call(f32[3]{0:T(128)S(1)} %pad_dynamic-slice_fusion.weight_ref, bf16[2048,256]{1,0:T(8,128)(2,1)S(1)} %bitcast.45, bf16[1440,768]{1,0:T(8,128)(2,1)S(1)} %bitcast.44, bf16[1440,768]{1,0:T(8,128)(2,1)S(1)} %bitcast.43, bf16[128,256]{1,0:T(8,128)(2,1)S(1)} %copy-done.7, f32[1,256]{1,0:T(1,128)S(1)} %bitcast.51, ...), custom_call_target="tpu_custom_call" | custom-call | tf_op jit(solution)/shard_map/columns/pallas_call | solution.py:341
  151.4 38.1 %all_to_all.31 = bf16[256,8,256]{2,1,0:T(8,128)(2,1)S(1)} all-to-all(bf16[256,8,256]{2,1,0:T(8,128)(2,1)S(1)} %bitcast.46), channel_id=1, replica_groups=mesh['ord'=8,'lat'=16,'lev'=2] {'lat','ord','lev'}, dimensions={0} | all-to-all | bytes 2097152 | tf_op jit(solution)/shard_map/all_to_all | solution.py:561
  189.5 3.7 %forward.1 = bf16[16,2,3,40,128]{4,3,2,1,0:T(8,128)(2,1)S(1)} custom-call(s32[4]{0:T(128)S(1)} %and_select_fusion.class_ref, bf16[2048,256]{1,0:T(8,128)(2,1)S(1)} %bitcast.47, bf16[3,768,768]{2,1,0:T(8,128)(2,1)S(1)} %copy-done), custom_call_target="tpu_custom_call" | custom-call | tf_op jit(solution)/shard_map/forward/pallas_call | solution.py:404
  193.2 30.9 %all_to_all.32 = bf16[32,3,40,128]{3,2,1,0:T(8,128)(2,1)S(1)} all-to-all(bf16[32,3,40,128]{3,2,1,0:T(8,128)(2,1)S(1)} %bitcast.50), channel_id=1, replica_groups=mesh['ord'=8,'lat'=16,'lev'=2] {'lat','lev'}, dimensions={0} | all-to-all | bytes 1966080 | tf_op jit(solution)/shard_map/all_to_all | solution.py:567
  224.1 2.9 %update.1 = f32[45,112,90]{2,1,0:T(8,128)} custom-call(s32[2]{0:T(128)S(1)} %copy-done.8, f32[45]{0:T(128)S(1)} %add_divide_fusion.damping_ref, f32[45,112,90]{2,1,0:T(8,128)S(1)} %bitcast.42, bf16[4,24,40,128]{3,2,1,0:T(8,128)(2,1)S(1)} %bitcast.49, bf16[8,224,128]{2,1,0:T(8,128)(2,1)S(1)} %copy-done.5), custom_call_target="tpu_custom_call" | custom-call | tf_op jit(solution)/shard_map/update/pallas_call | solution.py:463
  (56 shorter events, 2.2 us)
Async XLA Ops:
  6.4 30.9 %all-to-all-start = ((bf16[4,4,3,48,384]{4,3,2,1,0:T(8,128)(2,1)}), bf16[4,4,3,48,384]{4,3,2,1,0:T(8,128)(2,1)S(1)}, u32[]{:S(2)}, u32[]{:S(2)}) async-start(bf16[4,4,3,48,384]{4,3,2,1,0:T(8,128)(2,1)} %get-tuple-element.33), calls=%async_computation | async-start | bytes 3538944 | tf_op jit(solution)/shard_map/all_to_all | solution.py:484
  12.3 23.6 %collective-permute-start = (bf16[4,3,48,384]{3,2,1,0:T(8,128)(2,1)}, bf16[4,3,48,384]{3,2,1,0:T(8,128)(2,1)S(1)}, u32[]{:S(2)}, u32[]{:S(2)}) collective-permute-start(bf16[4,3,48,384]{3,2,1,0:T(8,128)(2,1)} %get-tuple-element.35), channel_id=1, source_target_pairs={{0,2},{2,4},{4,6},{6,1},{1,3},{3,5},{5,7},{7,0},{8,10},{10,12},{12... | collective-permute-start | bytes 1327112 | tf_op jit(solution)/shard_map/ppermute | solution.py:479
  13.2 22.7 %collective-permute-start.1 = (bf16[4,3,48,384]{3,2,1,0:T(8,128)(2,1)}, bf16[4,3,48,384]{3,2,1,0:T(8,128)(2,1)S(1)}, u32[]{:S(2)}, u32[]{:S(2)}) collective-permute-start(bf16[4,3,48,384]{3,2,1,0:T(8,128)(2,1)} %get-tuple-element.36), channel_id=1, source_target_pairs={{0,7},{2,0},{4,2},{6,4},{1,6},{3,1},{5,3},{7,5},{8,15},{10,8},{12,... | collective-permute-start | bytes 1327112 | tf_op jit(solution)/shard_map/ppermute | solution.py:479
  17.1 17.2 %collective-permute-start.2 = (bf16[4,3,24,384]{3,2,1,0:T(8,128)(2,1)}, bf16[4,3,24,384]{3,2,1,0:T(8,128)(2,1)S(1)}, u32[]{:S(2)}, u32[]{:S(2)}) collective-permute-start(bf16[4,3,24,384]{3,2,1,0:T(8,128)(2,1)} %get-tuple-element.37), channel_id=1, source_target_pairs={{0,4},{2,6},{4,1},{6,3},{1,5},{3,7},{5,0},{7,2},{8,12},{10,14},{12... | collective-permute-start | bytes 663560 | tf_op jit(solution)/shard_map/ppermute | solution.py:479
  17.1 18.7 %collective-permute-start.3 = (bf16[4,3,24,384]{3,2,1,0:T(8,128)(2,1)}, bf16[4,3,24,384]{3,2,1,0:T(8,128)(2,1)S(1)}, u32[]{:S(2)}, u32[]{:S(2)}) collective-permute-start(bf16[4,3,24,384]{3,2,1,0:T(8,128)(2,1)} %get-tuple-element.38), channel_id=1, source_target_pairs={{0,5},{2,7},{4,0},{6,2},{1,4},{3,6},{5,1},{7,3},{8,13},{10,15},{12... | collective-permute-start | bytes 663560 | tf_op jit(solution)/shard_map/ppermute | solution.py:479
  21.9 14.0 %copy-start.12 = (bf16[4,3,48,384]{3,2,1,0:T(8,128)(2,1)S(1)}, bf16[4,3,48,384]{3,2,1,0:T(8,128)(2,1)}, u32[]{:S(2)}) copy-start(bf16[4,3,48,384]{3,2,1,0:T(8,128)(2,1)} %get-tuple-element.34) | copy-start | bytes 1327108
  37.4 1.9 copy-start.10
  39.3 38.7 %copy-start.17 = (f32[45]{0:T(128)S(1)}, f32[45]{0:T(128)}, u32[]{:S(2)}) copy-start(f32[45]{0:T(128)} %param.12) | copy-start | bytes 544
  39.3 38.8 %copy-start.18 = (s32[4]{0:T(128)S(1)}, s32[4]{0:T(128)}, u32[]{:S(2)}) copy-start(s32[4]{0:T(128)} %constant.211.clone) | copy-start | bytes 52
  39.3 29.1 %all-to-all-start.1 = ((bf16[4,4,3,48,384]{4,3,2,1,0:T(8,128)(2,1)}), bf16[4,4,3,48,384]{4,3,2,1,0:T(8,128)(2,1)S(1)}, u32[]{:S(2)}, u32[]{:S(2)}) async-start(bf16[4,4,3,48,384]{4,3,2,1,0:T(8,128)(2,1)} %pad_maximum_fusion), calls=%async_computation.1 | async-start | bytes 3538944 | tf_op jit(solution)/shard_map/all_to_all | solution.py:484
  44.2 24.2 %collective-permute-start.4 = (bf16[4,3,48,384]{3,2,1,0:T(8,128)(2,1)}, bf16[4,3,48,384]{3,2,1,0:T(8,128)(2,1)S(1)}, u32[]{:S(2)}, u32[]{:S(2)}) collective-permute-start(bf16[4,3,48,384]{3,2,1,0:T(8,128)(2,1)} %get-tuple-element.40), channel_id=1, source_target_pairs={{0,2},{2,4},{4,6},{6,1},{1,3},{3,5},{5,7},{7,0},{8,10},{10,12},{12... | collective-permute-start | bytes 1327112 | tf_op jit(solution)/shard_map/ppermute | solution.py:479
  46.3 22.1 %collective-permute-start.5 = (bf16[4,3,48,384]{3,2,1,0:T(8,128)(2,1)}, bf16[4,3,48,384]{3,2,1,0:T(8,128)(2,1)S(1)}, u32[]{:S(2)}, u32[]{:S(2)}) collective-permute-start(bf16[4,3,48,384]{3,2,1,0:T(8,128)(2,1)} %get-tuple-element.41), channel_id=1, source_target_pairs={{0,7},{2,0},{4,2},{6,4},{1,6},{3,1},{5,3},{7,5},{8,15},{10,8},{12,... | collective-permute-start | bytes 1327112 | tf_op jit(solution)/shard_map/ppermute | solution.py:479
  47.4 16.9 %collective-permute-start.6 = (bf16[4,3,24,384]{3,2,1,0:T(8,128)(2,1)}, bf16[4,3,24,384]{3,2,1,0:T(8,128)(2,1)S(1)}, u32[]{:S(2)}, u32[]{:S(2)}) collective-permute-start(bf16[4,3,24,384]{3,2,1,0:T(8,128)(2,1)} %get-tuple-element.42), channel_id=1, source_target_pairs={{0,4},{2,6},{4,1},{6,3},{1,5},{3,7},{5,0},{7,2},{8,12},{10,14},{12... | collective-permute-start | bytes 663560 | tf_op jit(solution)/shard_map/ppermute | solution.py:479
  51.4 17.0 %collective-permute-start.7 = (bf16[4,3,24,384]{3,2,1,0:T(8,128)(2,1)}, bf16[4,3,24,384]{3,2,1,0:T(8,128)(2,1)S(1)}, u32[]{:S(2)}, u32[]{:S(2)}) collective-permute-start(bf16[4,3,24,384]{3,2,1,0:T(8,128)(2,1)} %get-tuple-element.43), channel_id=1, source_target_pairs={{0,5},{2,7},{4,0},{6,2},{1,4},{3,6},{5,1},{7,3},{8,13},{10,15},{12... | collective-permute-start | bytes 663560 | tf_op jit(solution)/shard_map/ppermute | solution.py:479
  64.3 13.7 %copy-start.15 = (bf16[4,3,24,384]{3,2,1,0:T(8,128)(2,1)}, bf16[4,3,24,384]{3,2,1,0:T(8,128)(2,1)S(1)}, u32[]{:S(2)}) copy-start(bf16[4,3,24,384]{3,2,1,0:T(8,128)(2,1)S(1)} %collective-permute-done.6.a_low_ref) | copy-start | bytes 663556
  68.4 9.7 %copy-start.16 = (bf16[4,3,24,384]{3,2,1,0:T(8,128)(2,1)}, bf16[4,3,24,384]{3,2,1,0:T(8,128)(2,1)S(1)}, u32[]{:S(2)}) copy-start(bf16[4,3,24,384]{3,2,1,0:T(8,128)(2,1)S(1)} %collective-permute-done.7.a_high_ref) | copy-start | bytes 663556
  68.4 9.7 %copy-start.13 = (bf16[4,3,48,384]{3,2,1,0:T(8,128)(2,1)}, bf16[4,3,48,384]{3,2,1,0:T(8,128)(2,1)S(1)}, u32[]{:S(2)}) copy-start(bf16[4,3,48,384]{3,2,1,0:T(8,128)(2,1)S(1)} %collective-permute-done.4.a_left_ref) | copy-start | bytes 1327108
  68.4 9.7 %copy-start.14 = (bf16[4,3,48,384]{3,2,1,0:T(8,128)(2,1)}, bf16[4,3,48,384]{3,2,1,0:T(8,128)(2,1)S(1)}, u32[]{:S(2)}) copy-start(bf16[4,3,48,384]{3,2,1,0:T(8,128)(2,1)S(1)} %collective-permute-done.5.a_right_ref) | copy-start | bytes 1327108
  68.4 9.7 %copy-start.11 = (bf16[4,4,3,48,384]{4,3,2,1,0:T(8,128)(2,1)}, bf16[4,4,3,48,384]{4,3,2,1,0:T(8,128)(2,1)S(1)}, u32[]{:S(2)}) copy-start(bf16[4,4,3,48,384]{4,3,2,1,0:T(8,128)(2,1)S(1)} %all-to-all-done.1.b_ref) | copy-start | bytes 5308420
  68.4 28.0 %all-to-all-start.2 = ((bf16[32,3,40,128]{3,2,1,0:T(8,128)(2,1)}), bf16[32,3,40,128]{3,2,1,0:T(8,128)(2,1)}, u32[]{:S(2)}, u32[]{:S(2)}) async-start(bf16[32,3,40,128]{3,2,1,0:T(8,128)(2,1)} %bitcast.52), calls=%async_computation.2 | async-start | bytes 1966080 | tf_op jit(solution)/shard_map/all_to_all | solution.py:530
  84.0 12.4 %copy-start = (bf16[3,768,768]{2,1,0:T(8,128)(2,1)S(1)}, bf16[3,768,768]{2,1,0:T(8,128)(2,1)}, u32[]{:S(2)}) copy-start(bf16[3,768,768]{2,1,0:T(8,128)(2,1)} %assemble.1.table_ref) | copy-start | bytes 10616836
  96.4 44.8 %copy-start.2 = (bf16[45,32,768]{2,1,0:T(8,128)(2,1)S(1)}, bf16[45,32,768]{2,1,0:T(8,128)(2,1)}, u32[]{:S(2)}) copy-start(bf16[45,32,768]{2,1,0:T(8,128)(2,1)} %get-tuple-element.65) | copy-start | bytes 6635524
  96.4 44.8 %copy-start.3 = (bf16[45,32,768]{2,1,0:T(8,128)(2,1)S(1)}, bf16[45,32,768]{2,1,0:T(8,128)(2,1)}, u32[]{:S(2)}) copy-start(bf16[45,32,768]{2,1,0:T(8,128)(2,1)} %get-tuple-element.66) | copy-start | bytes 6635524
  96.4 44.8 %copy-start.6 = (bf16[256,128]{1,0:T(8,128)(2,1)S(1)}, bf16[256,128]{1,0:T(8,128)(2,1)}, u32[]{:S(2)}) copy-start(bf16[256,128]{1,0:T(8,128)(2,1)} %pad.14.w_out_ref) | copy-start | bytes 196612
  96.4 44.8 %copy-start.7 = (bf16[128,256]{1,0:T(8,128)(2,1)S(1)}, bf16[128,256]{1,0:T(8,128)(2,1)}, u32[]{:S(2)}) copy-start(bf16[128,256]{1,0:T(8,128)(2,1)} %pad.13.w_in_ref) | copy-start | bytes 196612
  96.4 44.8 %copy-start.9 = (f32[256]{0:T(256)S(1)}, f32[256]{0:T(256)}, u32[]{:S(2)}) copy-start(f32[256]{0:T(256)} %param.14) | copy-start | bytes 3076
  101.0 40.3 %copy-start.4 = (bf16[4,256,256]{2,1,0:T(8,128)(2,1)S(1)}, bf16[4,256,256]{2,1,0:T(8,128)(2,1)}, u32[]{:S(2)}) copy-start(bf16[4,256,256]{2,1,0:T(8,128)(2,1)} %w_hid_ref.1) | copy-start | bytes 1572868
  189.5 34.6 %copy-start.1 = (f32[90,45,8,7,2]{0,4,3,2,1:T(2,128)S(1)}, f32[90,45,8,7,2]{0,4,3,2,1:T(2,128)}, u32[]{:S(2)}) copy-start(f32[90,45,8,7,2]{0,4,3,2,1:T(2,128)} %param.10) | copy-start | bytes 5443204
  189.5 34.6 %copy-start.8 = (s32[2]{0:T(128)S(1)}, s32[2]{0:T(128)}, u32[]{:S(2)}) copy-start(s32[2]{0:T(128)} %pad_add_fusion.at_ref) | copy-start | bytes 28
  193.2 30.9 %copy-start.5 = (bf16[8,224,128]{2,1,0:T(8,128)(2,1)S(1)}, bf16[8,224,128]{2,1,0:T(8,128)(2,1)}, u32[]{:S(2)}) copy-start(bf16[8,224,128]{2,1,0:T(8,128)(2,1)} %constant.212.clone.maps_ref) | copy-start | bytes 1376260

commit v10 on v9

--- a/solution.py
+++ b/solution.py
@@ -144,26 +144,28 @@
     )(at, state, state)
 
 
-def pack_kernel(own_ref, in_ref, a_ref, *b_refs):
+def pack_kernel(z_ref, in_ref, a_ref, *b_refs):
     degrees, lats = in_ref.shape[1:]
     half, rows = a_ref.shape[-1], a_ref.shape[-2]
     split = rows // 2
+    ring = [lax.rem(z_ref[0] + (Z_RING + step), Z_RING) for step in (0, 1, -1, 2, -2)]
+    own = [OWN * (2 * lax.rem(z, Z_LOW) + lax.div(z, Z_LOW)) for z in ring]
     a_ref[...] = jnp.zeros_like(a_ref)
     for ref in b_refs:
         ref[...] = jnp.zeros_like(ref)
     for k in range(3):
-        mine = in_ref[pl.ds(own_ref[k], OWN)]
+        mine = in_ref[pl.ds(own[k], OWN)]
         a_ref[0, k, :, :degrees, :] = mine[:, :, :half]
         b_refs[k][0, :, :degrees, : lats - half] = mine[:, :, half:]
-    mine = in_ref[pl.ds(own_ref[3], OWN)]
+    mine = in_ref[pl.ds(own[3], OWN)]
     a_ref[0, 3, :, :split, :] = mine[:, :split, :half]
     b_refs[3][0, :, :, : lats - half] = mine[:, :split, half:]
-    mine = in_ref[pl.ds(own_ref[4], OWN)]
+    mine = in_ref[pl.ds(own[4], OWN)]
     a_ref[0, 3, :, split:degrees, :] = mine[:, split:, :half]
     b_refs[4][0, :, : degrees - split, : lats - half] = mine[:, split:, half:]
 
 
-def pack_table(own, legendre, half, rows):
+def pack_table(z_at, legendre, half, rows):
     _, degrees, lats = legendre.shape
     group = OWN * Z_RING
     b_shape = lambda r: jax.ShapeDtypeStruct((LAT_X, OWN, r, half), bf16)
@@ -185,7 +187,7 @@
         + [b_shape(r) for r in b_rows],
         compiler_params=pltpu.CompilerParams(vmem_limit_bytes=60 * 2**20),
         name="pack_table",
-    )(own, legendre)
+    )(z_at, legendre)
 
 
 def assemble_kernel(a_own_ref, a_left_ref, a_right_ref, a_low_ref, a_high_ref, b_ref, out_ref):
@@ -501,14 +503,15 @@
     state = spectral_state.transpose(1, 2, 3, 4, 0).reshape(degree_local, channels, order_local)
 
     z_at = lev_at * Z_LOW + lat_at % Z_LOW
-    ring = (z_at + jnp.array([0, 1, -1, 2, -2], jnp.int32)) % Z_RING
-    own = OWN * (2 * (ring % Z_LOW) + ring // Z_LOW)
-    a_all, b_own, *b_rest = pack_table(own, legendre, HALF, rows)
+    a_all, b_own, *b_rest = pack_table(z_at[None], legendre, HALF, rows)
     b_left, b_right, b_low, b_high = (along_z(v, k) for v, k in zip(b_rest, (1, -1, 2, -2)))
     a_all = along_x(a_all)
+    a_cut = [a_all[:, 1], a_all[:, 2], a_all[:, 3, :, : rows // 2], a_all[:, 3, :, rows // 2 :]]
+    a_cut, b_left, b_right, b_low, b_high = lax.optimization_barrier(
+        (a_cut, b_left, b_right, b_low, b_high)
+    )
     b_far = jnp.concatenate([b_low, b_high], axis=2)
     b_all = jnp.stack([b_own, b_left, b_right, b_far], axis=1)
-    a_cut = [a_all[:, 1], a_all[:, 2], a_all[:, 3, :, : rows // 2], a_all[:, 3, :, rows // 2 :]]
     coefficients = prep(at, state, sent)
     a_cut, b_all, coefficients = lax.optimization_barrier((a_cut, b_all, coefficients))
     a_near = [along_z(a_cut[0], 1), along_z(a_cut[1], -1)]

time: 228 us -> 232 us (1.018)
    ppermute x8, waiting for transfers between devices: 25.4 us -> 18.8 us  [along_z(): return lax.ppermute(value, ('lat', 'lev'), pairs)]
    all_to_all x2, waiting for transfers between devices: 0.01 us -> 5.91 us  [along_x(): lax.all_to_all(value, 'lat', 0, 0, axis_index_groups=groups, tiled=True)]
  transfers between devices with their start and end apart: 11 -> 11, of which waited for: 5 -> 6; matrix products, arithmetic and copies ran while one was open for 5% -> 5% of each run, Pallas kernels for 4% -> 4%
where the time goes in v10:
time: 232 us; the launch traced here: 231 us
  blocking collectives  109 us (47%)
  Pallas kernels  36.7 us (16%)
  starting transfers between devices  34.8 us (15%)
  waiting for transfers between devices  34.3 us (15%)
  other arithmetic  10.5 us (5%)
  local copies, waits for them, and re-layouts  4.94 us (2%)
    all_to_all x1, blocking collectives, on_device(): lax.all_to_all(fourier.reshape(peers, 8, -1), everyone, 0, 0, tiled=True)  40.4 us
    all_to_all x1, blocking collectives, on_device(): lax.all_to_all(weighted.reshape(peers, 8, -1), everyone, 0, 0, tiled=True)  38.1 us
    all_to_all x1, blocking collectives, on_device(): forcing = lax.all_to_all(forcing, ('lat', 'lev'), 0, 0, tiled=True)  30.9 us
    ppermute x8, waiting for transfers between devices, along_z(): return lax.ppermute(value, ('lat', 'lev'), pairs)  18.8 us
    ppermute x8, starting transfers between devices, along_z(): return lax.ppermute(value, ('lat', 'lev'), pairs)  15.9 us
    all_to_all x2, starting transfers between devices, along_x(): lax.all_to_all(value, 'lat', 0, 0, axis_index_groups=groups, tiled=True)  10.7 us
    pallas_call x1, Pallas kernels, columns(): pl.pallas_call(functools.partial(column_kernel, x_rows=X_ROWS, width=widt...  10.4 us
    all_to_all x1, waiting for transfers between devices, on_device(): lax.all_to_all(coefficients, ('lat', 'lev'), 0, 0, tiled=True)  9.68 us
  transfers between devices with their start and end apart: 11, of which 6 were waited for; matrix products, arithmetic and copies ran while one was open for 5% of the time, Pallas kernels for 4%

profile of v10, /device:TPU:2, one launch (start us, length us, event | category | flops | bytes accessed | tf_op | source)
XLA Modules:
  0.0 230.9 jit_solution(6870779329727925261)
XLA Ops:
  0.0 5.2 %pack_table.1 = (bf16[4,4,3,48,384]{4,3,2,1,0:T(8,128)(2,1)}, bf16[4,3,48,384]{3,2,1,0:T(8,128)(2,1)}, bf16[4,3,48,384]{3,2,1,0:T(8,128)(2,1)}, bf16[4,3,48,384]...) custom-call(s32[1]{0:T(128)} %bitcast.2.z_ref, bf16[90,45,720]{2,1,0:T(8,128)(2,1)} %in_ref.1), custom_call_target="tpu_custom_call" | custom-call | tf_op jit(solution)/shard_map/pack_table/pallas_call | solution.py:174
  5.2 5.8 %all-to-all-start = ((bf16[4,4,3,48,384]{4,3,2,1,0:T(8,128)(2,1)}), bf16[4,4,3,48,384]{4,3,2,1,0:T(8,128)(2,1)S(1)}, u32[]{:S(2)}, u32[]{:S(2)}) async-start(bf16[4,4,3,48,384]{4,3,2,1,0:T(8,128)(2,1)} %get-tuple-element.41), calls=%async_computation | async-start | bytes 3538944 | tf_op jit(solution)/shard_map/all_to_all | solution.py:486
  11.0 2.3 collective-permute-start.2
  13.3 3.0 %collective-permute-start.3 = (bf16[4,3,24,384]{3,2,1,0:T(8,128)(2,1)}, bf16[4,3,24,384]{3,2,1,0:T(8,128)(2,1)}, u32[]{:S(2)}, u32[]{:S(2)}) collective-permute-start(bf16[4,3,24,384]{3,2,1,0:T(8,128)(2,1)} %get-tuple-element.45), channel_id=1, source_target_pairs={{0,5},{2,7},{4,0},{6,2},{1,4},{3,6},{5,1},{7,3},{8,13},{10,15},{12... | collective-permute-start | bytes 663560 | tf_op jit(solution)/shard_map/ppermute | solution.py:481
  16.4 1.0 collective-permute-start
  17.4 2.2 collective-permute-start.1
  20.3 5.2 %prep.1 = bf16[4,24,40,128]{3,2,1,0:T(8,128)(2,1)} custom-call(s32[2]{0:T(128)} %pad_add_fusion.at_ref, f32[45,112,90]{2,1,0:T(8,128)} %bitcast.41, f32[45,112,90]{2,1,0:T(8,128)} %bitcast.42), custom_call_target="tpu_custom_call" | custom-call | flops 1000000 | bytes 4000000 | tf_op jit(solution)/shard_map/prep/pallas_call | solution.py:131
  25.5 5.9 %all-to-all-done.a_own_ref = bf16[4,4,3,48,384]{4,3,2,1,0:T(8,128)(2,1)S(1)} async-done(((bf16[4,4,3,48,384]{4,3,2,1,0:T(8,128)(2,1)}), bf16[4,4,3,48,384]{4,3,2,1,0:T(8,128)(2,1)S(1)}, u32[]{:S(2)}, u32[]{:S(2)}) %all-to-all-start) | async-done | bytes 1769504 | tf_op jit(solution)/shard_map/all_to_all | solution.py:486
  31.5 0.9 slice_bitcast_fusion.2
  32.5 2.7 %collective-permute-done = bf16[4,3,48,384]{3,2,1,0:T(8,128)(2,1)S(1)} collective-permute-done((bf16[4,3,48,384]{3,2,1,0:T(8,128)(2,1)}, bf16[4,3,48,384]{3,2,1,0:T(8,128)(2,1)S(1)}, u32[]{:S(2)}, u32[]{:S(2)}) %collective-permute-start) | collective-permute-done | bytes 442400 | tf_op jit(solution)/shard_map/ppermute | solution.py:481
  35.2 1.3 collective-permute-done.1
  36.5 1.1 maximum_bitcast_fusion
  37.6 2.5 %pad_maximum_fusion = bf16[4,4,3,48,384]{4,3,2,1,0:T(8,128)(2,1)} fusion(bf16[4,1,3,48,384]{4,3,2,1,0:T(8,128)(2,1)S(1)} %maximum_bitcast_fusion, bf16[4,1,3,48,384]{4,3,2,1,0:T(8,128)(2,1)} %bitcast.9, bf16[4,1,3,48,384]{4,3,2,1,0:T(8,128)(2,1)S(1)} %bitcast.54, bf16[4,1,3,48,384]{4,3,2,1,0:T(8,128)(2,1)S(1)} %bitcast.53), kind=kLoop, calls=%fused_computation.2 | loop fusion | flops 2654208 | bytes 3538944 | tf_op jit(solution)/shard_map/stack | solution.py:514
  40.1 4.9 %all-to-all-start.1 = ((bf16[4,4,3,48,384]{4,3,2,1,0:T(8,128)(2,1)}), bf16[4,4,3,48,384]{4,3,2,1,0:T(8,128)(2,1)S(1)}, u32[]{:S(2)}, u32[]{:S(2)}) async-start(bf16[4,4,3,48,384]{4,3,2,1,0:T(8,128)(2,1)} %pad_maximum_fusion), calls=%async_computation.1 | async-start | bytes 3538944 | tf_op jit(solution)/shard_map/all_to_all | solution.py:486
  45.1 1.0 collective-permute-start.4
  46.1 2.2 collective-permute-start.5
  48.3 1.6 collective-permute-start.6
  49.9 2.5 %collective-permute-start.7 = (bf16[4,3,24,384]{3,2,1,0:T(8,128)(2,1)}, bf16[4,3,24,384]{3,2,1,0:T(8,128)(2,1)S(1)}, u32[]{:S(2)}, u32[]{:S(2)}) collective-permute-start(bf16[4,3,24,384]{3,2,1,0:T(8,128)(2,1)} %get-tuple-element.59), channel_id=1, source_target_pairs={{0,5},{2,7},{4,0},{6,2},{1,4},{3,6},{5,1},{7,3},{8,13},{10,15},{12... | collective-permute-start | bytes 663560 | tf_op jit(solution)/shard_map/ppermute | solution.py:481
  53.1 13.0 %collective-permute-done.6.a_low_ref = bf16[4,3,24,384]{3,2,1,0:T(8,128)(2,1)S(1)} collective-permute-done((bf16[4,3,24,384]{3,2,1,0:T(8,128)(2,1)}, bf16[4,3,24,384]{3,2,1,0:T(8,128)(2,1)S(1)}, u32[]{:S(2)}, u32[]{:S(2)}) %collective-permute-start.6) | collective-permute-done | bytes 221216 | tf_op jit(solution)/shard_map/ppermute | solution.py:481
  66.1 1.7 collective-permute-done.7.a_high_ref
  68.5 8.1 %all-to-all-start.2 = ((bf16[32,3,40,128]{3,2,1,0:T(8,128)(2,1)}), bf16[32,3,40,128]{3,2,1,0:T(8,128)(2,1)}, u32[]{:S(2)}, u32[]{:S(2)}) async-start(bf16[32,3,40,128]{3,2,1,0:T(8,128)(2,1)} %bitcast.13), calls=%async_computation.2 | async-start | bytes 1966080 | tf_op jit(solution)/shard_map/all_to_all | solution.py:533
  77.6 1.5 pad.13.w_in_ref
  80.5 4.8 %assemble.1.table_ref = bf16[3,768,768]{2,1,0:T(8,128)(2,1)} custom-call(bf16[4,4,3,48,384]{4,3,2,1,0:T(8,128)(2,1)} %copy-done.10, bf16[4,3,48,384]{3,2,1,0:T(8,128)(2,1)} %copy-done.13, bf16[4,3,48,384]{3,2,1,0:T(8,128)(2,1)} %copy-done.14, bf16[4,3,24,384]{3,2,1,0:T(8,128)(2,1)} %copy-done.15, bf16[4,3,24,384]{3,2,1,0:T(8,128)(2,1)} %copy-done.16, ...), custom_call_target="tpu_custom_call" | custom-call | flops 1000000 | bytes 8000000 | tf_op jit(solution)/shard_map/assemble/pallas_call | solution.py:207
  86.4 3.8 %negate_convert_fusion = (bf16[45,32,768]{2,1,0:T(8,128)(2,1)}, bf16[45,32,768]{2,1,0:T(8,128)(2,1)}) fusion(f32[32,768]{1,0:T(8,128)S(1)} %get-tuple-element.86, f32[45,768]{1,0:T(8,128)S(1)} %get-tuple-element.84, f32[32,768]{1,0:T(8,128)S(1)} %get-tuple-element.85, f32[45,768]{1,0:T(8,128)S(1)} %get-tuple-element.83), kind=kLoop, calls=%fused_computation | loop fusion | flops 9953280 | bytes 4896768 | tf_op jit(solution)/shard_map/convert_element_type | solution.py:48
  90.3 9.7 %all-to-all-done.2 = bf16[32,3,40,128]{3,2,1,0:T(8,128)(2,1)} async-done(((bf16[32,3,40,128]{3,2,1,0:T(8,128)(2,1)}), bf16[32,3,40,128]{3,2,1,0:T(8,128)(2,1)}, u32[]{:S(2)}, u32[]{:S(2)}) %all-to-all-start.2) | async-done | bytes 983072 | tf_op jit(solution)/shard_map/all_to_all | solution.py:533
  100.0 4.5 %inverse.1 = bf16[2048,256]{1,0:T(8,128)(2,1)S(1)} custom-call(s32[4]{0:T(128)S(1)} %and_select_fusion.class_ref, bf16[3,768,768]{2,1,0:T(8,128)(2,1)S(1)} %copy-done, bf16[16,2,3,40,128]{4,3,2,1,0:T(8,128)(2,1)} %bitcast.14.coef_ref), custom_call_target="tpu_custom_call" | custom-call | tf_op jit(solution)/shard_map/inverse/pallas_call | solution.py:273
  104.5 40.4 %all_to_all.30 = bf16[256,8,256]{2,1,0:T(8,128)(2,1)S(1)} all-to-all(bf16[256,8,256]{2,1,0:T(8,128)(2,1)S(1)} %bitcast.49), channel_id=1, replica_groups=mesh['ord'=8,'lat'=16,'lev'=2] {'lat','ord','lev'}, dimensions={0} | all-to-all | bytes 2097152 | tf_op jit(solution)/shard_map/all_to_all | solution.py:551
  145.0 10.4 %columns.1 = bf16[2048,256]{1,0:T(8,128)(2,1)S(1)} custom-call(f32[3]{0:T(128)S(1)} %pad_dynamic-slice_fusion.weight_ref, bf16[2048,256]{1,0:T(8,128)(2,1)S(1)} %bitcast.46, bf16[1440,768]{1,0:T(8,128)(2,1)S(1)} %bitcast.45, bf16[1440,768]{1,0:T(8,128)(2,1)S(1)} %bitcast.44, bf16[128,256]{1,0:T(8,128)(2,1)S(1)} %copy-done.7, f32[1,256]{1,0:T(1,128)S(1)} %bitcast.52, ...), custom_call_target="tpu_custom_call" | custom-call | tf_op jit(solution)/shard_map/columns/pallas_call | solution.py:343
  155.3 38.1 %all_to_all.31 = bf16[256,8,256]{2,1,0:T(8,128)(2,1)S(1)} all-to-all(bf16[256,8,256]{2,1,0:T(8,128)(2,1)S(1)} %bitcast.47), channel_id=1, replica_groups=mesh['ord'=8,'lat'=16,'lev'=2] {'lat','ord','lev'}, dimensions={0} | all-to-all | bytes 2097152 | tf_op jit(solution)/shard_map/all_to_all | solution.py:564
  193.4 3.6 %forward.1 = bf16[16,2,3,40,128]{4,3,2,1,0:T(8,128)(2,1)S(1)} custom-call(s32[4]{0:T(128)S(1)} %and_select_fusion.class_ref, bf16[2048,256]{1,0:T(8,128)(2,1)S(1)} %bitcast.48, bf16[3,768,768]{2,1,0:T(8,128)(2,1)S(1)} %copy-done), custom_call_target="tpu_custom_call" | custom-call | tf_op jit(solution)/shard_map/forward/pallas_call | solution.py:406
  197.1 30.9 %all_to_all.32 = bf16[32,3,40,128]{3,2,1,0:T(8,128)(2,1)S(1)} all-to-all(bf16[32,3,40,128]{3,2,1,0:T(8,128)(2,1)S(1)} %bitcast.51), channel_id=1, replica_groups=mesh['ord'=8,'lat'=16,'lev'=2] {'lat','lev'}, dimensions={0} | all-to-all | bytes 1966080 | tf_op jit(solution)/shard_map/all_to_all | solution.py:570
  228.0 2.9 %update.1 = f32[45,112,90]{2,1,0:T(8,128)} custom-call(s32[2]{0:T(128)S(1)} %copy-done.8, f32[45]{0:T(128)S(1)} %add_divide_fusion.damping_ref, f32[45,112,90]{2,1,0:T(8,128)S(1)} %bitcast.43, bf16[4,24,40,128]{3,2,1,0:T(8,128)(2,1)S(1)} %bitcast.50, bf16[8,224,128]{2,1,0:T(8,128)(2,1)S(1)} %copy-done.5), custom_call_target="tpu_custom_call" | custom-call | tf_op jit(solution)/shard_map/update/pallas_call | solution.py:465
  (55 shorter events, 5.6 us)
Async XLA Ops:
  5.2 26.2 %all-to-all-start = ((bf16[4,4,3,48,384]{4,3,2,1,0:T(8,128)(2,1)}), bf16[4,4,3,48,384]{4,3,2,1,0:T(8,128)(2,1)S(1)}, u32[]{:S(2)}, u32[]{:S(2)}) async-start(bf16[4,4,3,48,384]{4,3,2,1,0:T(8,128)(2,1)} %get-tuple-element.41), calls=%async_computation | async-start | bytes 3538944 | tf_op jit(solution)/shard_map/all_to_all | solution.py:486
  11.0 21.4 %collective-permute-start.2 = (bf16[4,3,24,384]{3,2,1,0:T(8,128)(2,1)}, bf16[4,3,24,384]{3,2,1,0:T(8,128)(2,1)}, u32[]{:S(2)}, u32[]{:S(2)}) collective-permute-start(bf16[4,3,24,384]{3,2,1,0:T(8,128)(2,1)} %get-tuple-element.44), channel_id=1, source_target_pairs={{0,4},{2,6},{4,1},{6,3},{1,5},{3,7},{5,0},{7,2},{8,12},{10,14},{12... | collective-permute-start | bytes 663560 | tf_op jit(solution)/shard_map/ppermute | solution.py:481
  13.3 19.1 %collective-permute-start.3 = (bf16[4,3,24,384]{3,2,1,0:T(8,128)(2,1)}, bf16[4,3,24,384]{3,2,1,0:T(8,128)(2,1)}, u32[]{:S(2)}, u32[]{:S(2)}) collective-permute-start(bf16[4,3,24,384]{3,2,1,0:T(8,128)(2,1)} %get-tuple-element.45), channel_id=1, source_target_pairs={{0,5},{2,7},{4,0},{6,2},{1,4},{3,6},{5,1},{7,3},{8,13},{10,15},{12... | collective-permute-start | bytes 663560 | tf_op jit(solution)/shard_map/ppermute | solution.py:481
  16.4 18.8 %collective-permute-start = (bf16[4,3,48,384]{3,2,1,0:T(8,128)(2,1)}, bf16[4,3,48,384]{3,2,1,0:T(8,128)(2,1)S(1)}, u32[]{:S(2)}, u32[]{:S(2)}) collective-permute-start(bf16[4,3,48,384]{3,2,1,0:T(8,128)(2,1)} %get-tuple-element.42), channel_id=1, source_target_pairs={{0,2},{2,4},{4,6},{6,1},{1,3},{3,5},{5,7},{7,0},{8,10},{10,12},{12... | collective-permute-start | bytes 1327112 | tf_op jit(solution)/shard_map/ppermute | solution.py:481
  17.4 19.1 %collective-permute-start.1 = (bf16[4,3,48,384]{3,2,1,0:T(8,128)(2,1)}, bf16[4,3,48,384]{3,2,1,0:T(8,128)(2,1)}, u32[]{:S(2)}, u32[]{:S(2)}) collective-permute-start(bf16[4,3,48,384]{3,2,1,0:T(8,128)(2,1)} %get-tuple-element.43), channel_id=1, source_target_pairs={{0,7},{2,0},{4,2},{6,4},{1,6},{3,1},{5,3},{7,5},{8,15},{10,8},{12,... | collective-permute-start | bytes 1327112 | tf_op jit(solution)/shard_map/ppermute | solution.py:481
  25.5 12.1 %copy-start.12 = (bf16[4,3,48,384]{3,2,1,0:T(8,128)(2,1)S(1)}, bf16[4,3,48,384]{3,2,1,0:T(8,128)(2,1)}, u32[]{:S(2)}) copy-start(bf16[4,3,48,384]{3,2,1,0:T(8,128)(2,1)} %get-tuple-element.50) | copy-start | bytes 1327108
  31.4 8.7 %copy-start.10 = (bf16[4,4,3,48,384]{4,3,2,1,0:T(8,128)(2,1)}, bf16[4,4,3,48,384]{4,3,2,1,0:T(8,128)(2,1)S(1)}, u32[]{:S(2)}) copy-start(bf16[4,4,3,48,384]{4,3,2,1,0:T(8,128)(2,1)S(1)} %all-to-all-done.a_own_ref) | copy-start | bytes 5308420
  40.1 39.6 %copy-start.18 = (f32[45]{0:T(128)S(1)}, f32[45]{0:T(128)}, u32[]{:S(2)}) copy-start(f32[45]{0:T(128)} %param.11) | copy-start | bytes 544
  40.1 28.4 %all-to-all-start.1 = ((bf16[4,4,3,48,384]{4,3,2,1,0:T(8,128)(2,1)}), bf16[4,4,3,48,384]{4,3,2,1,0:T(8,128)(2,1)S(1)}, u32[]{:S(2)}, u32[]{:S(2)}) async-start(bf16[4,4,3,48,384]{4,3,2,1,0:T(8,128)(2,1)} %pad_maximum_fusion), calls=%async_computation.1 | async-start | bytes 3538944 | tf_op jit(solution)/shard_map/all_to_all | solution.py:486
  45.1 22.7 %collective-permute-start.4 = (bf16[4,3,48,384]{3,2,1,0:T(8,128)(2,1)S(1)}, bf16[4,3,48,384]{3,2,1,0:T(8,128)(2,1)S(1)}, u32[]{:S(2)}, u32[]{:S(2)}) collective-permute-start(bf16[4,3,48,384]{3,2,1,0:T(8,128)(2,1)S(1)} %get-tuple-element.56), channel_id=1, source_target_pairs={{0,2},{2,4},{4,6},{6,1},{1,3},{3,5},{5,7},{7,0},{8,10},{10,12},{12... | collective-permute-start | bytes 1327112 | tf_op jit(solution)/shard_map/ppermute | solution.py:481
  46.1 22.4 %collective-permute-start.5 = (bf16[4,3,48,384]{3,2,1,0:T(8,128)(2,1)S(1)}, bf16[4,3,48,384]{3,2,1,0:T(8,128)(2,1)S(1)}, u32[]{:S(2)}, u32[]{:S(2)}) collective-permute-start(bf16[4,3,48,384]{3,2,1,0:T(8,128)(2,1)S(1)} %get-tuple-element.57), channel_id=1, source_target_pairs={{0,7},{2,0},{4,2},{6,4},{1,6},{3,1},{5,3},{7,5},{8,15},{10,8},{12,... | collective-permute-start | bytes 1327112 | tf_op jit(solution)/shard_map/ppermute | solution.py:481
  48.3 17.8 %collective-permute-start.6 = (bf16[4,3,24,384]{3,2,1,0:T(8,128)(2,1)}, bf16[4,3,24,384]{3,2,1,0:T(8,128)(2,1)S(1)}, u32[]{:S(2)}, u32[]{:S(2)}) collective-permute-start(bf16[4,3,24,384]{3,2,1,0:T(8,128)(2,1)} %get-tuple-element.58), channel_id=1, source_target_pairs={{0,4},{2,6},{4,1},{6,3},{1,5},{3,7},{5,0},{7,2},{8,12},{10,14},{12... | collective-permute-start | bytes 663560 | tf_op jit(solution)/shard_map/ppermute | solution.py:481
  49.9 17.9 %collective-permute-start.7 = (bf16[4,3,24,384]{3,2,1,0:T(8,128)(2,1)}, bf16[4,3,24,384]{3,2,1,0:T(8,128)(2,1)S(1)}, u32[]{:S(2)}, u32[]{:S(2)}) collective-permute-start(bf16[4,3,24,384]{3,2,1,0:T(8,128)(2,1)} %get-tuple-element.59), channel_id=1, source_target_pairs={{0,5},{2,7},{4,0},{6,2},{1,4},{3,6},{5,1},{7,3},{8,13},{10,15},{12... | collective-permute-start | bytes 663560 | tf_op jit(solution)/shard_map/ppermute | solution.py:481
  66.1 1.7 copy-start.15
  67.8 0.7 copy-start.16
  68.5 12.0 %copy-start.13 = (bf16[4,3,48,384]{3,2,1,0:T(8,128)(2,1)}, bf16[4,3,48,384]{3,2,1,0:T(8,128)(2,1)S(1)}, u32[]{:S(2)}) copy-start(bf16[4,3,48,384]{3,2,1,0:T(8,128)(2,1)S(1)} %collective-permute-done.4.a_left_ref) | copy-start | bytes 1327108
  68.5 12.0 %copy-start.14 = (bf16[4,3,48,384]{3,2,1,0:T(8,128)(2,1)}, bf16[4,3,48,384]{3,2,1,0:T(8,128)(2,1)S(1)}, u32[]{:S(2)}) copy-start(bf16[4,3,48,384]{3,2,1,0:T(8,128)(2,1)S(1)} %collective-permute-done.5.a_right_ref) | copy-start | bytes 1327108
  68.5 12.0 %copy-start.11 = (bf16[4,4,3,48,384]{4,3,2,1,0:T(8,128)(2,1)}, bf16[4,4,3,48,384]{4,3,2,1,0:T(8,128)(2,1)S(1)}, u32[]{:S(2)}) copy-start(bf16[4,4,3,48,384]{4,3,2,1,0:T(8,128)(2,1)S(1)} %all-to-all-done.1.b_ref) | copy-start | bytes 5308420
  68.5 31.4 %all-to-all-start.2 = ((bf16[32,3,40,128]{3,2,1,0:T(8,128)(2,1)}), bf16[32,3,40,128]{3,2,1,0:T(8,128)(2,1)}, u32[]{:S(2)}, u32[]{:S(2)}) async-start(bf16[32,3,40,128]{3,2,1,0:T(8,128)(2,1)} %bitcast.13), calls=%async_computation.2 | async-start | bytes 1966080 | tf_op jit(solution)/shard_map/all_to_all | solution.py:533
  80.5 5.2 %copy-start.17 = (pred[768]{0:T(1024)(128)(4,1)S(1)}, pred[768]{0:T(1024)(128)(4,1)}, u32[]{:S(2)}) copy-start(pred[768]{0:T(1024)(128)(4,1)} %fusion.36) | copy-start | bytes 2308
  86.4 13.5 %copy-start = (bf16[3,768,768]{2,1,0:T(8,128)(2,1)S(1)}, bf16[3,768,768]{2,1,0:T(8,128)(2,1)}, u32[]{:S(2)}) copy-start(bf16[3,768,768]{2,1,0:T(8,128)(2,1)} %assemble.1.table_ref) | copy-start | bytes 10616836
  99.9 45.0 %copy-start.2 = (bf16[45,32,768]{2,1,0:T(8,128)(2,1)S(1)}, bf16[45,32,768]{2,1,0:T(8,128)(2,1)}, u32[]{:S(2)}) copy-start(bf16[45,32,768]{2,1,0:T(8,128)(2,1)} %get-tuple-element.81) | copy-start | bytes 6635524
  99.9 45.0 %copy-start.3 = (bf16[45,32,768]{2,1,0:T(8,128)(2,1)S(1)}, bf16[45,32,768]{2,1,0:T(8,128)(2,1)}, u32[]{:S(2)}) copy-start(bf16[45,32,768]{2,1,0:T(8,128)(2,1)} %get-tuple-element.82) | copy-start | bytes 6635524
  99.9 45.0 %copy-start.6 = (bf16[256,128]{1,0:T(8,128)(2,1)S(1)}, bf16[256,128]{1,0:T(8,128)(2,1)}, u32[]{:S(2)}) copy-start(bf16[256,128]{1,0:T(8,128)(2,1)} %pad.14.w_out_ref) | copy-start | bytes 196612
  99.9 45.0 %copy-start.7 = (bf16[128,256]{1,0:T(8,128)(2,1)S(1)}, bf16[128,256]{1,0:T(8,128)(2,1)}, u32[]{:S(2)}) copy-start(bf16[128,256]{1,0:T(8,128)(2,1)} %pad.13.w_in_ref) | copy-start | bytes 196612
  100.0 45.0 %copy-start.9 = (f32[256]{0:T(256)S(1)}, f32[256]{0:T(256)}, u32[]{:S(2)}) copy-start(f32[256]{0:T(256)} %param.13) | copy-start | bytes 3076
  104.5 40.5 %copy-start.4 = (bf16[4,256,256]{2,1,0:T(8,128)(2,1)S(1)}, bf16[4,256,256]{2,1,0:T(8,128)(2,1)}, u32[]{:S(2)}) copy-start(bf16[4,256,256]{2,1,0:T(8,128)(2,1)} %w_hid_ref.1) | copy-start | bytes 1572868
  193.4 34.5 %copy-start.1 = (f32[90,45,8,7,2]{0,4,3,2,1:T(2,128)S(1)}, f32[90,45,8,7,2]{0,4,3,2,1:T(2,128)}, u32[]{:S(2)}) copy-start(f32[90,45,8,7,2]{0,4,3,2,1:T(2,128)} %param.9) | copy-start | bytes 5443204
  193.4 34.5 %copy-start.8 = (s32[2]{0:T(128)S(1)}, s32[2]{0:T(128)}, u32[]{:S(2)}) copy-start(s32[2]{0:T(128)} %pad_add_fusion.at_ref) | copy-start | bytes 28
  197.1 30.9 %copy-start.5 = (bf16[8,224,128]{2,1,0:T(8,128)(2,1)S(1)}, bf16[8,224,128]{2,1,0:T(8,128)(2,1)}, u32[]{:S(2)}) copy-start(bf16[8,224,128]{2,1,0:T(8,128)(2,1)} %constant.185.clone.maps_ref) | copy-start | bytes 1376260

commit v11 on v10

--- a/solution.py
+++ b/solution.py
@@ -506,12 +506,9 @@
     a_all, b_own, *b_rest = pack_table(z_at[None], legendre, HALF, rows)
     b_left, b_right, b_low, b_high = (along_z(v, k) for v, k in zip(b_rest, (1, -1, 2, -2)))
     a_all = along_x(a_all)
-    a_cut = [a_all[:, 1], a_all[:, 2], a_all[:, 3, :, : rows // 2], a_all[:, 3, :, rows // 2 :]]
-    a_cut, b_left, b_right, b_low, b_high = lax.optimization_barrier(
-        (a_cut, b_left, b_right, b_low, b_high)
-    )
     b_far = jnp.concatenate([b_low, b_high], axis=2)
     b_all = jnp.stack([b_own, b_left, b_right, b_far], axis=1)
+    a_cut = [a_all[:, 1], a_all[:, 2], a_all[:, 3, :, : rows // 2], a_all[:, 3, :, rows // 2 :]]
     coefficients = prep(at, state, sent)
     a_cut, b_all, coefficients = lax.optimization_barrier((a_cut, b_all, coefficients))
     a_near = [along_z(a_cut[0], 1), along_z(a_cut[1], -1)]

time: 232 us -> 227 us (0.978)
  other arithmetic: 10.5 us -> 7.21 us
    ppermute x8, waiting for transfers between devices: 18.8 us -> 25.4 us  [along_z(): return lax.ppermute(value, ('lat', 'lev'), pairs)]
    all_to_all x2, waiting for transfers between devices: 5.91 us -> 0.01 us  [along_x(): lax.all_to_all(value, 'lat', 0, 0, axis_index_groups=groups, tiled=True)]
  transfers between devices with their start and end apart: 11 -> 11, of which waited for: 6 -> 5; matrix products, arithmetic and copies ran while one was open for 5% -> 5% of each run, Pallas kernels for 4% -> 4%
where the time goes in v11:
time: 227 us; the launch traced here: 226 us
  blocking collectives  109 us (48%)
  Pallas kernels  36.6 us (16%)
  waiting for transfers between devices  33.9 us (15%)
  starting transfers between devices  33.6 us (15%)
  other arithmetic  7.21 us (3%)
  local copies, waits for them, and re-layouts  5.07 us (2%)
    all_to_all x1, blocking collectives, on_device(): lax.all_to_all(fourier.reshape(peers, 8, -1), everyone, 0, 0, tiled=True)  40.2 us
    all_to_all x1, blocking collectives, on_device(): lax.all_to_all(weighted.reshape(peers, 8, -1), everyone, 0, 0, tiled=True)  38.1 us
    all_to_all x1, blocking collectives, on_device(): forcing = lax.all_to_all(forcing, ('lat', 'lev'), 0, 0, tiled=True)  30.9 us
    ppermute x8, waiting for transfers between devices, along_z(): return lax.ppermute(value, ('lat', 'lev'), pairs)  25.4 us
    ppermute x8, starting transfers between devices, along_z(): return lax.ppermute(value, ('lat', 'lev'), pairs)  16.4 us
    all_to_all x2, starting transfers between devices, along_x(): lax.all_to_all(value, 'lat', 0, 0, axis_index_groups=groups, tiled=True)  10.7 us
    pallas_call x1, Pallas kernels, columns(): pl.pallas_call(functools.partial(column_kernel, x_rows=X_ROWS, width=widt...  10.1 us
    all_to_all x1, waiting for transfers between devices, on_device(): lax.all_to_all(coefficients, ('lat', 'lev'), 0, 0, tiled=True)  8.55 us
  transfers between devices with their start and end apart: 11, of which 5 were waited for; matrix products, arithmetic and copies ran while one was open for 5% of the time, Pallas kernels for 4%

profile of v11, /device:TPU:2, one launch (start us, length us, event | category | flops | bytes accessed | tf_op | source)
XLA Modules:
  0.0 225.8 jit_solution(17700803141706795714)
XLA Ops:
  0.0 5.2 %pack_table.1 = (bf16[4,4,3,48,384]{4,3,2,1,0:T(8,128)(2,1)}, bf16[4,3,48,384]{3,2,1,0:T(8,128)(2,1)}, bf16[4,3,48,384]{3,2,1,0:T(8,128)(2,1)}, bf16[4,3,48,384]...) custom-call(s32[1]{0:T(128)} %bitcast.2.z_ref, bf16[90,45,720]{2,1,0:T(8,128)(2,1)} %in_ref.1), custom_call_target="tpu_custom_call" | custom-call | tf_op jit(solution)/shard_map/pack_table/pallas_call | solution.py:174
  5.2 5.8 %all-to-all-start = ((bf16[4,4,3,48,384]{4,3,2,1,0:T(8,128)(2,1)}), bf16[4,4,3,48,384]{4,3,2,1,0:T(8,128)(2,1)S(1)}, u32[]{:S(2)}, u32[]{:S(2)}) async-start(bf16[4,4,3,48,384]{4,3,2,1,0:T(8,128)(2,1)} %get-tuple-element.33), calls=%async_computation | async-start | bytes 3538944 | tf_op jit(solution)/shard_map/all_to_all | solution.py:486
  11.0 0.9 collective-permute-start
  12.0 3.9 %collective-permute-start.1 = (bf16[4,3,48,384]{3,2,1,0:T(8,128)(2,1)}, bf16[4,3,48,384]{3,2,1,0:T(8,128)(2,1)S(1)}, u32[]{:S(2)}, u32[]{:S(2)}) collective-permute-start(bf16[4,3,48,384]{3,2,1,0:T(8,128)(2,1)} %get-tuple-element.36), channel_id=1, source_target_pairs={{0,7},{2,0},{4,2},{6,4},{1,6},{3,1},{5,3},{7,5},{8,15},{10,8},{12,... | collective-permute-start | bytes 1327112 | tf_op jit(solution)/shard_map/ppermute | solution.py:481
  15.9 4.1 %collective-permute-start.3 = (bf16[4,3,24,384]{3,2,1,0:T(8,128)(2,1)}, bf16[4,3,24,384]{3,2,1,0:T(8,128)(2,1)S(1)}, u32[]{:S(2)}, u32[]{:S(2)}) collective-permute-start(bf16[4,3,24,384]{3,2,1,0:T(8,128)(2,1)} %get-tuple-element.38), channel_id=1, source_target_pairs={{0,5},{2,7},{4,0},{6,2},{1,4},{3,6},{5,1},{7,3},{8,13},{10,15},{12... | collective-permute-start | bytes 663560 | tf_op jit(solution)/shard_map/ppermute | solution.py:481
  20.7 5.3 %prep.1 = bf16[4,24,40,128]{3,2,1,0:T(8,128)(2,1)} custom-call(s32[2]{0:T(128)} %pad_add_fusion.at_ref, f32[45,112,90]{2,1,0:T(8,128)} %bitcast.41, f32[45,112,90]{2,1,0:T(8,128)} %bitcast.42), custom_call_target="tpu_custom_call" | custom-call | flops 1000000 | bytes 4000000 | tf_op jit(solution)/shard_map/prep/pallas_call | solution.py:131
  26.0 7.1 %collective-permute-done.2 = bf16[4,3,24,384]{3,2,1,0:T(8,128)(2,1)S(1)} collective-permute-done((bf16[4,3,24,384]{3,2,1,0:T(8,128)(2,1)}, bf16[4,3,24,384]{3,2,1,0:T(8,128)(2,1)S(1)}, u32[]{:S(2)}, u32[]{:S(2)}) %collective-permute-start.2) | collective-permute-done | bytes 221216 | tf_op jit(solution)/shard_map/ppermute | solution.py:481
  33.1 1.4 collective-permute-done.3
  34.7 1.5 pad_maximum_fusion
  36.2 0.9 slice_bitcast_fusion.2
  37.0 1.0 slice_bitcast_fusion
  38.1 4.9 %all-to-all-start.1 = ((bf16[4,4,3,48,384]{4,3,2,1,0:T(8,128)(2,1)}), bf16[4,4,3,48,384]{4,3,2,1,0:T(8,128)(2,1)S(1)}, u32[]{:S(2)}, u32[]{:S(2)}) async-start(bf16[4,4,3,48,384]{4,3,2,1,0:T(8,128)(2,1)} %pad_maximum_fusion), calls=%async_computation.1 | async-start | bytes 3538944 | tf_op jit(solution)/shard_map/all_to_all | solution.py:486
  43.0 2.1 collective-permute-start.4
  45.1 1.1 collective-permute-start.5
  46.2 4.0 %collective-permute-start.6 = (bf16[4,3,24,384]{3,2,1,0:T(8,128)(2,1)}, bf16[4,3,24,384]{3,2,1,0:T(8,128)(2,1)S(1)}, u32[]{:S(2)}, u32[]{:S(2)}) collective-permute-start(bf16[4,3,24,384]{3,2,1,0:T(8,128)(2,1)} %get-tuple-element.42), channel_id=1, source_target_pairs={{0,4},{2,6},{4,1},{6,3},{1,5},{3,7},{5,0},{7,2},{8,12},{10,14},{12... | collective-permute-start | bytes 663560 | tf_op jit(solution)/shard_map/ppermute | solution.py:481
  50.4 12.7 %collective-permute-done.6.a_low_ref = bf16[4,3,24,384]{3,2,1,0:T(8,128)(2,1)S(1)} collective-permute-done((bf16[4,3,24,384]{3,2,1,0:T(8,128)(2,1)}, bf16[4,3,24,384]{3,2,1,0:T(8,128)(2,1)S(1)}, u32[]{:S(2)}, u32[]{:S(2)}) %collective-permute-start.6) | collective-permute-done | bytes 221216 | tf_op jit(solution)/shard_map/ppermute | solution.py:481
  63.1 4.1 %collective-permute-done.7.a_high_ref = bf16[4,3,24,384]{3,2,1,0:T(8,128)(2,1)S(1)} collective-permute-done((bf16[4,3,24,384]{3,2,1,0:T(8,128)(2,1)}, bf16[4,3,24,384]{3,2,1,0:T(8,128)(2,1)S(1)}, u32[]{:S(2)}, u32[]{:S(2)}) %collective-permute-start.7) | collective-permute-done | bytes 221216 | tf_op jit(solution)/shard_map/ppermute | solution.py:481
  67.2 6.4 %all-to-all-start.2 = ((bf16[32,3,40,128]{3,2,1,0:T(8,128)(2,1)}), bf16[32,3,40,128]{3,2,1,0:T(8,128)(2,1)}, u32[]{:S(2)}, u32[]{:S(2)}) async-start(bf16[32,3,40,128]{3,2,1,0:T(8,128)(2,1)} %bitcast.53), calls=%async_computation.2 | async-start | bytes 1966080 | tf_op jit(solution)/shard_map/all_to_all | solution.py:530
  73.7 0.9 copy.17
  74.6 1.5 pad.13.w_in_ref
  76.1 0.6 pad.14.w_out_ref
  76.9 4.8 %assemble.1.table_ref = bf16[3,768,768]{2,1,0:T(8,128)(2,1)} custom-call(bf16[4,4,3,48,384]{4,3,2,1,0:T(8,128)(2,1)} %copy-done.10, bf16[4,3,48,384]{3,2,1,0:T(8,128)(2,1)} %copy-done.13, bf16[4,3,48,384]{3,2,1,0:T(8,128)(2,1)} %copy-done.14, bf16[4,3,24,384]{3,2,1,0:T(8,128)(2,1)} %copy-done.15, bf16[4,3,24,384]{3,2,1,0:T(8,128)(2,1)} %copy-done.16, ...), custom_call_target="tpu_custom_call" | custom-call | flops 1000000 | bytes 8000000 | tf_op jit(solution)/shard_map/assemble/pallas_call | solution.py:207
  82.1 0.7 cosine_select_fusion
  82.8 3.8 %negate_convert_fusion = (bf16[45,32,768]{2,1,0:T(8,128)(2,1)}, bf16[45,32,768]{2,1,0:T(8,128)(2,1)}) fusion(f32[32,768]{1,0:T(8,128)S(1)} %get-tuple-element.70, f32[45,768]{1,0:T(8,128)S(1)} %get-tuple-element.68, f32[32,768]{1,0:T(8,128)S(1)} %get-tuple-element.69, f32[45,768]{1,0:T(8,128)S(1)} %get-tuple-element.67), kind=kLoop, calls=%fused_computation | loop fusion | flops 9953280 | bytes 4896768 | tf_op jit(solution)/shard_map/convert_element_type | solution.py:48
  86.6 8.5 %all-to-all-done.2 = bf16[32,3,40,128]{3,2,1,0:T(8,128)(2,1)} async-done(((bf16[32,3,40,128]{3,2,1,0:T(8,128)(2,1)}), bf16[32,3,40,128]{3,2,1,0:T(8,128)(2,1)}, u32[]{:S(2)}, u32[]{:S(2)}) %all-to-all-start.2) | async-done | bytes 983072 | tf_op jit(solution)/shard_map/all_to_all | solution.py:530
  95.2 4.6 %inverse.1 = bf16[2048,256]{1,0:T(8,128)(2,1)S(1)} custom-call(s32[4]{0:T(128)S(1)} %and_select_fusion.class_ref, bf16[3,768,768]{2,1,0:T(8,128)(2,1)S(1)} %copy-done, bf16[16,2,3,40,128]{4,3,2,1,0:T(8,128)(2,1)} %bitcast.14.coef_ref), custom_call_target="tpu_custom_call" | custom-call | tf_op jit(solution)/shard_map/inverse/pallas_call | solution.py:273
  99.8 40.2 %all_to_all.30 = bf16[256,8,256]{2,1,0:T(8,128)(2,1)S(1)} all-to-all(bf16[256,8,256]{2,1,0:T(8,128)(2,1)S(1)} %bitcast.49), channel_id=1, replica_groups=mesh['ord'=8,'lat'=16,'lev'=2] {'lat','ord','lev'}, dimensions={0} | all-to-all | bytes 2097152 | tf_op jit(solution)/shard_map/all_to_all | solution.py:548
  140.1 10.1 %columns.1 = bf16[2048,256]{1,0:T(8,128)(2,1)S(1)} custom-call(f32[3]{0:T(128)S(1)} %pad_dynamic-slice_fusion.weight_ref, bf16[2048,256]{1,0:T(8,128)(2,1)S(1)} %bitcast.46, bf16[1440,768]{1,0:T(8,128)(2,1)S(1)} %bitcast.45, bf16[1440,768]{1,0:T(8,128)(2,1)S(1)} %bitcast.44, bf16[128,256]{1,0:T(8,128)(2,1)S(1)} %copy-done.7, f32[1,256]{1,0:T(1,128)S(1)} %bitcast.52, ...), custom_call_target="tpu_custom_call" | custom-call | tf_op jit(solution)/shard_map/columns/pallas_call | solution.py:343
  150.2 38.1 %all_to_all.31 = bf16[256,8,256]{2,1,0:T(8,128)(2,1)S(1)} all-to-all(bf16[256,8,256]{2,1,0:T(8,128)(2,1)S(1)} %bitcast.47), channel_id=1, replica_groups=mesh['ord'=8,'lat'=16,'lev'=2] {'lat','ord','lev'}, dimensions={0} | all-to-all | bytes 2097152 | tf_op jit(solution)/shard_map/all_to_all | solution.py:561
  188.3 3.7 %forward.1 = bf16[16,2,3,40,128]{4,3,2,1,0:T(8,128)(2,1)S(1)} custom-call(s32[4]{0:T(128)S(1)} %and_select_fusion.class_ref, bf16[2048,256]{1,0:T(8,128)(2,1)S(1)} %bitcast.48, bf16[3,768,768]{2,1,0:T(8,128)(2,1)S(1)} %copy-done), custom_call_target="tpu_custom_call" | custom-call | tf_op jit(solution)/shard_map/forward/pallas_call | solution.py:406
  192.0 30.9 %all_to_all.32 = bf16[32,3,40,128]{3,2,1,0:T(8,128)(2,1)S(1)} all-to-all(bf16[32,3,40,128]{3,2,1,0:T(8,128)(2,1)S(1)} %bitcast.51), channel_id=1, replica_groups=mesh['ord'=8,'lat'=16,'lev'=2] {'lat','lev'}, dimensions={0} | all-to-all | bytes 1966080 | tf_op jit(solution)/shard_map/all_to_all | solution.py:567
  222.9 2.9 %update.1 = f32[45,112,90]{2,1,0:T(8,128)} custom-call(s32[2]{0:T(128)S(1)} %copy-done.8, f32[45]{0:T(128)S(1)} %add_divide_fusion.damping_ref, f32[45,112,90]{2,1,0:T(8,128)S(1)} %bitcast.43, bf16[4,24,40,128]{3,2,1,0:T(8,128)(2,1)S(1)} %bitcast.50, bf16[8,224,128]{2,1,0:T(8,128)(2,1)S(1)} %copy-done.5), custom_call_target="tpu_custom_call" | custom-call | tf_op jit(solution)/shard_map/update/pallas_call | solution.py:465
  (55 shorter events, 1.5 us)
Async XLA Ops:
  5.2 31.0 %all-to-all-start = ((bf16[4,4,3,48,384]{4,3,2,1,0:T(8,128)(2,1)}), bf16[4,4,3,48,384]{4,3,2,1,0:T(8,128)(2,1)S(1)}, u32[]{:S(2)}, u32[]{:S(2)}) async-start(bf16[4,4,3,48,384]{4,3,2,1,0:T(8,128)(2,1)} %get-tuple-element.33), calls=%async_computation | async-start | bytes 3538944 | tf_op jit(solution)/shard_map/all_to_all | solution.py:486
  11.0 23.6 %collective-permute-start = (bf16[4,3,48,384]{3,2,1,0:T(8,128)(2,1)}, bf16[4,3,48,384]{3,2,1,0:T(8,128)(2,1)S(1)}, u32[]{:S(2)}, u32[]{:S(2)}) collective-permute-start(bf16[4,3,48,384]{3,2,1,0:T(8,128)(2,1)} %get-tuple-element.35), channel_id=1, source_target_pairs={{0,2},{2,4},{4,6},{6,1},{1,3},{3,5},{5,7},{7,0},{8,10},{10,12},{12... | collective-permute-start | bytes 1327112 | tf_op jit(solution)/shard_map/ppermute | solution.py:481
  12.0 22.7 %collective-permute-start.1 = (bf16[4,3,48,384]{3,2,1,0:T(8,128)(2,1)}, bf16[4,3,48,384]{3,2,1,0:T(8,128)(2,1)S(1)}, u32[]{:S(2)}, u32[]{:S(2)}) collective-permute-start(bf16[4,3,48,384]{3,2,1,0:T(8,128)(2,1)} %get-tuple-element.36), channel_id=1, source_target_pairs={{0,7},{2,0},{4,2},{6,4},{1,6},{3,1},{5,3},{7,5},{8,15},{10,8},{12,... | collective-permute-start | bytes 1327112 | tf_op jit(solution)/shard_map/ppermute | solution.py:481
  15.9 17.2 %collective-permute-start.2 = (bf16[4,3,24,384]{3,2,1,0:T(8,128)(2,1)}, bf16[4,3,24,384]{3,2,1,0:T(8,128)(2,1)S(1)}, u32[]{:S(2)}, u32[]{:S(2)}) collective-permute-start(bf16[4,3,24,384]{3,2,1,0:T(8,128)(2,1)} %get-tuple-element.37), channel_id=1, source_target_pairs={{0,4},{2,6},{4,1},{6,3},{1,5},{3,7},{5,0},{7,2},{8,12},{10,14},{12... | collective-permute-start | bytes 663560 | tf_op jit(solution)/shard_map/ppermute | solution.py:481
  15.9 18.7 %collective-permute-start.3 = (bf16[4,3,24,384]{3,2,1,0:T(8,128)(2,1)}, bf16[4,3,24,384]{3,2,1,0:T(8,128)(2,1)S(1)}, u32[]{:S(2)}, u32[]{:S(2)}) collective-permute-start(bf16[4,3,24,384]{3,2,1,0:T(8,128)(2,1)} %get-tuple-element.38), channel_id=1, source_target_pairs={{0,5},{2,7},{4,0},{6,2},{1,4},{3,6},{5,1},{7,3},{8,13},{10,15},{12... | collective-permute-start | bytes 663560 | tf_op jit(solution)/shard_map/ppermute | solution.py:481
  20.7 14.0 %copy-start.12 = (bf16[4,3,48,384]{3,2,1,0:T(8,128)(2,1)S(1)}, bf16[4,3,48,384]{3,2,1,0:T(8,128)(2,1)}, u32[]{:S(2)}) copy-start(bf16[4,3,48,384]{3,2,1,0:T(8,128)(2,1)} %get-tuple-element.34) | copy-start | bytes 1327108
  36.2 1.9 copy-start.10
  38.1 38.7 %copy-start.17 = (f32[45]{0:T(128)S(1)}, f32[45]{0:T(128)}, u32[]{:S(2)}) copy-start(f32[45]{0:T(128)} %param.11) | copy-start | bytes 544
  38.1 38.8 %copy-start.18 = (s32[4]{0:T(128)S(1)}, s32[4]{0:T(128)}, u32[]{:S(2)}) copy-start(s32[4]{0:T(128)} %constant.184.clone) | copy-start | bytes 52
  38.1 29.1 %all-to-all-start.1 = ((bf16[4,4,3,48,384]{4,3,2,1,0:T(8,128)(2,1)}), bf16[4,4,3,48,384]{4,3,2,1,0:T(8,128)(2,1)S(1)}, u32[]{:S(2)}, u32[]{:S(2)}) async-start(bf16[4,4,3,48,384]{4,3,2,1,0:T(8,128)(2,1)} %pad_maximum_fusion), calls=%async_computation.1 | async-start | bytes 3538944 | tf_op jit(solution)/shard_map/all_to_all | solution.py:486
  43.0 24.2 %collective-permute-start.4 = (bf16[4,3,48,384]{3,2,1,0:T(8,128)(2,1)}, bf16[4,3,48,384]{3,2,1,0:T(8,128)(2,1)S(1)}, u32[]{:S(2)}, u32[]{:S(2)}) collective-permute-start(bf16[4,3,48,384]{3,2,1,0:T(8,128)(2,1)} %get-tuple-element.40), channel_id=1, source_target_pairs={{0,2},{2,4},{4,6},{6,1},{1,3},{3,5},{5,7},{7,0},{8,10},{10,12},{12... | collective-permute-start | bytes 1327112 | tf_op jit(solution)/shard_map/ppermute | solution.py:481
  45.1 22.1 %collective-permute-start.5 = (bf16[4,3,48,384]{3,2,1,0:T(8,128)(2,1)}, bf16[4,3,48,384]{3,2,1,0:T(8,128)(2,1)S(1)}, u32[]{:S(2)}, u32[]{:S(2)}) collective-permute-start(bf16[4,3,48,384]{3,2,1,0:T(8,128)(2,1)} %get-tuple-element.41), channel_id=1, source_target_pairs={{0,7},{2,0},{4,2},{6,4},{1,6},{3,1},{5,3},{7,5},{8,15},{10,8},{12,... | collective-permute-start | bytes 1327112 | tf_op jit(solution)/shard_map/ppermute | solution.py:481
  46.2 16.9 %collective-permute-start.6 = (bf16[4,3,24,384]{3,2,1,0:T(8,128)(2,1)}, bf16[4,3,24,384]{3,2,1,0:T(8,128)(2,1)S(1)}, u32[]{:S(2)}, u32[]{:S(2)}) collective-permute-start(bf16[4,3,24,384]{3,2,1,0:T(8,128)(2,1)} %get-tuple-element.42), channel_id=1, source_target_pairs={{0,4},{2,6},{4,1},{6,3},{1,5},{3,7},{5,0},{7,2},{8,12},{10,14},{12... | collective-permute-start | bytes 663560 | tf_op jit(solution)/shard_map/ppermute | solution.py:481
  50.2 17.0 %collective-permute-start.7 = (bf16[4,3,24,384]{3,2,1,0:T(8,128)(2,1)}, bf16[4,3,24,384]{3,2,1,0:T(8,128)(2,1)S(1)}, u32[]{:S(2)}, u32[]{:S(2)}) collective-permute-start(bf16[4,3,24,384]{3,2,1,0:T(8,128)(2,1)} %get-tuple-element.43), channel_id=1, source_target_pairs={{0,5},{2,7},{4,0},{6,2},{1,4},{3,6},{5,1},{7,3},{8,13},{10,15},{12... | collective-permute-start | bytes 663560 | tf_op jit(solution)/shard_map/ppermute | solution.py:481
  63.1 13.7 %copy-start.15 = (bf16[4,3,24,384]{3,2,1,0:T(8,128)(2,1)}, bf16[4,3,24,384]{3,2,1,0:T(8,128)(2,1)S(1)}, u32[]{:S(2)}) copy-start(bf16[4,3,24,384]{3,2,1,0:T(8,128)(2,1)S(1)} %collective-permute-done.6.a_low_ref) | copy-start | bytes 663556
  67.2 9.7 %copy-start.16 = (bf16[4,3,24,384]{3,2,1,0:T(8,128)(2,1)}, bf16[4,3,24,384]{3,2,1,0:T(8,128)(2,1)S(1)}, u32[]{:S(2)}) copy-start(bf16[4,3,24,384]{3,2,1,0:T(8,128)(2,1)S(1)} %collective-permute-done.7.a_high_ref) | copy-start | bytes 663556
  67.2 9.7 %copy-start.13 = (bf16[4,3,48,384]{3,2,1,0:T(8,128)(2,1)}, bf16[4,3,48,384]{3,2,1,0:T(8,128)(2,1)S(1)}, u32[]{:S(2)}) copy-start(bf16[4,3,48,384]{3,2,1,0:T(8,128)(2,1)S(1)} %collective-permute-done.4.a_left_ref) | copy-start | bytes 1327108
  67.2 9.7 %copy-start.14 = (bf16[4,3,48,384]{3,2,1,0:T(8,128)(2,1)}, bf16[4,3,48,384]{3,2,1,0:T(8,128)(2,1)S(1)}, u32[]{:S(2)}) copy-start(bf16[4,3,48,384]{3,2,1,0:T(8,128)(2,1)S(1)} %collective-permute-done.5.a_right_ref) | copy-start | bytes 1327108
  67.2 9.7 %copy-start.11 = (bf16[4,4,3,48,384]{4,3,2,1,0:T(8,128)(2,1)}, bf16[4,4,3,48,384]{4,3,2,1,0:T(8,128)(2,1)S(1)}, u32[]{:S(2)}) copy-start(bf16[4,4,3,48,384]{4,3,2,1,0:T(8,128)(2,1)S(1)} %all-to-all-done.1.b_ref) | copy-start | bytes 5308420
  67.2 28.0 %all-to-all-start.2 = ((bf16[32,3,40,128]{3,2,1,0:T(8,128)(2,1)}), bf16[32,3,40,128]{3,2,1,0:T(8,128)(2,1)}, u32[]{:S(2)}, u32[]{:S(2)}) async-start(bf16[32,3,40,128]{3,2,1,0:T(8,128)(2,1)} %bitcast.53), calls=%async_computation.2 | async-start | bytes 1966080 | tf_op jit(solution)/shard_map/all_to_all | solution.py:530
  82.8 12.4 %copy-start = (bf16[3,768,768]{2,1,0:T(8,128)(2,1)S(1)}, bf16[3,768,768]{2,1,0:T(8,128)(2,1)}, u32[]{:S(2)}) copy-start(bf16[3,768,768]{2,1,0:T(8,128)(2,1)} %assemble.1.table_ref) | copy-start | bytes 10616836
  95.2 44.8 %copy-start.2 = (bf16[45,32,768]{2,1,0:T(8,128)(2,1)S(1)}, bf16[45,32,768]{2,1,0:T(8,128)(2,1)}, u32[]{:S(2)}) copy-start(bf16[45,32,768]{2,1,0:T(8,128)(2,1)} %get-tuple-element.65) | copy-start | bytes 6635524
  95.2 44.8 %copy-start.3 = (bf16[45,32,768]{2,1,0:T(8,128)(2,1)S(1)}, bf16[45,32,768]{2,1,0:T(8,128)(2,1)}, u32[]{:S(2)}) copy-start(bf16[45,32,768]{2,1,0:T(8,128)(2,1)} %get-tuple-element.66) | copy-start | bytes 6635524
  95.2 44.8 %copy-start.6 = (bf16[256,128]{1,0:T(8,128)(2,1)S(1)}, bf16[256,128]{1,0:T(8,128)(2,1)}, u32[]{:S(2)}) copy-start(bf16[256,128]{1,0:T(8,128)(2,1)} %pad.14.w_out_ref) | copy-start | bytes 196612
  95.2 44.8 %copy-start.7 = (bf16[128,256]{1,0:T(8,128)(2,1)S(1)}, bf16[128,256]{1,0:T(8,128)(2,1)}, u32[]{:S(2)}) copy-start(bf16[128,256]{1,0:T(8,128)(2,1)} %pad.13.w_in_ref) | copy-start | bytes 196612
  95.2 44.8 %copy-start.9 = (f32[256]{0:T(256)S(1)}, f32[256]{0:T(256)}, u32[]{:S(2)}) copy-start(f32[256]{0:T(256)} %param.13) | copy-start | bytes 3076
  99.8 40.3 %copy-start.4 = (bf16[4,256,256]{2,1,0:T(8,128)(2,1)S(1)}, bf16[4,256,256]{2,1,0:T(8,128)(2,1)}, u32[]{:S(2)}) copy-start(bf16[4,256,256]{2,1,0:T(8,128)(2,1)} %w_hid_ref.1) | copy-start | bytes 1572868
  188.3 34.6 %copy-start.1 = (f32[90,45,8,7,2]{0,4,3,2,1:T(2,128)S(1)}, f32[90,45,8,7,2]{0,4,3,2,1:T(2,128)}, u32[]{:S(2)}) copy-start(f32[90,45,8,7,2]{0,4,3,2,1:T(2,128)} %param.9) | copy-start | bytes 5443204
  188.3 34.6 %copy-start.8 = (s32[2]{0:T(128)S(1)}, s32[2]{0:T(128)}, u32[]{:S(2)}) copy-start(s32[2]{0:T(128)} %pad_add_fusion.at_ref) | copy-start | bytes 28
  192.0 30.9 %copy-start.5 = (bf16[8,224,128]{2,1,0:T(8,128)(2,1)S(1)}, bf16[8,224,128]{2,1,0:T(8,128)(2,1)}, u32[]{:S(2)}) copy-start(bf16[8,224,128]{2,1,0:T(8,128)(2,1)} %constant.185.clone.maps_ref) | copy-start | bytes 1376260
